TPU v7x, 32 devices: a whole 2x2x4 slice. The times are simulated.
32 devices in a mesh: seq: 16 (over z, x, core), mp: 2 (over y).
Axes of the slice: x: 2, y: 2, z: 4, core: 2. Of those that a mesh axis runs over, the one named last changes fastest.
Arguments:
- inputs: bfloat16 [8192, 768], P('seq')
- cluster_ids: int32 [12, 8192], P('mp', 'seq'), may hold values from 0 to 127, as said below
- norm_one_gain: float32 [768], replicated, may hold values from 0.1 to 1.9
- norm_one_shift: float32 [768], replicated, may hold values from -3 to 3
- query_weight: bfloat16 [768, 768], P(None, 'mp'), may hold values from -1 to 1
- keyval_weight: bfloat16 [768, 2, 768], P(None, None, 'mp'), may hold values from -0.21875 to 0.21875
- out_weight: bfloat16 [768, 768], P('mp'), may hold values from -0.875 to 0.875
- norm_two_gain: float32 [768], replicated, may hold values from 0.1 to 1.9
- norm_two_shift: float32 [768], replicated, may hold values from -3 to 3
- up_weight: bfloat16 [768, 3072], P(None, 'mp'), may hold values from -0.21875 to 0.21875
- up_bias: float32 [3072], P('mp'), may hold values from -3 to 3
- down_weight: bfloat16 [3072, 768], P('mp'), may hold values from -0.109375 to 0.109375
- down_bias: float32 [768], replicated, may hold values from -2 to 2
- cotangent: bfloat16 [8192, 768], P('seq'), may hold values from -6 to 6
- loss_mask: int32 [8192], P('seq'), may hold values 0 or 1
Outputs:
- block_output: bfloat16 [8192, 768], P('seq')
- input_grad: bfloat16 [8192, 768], P('seq')
- norm_one_gain_grad: float32 [768], P('seq')
- norm_one_shift_grad: float32 [768], P('seq')
- query_weight_grad: float32 [768, 768], P('seq', 'mp')
- keyval_weight_grad: float32 [768, 2, 768], P('seq', None, 'mp')
- out_weight_grad: float32 [768, 768], P('mp', 'seq')
- norm_two_gain_grad: float32 [768], P('seq')
- norm_two_shift_grad: float32 [768], P('seq')
- up_weight_grad: float32 [768, 3072], P('seq', 'mp')
- up_bias_grad: float32 [3072], P('mp')
- down_weight_grad: float32 [3072, 768], P('mp', 'seq')
- down_bias_grad: float32 [768], P('seq')
Inputs may be any that keep to these rules, and one draw needn't show every extreme that they name: `cluster_ids`: cluster numbers of one head in one sequence.
All inputs are finite; a program needn't handle non-finite values. No bound on the sum of `loss_mask` on one device may be relied on, other than what follows from the above.
Results may differ from a plain program's by a relative error of at most 0.015.
The roundings to bfloat16 on the way count: a program that leaves them out, or rounds other values in their place, can miss the bound.
Values may be sent and summed in bfloat16 or wider, within the bound.
No kernel may reach another device: no remote copies, remote signals or barrier semaphores. Data moves between devices by JAX's collectives and lax.ppermute only.
A program may use at most 192 MiB of HBM per device.

v0:
```python
import jax
import jax.numpy as jnp
from jax import lax
from jax.sharding import PartitionSpec as P

HD = 64
C = 128
SEQS = 4


highest = lax.Precision.HIGHEST
epsilon = 1e-05


def layer_norm(values, gain_vector, shift_vector):
    row_mean = jnp.mean(values, axis=-1, keepdims=True)
    centred = values - row_mean
    spread = jnp.mean(centred * centred, axis=-1, keepdims=True)
    return centred * lax.rsqrt(spread + epsilon) * gain_vector + shift_vector


def exact_gelu(values):
    return jax.nn.gelu(values, approximate=False)


def on_device(
    inputs,
    cluster_ids,
    norm_one_gain,
    norm_one_shift,
    query_weight,
    keyval_weight,
    out_weight,
    norm_two_gain,
    norm_two_shift,
    up_weight,
    up_bias,
    down_weight,
    down_bias,
    cotangent,
    loss_mask,
):
    local_heads = cluster_ids.shape[0]
    tok_rows = inputs.shape[0]
    local_width = query_weight.shape[1]
    groups = SEQS
    segment = tok_rows // groups
    clusters = C
    score_scale = HD ** (-0.5)
    input_float = inputs.astype(jnp.float32)
    normed_one = layer_norm(input_float, norm_one_gain, norm_one_shift).astype(jnp.bfloat16)
    queries = jnp.dot(normed_one, query_weight, preferred_element_type=jnp.float32)
    key_value = jnp.einsum(
        "td,dkf->tkf", normed_one, keyval_weight, preferred_element_type=jnp.float32
    ).astype(jnp.bfloat16)
    keys_local = key_value[:, 0].reshape(groups, segment, local_heads, HD)
    values_local = key_value[:, 1].reshape(groups, segment, local_heads, HD)
    labels = cluster_ids.reshape(local_heads, groups, segment)
    member = (labels[..., None] == jnp.arange(clusters, dtype=jnp.int32)).astype(jnp.float32)
    query_blocks = queries.reshape(groups, segment, local_heads, HD)
    partial_sums = jnp.einsum("hsjc,sjhe->cshe", member, query_blocks, precision=highest)
    partial_counts = jnp.sum(member, axis=2).transpose(1, 0, 2)
    owned_sums, owned_counts = (
        lax.psum_scatter(partial_sums, "seq", scatter_dimension=0, tiled=True),
        lax.psum_scatter(partial_counts, "seq", scatter_dimension=2, tiled=True),
    )
    owned_centroid = owned_sums / jnp.maximum(owned_counts, 1.0).transpose(2, 0, 1)[..., None]
    owned_rounded = owned_centroid.astype(jnp.bfloat16)
    owned = owned_rounded.shape[0]
    key_rows = key_value[:, 0].reshape(groups, segment, local_width).swapaxes(0, 1)
    value_rows = key_value[:, 1].reshape(groups, segment, local_width).swapaxes(0, 1)
    key_block = lax.all_gather(key_rows, "seq", axis=0, tiled=True)
    value_block = lax.all_gather(value_rows, "seq", axis=0, tiled=True)
    row_count = key_block.shape[0]
    key_block = key_block.reshape(row_count, groups, local_heads, HD)
    value_block = value_block.reshape(row_count, groups, local_heads, HD)
    block_scores = (
        jnp.einsum("cshe,jshe->shjc", owned_rounded, key_block, preferred_element_type=jnp.float32)
        * score_scale
    )
    run_max = jnp.full((groups, local_heads, owned), -1e30, jnp.float32)
    new_max = jnp.maximum(run_max, jnp.max(block_scores, axis=2))
    block_weights = jnp.exp(block_scores - new_max[:, :, None, :])
    new_total = jnp.sum(block_weights, axis=2)
    new_out = jnp.einsum(
        "shjc,jshe->cshe", block_weights, value_block.astype(jnp.float32), precision=highest
    )
    owned_out = new_out / new_total.transpose(2, 0, 1)[..., None]
    owned_log = new_max + jnp.log(new_total)
    centroid_out, centroid, log_total, counts = (
        lax.all_gather(owned_out, "seq", axis=0, tiled=True),
        lax.all_gather(owned_centroid, "seq", axis=0, tiled=True),
        lax.all_gather(owned_log, "seq", axis=2, tiled=True),
        lax.all_gather(owned_counts, "seq", axis=2, tiled=True),
    )
    rounded_centroid = centroid.astype(jnp.bfloat16)
    out_rounded = centroid_out.astype(jnp.bfloat16)
    member_low = member.astype(jnp.bfloat16)
    attended = (
        jnp.einsum("hsjc,cshe->sjhe", member_low, out_rounded, preferred_element_type=jnp.float32)
        .astype(jnp.bfloat16)
        .reshape(tok_rows, local_width)
    )
    mixed = lax.psum(
        jnp.dot(attended, out_weight, preferred_element_type=jnp.float32).astype(jnp.bfloat16), "mp"
    ).astype(jnp.float32)
    residual = input_float + mixed
    normed_two = layer_norm(residual, norm_two_gain, norm_two_shift).astype(jnp.bfloat16)
    hidden_pre = jnp.dot(normed_two, up_weight, preferred_element_type=jnp.float32) + up_bias
    activated = exact_gelu(hidden_pre).astype(jnp.bfloat16)
    down_part = jnp.dot(activated, down_weight, preferred_element_type=jnp.float32)
    branch = lax.psum(down_part.astype(jnp.bfloat16), "mp").astype(jnp.float32) + down_bias
    block_output = (residual + branch).astype(jnp.bfloat16)
    output_grad = cotangent.astype(jnp.float32) * loss_mask.astype(jnp.float32)[:, None]
    branch_grad = output_grad.astype(jnp.bfloat16)
    down_bias_part = jnp.sum(branch_grad.astype(jnp.float32), axis=0)
    down_weight_part = jnp.einsum(
        "tf,td->fd", activated, branch_grad, preferred_element_type=jnp.float32
    )
    act_grad = jnp.einsum("td,fd->tf", branch_grad, down_weight, preferred_element_type=jnp.float32)
    unused_value, gelu_pull = jax.vjp(exact_gelu, hidden_pre)
    hidden_grad = gelu_pull(act_grad)[0].astype(jnp.bfloat16)
    up_bias_part = jnp.sum(hidden_grad.astype(jnp.float32), axis=0)
    up_weight_part = jnp.einsum(
        "td,tf->df", normed_two, hidden_grad, preferred_element_type=jnp.float32
    )
    normed_two_grad = lax.psum(
        jnp.einsum("tf,df->td", hidden_grad, up_weight, preferred_element_type=jnp.float32).astype(
            jnp.bfloat16
        ),
        "mp",
    ).astype(jnp.float32)
    unused_norm, norm_two_pull = jax.vjp(layer_norm, residual, norm_two_gain, norm_two_shift)
    residual_part, norm_two_gain_part, norm_two_shift_part = norm_two_pull(normed_two_grad)
    residual_grad = output_grad + residual_part
    mixed_grad = residual_grad.astype(jnp.bfloat16)
    out_weight_part = jnp.einsum(
        "tf,td->fd", attended, mixed_grad, preferred_element_type=jnp.float32
    )
    attended_grad = jnp.einsum(
        "td,fd->tf", mixed_grad, out_weight, preferred_element_type=jnp.float32
    ).reshape(groups, segment, local_heads, HD)
    out_part = jnp.einsum("hsjc,sjhe->cshe", member, attended_grad, precision=highest)
    cluster_grad = lax.psum(out_part, "seq").astype(jnp.bfloat16)
    grad_float = cluster_grad.astype(jnp.float32)
    scores_again = (
        jnp.einsum(
            "cshe,sjhe->shjc", rounded_centroid, keys_local, preferred_element_type=jnp.float32
        )
        * score_scale
    )
    probability = jnp.exp(scores_again - log_total[:, :, None, :])
    prob_grad = jnp.einsum(
        "cshe,sjhe->shjc", grad_float, values_local.astype(jnp.float32), precision=highest
    )
    dot_terms = jnp.sum(grad_float * centroid_out, axis=3).transpose(1, 2, 0)
    score_grad = probability * (prob_grad - dot_terms[:, :, None, :]) * score_scale
    centroid_part = jnp.einsum(
        "shjc,sjhe->cshe", score_grad, keys_local.astype(jnp.float32), precision=highest
    )
    key_grad = jnp.einsum(
        "shjc,cshe->sjhe", score_grad, rounded_centroid.astype(jnp.float32), precision=highest
    )
    value_grad = jnp.einsum("shjc,cshe->sjhe", probability, grad_float, precision=highest)
    centroid_grad, up_bias_grad = lax.psum((centroid_part, up_bias_part), "seq")
    sum_grad = centroid_grad / jnp.maximum(counts, 1.0).transpose(2, 0, 1)[..., None]
    query_grad = (
        jnp.einsum("hsjc,cshe->sjhe", member, sum_grad, precision=highest)
        .reshape(tok_rows, local_width)
        .astype(jnp.bfloat16)
    )
    pair_grad = jnp.stack(
        [key_grad.reshape(tok_rows, local_width), value_grad.reshape(tok_rows, local_width)], axis=1
    ).astype(jnp.bfloat16)
    normed_one_part = jnp.einsum(
        "tf,df->td", query_grad, query_weight, preferred_element_type=jnp.float32
    )
    normed_one_part = normed_one_part + jnp.einsum(
        "tkf,dkf->td", pair_grad, keyval_weight, preferred_element_type=jnp.float32
    )
    normed_one_grad = lax.psum(normed_one_part.astype(jnp.bfloat16), "mp").astype(jnp.float32)
    unused_first, norm_one_pull = jax.vjp(layer_norm, input_float, norm_one_gain, norm_one_shift)
    input_part, norm_one_gain_part, norm_one_shift_part = norm_one_pull(normed_one_grad)
    input_grad = (residual_grad + input_part).astype(jnp.bfloat16)
    query_weight_part = jnp.einsum(
        "td,tf->df", normed_one, query_grad, preferred_element_type=jnp.float32
    )
    keyval_weight_part = jnp.einsum(
        "td,tkf->dkf", normed_one, pair_grad, preferred_element_type=jnp.float32
    )
    summed_grads = (
        lax.psum_scatter(norm_one_gain_part, "seq", scatter_dimension=0, tiled=True),
        lax.psum_scatter(norm_one_shift_part, "seq", scatter_dimension=0, tiled=True),
        lax.psum_scatter(query_weight_part, "seq", scatter_dimension=0, tiled=True),
        lax.psum_scatter(keyval_weight_part, "seq", scatter_dimension=0, tiled=True),
        lax.psum_scatter(out_weight_part, "seq", scatter_dimension=1, tiled=True),
        lax.psum_scatter(norm_two_gain_part, "seq", scatter_dimension=0, tiled=True),
        lax.psum_scatter(norm_two_shift_part, "seq", scatter_dimension=0, tiled=True),
        lax.psum_scatter(up_weight_part, "seq", scatter_dimension=0, tiled=True),
        lax.psum_scatter(down_weight_part, "seq", scatter_dimension=1, tiled=True),
        lax.psum_scatter(down_bias_part, "seq", scatter_dimension=0, tiled=True),
    )
    return (
        block_output,
        input_grad,
        summed_grads[0],
        summed_grads[1],
        summed_grads[2],
        summed_grads[3],
        summed_grads[4],
        summed_grads[5],
        summed_grads[6],
        summed_grads[7],
        up_bias_grad,
        summed_grads[8],
        summed_grads[9],
    )


def solution(mesh):
    placed = (
        P("seq", None),
        P("mp", "seq"),
        P(),
        P(),
        P(None, "mp"),
        P(None, None, "mp"),
        P("mp", None),
        P(),
        P(),
        P(None, "mp"),
        P("mp"),
        P("mp", None),
        P(),
        P("seq", None),
        P("seq"),
    )
    return jax.shard_map(
        on_device,
        mesh=mesh,
        in_specs=placed,
        out_specs=(
            P("seq", None),
            P("seq", None),
            P("seq"),
            P("seq"),
            P("seq", "mp"),
            P("seq", None, "mp"),
            P("mp", "seq"),
            P("seq"),
            P("seq"),
            P("seq", "mp"),
            P("mp"),
            P("mp", "seq"),
            P("seq"),
        ),
        check_vma=False,
    )
```

profile of v0, /device:TPU:0, one launch (start us, length us, event | category | flops | bytes accessed | tf_op | source)
XLA Modules:
  0.0 987.3 jit_solution(8222940301387594740)
XLA Ops:
  7.3 1.5 convert_reduce_fusion.3
  8.8 1.5 fusion.17
  10.9 1.6 fusion.88
  12.5 2.3 reshape.121
  14.8 3.1 fusion.30
  17.9 2.5 copy.176
  20.4 2.2 convolution_convert_fusion
  26.3 63.4 %all-reduce.1 = f32[4,6,128]{2,1,0:T(8,128)S(1)} all-reduce(f32[4,6,128]{2,1,0:T(8,128)S(1)} %bitcast.115), channel_id=3, replica_groups=mesh['seq'=16,'mp'=2] {'seq'}, use_global_device_ids=true, to_apply=%region_4.0.clone | all-reduce | flops 3072 | bytes 24576
  90.5 28.1 %all-reduce.22.cloned.1.call-done = f32[128,4,6,64]{3,1,2,0:T(4,128)} async-done(((f32[128,4,6,64]{3,1,2,0:T(4,128)}), f32[128,4,6,64]{3,1,2,0:T(4,128)}) %all-reduce.22.cloned.1.call-update) | async-done | bytes 786448
  119.7 62.1 %all-gather.5.cloned.1.call-done = bf16[2048,4,384]{2,0,1:T(8,128)(2,1)} async-done(((bf16[128,4,384]{2,0,1:T(8,128)(2,1)}), bf16[2048,4,384]{2,0,1:T(8,128)(2,1)}) %all-gather.5.cloned.1.call-update) | async-done | bytes 6291472 | tf_op jit(solution)/shard_map/all_gather | solution.py:72
  181.8 8.7 copy.172
  190.5 3.9 fusion.94
  196.0 48.7 %all-gather.3.cloned.1.call-done = bf16[2048,4,384]{2,0,1:T(8,128)(2,1)} async-done(((bf16[128,4,384]{2,0,1:T(8,128)(2,1)}), bf16[2048,4,384]{2,0,1:T(8,128)(2,1)}) %all-gather.3.cloned.1.call-update) | async-done | bytes 6291472 | tf_op jit(solution)/shard_map/all_gather | solution.py:73
  244.7 8.7 copy.171
  253.3 7.3 fusion.38
  260.7 26.5 %all_gather.20 = f32[128,4,6,64]{3,1,2,0:T(4,128)} all-gather(f32[8,4,6,64]{3,1,2,0:T(4,128)S(1)} %copy.179), channel_id=1, replica_groups=mesh['seq'=16,'mp'=2] {'seq'}, dimensions={0}, use_global_device_ids=true | all-gather | bytes 835584 | tf_op jit(solution)/shard_map/all_gather | solution.py:91
  287.2 2.4 copy.180
  289.7 1.9 fusion.35
  292.6 1.5 convolution_convert_fusion.3
  294.2 1.9 copy.182
  298.4 1.8 reshape_squeeze.14
  300.2 1.8 reshape_squeeze.15
  302.2 19.0 %all_gather.23 = f32[4,6,128]{1,0,2:T(4,128)S(1)} all-gather(f32[4,6,8]{1,0,2:T(4,128)S(1)} %copy.193), channel_id=1, replica_groups=mesh['seq'=16,'mp'=2] {'seq'}, dimensions={2}, use_global_device_ids=true | all-gather | bytes 13056 | tf_op jit(solution)/shard_map/all_gather | solution.py:94
  322.0 21.6 %all_gather.21 = bf16[128,4,6,64]{3,1,2,0:T(4,128)(2,1)} all-gather(bf16[8,4,6,64]{3,1,2,0:T(4,128)(2,1)S(1)} %copy-done.27), channel_id=1, replica_groups=mesh['seq'=16,'mp'=2] {'seq'}, dimensions={0}, use_global_device_ids=true | all-gather | bytes 417792 | tf_op jit(solution)/shard_map/all_gather | solution.py:92
  343.6 1.4 copy.183
  345.1 1.6 fusion.29
  347.8 9.1 multiply_convert_fusion
  356.9 2.9 convert_reduce_fusion
  361.0 2.3 convolution_convert_fusion.1
  363.4 1.4 log_add_fusion
  364.7 1.4 copy.185
  366.1 21.2 %all_gather.22 = f32[4,6,128]{1,0,2:T(4,128)} all-gather(f32[4,6,8]{1,0,2:T(4,128)} %copy.185), channel_id=1, replica_groups=mesh['seq'=16,'mp'=2] {'seq'}, dimensions={2}, use_global_device_ids=true | all-gather | bytes 13056 | tf_op jit(solution)/shard_map/all_gather | solution.py:93
  387.3 1.7 copy.186
  389.0 2.8 subtract_exponential_fusion
  391.7 3.9 convolution_convert_fusion.2
  396.0 2.9 fusion.19
  401.9 1.4 fusion.95
  403.3 2.3 reshape.123
  405.6 3.1 fusion.31
  408.7 70.1 %all-reduce.25 = bf16[128,4,6,64]{0,3,2,1:T(8,128)(2,1)S(1)} all-reduce(f32[128,4,6,64]{0,3,2,1:T(8,128)} %fusion.31), channel_id=1, replica_groups=mesh['seq'=16,'mp'=2] {'seq'}, use_global_device_ids=true, to_apply=%region_14.0 | all-reduce | flops 196608 | bytes 1179648 | tf_op jit(solution)/shard_map/psum | solution.py:144
  480.1 2.0 multiply_multiply_fusion.5
  482.1 2.4 fusion.33
  484.5 1.8 convolution_bitcast_fusion
  486.6 3.9 fusion.34
  491.6 1.9 stack_reshape.8
  493.5 1.9 copy.198
  498.6 3.5 fusion.39
  502.1 72.7 %all-reduce.20.cloned.1.call-done = f32[128,4,6,64]{0,3,2,1:T(8,128)} async-done(((f32[128,4,6,64]{0,3,2,1:T(8,128)}), f32[128,4,6,64]{0,3,2,1:T(8,128)}) %all-reduce.20.cloned.1.call-update) | async-done | bytes 786448 | tf_op jit(solution)/shard_map/psum | solution.py:165
  574.8 3.0 fusion.36
  578.9 1.5 fusion.21
  581.4 3.4 fusion.44
  585.9 2.8 fusion.58
  588.8 2.9 fusion.55
  591.8 5.5 fusion.85
  597.9 5.3 fusion.79
  603.9 27.3 %all-reduce.24.cloned.1.call-done = (bf16[512,768]{1,0:T(8,128)(2,1)}, bf16[512,768]{1,0:T(8,128)(2,1)}) async-done(((bf16[512,768]{1,0:T(8,128)(2,1)}, bf16[512,768]{1,0:T(8,128)(2,1)}), (bf16[512,768]{1,0:T(8,128)(2,1)}, bf16[512,768]{1,0:T(8,128)(2,1)})) %all-reduce.24.cloned.1.call-update) | async-done | bytes 1572880 | tf_op jit(solution)/shard_map/psum | solution.py:112
  631.3 1.8 convert_reduce_fusion.1
  634.0 61.6 %all-reduce.7 = (f32[768]{0:T(1024)S(1)}, f32[768]{0:T(1024)S(1)}, f32[768]{0:T(1024)S(1)}, f32[768]{0:T(1024)S(1)}, f32[1536]{0:T(1024)}, /*index=5*/f32[768]{0:T(1024)S(1)}) all-reduce(f32[768]{0:T(1024)S(1)} %get-tuple-element.93, f32[768]{0:T(1024)S(1)} %get-tuple-element.96, ...), channel_id=4, replica_groups=mesh['seq'=16,'mp'=2] {'seq'}, use_global_device_ids=true, to_apply=%region_21.0.clone | all-reduce | flops 5376 | bytes 43008
  698.6 3.7 add_convert_fusion.1
  702.3 1.6 copy.202
  703.9 55.9 %reduce-scatter.11.cloned.1.call-done = f32[384,48]{0,1:T(8,128)} async-done(((f32[384,768]{0,1:T(8,128)}), f32[384,48]{0,1:T(8,128)}) %reduce-scatter.11.cloned.1.call-update) | async-done | bytes 73744 | tf_op jit(solution)/shard_map/reduce_scatter | solution.py:196
  759.9 61.7 %reduce-scatter.7.cloned.1.call-done = f32[48,384]{1,0:T(8,128)} async-done(((f32[768,384]{1,0:T(8,128)}), f32[48,384]{1,0:T(8,128)}) %reduce-scatter.7.cloned.1.call-update) | async-done | bytes 73744 | tf_op jit(solution)/shard_map/reduce_scatter | solution.py:194
  821.6 79.5 %reduce-scatter.13.cloned.1.call-done = f32[48,1536]{1,0:T(8,128)} async-done(((f32[768,1536]{1,0:T(8,128)}), f32[48,1536]{1,0:T(8,128)}) %reduce-scatter.13.cloned.1.call-update) | async-done | bytes 294928 | tf_op jit(solution)/shard_map/reduce_scatter | solution.py:199
  901.1 78.9 %reduce-scatter.15.cloned.1.call-done = f32[1536,48]{0,1:T(8,128)} async-done(((f32[1536,768]{0,1:T(8,128)}), f32[1536,48]{0,1:T(8,128)}) %reduce-scatter.15.cloned.1.call-update) | async-done | bytes 294928 | tf_op jit(solution)/shard_map/reduce_scatter | solution.py:200
  (207 shorter events, 30.5 us)
Async XLA Ops:
  7.2 340.5 %copy-start = (bf16[768,1536]{1,0:T(8,128)(2,1)S(1)}, bf16[768,1536]{1,0:T(8,128)(2,1)}, u32[]{:S(2)}) copy-start(bf16[768,1536]{1,0:T(8,128)(2,1)} %param.24) | copy-start | bytes 7077892
  7.2 3.7 copy-start.1
  7.2 3.7 copy-start.35
  7.2 3.6 copy-start.65
  7.2 111.4 %all-reduce.22.cloned.1.call-start = ((), (), s32[]{:S(2)}) async-start(), calls=%async_computation.15 | async-start | bytes 3145728
  7.3 3.6 copy-start.22
  8.8 11.7 %copy-start.33 = (f32[512]{0:T(512)}, f32[512]{0:T(512)S(1)}, u32[]{:S(2)}) copy-start(f32[512]{0:T(512)S(1)} %broadcast_multiply_fusion.1) | copy-start | bytes 6148
  10.9 9.5 copy-start.43
  12.5 2.3 copy-start.29
  20.4 161.5 %all-gather.5.cloned.1.call-start = ((), (), s32[]{:S(2)}) async-start(), calls=%async_computation.6 | async-start | bytes 6684672 | tf_op jit(solution)/shard_map/all_gather | solution.py:72
  22.6 1.8 copy-start.69
  23.7 221.0 %all-gather.3.cloned.1.call-start = ((), (), s32[]{:S(2)}) async-start(), calls=%async_computation.5 | async-start | bytes 6684672 | tf_op jit(solution)/shard_map/all_gather | solution.py:73
  24.4 320.6 %all-reduce.16.cloned.1.call-start = ((), (), s32[]{:S(2)}) async-start(), calls=%async_computation.7 | async-start | bytes 1572864 | tf_op jit(solution)/shard_map/psum | solution.py:104
  119.7 70.8 %copy-start.26 = (bf16[8,4,6,64]{3,1,2,0:T(4,128)(2,1)}, bf16[8,4,6,64]{3,1,2,0:T(4,128)(2,1)S(1)}, u32[]{:S(2)}) copy-start(bf16[8,4,6,64]{3,1,2,0:T(4,128)(2,1)S(1)} %dynamic-slice_divide_fusion) | copy-start | bytes 73732
  194.4 58.9 %copy-start.31 = (f32[4,6,8]{2,1,0:T(8,128)}, f32[4,6,8]{2,1,0:T(8,128)S(1)}, u32[]{:S(2)}) copy-start(f32[4,6,8]{2,1,0:T(8,128)S(1)} %get-tuple-element.118) | copy-start | bytes 2308
  196.0 57.4 %copy-start.30 = (f32[4,6,8]{2,1,0:T(8,128)}, f32[4,6,8]{2,1,0:T(8,128)S(1)}, u32[]{:S(2)}) copy-start(f32[4,6,8]{2,1,0:T(8,128)S(1)} %fusion.26) | copy-start | bytes 2308
  289.7 3.0 copy-start.24
  292.6 3.5 copy-start.12
  294.1 101.9 %all-reduce.18.cloned.1.call-start = ((), (), s32[]{:S(2)}) async-start(), calls=%async_computation.8 | async-start | bytes 1572864 | tf_op jit(solution)/shard_map/psum | solution.py:127
  297.1 5.0 copy-start.32
  297.1 24.9 %copy-start.27 = (bf16[8,4,6,64]{3,1,2,0:T(4,128)(2,1)S(1)}, bf16[8,4,6,64]{3,1,2,0:T(4,128)(2,1)}, u32[]{:S(2)}) copy-start(bf16[8,4,6,64]{3,1,2,0:T(4,128)(2,1)} %copy-done.26) | copy-start | bytes 73732
  345.0 44.0 %copy-start.10 = (bf16[128,4,6,64]{0,3,2,1:T(8,128)(2,1)}, bf16[128,4,6,64]{0,3,2,1:T(8,128)(2,1)S(1)}, u32[]{:S(2)}) copy-start(bf16[128,4,6,64]{0,3,2,1:T(8,128)(2,1)S(1)} %copy.183) | copy-start | bytes 1179652
  345.1 2.6 copy-start.54
  345.1 2.6 copy-start.64
  345.1 2.6 copy-start.67
  346.7 10.2 %copy-start.40 = (f32[512]{0:T(512)}, f32[512]{0:T(512)S(1)}, u32[]{:S(2)}) copy-start(f32[512]{0:T(512)S(1)} %broadcast_multiply_fusion) | copy-start | bytes 6148
  347.7 9.2 copy-start.51
  347.7 9.2 copy-start.6
  347.7 9.2 copy-start.37
  347.8 9.2 copy-start.63
  363.3 211.5 %all-reduce.20.cloned.1.call-start = ((), (), s32[]{:S(2)}) async-start(), calls=%async_computation.9 | async-start | bytes 1572864 | tf_op jit(solution)/shard_map/psum | solution.py:165
  389.0 2.8 copy-start.15
  391.7 4.3 copy-start.41
  391.7 4.3 copy-start.52
  391.7 4.3 copy-start.55
  395.7 3.2 copy-start.50
  396.0 2.9 copy-start.3
  396.0 2.9 copy-start.14
  400.1 1.8 copy-start.25
  480.1 2.0 copy-start.11
  482.1 2.4 copy-start.13
  486.3 144.9 %all-reduce.24.cloned.1.call-start = ((), (), s32[]{:S(2)}) async-start(), calls=%async_computation.16 | async-start | bytes 3145728 | tf_op jit(solution)/shard_map/psum | solution.py:112
  486.6 3.9 copy-start.20
  490.5 4.9 copy-start.21
  498.6 76.2 %copy-start.60 = (f32[128,4,6]{0,2,1:T(8,128)S(1)}, f32[128,4,6]{0,2,1:T(8,128)}, u32[]{:S(2)}) copy-start(f32[128,4,6]{0,2,1:T(8,128)} %copy.194) | copy-start | bytes 36868
  574.8 4.1 copy-start.16
  574.8 4.1 copy-start.23
  580.5 121.8 %reduce-scatter.9.cloned.1.call-start = ((), (), s32[]{:S(2)}) async-start(), calls=%async_computation.11 | async-start | bytes 2506752 | tf_op jit(solution)/shard_map/reduce_scatter | solution.py:195
  584.8 175.0 %reduce-scatter.11.cloned.1.call-start = ((), (), s32[]{:S(2)}) async-start(), calls=%async_computation.12 | async-start | bytes 1253376 | tf_op jit(solution)/shard_map/reduce_scatter | solution.py:196
  588.7 3.0 copy-start.42
  588.7 3.0 copy-start.53
  588.7 3.0 copy-start.56
  588.7 3.0 copy-start.68
  588.7 232.8 %reduce-scatter.7.cloned.1.call-start = ((), (), s32[]{:S(2)}) async-start(), calls=%async_computation.10 | async-start | bytes 1253376 | tf_op jit(solution)/shard_map/reduce_scatter | solution.py:194
  591.7 309.4 %reduce-scatter.13.cloned.1.call-start = ((), (), s32[]{:S(2)}) async-start(), calls=%async_computation.13 | async-start | bytes 5013504 | tf_op jit(solution)/shard_map/reduce_scatter | solution.py:199
  597.3 382.7 %reduce-scatter.15.cloned.1.call-start = ((), (), s32[]{:S(2)}) async-start(), calls=%async_computation.14 | async-start | bytes 5013504 | tf_op jit(solution)/shard_map/reduce_scatter | solution.py:200
  603.3 29.8 %copy-start.48 = (f32[512]{0:T(512)S(1)}, f32[512]{0:T(512)}, u32[]{:S(2)}) copy-start(f32[512]{0:T(512)} %copy-done.47) | copy-start | bytes 6148
  631.2 1.8 copy-start.8
  631.2 2.8 copy-start.57
  631.2 2.8 copy-start.58
  631.3 2.8 copy-start.59
  631.3 2.8 copy-start.61
  631.3 67.3 %copy-start.46 = (f32[512]{0:T(512)S(1)}, f32[512]{0:T(512)}, u32[]{:S(2)}) copy-start(f32[512]{0:T(512)} %copy-done.45) | copy-start | bytes 6148
  631.3 67.3 %copy-start.62 = (f32[768]{0:T(1024)S(1)}, f32[768]{0:T(1024)}, u32[]{:S(2)}) copy-start(f32[768]{0:T(1024)} %param.27) | copy-start | bytes 9220
  (19 other events, 18.9 us)
Sparse Core Ops, SparseCore 0:
  20.5 98.1 all-reduce.21
  120.9 60.8 all-gather.4
  184.1 60.5 all-gather.2
  294.3 32.1 all-reduce.15
  363.4 32.5 all-reduce.17
  486.4 88.3 all-reduce.19
  580.6 50.6 all-reduce.23
  635.0 63.0 reduce-scatter.8
  702.7 57.0 reduce-scatter.10
  764.3 57.1 reduce-scatter.6
  826.5 74.5 reduce-scatter.12
  905.4 74.5 reduce-scatter.14
where the time goes:
time: 997 us; the launch traced here: 987 us
  waiting for transfers between devices  516 us (52%)
  blocking collectives  283 us (28%)
  matrix products  85 us (9%)
  local copies, waits for them, and re-layouts  62.3 us (6%)
  other arithmetic  22.5 us (2%)
  between operations  16.7 us (2%)
    unnamed x2, blocking collectives  125 us
    reduce_scatter x1, waiting for transfers between devices, on_device(): lax.psum_scatter(up_weight_part, 'seq', scatter_dimension=0, tiled=True)  79.5 us
    reduce_scatter x1, waiting for transfers between devices, on_device(): lax.psum_scatter(down_weight_part, 'seq', scatter_dimension=1, tiled=True)  78.9 us
    psum x1, waiting for transfers between devices, on_device(): centroid_grad, up_bias_grad = lax.psum((centroid_part, up_bias_part), 'seq')  72.7 us
    psum x1, blocking collectives, on_device(): cluster_grad = lax.psum(out_part, 'seq').astype(jnp.bfloat16)  70.1 us
    all_gather x1, waiting for transfers between devices, on_device(): key_block = lax.all_gather(key_rows, 'seq', axis=0, tiled=True)  62.1 us
    reduce_scatter x1, waiting for transfers between devices, on_device(): lax.psum_scatter(query_weight_part, 'seq', scatter_dimension=0, tiled=True)  61.7 us
    reduce_scatter x1, waiting for transfers between devices, on_device(): lax.psum_scatter(out_weight_part, 'seq', scatter_dimension=1, tiled=True)  55.9 us
  transfers between devices with their start and end apart: 12, of which 10 were waited for; matrix products, arithmetic and copies ran while one was open for 9% of the time, Pallas kernels for 0%

commit v1 on v0

v1 whole, which is shorter than its diff:
```python
import functools

import jax
import jax.numpy as jnp
from jax import lax
from jax.experimental import pallas as pl
from jax.experimental.pallas import tpu as pltpu
from jax.sharding import Mesh, PartitionSpec as P

HD = 64
C = 128
SEQS = 4
SUB = 8
EPS = 1e-05
SCALE = HD ** (-0.5)
F32 = jnp.float32
BF16 = jnp.bfloat16
NEAR = ("b2", "b1", "b0")
SEQ = ("g",) + NEAR
PAIRS = ((0, 1), (2, 3), (4, 5))
SWAP = [(0, 1), (1, 0)]


def dot_nn(a, b):
    return lax.dot_general(a, b, (((1,), (0,)), ((), ())), preferred_element_type=F32)


def dot_nt(a, b):
    return lax.dot_general(a, b, (((1,), (1,)), ((), ())), preferred_element_type=F32)


def dot_tn(a, b):
    return lax.dot_general(a, b, (((0,), (0,)), ((), ())), preferred_element_type=F32)


def call(kernel, outs, *args, scratch=(), flops=0, vmem=None, name=None, aliases=None, specs=None):
    moved = sum(a.size * a.dtype.itemsize for a in args) + sum(
        functools.reduce(lambda p, q: p * q, s, 1) * jnp.dtype(d).itemsize for s, d in outs
    )
    extra = {}
    if specs is not None:
        extra["in_specs"], extra["out_specs"] = specs
        extra["grid"] = (1,)
    return pl.pallas_call(
        kernel,
        out_shape=[jax.ShapeDtypeStruct(s, d) for s, d in outs],
        scratch_shapes=list(scratch),
        compiler_params=pltpu.CompilerParams(vmem_limit_bytes=vmem or 32 * 2**20),
        cost_estimate=pl.CostEstimate(flops=flops, bytes_accessed=moved, transcendentals=0),
        input_output_aliases=aliases or {},
        name=name,
        **extra,
    )(*args)


def left_half(shape):
    return lax.broadcasted_iota(jnp.int32, shape, 1) < HD


def roll_half(v):
    return pltpu.roll(v, HD, 1)


def normalise(v):
    centred = v - jnp.mean(v, axis=1, keepdims=True)
    inverse = lax.rsqrt(jnp.mean(centred * centred, axis=1, keepdims=True) + EPS)
    return centred * inverse, inverse


def norm_pull(unit, inverse, scaled_grad):
    return inverse * (
        scaled_grad
        - jnp.mean(scaled_grad, axis=1, keepdims=True)
        - unit * jnp.mean(scaled_grad * unit, axis=1, keepdims=True)
    )


def split(v):
    high = v.astype(BF16)
    low = (v - high.astype(F32)).astype(BF16)
    return high, low


def member_rows(ids_ref, head, start):
    row = ids_ref[head : head + 1, start : start + C]
    spot = lax.broadcasted_iota(jnp.int32, (C, C), 0)
    return jnp.where(spot == row, 1.0, 0.0).astype(F32)


def member_cols(ids_ref, head, start):
    col = ids_ref[start : start + C, head : head + 1]
    spot = lax.broadcasted_iota(jnp.int32, (C, C), 1)
    return jnp.where(spot == col, 1.0, 0.0).astype(BF16)


def cluster_pair(members, pair):
    high, low = split(pair)
    both = jnp.concatenate([high, low], axis=1)
    sums = []
    for m in members:
        r = dot_nn(m.astype(BF16), both)
        sums.append(r[:, :C] + r[:, C:])
    return jnp.where(left_half((C, C)), sums[0], sums[1])


def spread_pair(ids_ref, heads, start, pair):
    left = left_half((C, C))
    zero = jnp.zeros_like(pair)
    stacked = jnp.concatenate([jnp.where(left, pair, zero), jnp.where(left, zero, pair)], axis=0)
    picks = jnp.concatenate([member_cols(ids_ref, h, start) for h in heads], axis=1)
    return dot_nn(picks, stacked)


def project_kernel(x_ref, gain_ref, shift_ref, wq_ref, wkv_ref, ids_ref, normed_ref, send_ref, q_scr, kv_scr):
    for s in range(SEQS):
        rows = slice(s * C, (s + 1) * C)
        unit, unused = normalise(x_ref[rows, :].astype(F32))
        normed_ref[rows, :] = (unit * gain_ref[...] + shift_ref[...]).astype(BF16)
    width = wq_ref.shape[1]
    q_scr[...] = dot_nn(normed_ref[...], wq_ref[...])
    kv_scr[...] = dot_nn(normed_ref[...], wkv_ref[...]).astype(BF16)
    left = left_half((C, C))
    lane = lax.broadcasted_iota(jnp.int32, (C, C), 1)
    for s in range(SEQS):
        rows = slice(s * C, (s + 1) * C)
        sums, counts = [], []
        for p, heads in enumerate(PAIRS):
            members = [member_rows(ids_ref, h, s * C) for h in heads]
            sums.append(cluster_pair(members, q_scr[rows, p * C : (p + 1) * C]))
            counts += [jnp.sum(m, axis=1, keepdims=True) for m in members]
        keys = [kv_scr[rows, p * C : (p + 1) * C] for p in range(3)]
        values = [kv_scr[rows, width + p * C : width + (p + 1) * C] for p in range(3)]
        for t in range(2):
            full = 2 * t
            order = (0, 1, 2) if t == 0 else (4, 5, 3)
            tail = jnp.zeros((C, C), F32)
            for i, h in enumerate(order):
                tail = jnp.where(lane == HD + i, counts[h], tail)
            single = sums[1] if t == 0 else roll_half(sums[1])
            if t == 0:
                mixed = jnp.where(left, keys[1].astype(F32), roll_half(values[1].astype(F32)))
            else:
                mixed = jnp.where(left, roll_half(keys[1].astype(F32)), values[1].astype(F32))
            o = s * 2 + t
            send_ref[o, :, 0:C] = sums[full].astype(BF16)
            send_ref[o, :, C : 2 * C] = jnp.where(left, single, tail).astype(BF16)
            send_ref[o, :, 2 * C : 3 * C] = keys[full]
            send_ref[o, :, 3 * C : 4 * C] = values[full]
            send_ref[o, :, 4 * C : 5 * C] = mixed.astype(BF16)


def sum_kernel(recv_ref, out_ref):
    total = recv_ref[0].astype(F32)
    for i in range(1, SUB):
        total = total + recv_ref[i].astype(F32)
    out_ref[...] = total


def add_all(refs):
    total = refs[0][...]
    for r in refs[1:]:
        total = total + r[...]
    return total


def centroid_blocks(total):
    left = left_half((C, C))
    pair, tail = total[:, 0:C], total[:, C : 2 * C]
    count = [jnp.maximum(tail[:, HD + i : HD + i + 1], 1.0) for i in range(3)]
    zero = jnp.zeros((C, C), F32)
    pair = pair / jnp.where(left, count[0], count[1])
    single = tail / count[2]
    return (
        jnp.where(left, pair, zero).astype(BF16),
        jnp.where(left, zero, pair).astype(BF16),
        jnp.where(left, single, zero).astype(BF16),
    )


KEY_LANES = (2 * C, 2 * C, 4 * C)
VALUE_LANES = (3 * C, 3 * C, 4 * C)


def attend_kernel(*refs):
    recv_ref, sums, (part_ref, total_ref) = refs[0], refs[1:-2], refs[-2:]
    total = add_all(sums)
    total_ref[...] = total
    left = left_half((C, C))
    lane = lax.broadcasted_iota(jnp.int32, (C, C), 1)
    length = SUB * C
    outs = []
    stats = jnp.zeros((C, C), F32)
    for i, centroid in enumerate(centroid_blocks(total)):
        k = recv_ref[:, :, KEY_LANES[i] : KEY_LANES[i] + C].reshape(length, C)
        v = recv_ref[:, :, VALUE_LANES[i] : VALUE_LANES[i] + C].reshape(length, C)
        scores = dot_nt(centroid, k) * SCALE
        top = jnp.max(scores, axis=1, keepdims=True)
        weight = jnp.exp(scores - top)
        mass = jnp.sum(weight, axis=1, keepdims=True)
        outs.append(dot_nn(weight.astype(BF16), v))
        stats = jnp.where(lane == i, top, stats)
        stats = jnp.where(lane == 3 + i, mass, stats)
    part_ref[:, 0:C] = jnp.where(left, outs[0], outs[1])
    part_ref[:, C : 2 * C] = jnp.where(left, stats, outs[2])


def merge_kernel(*refs):
    parts, (fin_ref, send_ref) = refs[:-2], refs[-2:]
    left = left_half((C, C))
    lane = lax.broadcasted_iota(jnp.int32, (C, C), 1)
    tails = [r[:, C : 2 * C] for r in parts]
    stats = jnp.zeros((C, C), F32)
    scales = []
    for i in range(3):
        tops = [t[:, i : i + 1] for t in tails]
        top = functools.reduce(jnp.maximum, tops)
        factors = [jnp.exp(v - top) for v in tops]
        mass = sum(t[:, 3 + i : 4 + i] * f for t, f in zip(tails, factors))
        stats = jnp.where(lane == i, top, stats)
        stats = jnp.where(lane == 3 + i, mass, stats)
        scales.append([f / mass for f in factors])
    pair = sum(
        r[:, 0:C] * jnp.where(left, scales[0][j], scales[1][j]) for j, r in enumerate(parts)
    )
    single = sum(t * scales[2][j] for j, t in enumerate(tails))
    fin_ref[:, 0:C] = pair
    fin_ref[:, C : 2 * C] = jnp.where(left, stats, single)
    short = jnp.where(left_half((HD, C)), roll_half(single[0:HD]), single[HD:C])
    for o in range(send_ref.shape[0]):
        send_ref[o, 0:C, :] = pair.astype(BF16)
        send_ref[o, C : C + HD, :] = short.astype(BF16)


def middle_kernel(
    mp_ref, recv_ref, ids_ref, x_ref, wo_ref, wo_other_ref, gain_ref, shift_ref, up_ref, up_bias_ref,
    down_ref, bg_ref, attended_ref, residual_ref, normed_ref, active_ref, hidden_ref, back_ref,
    branch_ref, up_bias_out_ref, a_scr, w_scr,
):
    half = wo_ref.shape[0]
    mine = pl.multiple_of(mp_ref[0] * half, C)
    other = pl.multiple_of((1 - mp_ref[0]) * half, C)
    w_scr[pl.ds(mine, half), :] = wo_ref[...]
    w_scr[pl.ds(other, half), :] = wo_other_ref[...]
    short = left_half((HD, C))
    for s in range(SEQS):
        rows = slice(s * C, (s + 1) * C)
        for m in range(2):
            packs = [recv_ref[(s * 2 + t) * 2 + m] for t in range(2)]
            tails = [v[C : C + HD].astype(F32) for v in packs]
            middle = jnp.concatenate(
                [
                    jnp.where(short, tails[0], roll_half(tails[1])),
                    jnp.where(short, roll_half(tails[0]), tails[1]),
                ],
                axis=0,
            ).astype(BF16)
            for p, pair in enumerate((packs[0][0:C], middle, packs[1][0:C])):
                heads = [m * 6 + h for h in PAIRS[p]]
                a_scr[rows, m * half + p * C : m * half + (p + 1) * C] = spread_pair(
                    ids_ref, heads, s * C, pair
                ).astype(BF16)
    attended_ref[...] = a_scr[:, pl.ds(mine, half)]
    step = 256
    total_bias = jnp.zeros(up_bias_out_ref.shape, F32)
    for n in range(x_ref.shape[0] // step):
        rows = slice(n * step, (n + 1) * step)
        residual = x_ref[rows, :].astype(F32) + dot_nn(a_scr[rows, :], w_scr[...])
        residual_ref[rows, :] = residual
        unit, unused = normalise(residual)
        normed = (unit * gain_ref[...] + shift_ref[...]).astype(BF16)
        normed_ref[rows, :] = normed
        hidden = dot_nn(normed, up_ref[...]) + up_bias_ref[...]
        below = 0.5 * (1.0 + lax.erf(hidden * (0.5**0.5)))
        active_ref[rows, :] = (hidden * below).astype(BF16)
        slope = below + hidden * jnp.exp(-0.5 * hidden * hidden) * 0.3989422804014327
        hidden_grad = (slope * dot_nt(bg_ref[rows, :], down_ref[...])).astype(BF16)
        hidden_ref[rows, :] = hidden_grad
        total_bias = total_bias + jnp.sum(hidden_grad.astype(F32), axis=0, keepdims=True)
        back_ref[rows, :] = dot_nt(hidden_grad, up_ref[...]).astype(BF16)
        branch_ref[rows, :] = dot_nn(active_ref[rows, :], down_ref[...]).astype(BF16)
    up_bias_out_ref[...] = total_bias


def turn_kernel(
    back_ref, back_other_ref, residual_ref, gain_ref, bg_ref, wo_ref, ids_ref, up_bias_ref,
    residual_grad_ref, mixed_ref, send_ref, ag_scr, vec_scr,
):
    gain_sum = jnp.zeros(gain_ref.shape, F32)
    shift_sum = jnp.zeros(gain_ref.shape, F32)
    down_sum = jnp.zeros(gain_ref.shape, F32)
    for s in range(SEQS):
        rows = slice(s * C, (s + 1) * C)
        grad = back_ref[rows, :].astype(F32) + back_other_ref[rows, :].astype(F32)
        unit, inverse = normalise(residual_ref[rows, :])
        out_grad = bg_ref[rows, :].astype(F32)
        gain_sum = gain_sum + jnp.sum(grad * unit, axis=0, keepdims=True)
        shift_sum = shift_sum + jnp.sum(grad, axis=0, keepdims=True)
        down_sum = down_sum + jnp.sum(out_grad, axis=0, keepdims=True)
        residual_grad = out_grad + norm_pull(unit, inverse, grad * gain_ref[...])
        residual_grad_ref[rows, :] = residual_grad
        mixed_ref[rows, :] = residual_grad.astype(BF16)
    ag_scr[...] = dot_nt(mixed_ref[...], wo_ref[...])
    vec_scr[...] = jnp.zeros(vec_scr.shape, F32)
    spot = 0
    for v in (up_bias_ref[...], gain_sum, shift_sum, down_sum):
        for i in range(v.shape[1] // C):
            vec_scr[spot : spot + 1, :] = v[:, i * C : (i + 1) * C]
            spot += 1
    short = left_half((HD, C))
    for s in range(SEQS):
        rows = slice(s * C, (s + 1) * C)
        sums = []
        for p, heads in enumerate(PAIRS):
            members = [member_rows(ids_ref, h, s * C) for h in heads]
            sums.append(cluster_pair(members, ag_scr[rows, p * C : (p + 1) * C]))
        top, bottom = sums[1][0:HD], sums[1][HD:C]
        singles = (
            jnp.where(short, top, roll_half(bottom)),
            jnp.where(short, roll_half(top), bottom),
        )
        for t in range(2):
            o = s * 2 + t
            send_ref[o, 0:C, :] = sums[2 * t].astype(BF16)
            send_ref[o, C : C + HD, :] = singles[t].astype(BF16)
            vec = vec_scr[4 * o : 4 * o + 4, :]
            high = vec.astype(BF16).astype(F32)
            send_ref[o, C + HD : C + HD + 16, :] = jnp.concatenate(
                [high, vec - high, jnp.zeros((8, C), F32)], axis=0
            ).astype(BF16)


def attend_back_kernel(*refs):
    recv_ref, total_ref, fin_ref = refs[:3]
    sums, (cgrad_ref, vec_ref, send_ref) = refs[3:-3], refs[-3:]
    total = add_all(sums)
    left = left_half((C, C))
    zero = jnp.zeros((C, C), F32)
    lifted = total[C : C + HD]
    single = jnp.concatenate([roll_half(lifted), lifted], axis=0)
    grads = (
        jnp.where(left, total[0:C], zero).astype(BF16),
        jnp.where(left, zero, total[0:C]).astype(BF16),
        jnp.where(left, zero, single).astype(BF16),
    )
    vec_ref[...] = total[C + HD : C + HD + 4] + total[C + HD + 4 : C + HD + 8]
    centroids = centroid_blocks(total_ref[...])
    tail = fin_ref[:, C : 2 * C]
    outs = (fin_ref[:, 0:C], fin_ref[:, 0:C], tail)
    length = SUB * C
    probs, score_grads, cgrads = [], [], []
    for i in range(3):
        k = recv_ref[:, :, KEY_LANES[i] : KEY_LANES[i] + C].reshape(length, C)
        v = recv_ref[:, :, VALUE_LANES[i] : VALUE_LANES[i] + C].reshape(length, C)
        scores = dot_nt(centroids[i], k) * SCALE
        prob = jnp.exp(scores - tail[:, i : i + 1]) / tail[:, 3 + i : 4 + i]
        delta = jnp.sum(grads[i].astype(F32) * outs[i], axis=1, keepdims=True)
        score_grad = (prob * (dot_nt(grads[i], v) - delta) * SCALE).astype(BF16)
        cgrads.append(dot_nn(score_grad, k))
        probs.append(prob.astype(BF16))
        score_grads.append(score_grad)
    cgrad_ref[:, 0:C] = jnp.where(left, cgrads[0], cgrads[1])
    cgrad_ref[:, C : 2 * C] = cgrads[2]
    for lanes, lhs, rhs in (
        (2 * C, score_grads[0:2], centroids[0:2]),
        (3 * C, probs[0:2], grads[0:2]),
        (4 * C, (score_grads[2], probs[2]), (centroids[2], grads[2])),
    ):
        made = dot_tn(jnp.concatenate(lhs, axis=0), jnp.concatenate(rhs, axis=0))
        send_ref[:, :, lanes : lanes + C] = made.astype(BF16).reshape(SUB, C, C)


def finish_back_kernel(*refs):
    total_ref, vec_ref, cgrads, send_ref = refs[1], refs[2], refs[3:-1], refs[-1]
    grad = add_all(cgrads)
    left = left_half((C, C))
    tail = total_ref[:, C : 2 * C]
    count = [jnp.maximum(tail[:, HD + i : HD + i + 1], 1.0) for i in range(3)]
    pair = grad[:, 0:C] / jnp.where(left, count[0], count[1])
    single = grad[:, C : 2 * C] / count[2]
    vec = vec_ref[...]
    high = vec.astype(BF16).astype(F32)
    rows = []
    for v in (high, vec - high):
        rows += [roll_half(v), v]
    vec_block = jnp.concatenate(rows + [jnp.zeros((C - 16, C), F32)], axis=0)
    single = jnp.where(left, single, vec_block)
    for o in range(SUB):
        send_ref[o, :, 0:C] = pair.astype(BF16)
        send_ref[o, :, C : 2 * C] = single.astype(BF16)


def first_back_kernel(recv_ref, ids_ref, wq_ref, wkv_ref, grads_ref, part_ref):
    left = left_half((C, C))
    width = wq_ref.shape[1]
    for s in range(SEQS):
        rows = slice(s * C, (s + 1) * C)
        blocks = [recv_ref[s * 2 + t] for t in range(2)]
        q_tail = [b[:, C : 2 * C].astype(F32) for b in blocks]
        kv_tail = [b[:, 4 * C : 5 * C].astype(F32) for b in blocks]
        q_mid = jnp.where(left, q_tail[0], roll_half(q_tail[1])).astype(BF16)
        k_mid = jnp.where(left, kv_tail[0], roll_half(kv_tail[1])).astype(BF16)
        v_mid = jnp.where(left, roll_half(kv_tail[0]), kv_tail[1]).astype(BF16)
        for p, pair in enumerate((blocks[0][:, 0:C], q_mid, blocks[1][:, 0:C])):
            grads_ref[rows, p * C : (p + 1) * C] = spread_pair(
                ids_ref, PAIRS[p], s * C, pair
            ).astype(BF16)
        for n, (first, mid) in enumerate(((2 * C, k_mid), (3 * C, v_mid))):
            base = (n + 1) * width
            grads_ref[rows, base : base + C] = blocks[0][:, first : first + C]
            grads_ref[rows, base + C : base + 2 * C] = mid
            grads_ref[rows, base + 2 * C : base + 3 * C] = blocks[1][:, first : first + C]
    part_ref[...] = (
        dot_nt(grads_ref[:, 0:width], wq_ref[...])
        + dot_nt(grads_ref[:, width : 3 * width], wkv_ref[...])
    ).astype(BF16)


def weight_kernel(a_ref, b_ref, out_ref):
    out_ref[...] = dot_tn(a_ref[...], b_ref[...]).astype(BF16)


def weight_two_kernel(a_ref, b_ref, c_ref, d_ref, out_ref):
    width = b_ref.shape[1]
    out_ref[:, 0:width] = dot_tn(a_ref[...], b_ref[...]).astype(BF16)
    out_ref[:, width:] = dot_tn(c_ref[...], d_ref[...]).astype(BF16)


def last_kernel(part_ref, other_ref, x_ref, gain_ref, residual_grad_ref, input_grad_ref, vec_ref):
    gain_sum = jnp.zeros(gain_ref.shape, F32)
    shift_sum = jnp.zeros(gain_ref.shape, F32)
    for s in range(SEQS):
        rows = slice(s * C, (s + 1) * C)
        grad = part_ref[rows, :].astype(F32) + other_ref[rows, :].astype(F32)
        unit, inverse = normalise(x_ref[rows, :].astype(F32))
        gain_sum = gain_sum + jnp.sum(grad * unit, axis=0, keepdims=True)
        shift_sum = shift_sum + jnp.sum(grad, axis=0, keepdims=True)
        made = norm_pull(unit, inverse, grad * gain_ref[...])
        input_grad_ref[rows, :] = (residual_grad_ref[rows, :] + made).astype(BF16)
    vec_ref[0:1, :] = gain_sum
    vec_ref[1:2, :] = shift_sum


def on_device(
    inputs, cluster_ids, norm_one_gain, norm_one_shift, query_weight, keyval_weight, out_weight,
    norm_two_gain, norm_two_shift, up_weight, up_bias, down_weight, down_bias, cotangent, loss_mask,
):
    groups = lax.axis_size("g")
    devices = groups * SUB
    tokens, model = inputs.shape
    width = query_weight.shape[1]
    hidden = up_weight.shape[1]
    own = model // devices
    other = functools.partial(lax.ppermute, axis_name="mp", perm=SWAP)

    def across(v):
        if groups == 1:
            return [v]
        if groups == 2:
            return [v, lax.ppermute(v, "g", SWAP)]
        whole = lax.all_gather(v, "g", axis=0)
        return [whole[i] for i in range(groups)]

    mp_index = lax.axis_index("mp")
    row = lambda v: v.reshape(1, -1)
    ids_other = other(cluster_ids)
    wo_other = other(out_weight)
    wkv = keyval_weight.reshape(model, 2 * width)
    bg = cotangent * loss_mask.astype(BF16)[:, None]
    ids_cols = cluster_ids.T
    cols_other = ids_other.T
    ids_all = jnp.where(
        mp_index == 0,
        jnp.concatenate([ids_cols, cols_other], axis=1),
        jnp.concatenate([cols_other, ids_cols], axis=1),
    )

    normed_one, send_one = call(
        project_kernel,
        [((tokens, model), BF16), ((SUB, C, 5 * C), BF16)],
        inputs, row(norm_one_gain), row(norm_one_shift), query_weight, wkv, cluster_ids,
        scratch=[pltpu.VMEM((tokens, width), F32), pltpu.VMEM((tokens, 2 * width), BF16)],
        flops=2 * tokens * model * 3 * width,
        name="project",
    )
    recv_one = lax.all_to_all(send_one, NEAR, 0, 0)
    (sums,) = call(
        sum_kernel, [((C, 2 * C), F32)], recv_one, name="query_sums",
        specs=([pl.BlockSpec((SUB, C, 2 * C), lambda i: (0, 0, 0))], [pl.BlockSpec((C, 2 * C), lambda i: (0, 0))]),
    )
    part, total = call(
        attend_kernel, [((C, 2 * C), F32), ((C, 2 * C), F32)], recv_one, *across(sums), name="attend",
        flops=2 * 2 * 3 * C * SUB * C * C,
    )
    fin, send_two = call(
        merge_kernel, [((C, 2 * C), F32), ((2 * SUB, C + HD, C), BF16)], *across(part), name="merge"
    )
    recv_two = lax.all_to_all(send_two, NEAR + ("mp",), 0, 0)
    attended, residual, normed_two, active, hidden_grad, back, branch, up_bias_part = call(
        middle_kernel,
        [
            ((tokens, width), BF16), ((tokens, model), F32), ((tokens, model), BF16),
            ((tokens, hidden), BF16), ((tokens, hidden), BF16), ((tokens, model), BF16),
            ((tokens, model), BF16), ((1, hidden), F32),
        ],
        mp_index.reshape(1), recv_two, ids_all, inputs, out_weight, wo_other, row(norm_two_gain),
        row(norm_two_shift), up_weight, row(up_bias), down_weight, bg,
        scratch=[pltpu.VMEM((tokens, 2 * width), BF16), pltpu.VMEM((2 * width, model), BF16)],
        flops=2 * tokens * model * (2 * width + 4 * hidden),
        vmem=48 * 2**20, name="middle",
        specs=(
            [pl.BlockSpec(memory_space=pltpu.SMEM)] + [pl.BlockSpec(memory_space=pltpu.VMEM)] * 11,
            [pl.BlockSpec(memory_space=pltpu.VMEM)] * 8,
        ),
    )
    back_other = other(back)
    branch_other = other(branch)
    (ff_part,) = call(
        weight_two_kernel, [((model, 2 * hidden), BF16)], normed_two, hidden_grad, bg, active,
        flops=4 * tokens * model * hidden, name="ff_weights",
    )
    ff_sum = lax.psum_scatter(ff_part, SEQ, scatter_dimension=0, tiled=True)
    residual_grad, mixed_grad, send_three = call(
        turn_kernel,
        [((tokens, model), F32), ((tokens, model), BF16), ((SUB, C + HD + 16, C), BF16)],
        back, back_other, residual, row(norm_two_gain), bg, out_weight, cluster_ids, up_bias_part,
        scratch=[pltpu.VMEM((tokens, width), F32), pltpu.VMEM((32, C), F32)],
        flops=2 * tokens * model * width, name="turn",
    )
    recv_three = lax.all_to_all(send_three, NEAR, 0, 0)
    (grad_sums,) = call(sum_kernel, [((C + HD + 16, C), F32)], recv_three, name="grad_sums")
    cgrad, vec, send_four = call(
        attend_back_kernel,
        [((C, 2 * C), F32), ((4, C), F32), ((SUB, C, 5 * C), BF16)],
        recv_one, total, fin, *across(grad_sums), flops=2 * 5 * 3 * C * SUB * C * C, name="attend_back",
    )
    cgrads = across(cgrad)
    (send_four,) = call(
        finish_back_kernel, [((SUB, C, 5 * C), BF16)], send_four, total, vec, *cgrads,
        aliases={0: 0}, name="finish_back",
        specs=(
            [pl.BlockSpec(memory_space=pl.ANY)] + [pl.BlockSpec(memory_space=pltpu.VMEM)] * (2 + len(cgrads)),
            [pl.BlockSpec((SUB, C, 2 * C), lambda i: (0, 0, 0))],
        ),
    )
    recv_four = lax.all_to_all(send_four, NEAR, 0, 0)
    grads, first_part = call(
        first_back_kernel, [((tokens, 3 * width), BF16), ((tokens, model), BF16)],
        recv_four, ids_cols, query_weight, wkv, flops=2 * tokens * model * 3 * width, name="first_back",
    )
    first_other = other(first_part)
    (out_part,) = call(
        weight_kernel, [((model, width), BF16)], mixed_grad, attended, flops=2 * tokens * model * width,
        name="out_weights",
    )
    (qkv_part,) = call(
        weight_kernel, [((model, 3 * width), BF16)], normed_one, grads,
        flops=2 * tokens * model * 3 * width, name="qkv_weights",
    )
    input_grad, vec_one = call(
        last_kernel, [((tokens, model), BF16), ((2, model), F32)],
        first_part, first_other, inputs, row(norm_one_gain), residual_grad, name="last",
    )
    block_output = (
        residual + (branch.astype(F32) + branch_other.astype(F32)) + down_bias
    ).astype(BF16)

    def reduce_rows(v):
        spread = v.reshape(groups, 2, 2, 2, own, -1)
        for axis, at in (("b0", 3), ("b1", 2)):
            me = lax.axis_index(axis)
            theirs = lax.dynamic_index_in_dim(spread, 1 - me, at, keepdims=False)
            mine = lax.dynamic_index_in_dim(spread, me, at, keepdims=False)
            got = lax.ppermute(theirs, axis, SWAP)
            spread = (mine.astype(F32) + got.astype(F32)).astype(BF16)
        spread = spread.reshape(2 * groups, own, -1)
        return jnp.sum(lax.all_to_all(spread, ("g", "b2"), 0, 0).astype(F32), axis=0)

    tail_sum = reduce_rows(jnp.concatenate([qkv_part, out_part], axis=1))
    vec_send = vec_one.reshape(2, devices, own).swapaxes(0, 1).reshape(devices, 2 * own)
    vec_recv = lax.all_to_all(vec_send, SEQ, 0, 0, tiled=True).reshape(devices, 2, own)
    vec_sum = jnp.sum(vec_recv, axis=0)

    small = recv_four[:, 0:16, C + HD : 2 * C].astype(F32)
    small = small[:, 0:8] + small[:, 8:16]
    small = small.reshape(SUB, 2, 4, HD).swapaxes(1, 2).reshape(-1)
    start = lax.axis_index(SEQ) * own
    take = lambda base: lax.dynamic_slice(small, (base + start,), (own,))
    ff_sum = ff_sum.astype(F32)
    return (
        block_output,
        input_grad,
        vec_sum[0],
        vec_sum[1],
        tail_sum[:, 0:width],
        tail_sum[:, width : 3 * width].reshape(own, 2, width),
        tail_sum[:, 3 * width :].T,
        take(hidden),
        take(hidden + model),
        ff_sum[:, 0:hidden],
        small[0:hidden],
        ff_sum[:, hidden:].T,
        take(hidden + 2 * model),
    )


def solution(mesh):
    groups = mesh.shape["seq"] // SUB
    fine = Mesh(
        mesh.devices.reshape(groups, 2, 2, 2, mesh.shape["mp"]), ("g", "b2", "b1", "b0", "mp")
    )
    placed = (
        P(SEQ, None),
        P("mp", SEQ),
        P(),
        P(),
        P(None, "mp"),
        P(None, None, "mp"),
        P("mp", None),
        P(),
        P(),
        P(None, "mp"),
        P("mp"),
        P("mp", None),
        P(),
        P(SEQ, None),
        P(SEQ),
    )
    return jax.shard_map(
        on_device,
        mesh=fine,
        in_specs=placed,
        out_specs=(
            P(SEQ, None),
            P(SEQ, None),
            P(SEQ),
            P(SEQ),
            P(SEQ, "mp"),
            P(SEQ, None, "mp"),
            P("mp", SEQ),
            P(SEQ),
            P(SEQ),
            P(SEQ, "mp"),
            P("mp"),
            P("mp", SEQ),
            P(SEQ),
        ),
        check_vma=False,
    )
```

time: 997 us -> 271 us (0.27)
  waiting for transfers between devices: 516 us -> 122 us
  blocking collectives: 283 us -> 34.2 us
  matrix products: 85 us -> 0 us
  Pallas kernels: 0 us -> 33.4 us
  local copies, waits for them, and re-layouts: 62.3 us -> 30.3 us
  starting transfers between devices: 1.04 us -> 24 us
  other arithmetic: 22.5 us -> 11.2 us
    reduce_scatter x5 -> x1, waiting for transfers between devices: 276 us -> 6.53 us  [on_device(): ff_sum = lax.psum_scatter(ff_part, SEQ, scatter_dimension=0, tiled=True)]
    unnamed x2 -> x0, blocking collectives: 125 us -> none
    all_gather x2 -> x0, waiting for transfers between devices: 111 us -> none  [the longest x1 62.1 us: on_device(): key_block = lax.all_gather(key_rows, 'seq', axis=0, tiled=True)]
    psum x4 -> x0, waiting for transfers between devices: 100 us -> none  [the longest x1 72.7 us: on_device(): centroid_grad, up_bias_grad = lax.psum((centroid_part, up_bias_part), 'seq')]
    all_gather x4 -> x0, blocking collectives: 88.3 us -> none  [the longest x1 26.5 us: on_device(): lax.all_gather(owned_out, 'seq', axis=0, tiled=True)]
    ppermute x0 -> x11, waiting for transfers between devices: none -> 87.9 us  [the longest x4 28.9 us: across(): return [v, lax.ppermute(v, 'g', SWAP)]]
    dot_general x26 -> x0, matrix products: 85 us -> none  [the longest x1 9.12 us: on_device(): jnp.dot(normed_two, up_weight, preferred_element_type=jnp.float32) + up_bias]
    psum x1 -> x0, blocking collectives: 70.1 us -> none  [on_device(): cluster_grad = lax.psum(out_part, 'seq').astype(jnp.bfloat16)]
  transfers between devices with their start and end apart: 12 -> 16, of which waited for: 10 -> 13; matrix products, arithmetic and copies ran while one was open for 9% -> 6% of each run, Pallas kernels for 0% -> 4%
where the time goes in v1:
time: 271 us; the launch traced here: 270 us
  waiting for transfers between devices  122 us (45%)
  blocking collectives  34.2 us (13%)
  Pallas kernels  33.4 us (12%)
  local copies, waits for them, and re-layouts  30.3 us (11%)
  starting transfers between devices  24 us (9%)
  between operations  14.5 us (5%)
  other arithmetic  11.2 us (4%)
    pallas_call x14, Pallas kernels, call(): pl.pallas_call(kernel, out_shape=[jax.ShapeDtypeStruct(s, d) for s, d in...  33.4 us
    ppermute x4, waiting for transfers between devices, across(): return [v, lax.ppermute(v, 'g', SWAP)]  28.9 us
    ppermute x1, waiting for transfers between devices, on_device(): ids_other = other(cluster_ids)  25.2 us
    all_to_all x1, blocking collectives, on_device(): recv_one = lax.all_to_all(send_one, NEAR, 0, 0)  22.5 us
    unnamed x86, local copies, waits for them, and re-layouts  22 us
    ppermute x1, waiting for transfers between devices, on_device(): back_other = other(back)  18.7 us
    all_to_all x1, waiting for transfers between devices, reduce_rows(): lax.all_to_all(spread, ('g', 'b2'), 0, 0).astype(F32)  16 us
    ppermute x1, waiting for transfers between devices, on_device(): first_other = other(first_part)  12.2 us
  transfers between devices with their start and end apart: 16, of which 13 were waited for; matrix products, arithmetic and copies ran while one was open for 6% of the time, Pallas kernels for 4%

profile of v1, /device:TPU:0, one launch (start us, length us, event | category | flops | bytes accessed | tf_op | source)
XLA Modules:
  0.0 269.6 jit_solution(7815230409130490963)
XLA Ops:
  7.2 0.8 reshape.85.gain_ref
  8.0 0.7 reshape.86.shift_ref
  8.7 1.5 copy.48
  10.2 2.2 project.1
  12.5 22.5 %all_to_all.34.recv_ref.refs_0_ = bf16[8,128,640]{2,1,0:T(8,128)(2,1)S(1)} all-to-all(bf16[8,128,640]{2,1,0:T(8,128)(2,1)S(1)} %get-tuple-element.37), channel_id=1, replica_groups=mesh['g'=2,'b2'=2,'b1'=2,'b0'=2,'mp'=2] {'b2','b1','b0'}, dimensions={0} | all-to-all | bytes 2621440 | tf_op jit(solution)/shard_map/all_to_all | solution.py:485
  35.0 2.7 collective-permute-start
  37.7 6.3 %collective-permute-done.refs_2_ = f32[128,256]{1,0:T(8,128)S(1)} collective-permute-done((f32[128,256]{1,0:T(8,128)S(1)}, f32[128,256]{1,0:T(8,128)S(1)}, u32[]{:S(2)}, u32[]{:S(2)}) %collective-permute-start) | collective-permute-done | bytes 131104 | tf_op jit(solution)/shard_map/ppermute | solution.py:459
  44.0 1.3 attend.1
  46.0 8.4 %collective-permute-done.1.refs_1_ = f32[128,256]{1,0:T(8,128)S(1)} collective-permute-done((f32[128,256]{1,0:T(8,128)S(1)}, f32[128,256]{1,0:T(8,128)S(1)}, u32[]{:S(2)}, u32[]{:S(2)}) %collective-permute-start.1) | collective-permute-done | bytes 131104 | tf_op jit(solution)/shard_map/ppermute | solution.py:459
  54.4 1.4 merge.1
  55.8 4.0 %all-to-all-start.1 = ((bf16[16,192,128]{2,1,0:T(8,128)(2,1)}), bf16[16,192,128]{2,1,0:T(8,128)(2,1)S(1)}, u32[]{:S(2)}, u32[]{:S(2)}) async-start(bf16[16,192,128]{2,1,0:T(8,128)(2,1)} %get-tuple-element.39), calls=%async_computation.1 | async-start | bytes 1572864 | tf_op jit(solution)/shard_map/all_to_all | solution.py:497
  59.8 2.0 collective-permute-start.3
  62.1 2.1 broadcast_multiply_fusion.bg_ref.c_ref
  64.3 25.2 %collective-permute-done.2 = s32[6,512]{0,1:T(8,128)S(1)} collective-permute-done((s32[6,512]{0,1:T(8,128)S(1)}, s32[6,512]{0,1:T(8,128)S(1)}, u32[]{:S(2)}, u32[]{:S(2)}) %collective-permute-start.2) | collective-permute-done | bytes 12320 | tf_op jit(solution)/shard_map/ppermute | solution.py:465
  89.6 0.9 add_select_fusion.ids_ref
  90.5 1.1 copy-done.19
  91.6 0.9 copy-done.26
  92.6 12.5 %middle.1 = (bf16[512,384]{1,0:T(8,128)(2,1)S(1)}, f32[512,768]{1,0:T(8,128)}, bf16[512,768]{1,0:T(8,128)(2,1)S(1)}, bf16[512,1536]{1,0:T(8,128)(2,1)}, bf16[512...) custom-call(s32[1]{0:T(128)} %bitcast.mp_ref, ...), custom_call_target="tpu_custom_call" | custom-call | flops 5435817984 | bytes 15771652 | tf_op jit(solution)/shard_map/middle/pallas_call | solution.py:44
  105.1 0.8 copy-done.24
  106.2 18.7 %collective-permute-done.5.back_other_ref = bf16[512,768]{1,0:T(8,128)(2,1)S(1)} collective-permute-done((bf16[512,768]{1,0:T(8,128)(2,1)S(1)}, bf16[512,768]{1,0:T(8,128)(2,1)S(1)}, u32[]{:S(2)}, u32[]{:S(2)}) %collective-permute-start.5) | collective-permute-done | bytes 786464 | tf_op jit(solution)/shard_map/ppermute | solution.py:515
  124.9 1.4 copy-done.2
  126.3 2.4 turn.1
  128.8 1.1 copy-done.6
  129.9 11.8 %all_to_all.35.recv_ref = bf16[8,208,128]{2,1,0:T(8,128)(2,1)S(1)} all-to-all(bf16[8,208,128]{2,1,0:T(8,128)(2,1)S(1)} %get-tuple-element.46), channel_id=1, replica_groups=mesh['g'=2,'b2'=2,'b1'=2,'b0'=2,'mp'=2] {'b2','b1','b0'}, dimensions={0} | all-to-all | bytes 851968 | tf_op jit(solution)/shard_map/all_to_all | solution.py:529
  141.7 1.2 collective-permute-start.6
  143.0 6.5 %collective-permute-done.6.refs_4_ = f32[208,128]{1,0:T(8,128)S(1)} collective-permute-done((f32[208,128]{1,0:T(8,128)S(1)}, f32[208,128]{1,0:T(8,128)S(1)}, u32[]{:S(2)}, u32[]{:S(2)}) %collective-permute-start.6) | collective-permute-done | bytes 106528 | tf_op jit(solution)/shard_map/ppermute | solution.py:459
  149.5 2.7 attend_back.1
  152.2 7.7 %collective-permute-done.7.refs_4_ = f32[128,256]{1,0:T(8,128)S(1)} collective-permute-done((f32[128,256]{1,0:T(8,128)S(1)}, f32[128,256]{1,0:T(8,128)S(1)}, u32[]{:S(2)}, u32[]{:S(2)}) %collective-permute-start.7) | collective-permute-done | bytes 131104 | tf_op jit(solution)/shard_map/ppermute | solution.py:459
  159.9 1.0 finish_back.1
  160.9 3.7 %all-to-all-start.3 = ((bf16[8,128,640]{2,1,0:T(8,128)(2,1)}), bf16[8,128,640]{2,1,0:T(8,128)(2,1)S(1)}, u32[]{:S(2)}, u32[]{:S(2)}) async-start(bf16[8,128,640]{2,1,0:T(8,128)(2,1)} %finish_back.1), calls=%async_computation.3 | async-start | bytes 2621440 | tf_op jit(solution)/shard_map/all_to_all | solution.py:545
  164.7 1.4 copy-done.4
  166.1 1.4 copy-done.5
  167.5 2.6 ff_weights.1
  170.1 2.2 copy-done
  172.3 1.1 copy-done.15
  174.1 7.6 %all-to-all-done.3.recv_ref = bf16[8,128,640]{2,1,0:T(8,128)(2,1)S(1)} async-done(((bf16[8,128,640]{2,1,0:T(8,128)(2,1)}), bf16[8,128,640]{2,1,0:T(8,128)(2,1)S(1)}, u32[]{:S(2)}, u32[]{:S(2)}) %all-to-all-start.3) | async-done | bytes 1310752 | tf_op jit(solution)/shard_map/all_to_all | solution.py:545
  181.8 1.3 copy-done.9
  183.1 1.1 copy-done.31
  184.2 1.9 first_back.1
  186.2 0.9 copy-done.21
  187.0 1.2 qkv_weights.1
  188.5 1.4 copy-done.34
  189.8 1.2 dynamic-slice_bitcast_fusion
  191.6 2.6 collective-permute-done.9
  194.2 1.9 fusion
  196.2 1.0 copy-done.35
  197.2 1.6 collective-permute-start.10
  198.8 0.7 collective-permute-start.4
  199.5 12.2 %collective-permute-done.8.other_ref = bf16[512,768]{1,0:T(8,128)(2,1)} collective-permute-done((bf16[512,768]{1,0:T(8,128)(2,1)}, bf16[512,768]{1,0:T(8,128)(2,1)}, u32[]{:S(2)}, u32[]{:S(2)}) %collective-permute-start.8) | collective-permute-done | bytes 786464 | tf_op jit(solution)/shard_map/ppermute | solution.py:550
  211.7 1.1 copy-done.20
  212.9 1.1 copy-done.22
  214.0 3.4 %last.1 = (bf16[512,768]{1,0:T(8,128)(2,1)}, f32[2,768]{1,0:T(2,128)S(1)}) custom-call(bf16[512,768]{1,0:T(8,128)(2,1)S(1)} %copy-done.22, bf16[512,768]{1,0:T(8,128)(2,1)} %collective-permute-done.8.other_ref, bf16[512,768]{1,0:T(8,128)(2,1)S(1)} %copy-done.20, f32[1,768]{1,0:T(1,128)S(1)} %reshape.85.gain_ref, f32[512,768]{1,0:T(8,128)S(1)} %copy-done.7), custom_call_target="tpu_custom_call" | custom-call | bytes 4727808 | tf_op jit(solution)/shard_map/last/pallas_call | solution.py:44
  218.2 3.5 %all-to-all-start.4 = ((f32[16,1,96]{2,1,0:T(1,128)}), f32[16,1,96]{2,1,0:T(1,128)S(1)}, u32[]{:S(2)}, u32[]{:S(2)}) async-start(f32[16,1,96]{2,1,0:T(1,128)} %bitcast.4), calls=%async_computation.4 | async-start | bytes 16384 | tf_op jit(solution)/shard_map/all_to_all | solution.py:580
  221.9 2.2 fusion.1
  224.2 3.8 %all-to-all-done.4 = f32[16,1,96]{2,1,0:T(1,128)S(1)} async-done(((f32[16,1,96]{2,1,0:T(1,128)}), f32[16,1,96]{2,1,0:T(1,128)S(1)}, u32[]{:S(2)}, u32[]{:S(2)}) %all-to-all-start.4) | async-done | bytes 6176 | tf_op jit(solution)/shard_map/all_to_all | solution.py:580
  228.0 3.5 %all-to-all-start.5 = ((bf16[4,48,1536]{2,1,0:T(8,128)(2,1)}), bf16[4,48,1536]{2,1,0:T(8,128)(2,1)S(1)}, u32[]{:S(2)}, u32[]{:S(2)}) async-start(bf16[4,48,1536]{2,1,0:T(8,128)(2,1)} %bitcast.35), calls=%async_computation.5 | async-start | bytes 1179648 | tf_op jit(solution)/shard_map/all_to_all | solution.py:576
  231.5 2.6 add_convert_fusion
  234.3 0.7 slice.48
  236.2 16.0 %all-to-all-done.5 = bf16[4,48,1536]{2,1,0:T(8,128)(2,1)S(1)} async-done(((bf16[4,48,1536]{2,1,0:T(8,128)(2,1)}), bf16[4,48,1536]{2,1,0:T(8,128)(2,1)S(1)}, u32[]{:S(2)}, u32[]{:S(2)}) %all-to-all-start.5) | async-done | bytes 589856 | tf_op jit(solution)/shard_map/all_to_all | solution.py:576
  252.3 0.7 reshape.94
  253.7 6.5 %reduce-scatter.2.cloned.1.call-done = bf16[48,3072]{1,0:T(8,128)(2,1)} async-done(((bf16[768,3072]{1,0:T(8,128)(2,1)}), bf16[48,3072]{1,0:T(8,128)(2,1)}) %reduce-scatter.2.cloned.1.call-update) | async-done | bytes 294928 | tf_op jit(solution)/shard_map/reduce_scatter | solution.py:521
  260.2 1.1 convert_element_type.59
  261.3 0.7 slice_bitcast_fusion
  262.0 0.7 slice.56
  (104 shorter events, 6.4 us)
Async XLA Ops:
  7.2 3.0 %copy-start.18 = (bf16[512,768]{1,0:T(8,128)(2,1)S(1)}, bf16[512,768]{1,0:T(8,128)(2,1)}, u32[]{:S(2)}) copy-start(bf16[512,768]{1,0:T(8,128)(2,1)} %x_ref.5) | copy-start | bytes 2359300
  7.2 3.0 %copy-start.30 = (bf16[768,384]{1,0:T(8,128)(2,1)S(1)}, bf16[768,384]{1,0:T(8,128)(2,1)}, u32[]{:S(2)}) copy-start(bf16[768,384]{1,0:T(8,128)(2,1)} %wq_ref.3) | copy-start | bytes 1769476
  7.2 3.0 %copy-start.29 = (s32[6,512]{1,0:T(8,128)S(1)}, s32[6,512]{1,0:T(8,128)}, u32[]{:S(2)}) copy-start(s32[6,512]{1,0:T(8,128)} %ids_ref.3) | copy-start | bytes 36868
  10.2 2.2 copy-start.8
  12.5 22.6 %copy-start.12 = (bf16[512,768]{1,0:T(8,128)(2,1)}, bf16[512,768]{1,0:T(8,128)(2,1)S(1)}, u32[]{:S(2)}) copy-start(bf16[512,768]{1,0:T(8,128)(2,1)S(1)} %get-tuple-element.54.a_ref) | copy-start | bytes 2359300
  35.0 24.8 %copy-start.23 = (bf16[384,768]{1,0:T(8,128)(2,1)S(1)}, bf16[384,768]{1,0:T(8,128)(2,1)}, u32[]{:S(2)}) copy-start(bf16[384,768]{1,0:T(8,128)(2,1)} %wo_ref.3) | copy-start | bytes 1769476
  35.0 27.1 %copy-start.41 = (s32[512]{0:T(512)S(1)}, s32[512]{0:T(512)}, u32[]{:S(2)}) copy-start(s32[512]{0:T(512)} %param.29) | copy-start | bytes 6148
  35.0 8.9 %collective-permute-start = (f32[128,256]{1,0:T(8,128)S(1)}, f32[128,256]{1,0:T(8,128)S(1)}, u32[]{:S(2)}, u32[]{:S(2)}) collective-permute-start(f32[128,256]{1,0:T(8,128)S(1)} %query_sums.1.refs_1_), channel_id=1, source_target_pairs={{0,16},{16,0},{1,17},{17,1},{2,18},{18,2},{3,19},{19,3},{4,20},{20... | collective-permute-start | bytes 393224 | tf_op jit(solution)/shard_map/ppermute | solution.py:459
  45.3 0.7 copy-start.27
  46.0 8.4 %collective-permute-start.1 = (f32[128,256]{1,0:T(8,128)S(1)}, f32[128,256]{1,0:T(8,128)S(1)}, u32[]{:S(2)}, u32[]{:S(2)}) collective-permute-start(f32[128,256]{1,0:T(8,128)S(1)} %get-tuple-element.38.refs_0_), channel_id=1, source_target_pairs={{0,16},{16,0},{1,17},{17,1},{2,18},{18,2},{3,19},{19,3},{4,20},{20... | collective-permute-start | bytes 393224 | tf_op jit(solution)/shard_map/ppermute | solution.py:459
  55.7 4.0 %copy-start.32 = (f32[128,256]{1,0:T(8,128)}, f32[128,256]{1,0:T(8,128)S(1)}, u32[]{:S(2)}) copy-start(f32[128,256]{1,0:T(8,128)S(1)} %get-tuple-element.43.refs_2_) | copy-start | bytes 393220
  55.7 8.5 %copy-start.39 = (f32[768]{0:T(1024)S(1)}, f32[768]{0:T(1024)}, u32[]{:S(2)}) copy-start(f32[768]{0:T(1024)} %param.22) | copy-start | bytes 9220
  55.7 8.5 %copy-start.40 = (f32[768]{0:T(1024)S(1)}, f32[768]{0:T(1024)}, u32[]{:S(2)}) copy-start(f32[768]{0:T(1024)} %param.23) | copy-start | bytes 9220
  55.8 8.6 %copy-start.37 = (f32[1536]{0:T(1024)S(1)}, f32[1536]{0:T(1024)}, u32[]{:S(2)}) copy-start(f32[1536]{0:T(1024)} %param.25) | copy-start | bytes 18436
  55.8 34.7 %all-to-all-start.1 = ((bf16[16,192,128]{2,1,0:T(8,128)(2,1)}), bf16[16,192,128]{2,1,0:T(8,128)(2,1)S(1)}, u32[]{:S(2)}, u32[]{:S(2)}) async-start(bf16[16,192,128]{2,1,0:T(8,128)(2,1)} %get-tuple-element.39), calls=%async_computation.1 | async-start | bytes 1572864 | tf_op jit(solution)/shard_map/all_to_all | solution.py:497
  59.8 30.7 %collective-permute-start.3 = (bf16[384,768]{1,0:T(8,128)(2,1)S(1)}, bf16[384,768]{1,0:T(8,128)(2,1)}, u32[]{:S(2)}, u32[]{:S(2)}) collective-permute-start(bf16[384,768]{1,0:T(8,128)(2,1)S(1)} %copy-done.23), channel_id=1, source_target_pairs={{0,1},{1,0},{2,3},{3,2},{4,5},{5,4},{6,7},{7,6},{8,9},{9,8},{10,11... | collective-permute-start | bytes 1769480 | tf_op jit(solution)/shard_map/ppermute | solution.py:466
  61.9 28.6 %copy-start.10 = (s32[6,512]{0,1:T(8,128)}, s32[6,512]{0,1:T(8,128)S(1)}, u32[]{:S(2)}) copy-start(s32[6,512]{0,1:T(8,128)S(1)} %copy.43) | copy-start | bytes 36868
  61.9 27.6 %collective-permute-start.2 = (s32[6,512]{0,1:T(8,128)S(1)}, s32[6,512]{0,1:T(8,128)S(1)}, u32[]{:S(2)}, u32[]{:S(2)}) collective-permute-start(s32[6,512]{0,1:T(8,128)S(1)} %copy.43), channel_id=1, source_target_pairs={{0,1},{1,0},{2,3},{3,2},{4,5},{5,4},{6,7},{7,6},{8,9},{9,8},{10,11... | collective-permute-start | bytes 36872 | tf_op jit(solution)/shard_map/ppermute | solution.py:465
  90.5 1.1 copy-start.19
  91.6 0.9 copy-start.26
  92.6 32.4 %copy-start.1 = (bf16[512,768]{1,0:T(8,128)(2,1)S(1)}, bf16[512,768]{1,0:T(8,128)(2,1)}, u32[]{:S(2)}) copy-start(bf16[512,768]{1,0:T(8,128)(2,1)} %broadcast_multiply_fusion.bg_ref.c_ref) | copy-start | bytes 2359300
  105.1 0.8 copy-start.24
  105.9 22.9 %copy-start.16 = (bf16[512,768]{1,0:T(8,128)(2,1)}, bf16[512,768]{1,0:T(8,128)(2,1)S(1)}, u32[]{:S(2)}) copy-start(bf16[512,768]{1,0:T(8,128)(2,1)S(1)} %get-tuple-element.58.a_ref) | copy-start | bytes 2359300
  105.9 19.1 %collective-permute-start.5 = (bf16[512,768]{1,0:T(8,128)(2,1)S(1)}, bf16[512,768]{1,0:T(8,128)(2,1)S(1)}, u32[]{:S(2)}, u32[]{:S(2)}) collective-permute-start(bf16[512,768]{1,0:T(8,128)(2,1)S(1)} %get-tuple-element.44.back_ref), channel_id=1, source_target_pairs={{0,1},{1,0},{2,3},{3,2},{4,5},{5,4},{6,7},{7,6},{8,9},{9,8},{10,11... | collective-permute-start | bytes 2359304 | tf_op jit(solution)/shard_map/ppermute | solution.py:515
  124.9 1.4 copy-start.2
  126.3 23.1 %copy-start.28 = (f32[128,256]{1,0:T(8,128)S(1)}, f32[128,256]{1,0:T(8,128)}, u32[]{:S(2)}) copy-start(f32[128,256]{1,0:T(8,128)} %copy-done.27) | copy-start | bytes 393220
  126.3 23.1 %copy-start.33 = (f32[128,256]{1,0:T(8,128)S(1)}, f32[128,256]{1,0:T(8,128)}, u32[]{:S(2)}) copy-start(f32[128,256]{1,0:T(8,128)} %copy-done.32) | copy-start | bytes 393220
  128.7 1.1 copy-start.6
  129.9 11.8 %copy-start.14 = (bf16[512,768]{1,0:T(8,128)(2,1)}, bf16[512,768]{1,0:T(8,128)(2,1)S(1)}, u32[]{:S(2)}) copy-start(bf16[512,768]{1,0:T(8,128)(2,1)S(1)} %get-tuple-element.56.a_ref) | copy-start | bytes 2359300
  141.7 7.8 %collective-permute-start.6 = (f32[208,128]{1,0:T(8,128)S(1)}, f32[208,128]{1,0:T(8,128)S(1)}, u32[]{:S(2)}, u32[]{:S(2)}) collective-permute-start(f32[208,128]{1,0:T(8,128)S(1)} %grad_sums.1.refs_3_), channel_id=1, source_target_pairs={{0,16},{16,0},{1,17},{17,1},{2,18},{18,2},{3,19},{19,3},{4,20},{20... | collective-permute-start | bytes 319496 | tf_op jit(solution)/shard_map/ppermute | solution.py:459
  152.2 7.7 %collective-permute-start.7 = (f32[128,256]{1,0:T(8,128)S(1)}, f32[128,256]{1,0:T(8,128)S(1)}, u32[]{:S(2)}, u32[]{:S(2)}) collective-permute-start(f32[128,256]{1,0:T(8,128)S(1)} %get-tuple-element.49.refs_3_), channel_id=1, source_target_pairs={{0,16},{16,0},{1,17},{17,1},{2,18},{18,2},{3,19},{19,3},{4,20},{20... | collective-permute-start | bytes 393224 | tf_op jit(solution)/shard_map/ppermute | solution.py:459
  160.9 3.8 %copy-start.17 = (bf16[512,768]{1,0:T(8,128)(2,1)S(1)}, bf16[512,768]{1,0:T(8,128)(2,1)}, u32[]{:S(2)}) copy-start(bf16[512,768]{1,0:T(8,128)(2,1)} %copy-done.16) | copy-start | bytes 2359300
  160.9 20.9 %all-to-all-start.3 = ((bf16[8,128,640]{2,1,0:T(8,128)(2,1)}), bf16[8,128,640]{2,1,0:T(8,128)(2,1)S(1)}, u32[]{:S(2)}, u32[]{:S(2)}) async-start(bf16[8,128,640]{2,1,0:T(8,128)(2,1)} %finish_back.1), calls=%async_computation.3 | async-start | bytes 2621440 | tf_op jit(solution)/shard_map/all_to_all | solution.py:545
  164.6 95.6 %reduce-scatter.2.cloned.1.call-start = ((), (), s32[]{:S(2)}) async-start(), calls=%async_computation.7 | async-start | bytes 5013504 | tf_op jit(solution)/shard_map/reduce_scatter | solution.py:521
  164.6 1.4 copy-start.4
  166.1 1.4 copy-start.5
  170.1 2.2 copy-start
  172.3 1.1 copy-start.15
  172.3 1.2 copy-start.25
  172.3 9.5 %copy-start.11 = (s32[6,512]{0,1:T(8,128)S(1)}, s32[6,512]{0,1:T(8,128)}, u32[]{:S(2)}) copy-start(s32[6,512]{0,1:T(8,128)} %copy-done.10) | copy-start | bytes 36868
  181.8 1.3 copy-start.9
  183.1 1.1 copy-start.31
  184.2 2.8 %copy-start.13 = (bf16[512,768]{1,0:T(8,128)(2,1)S(1)}, bf16[512,768]{1,0:T(8,128)(2,1)}, u32[]{:S(2)}) copy-start(bf16[512,768]{1,0:T(8,128)(2,1)} %copy-done.12) | copy-start | bytes 2359300
  186.2 0.9 copy-start.21
  188.4 1.4 copy-start.34
  191.1 3.2 %collective-permute-start.9 = (bf16[2,2,2,48,1536]{4,3,2,1,0:T(8,128)(2,1)}, bf16[2,2,2,48,1536]{4,3,2,1,0:T(8,128)(2,1)}, u32[]{:S(2)}, u32[]{:S(2)}) collective-permute-start(bf16[2,2,2,48,1536]{4,3,2,1,0:T(8,128)(2,1)} %dynamic-slice_bitcast_fusion), channel_id=1, source_target_pairs={{0,2},{2,0},{1,3},{3,1},{4,6},{6,4},{5,7},{7,5},{8,10},{10,8},{9,1... | collective-permute-start | bytes 3538952 | tf_op jit(solution)/shard_map/ppermute | solution.py:573
  191.1 20.7 %copy-start.7 = (f32[512,768]{1,0:T(8,128)S(1)}, f32[512,768]{1,0:T(8,128)}, u32[]{:S(2)}) copy-start(f32[512,768]{1,0:T(8,128)} %copy-done.6) | copy-start | bytes 4718596
  191.1 20.7 %collective-permute-start.8 = (bf16[512,768]{1,0:T(8,128)(2,1)}, bf16[512,768]{1,0:T(8,128)(2,1)}, u32[]{:S(2)}, u32[]{:S(2)}) collective-permute-start(bf16[512,768]{1,0:T(8,128)(2,1)} %copy-done.21), channel_id=1, source_target_pairs={{0,1},{1,0},{2,3},{3,2},{4,5},{5,4},{6,7},{7,6},{8,9},{9,8},{10,11... | collective-permute-start | bytes 2359304 | tf_op jit(solution)/shard_map/ppermute | solution.py:550
  196.2 1.0 copy-start.35
  197.2 24.7 %collective-permute-start.10 = (bf16[2,2,48,1536]{3,2,1,0:T(8,128)(2,1)S(1)}, bf16[2,2,48,1536]{3,2,1,0:T(8,128)(2,1)}, u32[]{:S(2)}, u32[]{:S(2)}) collective-permute-start(bf16[2,2,48,1536]{3,2,1,0:T(8,128)(2,1)S(1)} %dynamic-slice_bitcast_fusion.1), channel_id=1, source_target_pairs={{0,4},{4,0},{1,5},{5,1},{2,6},{6,2},{3,7},{7,3},{8,12},{12,8},{9,1... | collective-permute-start | bytes 1769480 | tf_op jit(solution)/shard_map/ppermute | solution.py:573
  198.8 32.6 %collective-permute-start.4 = (bf16[512,768]{1,0:T(8,128)(2,1)}, bf16[512,768]{1,0:T(8,128)(2,1)}, u32[]{:S(2)}, u32[]{:S(2)}) collective-permute-start(bf16[512,768]{1,0:T(8,128)(2,1)} %get-tuple-element.41), channel_id=1, source_target_pairs={{0,1},{1,0},{2,3},{3,2},{4,5},{5,4},{6,7},{7,6},{8,9},{9,8},{10,11... | collective-permute-start | bytes 2359304 | tf_op jit(solution)/shard_map/ppermute | solution.py:516
  211.7 1.1 copy-start.20
  212.9 1.1 copy-start.22
  217.4 14.0 %copy-start.3 = (f32[512,768]{1,0:T(8,128)S(1)}, f32[512,768]{1,0:T(8,128)}, u32[]{:S(2)}) copy-start(f32[512,768]{1,0:T(8,128)} %get-tuple-element.40.residual_ref) | copy-start | bytes 4718596
  217.4 14.1 %copy-start.38 = (f32[768]{0:T(1024)S(1)}, f32[768]{0:T(1024)}, u32[]{:S(2)}) copy-start(f32[768]{0:T(1024)} %param.27) | copy-start | bytes 9220
  218.2 9.8 %all-to-all-start.4 = ((f32[16,1,96]{2,1,0:T(1,128)}), f32[16,1,96]{2,1,0:T(1,128)S(1)}, u32[]{:S(2)}, u32[]{:S(2)}) async-start(f32[16,1,96]{2,1,0:T(1,128)} %bitcast.4), calls=%async_computation.4 | async-start | bytes 16384 | tf_op jit(solution)/shard_map/all_to_all | solution.py:580
  228.0 24.2 %all-to-all-start.5 = ((bf16[4,48,1536]{2,1,0:T(8,128)(2,1)}), bf16[4,48,1536]{2,1,0:T(8,128)(2,1)S(1)}, u32[]{:S(2)}, u32[]{:S(2)}) async-start(bf16[4,48,1536]{2,1,0:T(8,128)(2,1)} %bitcast.35), calls=%async_computation.5 | async-start | bytes 1179648 | tf_op jit(solution)/shard_map/all_to_all | solution.py:576
  260.2 1.8 copy-start.36
Sparse Core Ops, SparseCore 0:
  172.4 87.7 reduce-scatter.1

commit v2 on v1

v2 whole, which is shorter than its diff:
```python
import functools

import jax
import jax.numpy as jnp
from jax import lax
from jax.experimental import pallas as pl
from jax.experimental.pallas import tpu as pltpu
from jax.sharding import Mesh, PartitionSpec as P

HD = 64
C = 128
SEQS = 4
SUB = 8
PACK = 208
EPS = 1e-05
SCALE = HD ** (-0.5)
F32 = jnp.float32
BF16 = jnp.bfloat16
NEAR = ("b2", "b1", "b0")
SEQ = ("g",) + NEAR
PAIRS = ((0, 1), (2, 3), (4, 5))
SWAP = [(0, 1), (1, 0)]


def dot_nn(a, b):
    return lax.dot_general(a, b, (((1,), (0,)), ((), ())), preferred_element_type=F32)


def dot_nt(a, b):
    return lax.dot_general(a, b, (((1,), (1,)), ((), ())), preferred_element_type=F32)


def dot_tn(a, b):
    return lax.dot_general(a, b, (((0,), (0,)), ((), ())), preferred_element_type=F32)


def call(kernel, outs, *args, scratch=(), flops=0, vmem=None, name=None, aliases=None, specs=None):
    moved = sum(a.size * a.dtype.itemsize for a in args) + sum(
        functools.reduce(lambda p, q: p * q, s, 1) * jnp.dtype(d).itemsize for s, d in outs
    )
    extra = {}
    if specs is not None:
        extra["in_specs"], extra["out_specs"] = specs
        extra["grid"] = (1,)
    return pl.pallas_call(
        kernel,
        out_shape=[jax.ShapeDtypeStruct(s, d) for s, d in outs],
        scratch_shapes=list(scratch),
        compiler_params=pltpu.CompilerParams(vmem_limit_bytes=vmem or 32 * 2**20),
        cost_estimate=pl.CostEstimate(flops=flops, bytes_accessed=moved, transcendentals=0),
        input_output_aliases=aliases or {},
        name=name,
        **extra,
    )(*args)


def left_half(shape):
    return lax.broadcasted_iota(jnp.int32, shape, 1) < HD


def roll_half(v):
    return pltpu.roll(v, HD, 1)


def normalise(v):
    centred = v - jnp.mean(v, axis=1, keepdims=True)
    inverse = lax.rsqrt(jnp.mean(centred * centred, axis=1, keepdims=True) + EPS)
    return centred * inverse, inverse


def norm_pull(unit, inverse, scaled_grad):
    return inverse * (
        scaled_grad
        - jnp.mean(scaled_grad, axis=1, keepdims=True)
        - unit * jnp.mean(scaled_grad * unit, axis=1, keepdims=True)
    )


def split(v):
    high = v.astype(BF16)
    low = (v - high.astype(F32)).astype(BF16)
    return high, low


def member_rows(ids_ref, head, start):
    row = ids_ref[head : head + 1, start : start + C]
    spot = lax.broadcasted_iota(jnp.int32, (C, C), 0)
    return jnp.where(spot == row, 1.0, 0.0).astype(F32)


def label_columns(labels):
    rows = []
    for v in labels:
        rows += [v.astype(F32), jnp.zeros((8 - v.shape[0], C), F32)]
    rows.append(jnp.zeros((C - 8 * len(labels), C), F32))
    return jnp.concatenate(rows, axis=0).T


def member_cols(columns, spot):
    lane = lax.broadcasted_iota(jnp.int32, (C, C), 1).astype(F32)
    return jnp.where(lane == columns[:, spot : spot + 1], 1.0, 0.0).astype(BF16)


def cluster_pair(members, pair):
    high, low = split(pair)
    both = jnp.concatenate([high, low], axis=1)
    sums = []
    for m in members:
        r = dot_nn(m.astype(BF16), both)
        sums.append(r[:, :C] + r[:, C:])
    return jnp.where(left_half((C, C)), sums[0], sums[1])


def spread_pair(columns, spots, pair):
    left = left_half((C, C))
    zero = jnp.zeros_like(pair)
    stacked = jnp.concatenate([jnp.where(left, pair, zero), jnp.where(left, zero, pair)], axis=0)
    picks = jnp.concatenate([member_cols(columns, spot) for spot in spots], axis=1)
    return dot_nn(picks, stacked)


def project_kernel(x_ref, gain_ref, shift_ref, wq_ref, wkv_ref, ids_ref, normed_ref, send_ref, q_scr, kv_scr):
    for s in range(SEQS):
        rows = slice(s * C, (s + 1) * C)
        unit, unused = normalise(x_ref[rows, :].astype(F32))
        normed_ref[rows, :] = (unit * gain_ref[...] + shift_ref[...]).astype(BF16)
    width = wq_ref.shape[1]
    q_scr[...] = dot_nn(normed_ref[...], wq_ref[...])
    kv_scr[...] = dot_nn(normed_ref[...], wkv_ref[...]).astype(BF16)
    left = left_half((C, C))
    lane = lax.broadcasted_iota(jnp.int32, (C, C), 1)
    for s in range(SEQS):
        rows = slice(s * C, (s + 1) * C)
        sums, counts = [], []
        for p, heads in enumerate(PAIRS):
            members = [member_rows(ids_ref, h, s * C) for h in heads]
            sums.append(cluster_pair(members, q_scr[rows, p * C : (p + 1) * C]))
            counts += [jnp.sum(m, axis=1, keepdims=True) for m in members]
        keys = [kv_scr[rows, p * C : (p + 1) * C] for p in range(3)]
        values = [kv_scr[rows, width + p * C : width + (p + 1) * C] for p in range(3)]
        for t in range(2):
            full = 2 * t
            order = (0, 1, 2) if t == 0 else (4, 5, 3)
            tail = jnp.zeros((C, C), F32)
            for i, h in enumerate(order):
                tail = jnp.where(lane == HD + i, counts[h], tail)
            single = sums[1] if t == 0 else roll_half(sums[1])
            if t == 0:
                mixed = jnp.where(left, keys[1].astype(F32), roll_half(values[1].astype(F32)))
            else:
                mixed = jnp.where(left, roll_half(keys[1].astype(F32)), values[1].astype(F32))
            o = s * 2 + t
            send_ref[o, :, 0:C] = sums[full].astype(BF16)
            send_ref[o, :, C : 2 * C] = jnp.where(left, single, tail).astype(BF16)
            send_ref[o, :, 2 * C : 3 * C] = keys[full]
            send_ref[o, :, 3 * C : 4 * C] = values[full]
            send_ref[o, :, 4 * C : 5 * C] = mixed.astype(BF16)


def sum_kernel(recv_ref, out_ref):
    total = recv_ref[0].astype(F32)
    for i in range(1, SUB):
        total = total + recv_ref[i].astype(F32)
    out_ref[...] = total


def add_all(refs):
    total = refs[0][...]
    for r in refs[1:]:
        total = total + r[...]
    return total


def centroid_blocks(total):
    left = left_half((C, C))
    pair, tail = total[:, 0:C], total[:, C : 2 * C]
    count = [jnp.maximum(tail[:, HD + i : HD + i + 1], 1.0) for i in range(3)]
    zero = jnp.zeros((C, C), F32)
    pair = pair / jnp.where(left, count[0], count[1])
    single = tail / count[2]
    return (
        jnp.where(left, pair, zero).astype(BF16),
        jnp.where(left, zero, pair).astype(BF16),
        jnp.where(left, single, zero).astype(BF16),
    )


KEY_LANES = (2 * C, 2 * C, 4 * C)
VALUE_LANES = (3 * C, 3 * C, 4 * C)


def attend_kernel(*refs):
    recv_ref, sums, (part_ref, total_ref) = refs[0], refs[3:-2], refs[-2:]
    total = add_all(sums)
    total_ref[...] = total
    left = left_half((C, C))
    lane = lax.broadcasted_iota(jnp.int32, (C, C), 1)
    length = SUB * C
    outs = []
    stats = jnp.zeros((C, C), F32)
    for i, centroid in enumerate(centroid_blocks(total)):
        k = recv_ref[:, :, KEY_LANES[i] : KEY_LANES[i] + C].reshape(length, C)
        v = recv_ref[:, :, VALUE_LANES[i] : VALUE_LANES[i] + C].reshape(length, C)
        scores = dot_nt(centroid, k) * SCALE
        top = jnp.max(scores, axis=1, keepdims=True).astype(BF16).astype(F32)
        weight = jnp.exp(scores - top)
        mass = jnp.sum(weight, axis=1, keepdims=True)
        high = mass.astype(BF16).astype(F32)
        outs.append(dot_nn(weight.astype(BF16), v))
        for spot, column in ((i, top), (3 + i, high), (6 + i, mass - high)):
            stats = jnp.where(lane == spot, column, stats)
    part_ref[:, 0:C] = jnp.where(left, outs[0], outs[1]).astype(BF16)
    part_ref[:, C : 2 * C] = jnp.where(left, stats, outs[2]).astype(BF16)


def merge_kernel(*refs):
    parts, (fin_ref, send_ref) = refs[:-2], refs[-2:]
    left = left_half((C, C))
    lane = lax.broadcasted_iota(jnp.int32, (C, C), 1)
    tails = [r[:, C : 2 * C].astype(F32) for r in parts]
    stats = jnp.zeros((C, C), F32)
    scales = []
    for i in range(3):
        tops = [t[:, i : i + 1] for t in tails]
        top = functools.reduce(jnp.maximum, tops)
        factors = [jnp.exp(v - top) for v in tops]
        masses = [t[:, 3 + i : 4 + i] + t[:, 6 + i : 7 + i] for t in tails]
        mass = sum(m * f for m, f in zip(masses, factors))
        stats = jnp.where(lane == i, top, stats)
        stats = jnp.where(lane == 3 + i, mass, stats)
        scales.append([f / mass for f in factors])
    pair = sum(
        r[:, 0:C].astype(F32) * jnp.where(left, scales[0][j], scales[1][j])
        for j, r in enumerate(parts)
    )
    single = sum(t * scales[2][j] for j, t in enumerate(tails))
    fin_ref[:, 0:C] = pair
    fin_ref[:, C : 2 * C] = jnp.where(left, stats, single)
    short = jnp.where(left_half((HD, C)), roll_half(single[0:HD]), single[HD:C])
    for o in range(send_ref.shape[0]):
        send_ref[o, 0:C, :] = pair.astype(BF16)
        send_ref[o, C : C + HD, :] = short.astype(BF16)


def middle_kernel(
    recv_ref, ids_ref, ids_other_ref, x_ref, wo_ref, wo_other_ref, gain_ref, shift_ref, up_ref,
    up_bias_ref, down_ref, bg_ref, attended_ref, residual_ref, normed_ref, active_ref, hidden_ref,
    back_ref, up_bias_out_ref, a_scr, w_scr,
):
    half = wo_ref.shape[0]
    me = lax.axis_index("mp")
    mine = pl.multiple_of(me * half, C)
    theirs = pl.multiple_of((1 - me) * half, C)
    w_scr[pl.ds(mine, half), :] = wo_ref[...]
    w_scr[pl.ds(theirs, half), :] = wo_other_ref[...]
    short = left_half((HD, C))
    for s in range(x_ref.shape[0] // C):
        rows = slice(s * C, (s + 1) * C)
        own, far = ids_ref[:, rows], ids_other_ref[:, rows]
        columns = label_columns((jnp.where(me == 0, own, far), jnp.where(me == 0, far, own)))
        for m in range(2):
            packs = [recv_ref[(s * 2 + t) * 2 + m] for t in range(2)]
            tails = [v[C : C + HD].astype(F32) for v in packs]
            middle = jnp.concatenate(
                [
                    jnp.where(short, tails[0], roll_half(tails[1])),
                    jnp.where(short, roll_half(tails[0]), tails[1]),
                ],
                axis=0,
            ).astype(BF16)
            for p, pair in enumerate((packs[0][0:C], middle, packs[1][0:C])):
                spots = [m * 8 + h for h in PAIRS[p]]
                a_scr[rows, m * half + p * C : m * half + (p + 1) * C] = spread_pair(
                    columns, spots, pair
                ).astype(BF16)
    attended_ref[...] = a_scr[:, pl.ds(mine, half)]
    residual = x_ref[...].astype(F32) + dot_nn(a_scr[...], w_scr[...])
    residual_ref[...] = residual
    unit, unused = normalise(residual)
    normed = (unit * gain_ref[...] + shift_ref[...]).astype(BF16)
    normed_ref[...] = normed
    hidden = dot_nn(normed, up_ref[...]) + up_bias_ref[...]
    below = 0.5 * (1.0 + lax.erf(hidden * (0.5**0.5)))
    active_ref[...] = (hidden * below).astype(BF16)
    slope = below + hidden * jnp.exp(-0.5 * hidden * hidden) * 0.3989422804014327
    hidden_grad = (slope * dot_nt(bg_ref[...], down_ref[...])).astype(BF16)
    hidden_ref[...] = hidden_grad
    up_bias_out_ref[...] = jnp.sum(hidden_grad.astype(F32), axis=0, keepdims=True)
    back_ref[...] = dot_nt(hidden_grad, up_ref[...]).astype(BF16)


def branch_kernel(one_ref, two_ref, down_ref, after_ref, branch_ref):
    half = one_ref.shape[0]
    branch_ref[0:half, :] = dot_nn(one_ref[...], down_ref[...]).astype(BF16)
    branch_ref[half:, :] = dot_nn(two_ref[...], down_ref[...]).astype(BF16)


def output_kernel(one_ref, two_ref, branch_ref, other_ref, bias_ref, out_ref):
    half = one_ref.shape[0]
    for i, r in enumerate((one_ref, two_ref)):
        rows = slice(i * half, (i + 1) * half)
        total = branch_ref[rows, :].astype(F32) + other_ref[rows, :].astype(F32)
        out_ref[rows, :] = (r[...] + (total + bias_ref[...])).astype(BF16)


def turn_kernel(
    back_one_ref, back_two_ref, other_one_ref, other_two_ref, residual_one_ref, residual_two_ref,
    gain_ref, bg_ref, wo_ref, ids_ref, bias_one_ref, bias_two_ref,
    residual_grad_ref, mixed_ref, send_ref, ag_scr, vec_scr,
):
    me = lax.axis_index("mp")
    gain_sum = jnp.zeros(gain_ref.shape, F32)
    shift_sum = jnp.zeros(gain_ref.shape, F32)
    down_sum = jnp.zeros(gain_ref.shape, F32)
    halves = (
        (back_one_ref, other_one_ref, residual_one_ref), (back_two_ref, other_two_ref, residual_two_ref)
    )
    for s in range(SEQS):
        rows = slice(s * C, (s + 1) * C)
        inner = slice((s % 2) * C, (s % 2 + 1) * C)
        back_ref, other_ref, residual_ref = halves[s // 2]
        grad = back_ref[inner, :].astype(F32) + other_ref[inner, :].astype(F32)
        unit, inverse = normalise(residual_ref[inner, :])
        out_grad = bg_ref[rows, :].astype(F32)
        gain_sum = gain_sum + jnp.sum(grad * unit, axis=0, keepdims=True)
        shift_sum = shift_sum + jnp.sum(grad, axis=0, keepdims=True)
        down_sum = down_sum + jnp.sum(out_grad, axis=0, keepdims=True)
        residual_grad = out_grad + norm_pull(unit, inverse, grad * gain_ref[...])

        @pl.when(me == s // 2)
        def keep_own():
            residual_grad_ref[inner, :] = residual_grad

        mixed_ref[rows, :] = residual_grad.astype(BF16)
    ag_scr[...] = dot_nt(mixed_ref[...], wo_ref[...])
    vec_scr[...] = jnp.zeros(vec_scr.shape, F32)
    spot = 0
    for v in (bias_one_ref[...] + bias_two_ref[...], gain_sum, shift_sum, down_sum):
        for i in range(v.shape[1] // C):
            vec_scr[spot : spot + 1, :] = v[:, i * C : (i + 1) * C]
            spot += 1
    short = left_half((HD, C))
    for s in range(SEQS):
        rows = slice(s * C, (s + 1) * C)
        sums = []
        for p, heads in enumerate(PAIRS):
            members = [member_rows(ids_ref, h, s * C) for h in heads]
            sums.append(cluster_pair(members, ag_scr[rows, p * C : (p + 1) * C]))
        top, bottom = sums[1][0:HD], sums[1][HD:C]
        singles = (
            jnp.where(short, top, roll_half(bottom)),
            jnp.where(short, roll_half(top), bottom),
        )
        for t in range(2):
            o = s * 2 + t
            send_ref[o, 0:C, :] = sums[2 * t].astype(BF16)
            send_ref[o, C : C + HD, :] = singles[t].astype(BF16)
            vec = vec_scr[4 * o : 4 * o + 4, :]
            high = vec.astype(BF16).astype(F32)
            send_ref[o, C + HD : PACK, :] = jnp.concatenate(
                [high, vec - high, jnp.zeros((8, C), F32)], axis=0
            ).astype(BF16)


def grad_sum_kernel(recv_ref, out_ref):
    total = recv_ref[0].astype(F32)
    for i in range(1, SUB):
        total = total + recv_ref[i].astype(F32)
    out_ref[0 : C + HD, :] = total[0 : C + HD].astype(BF16)
    vec = total[C + HD : C + HD + 4] + total[C + HD + 4 : C + HD + 8]
    high = vec.astype(BF16).astype(F32)
    out_ref[C + HD : PACK, :] = jnp.concatenate(
        [high, vec - high, jnp.zeros((8, C), F32)], axis=0
    ).astype(BF16)


def lift(short):
    return jnp.concatenate([roll_half(short), short], axis=0)


def attend_back_kernel(*refs):
    recv_ref, total_ref, fin_ref = refs[:3]
    sums, (cgrad_ref, vec_ref, send_ref) = refs[3:-3], refs[-3:]
    total = sums[0][...].astype(F32)
    for r in sums[1:]:
        total = total + r[...].astype(F32)
    left = left_half((C, C))
    zero = jnp.zeros((C, C), F32)
    single = lift(total[C : C + HD])
    grads = (
        jnp.where(left, total[0:C], zero).astype(BF16),
        jnp.where(left, zero, total[0:C]).astype(BF16),
        jnp.where(left, zero, single).astype(BF16),
    )
    vec_ref[...] = total[C + HD : C + HD + 4] + total[C + HD + 4 : C + HD + 8]
    centroids = centroid_blocks(total_ref[...])
    tail = fin_ref[:, C : 2 * C]
    outs = (fin_ref[:, 0:C], fin_ref[:, 0:C], tail)
    length = SUB * C
    probs, score_grads, cgrads = [], [], []
    for i in range(3):
        k = recv_ref[:, :, KEY_LANES[i] : KEY_LANES[i] + C].reshape(length, C)
        v = recv_ref[:, :, VALUE_LANES[i] : VALUE_LANES[i] + C].reshape(length, C)
        scores = dot_nt(centroids[i], k) * SCALE
        prob = jnp.exp(scores - tail[:, i : i + 1]) / tail[:, 3 + i : 4 + i]
        delta = jnp.sum(grads[i].astype(F32) * outs[i], axis=1, keepdims=True)
        score_grad = (prob * (dot_nt(grads[i], v) - delta) * SCALE).astype(BF16)
        cgrads.append(dot_nn(score_grad, k))
        probs.append(prob.astype(BF16))
        score_grads.append(score_grad)
    cgrad_ref[0:C, :] = jnp.where(left, cgrads[0], cgrads[1]).astype(BF16)
    single = cgrads[2]
    cgrad_ref[C : C + HD, :] = jnp.where(
        left_half((HD, C)), single[0:HD], roll_half(single[HD:C])
    ).astype(BF16)
    for n, (lhs, rhs) in enumerate((
        (score_grads[0:2], centroids[0:2]),
        (probs[0:2], grads[0:2]),
        ((score_grads[2], probs[2]), (centroids[2], grads[2])),
    )):
        made = dot_tn(jnp.concatenate(lhs, axis=0), jnp.concatenate(rhs, axis=0))
        send_ref[:, :, n * C : (n + 1) * C] = made.astype(BF16).reshape(SUB, C, C)


def finish_back_kernel(*refs):
    total_ref, vec_ref, cgrads, send_ref = refs[0], refs[1], refs[2:-1], refs[-1]
    grad = cgrads[0][...].astype(F32)
    for r in cgrads[1:]:
        grad = grad + r[...].astype(F32)
    left = left_half((C, C))
    short = left_half((HD, C))
    tail = total_ref[:, C : 2 * C]
    count = [jnp.maximum(tail[:, HD + i : HD + i + 1], 1.0) for i in range(3)]
    pair = grad[0:C] / jnp.where(left, count[0], count[1])
    single = grad[C : C + HD] / jnp.where(short, count[2][0:HD], count[2][HD:C])
    vec = vec_ref[...]
    high = vec.astype(BF16).astype(F32)
    extra = jnp.concatenate([high, vec - high, jnp.zeros((8, C), F32)], axis=0)
    for o in range(SUB):
        send_ref[o, 0:C, :] = pair.astype(BF16)
        send_ref[o, C : C + HD, :] = single.astype(BF16)
        send_ref[o, C + HD : PACK, :] = extra.astype(BF16)


def gather_kernel(recv_ref, grads_ref):
    left = left_half((C, C))
    width = grads_ref.shape[1] // 2
    for s in range(SEQS):
        rows = slice(s * C, (s + 1) * C)
        blocks = [recv_ref[s * 2 + t] for t in range(2)]
        tail = [b[:, 2 * C : 3 * C].astype(F32) for b in blocks]
        k_mid = jnp.where(left, tail[0], roll_half(tail[1])).astype(BF16)
        v_mid = jnp.where(left, roll_half(tail[0]), tail[1]).astype(BF16)
        for n, mid in enumerate((k_mid, v_mid)):
            base = n * width
            first = n * C
            grads_ref[rows, base : base + C] = blocks[0][:, first : first + C]
            grads_ref[rows, base + C : base + 2 * C] = mid
            grads_ref[rows, base + 2 * C : base + 3 * C] = blocks[1][:, first : first + C]


def first_back_kernel(recv_ref, ids_ref, wq_ref, wkv_ref, kv_ref, grads_ref, keep_ref, give_ref, scr):
    short = left_half((HD, C))
    for s in range(SEQS):
        rows = slice(s * C, (s + 1) * C)
        columns = label_columns((ids_ref[:, rows],))
        packs = [recv_ref[s * 2 + t] for t in range(2)]
        tails = [v[C : C + HD].astype(F32) for v in packs]
        first = [jnp.where(short, tails[0], roll_half(tails[1])), jnp.where(short, roll_half(tails[0]), tails[1])]
        middle = jnp.concatenate(first, axis=0).astype(BF16)
        for p, pair in enumerate((packs[0][0:C], middle, packs[1][0:C])):
            grads_ref[rows, p * C : (p + 1) * C] = spread_pair(columns, PAIRS[p], pair).astype(BF16)
    scr[...] = (
        dot_nt(grads_ref[...], wq_ref[...]) + dot_nt(kv_ref[...], wkv_ref[...])
    ).astype(BF16)
    half = keep_ref.shape[0]
    me = lax.axis_index("mp")
    keep_ref[...] = scr[pl.ds(pl.multiple_of(me * half, C), half), :]
    give_ref[...] = scr[pl.ds(pl.multiple_of((1 - me) * half, C), half), :]


def last_kernel(keep_ref, got_ref, x_ref, gain_ref, residual_grad_ref, input_grad_ref, vec_ref):
    half = keep_ref.shape[0]
    start = lax.axis_index("mp") * half
    gain_sum = jnp.zeros((1, x_ref.shape[1]), F32)
    shift_sum = jnp.zeros((1, x_ref.shape[1]), F32)
    for s in range(half // C):
        rows = slice(s * C, (s + 1) * C)
        x = x_ref[pl.ds(pl.multiple_of(start + s * C, C), C), :].astype(F32)
        grad = keep_ref[rows, :].astype(F32) + got_ref[rows, :].astype(F32)
        unit, inverse = normalise(x)
        gain_sum = gain_sum + jnp.sum(grad * unit, axis=0, keepdims=True)
        shift_sum = shift_sum + jnp.sum(grad, axis=0, keepdims=True)
        made = norm_pull(unit, inverse, grad * gain_ref[...])
        input_grad_ref[rows, :] = (residual_grad_ref[rows, :] + made).astype(BF16)
    vec_ref[0:1, :] = gain_sum
    vec_ref[1:2, :] = shift_sum


def join_kernel(own_ref, got_ref, out_ref):
    half = own_ref.shape[0]
    me = lax.axis_index("mp")
    out_ref[pl.ds(pl.multiple_of(me * half, C), half), :] = own_ref[...]
    out_ref[pl.ds(pl.multiple_of((1 - me) * half, C), half), :] = got_ref[...]


def weight_kernel(order, counts, *refs):
    pairs, (keep_ref, give_ref, scr) = refs[:-3], refs[-3:]
    base = 0
    spot = 0
    for n in counts:
        width = pairs[spot + 1].shape[1]
        made = sum(dot_tn(pairs[spot + 2 * i][...], pairs[spot + 2 * i + 1][...]) for i in range(n))
        scr[:, base : base + width] = made.astype(BF16)
        base += width
        spot += 2 * n
    own = scr.shape[0] // 16
    me = lax.axis_index(order[0])
    for j, place in enumerate(row_order(order[1:])):
        for bit, out_ref in ((me, keep_ref), (1 - me, give_ref)):
            start = (place + bit * WEIGHT[order[0]]) * own
            out_ref[j * own : (j + 1) * own, :] = scr[pl.ds(pl.multiple_of(start, 16), own), :]


def fold_kernel(axis, keep_ref, got_ref, next_keep_ref, next_give_ref):
    half = next_keep_ref.shape[0]
    me = lax.axis_index(axis)
    for bit, out_ref in ((me, next_keep_ref), (1 - me, next_give_ref)):
        rows = pl.ds(pl.multiple_of(bit * half, 16), half)
        out_ref[...] = (keep_ref[rows, :].astype(F32) + got_ref[rows, :].astype(F32)).astype(BF16)


def close_kernel(keep_ref, got_ref, out_ref):
    out_ref[...] = keep_ref[...].astype(F32) + got_ref[...].astype(F32)


def plain_weight_kernel(counts, *refs):
    pairs, out_ref = refs[:-1], refs[-1]
    base = 0
    spot = 0
    for n in counts:
        width = pairs[spot + 1].shape[1]
        made = sum(dot_tn(pairs[spot + 2 * i][...], pairs[spot + 2 * i + 1][...]) for i in range(n))
        out_ref[:, base : base + width] = made
        base += width
        spot += 2 * n


WEIGHT = {"g": 8, "b2": 4, "b1": 2, "b0": 1}


def row_order(axes):
    places = [0]
    for axis in axes:
        places = [p + bit * WEIGHT[axis] for p in places for bit in (0, 1)]
    return places


def on_device(
    inputs, cluster_ids, norm_one_gain, norm_one_shift, query_weight, keyval_weight, out_weight,
    norm_two_gain, norm_two_shift, up_weight, up_bias, down_weight, down_bias, cotangent, loss_mask,
):
    groups = lax.axis_size("g")
    devices = groups * SUB
    tokens, model = inputs.shape
    width = query_weight.shape[1]
    hidden = up_weight.shape[1]
    half = tokens // 2
    own = model // devices
    other = functools.partial(lax.ppermute, axis_name="mp", perm=SWAP)
    row = lambda v: v.reshape(1, -1)
    whole = pl.BlockSpec(memory_space=pltpu.VMEM)
    unread = pl.BlockSpec(memory_space=pl.ANY)

    def across(v):
        if groups == 1:
            return [v]
        if groups == 2:
            return [v, lax.ppermute(v, "g", SWAP)]
        gathered = lax.all_gather(v, "g", axis=0)
        return [gathered[i] for i in range(groups)]

    def weight_terms(order, name, *sides):
        counts = tuple(len(side) for side in sides)
        flat = [v for side in sides for pair in side for v in pair]
        columns = sum(side[0][1].shape[1] for side in sides)
        flops = 2 * tokens * model * columns
        if groups != 2 or own % 16:
            (part,) = call(
                functools.partial(plain_weight_kernel, counts), [((model, columns), F32)], *flat,
                flops=flops, name=name, vmem=48 * 2**20,
            )
            return lax.psum_scatter(part, SEQ, scatter_dimension=0, tiled=True)
        return tuple(call(
            functools.partial(weight_kernel, order, counts),
            [((model // 2, columns), BF16), ((model // 2, columns), BF16)], *flat,
            scratch=[pltpu.VMEM((model, columns), BF16)], flops=flops, name=name, vmem=48 * 2**20,
        ))

    def reduce_terms(order, terms, name):
        if groups != 2 or own % 16:
            return terms
        keep, give = terms
        for step, axis in enumerate(order):
            got = lax.ppermute(give, axis, SWAP)
            rows, columns = keep.shape
            if step == len(order) - 1:
                return call(close_kernel, [(keep.shape, F32)], keep, got, name=name + "_end")[0]
            shape = (rows // 2, columns)
            keep, give = call(
                functools.partial(fold_kernel, order[step + 1]), [(shape, BF16), (shape, BF16)], keep, got,
                name=name + "_" + axis,
            )

    ids_other = other(cluster_ids)
    wo_other = other(out_weight)
    wkv = keyval_weight.reshape(model, 2 * width)
    bg = cotangent * loss_mask.astype(BF16)[:, None]

    normed_one, send_one = call(
        project_kernel,
        [((tokens, model), BF16), ((SUB, C, 5 * C), BF16)],
        inputs, row(norm_one_gain), row(norm_one_shift), query_weight, wkv, cluster_ids,
        scratch=[pltpu.VMEM((tokens, width), F32), pltpu.VMEM((tokens, 2 * width), BF16)],
        flops=2 * tokens * model * 3 * width,
        name="project",
    )
    recv_one = lax.all_to_all(send_one, NEAR, 0, 0)
    (sums,) = call(
        sum_kernel, [((C, 2 * C), F32)], recv_one, name="query_sums",
        specs=([pl.BlockSpec((SUB, C, 2 * C), lambda i: (0, 0, 0))], [pl.BlockSpec((C, 2 * C), lambda i: (0, 0))]),
    )
    sums = across(sums)
    part, total = call(
        attend_kernel, [((C, 2 * C), BF16), ((C, 2 * C), F32)], recv_one, ids_other, wo_other, *sums,
        name="attend", flops=2 * 2 * 3 * C * SUB * C * C,
        specs=([whole, unread, unread] + [whole] * len(sums), [whole] * 2),
    )
    fin, send_two = call(
        merge_kernel, [((C, 2 * C), F32), ((2 * SUB, C + HD, C), BF16)], *across(part), name="merge"
    )
    recv_two = lax.all_to_all(send_two, NEAR + ("mp",), 0, 0)
    halves = []
    for n in range(2):
        rows = lambda cols, n=n: pl.BlockSpec((half, cols), lambda i: (n, 0))
        lanes = pl.BlockSpec((cluster_ids.shape[0], half), lambda i, n=n: (0, n))
        halves.append(call(
            middle_kernel,
            [
                ((half, width), BF16), ((half, model), F32), ((half, model), BF16),
                ((half, hidden), BF16), ((half, hidden), BF16), ((half, model), BF16),
                ((1, hidden), F32),
            ],
            recv_two, cluster_ids, ids_other, inputs, out_weight, wo_other, row(norm_two_gain),
            row(norm_two_shift), up_weight, row(up_bias), down_weight, bg,
            scratch=[pltpu.VMEM((half, 2 * width), BF16), pltpu.VMEM((2 * width, model), BF16)],
            flops=2 * half * model * (2 * width + 3 * hidden),
            vmem=48 * 2**20, name="middle",
            specs=(
                [pl.BlockSpec((SUB, C + HD, C), lambda i, n=n: (n, 0, 0)), lanes, lanes, rows(model)]
                + [whole] * 7 + [rows(model)],
                [whole] * 7,
            ),
        ))
    attended, residual, normed_two, active, hidden_grad, back, bias_part = zip(*halves)
    back_other = [other(v) for v in back]
    up_order = ("b0", "b1", "b2", "g")
    down_order = ("b0", "b2", "b1", "g")
    up_terms = weight_terms(up_order, "up_terms", list(zip(normed_two, hidden_grad)))
    bg_halves = (bg[:half], bg[half:])
    down_terms = weight_terms(down_order, "down_terms", list(zip(bg_halves, active)))
    residual_grad, mixed_grad, send_three = call(
        turn_kernel,
        [((half, model), F32), ((tokens, model), BF16), ((SUB, PACK, C), BF16)],
        *back, *back_other, *residual, row(norm_two_gain), bg, out_weight, cluster_ids, *bias_part,
        scratch=[pltpu.VMEM((tokens, width), F32), pltpu.VMEM((32, C), F32)],
        flops=2 * tokens * model * width, name="turn",
    )
    recv_three = lax.all_to_all(send_three, NEAR, 0, 0)
    up_sum = reduce_terms(up_order, up_terms, "up")
    down_sum = reduce_terms(down_order, down_terms, "down")
    (branch,) = call(
        branch_kernel, [((tokens, model), BF16)], *active, down_weight, back_other[1],
        flops=2 * tokens * model * hidden, name="branch", specs=([whole] * 3 + [unread], [whole]),
    )
    branch_other = other(branch)
    (block_output,) = call(
        output_kernel, [((tokens, model), BF16)], *residual, branch, branch_other, row(down_bias), name="output"
    )
    (grad_sums,) = call(grad_sum_kernel, [((PACK, C), BF16)], recv_three, name="grad_sums")
    cgrad, vec, send_four = call(
        attend_back_kernel,
        [((C + HD, C), BF16), ((4, C), F32), ((SUB, C, 3 * C), BF16)],
        recv_one, total, fin, *across(grad_sums), flops=2 * 5 * 3 * C * SUB * C * C, name="attend_back",
    )
    recv_four = lax.all_to_all(send_four, NEAR, 0, 0)
    (send_five,) = call(
        finish_back_kernel, [((SUB, PACK, C), BF16)], total, vec, *across(cgrad), name="finish_back"
    )
    recv_five = lax.all_to_all(send_five, NEAR, 0, 0)
    (kv_grads,) = call(gather_kernel, [((tokens, 2 * width), BF16)], recv_four, name="gather")
    kv_order = ("b0", "b1", "b2", "g")
    mixed_halves = (mixed_grad[:half], mixed_grad[half:])
    kv_terms = weight_terms(
        kv_order, "kv_terms", [(normed_one, kv_grads)], list(zip(mixed_halves, attended))
    )
    q_grads, keep, give = call(
        first_back_kernel,
        [((tokens, width), BF16), ((half, model), BF16), ((half, model), BF16)],
        recv_five, cluster_ids, query_weight, wkv, kv_grads,
        scratch=[pltpu.VMEM((tokens, model), BF16)], flops=2 * tokens * model * 3 * width, name="first_back",
    )
    got = other(give)
    q_terms = weight_terms(kv_order, "q_terms", [(normed_one, q_grads)])
    grad_half, vec_one = call(
        last_kernel, [((half, model), BF16), ((2, model), F32)],
        keep, got, inputs, row(norm_one_gain), residual_grad, name="last",
    )
    (input_grad,) = call(join_kernel, [((tokens, model), BF16)], grad_half, other(grad_half), name="join")
    kv_sum = reduce_terms(kv_order, kv_terms, "kv")
    q_sum = reduce_terms(kv_order, q_terms, "q")
    vec_send = jnp.broadcast_to(
        vec_one.reshape(2, devices, own).swapaxes(0, 1).reshape(devices, 1, 2 * own), (devices, 2, 2 * own)
    ).reshape(2 * devices, 2 * own)
    vec_recv = lax.all_to_all(vec_send, SEQ + ("mp",), 0, 0, tiled=True)
    vec_sum = jnp.sum(vec_recv, axis=0).reshape(2, own)

    small = recv_five[:, C + HD : C + HD + 8, :].astype(F32)
    small = (small[:, 0:4] + small[:, 4:8]).reshape(-1)
    start = lax.axis_index(SEQ) * own
    take = lambda base: lax.dynamic_slice(small, (base + start,), (own,))
    return (
        block_output,
        input_grad,
        vec_sum[0],
        vec_sum[1],
        q_sum,
        kv_sum[:, 0 : 2 * width].reshape(own, 2, width),
        kv_sum[:, 2 * width :].T,
        take(hidden),
        take(hidden + model),
        up_sum,
        small[0:hidden],
        down_sum.T,
        take(hidden + 2 * model),
    )


def solution(mesh):
    groups = mesh.shape["seq"] // SUB
    fine = Mesh(
        mesh.devices.reshape(groups, 2, 2, 2, mesh.shape["mp"]), ("g", "b2", "b1", "b0", "mp")
    )
    placed = (
        P(SEQ, None),
        P("mp", SEQ),
        P(),
        P(),
        P(None, "mp"),
        P(None, None, "mp"),
        P("mp", None),
        P(),
        P(),
        P(None, "mp"),
        P("mp"),
        P("mp", None),
        P(),
        P(SEQ, None),
        P(SEQ),
    )
    return jax.shard_map(
        on_device,
        mesh=fine,
        in_specs=placed,
        out_specs=(
            P(SEQ, None),
            P(SEQ, None),
            P(SEQ),
            P(SEQ),
            P(SEQ, "mp"),
            P(SEQ, None, "mp"),
            P("mp", SEQ),
            P(SEQ),
            P(SEQ),
            P(SEQ, "mp"),
            P("mp"),
            P("mp", SEQ),
            P(SEQ),
        ),
        check_vma=False,
    )
```

time: 271 us -> 233 us (0.86)
  waiting for transfers between devices: 122 us -> 70.6 us
  starting transfers between devices: 24 us -> 51.6 us
  Pallas kernels: 33.4 us -> 59.4 us
  blocking collectives: 34.2 us -> 11.2 us
  between operations: 14.5 us -> 1.44 us
  other arithmetic: 11.2 us -> 3.03 us
  local copies, waits for them, and re-layouts: 30.3 us -> 34.5 us
    pallas_call x14 -> x36, Pallas kernels: 33.4 us -> 59.4 us  [call(): pl.pallas_call(kernel, out_shape=[jax.ShapeDtypeStruct(s, d) for s, d in...]
    ppermute x1, waiting for transfers between devices: 25.2 us -> 2.22 us  [on_device(): ids_other = other(cluster_ids)]
    all_to_all x1 -> x0, blocking collectives: 22.5 us -> none  [on_device(): recv_one = lax.all_to_all(send_one, NEAR, 0, 0)]
    ppermute x4 -> x20, starting transfers between devices: 2.49 us -> 20.2 us  [the longest x16 16.6 us: reduce_terms(): got = lax.ppermute(give, axis, SWAP)]
    ppermute x4, waiting for transfers between devices: 28.9 us -> 15.9 us  [across(): return [v, lax.ppermute(v, 'g', SWAP)]]
    ppermute x4 -> x20, waiting for transfers between devices: 33.8 us -> 22.3 us  [the longest x16 12.4 us: reduce_terms(): got = lax.ppermute(give, axis, SWAP)]
    all_to_all x1, waiting for transfers between devices: 0.01 us -> 11 us  [on_device(): recv_two = lax.all_to_all(send_two, NEAR + ('mp',), 0, 0)]
    unnamed x86 -> x175, local copies, waits for them, and re-layouts: 22 us -> 29.5 us
  transfers between devices with their start and end apart: 16 -> 32, of which waited for: 13 -> 15; matrix products, arithmetic and copies ran while one was open for 6% -> 3% of each run, Pallas kernels for 4% -> 19%
where the time goes in v2:
time: 233 us; the launch traced here: 232 us
  waiting for transfers between devices  70.6 us (30%)
  Pallas kernels  59.4 us (25%)
  starting transfers between devices  51.6 us (22%)
  local copies, waits for them, and re-layouts  34.5 us (15%)
  blocking collectives  11.2 us (5%)
  other arithmetic  3.03 us (1%)
    pallas_call x36, Pallas kernels, call(): pl.pallas_call(kernel, out_shape=[jax.ShapeDtypeStruct(s, d) for s, d in...  59.4 us
    unnamed x175, local copies, waits for them, and re-layouts  29.5 us
    ppermute x16, starting transfers between devices, reduce_terms(): got = lax.ppermute(give, axis, SWAP)  16.6 us
    ppermute x4, waiting for transfers between devices, across(): return [v, lax.ppermute(v, 'g', SWAP)]  15.9 us
    all_to_all x1, waiting for transfers between devices, on_device(): recv_one = lax.all_to_all(send_one, NEAR, 0, 0)  15.7 us
    ppermute x16, waiting for transfers between devices, reduce_terms(): got = lax.ppermute(give, axis, SWAP)  12.4 us
    all_to_all x1, blocking collectives, on_device(): recv_three = lax.all_to_all(send_three, NEAR, 0, 0)  11.2 us
    all_to_all x1, waiting for transfers between devices, on_device(): recv_two = lax.all_to_all(send_two, NEAR + ('mp',), 0, 0)  11 us
  transfers between devices with their start and end apart: 32, of which 15 were waited for; matrix products, arithmetic and copies ran while one was open for 3% of the time, Pallas kernels for 19%

profile of v2, /device:TPU:0, one launch (start us, length us, event | category | flops | bytes accessed | tf_op | source)
XLA Modules:
  0.0 231.7 jit_solution(5504603560129041088)
XLA Ops:
  0.7 1.6 copy.30
  2.4 2.2 project.1
  4.6 1.1 copy-done.13
  6.6 5.4 %all-to-all-start = ((bf16[8,128,640]{2,1,0:T(8,128)(2,1)}), bf16[8,128,640]{2,1,0:T(8,128)(2,1)S(1)}, u32[]{:S(2)}, u32[]{:S(2)}) async-start(bf16[8,128,640]{2,1,0:T(8,128)(2,1)} %copy-done.13), calls=%async_computation | async-start | bytes 2621440 | tf_op jit(solution)/shard_map/all_to_all | solution.py:628
  11.9 1.6 collective-permute-start.1
  13.5 15.7 %all-to-all-done.recv_ref.refs_0_ = bf16[8,128,640]{2,1,0:T(8,128)(2,1)S(1)} async-done(((bf16[8,128,640]{2,1,0:T(8,128)(2,1)}), bf16[8,128,640]{2,1,0:T(8,128)(2,1)S(1)}, u32[]{:S(2)}, u32[]{:S(2)}) %all-to-all-start) | async-done | bytes 1310752 | tf_op jit(solution)/shard_map/all_to_all | solution.py:628
  29.3 2.7 %collective-permute-start.2 = (f32[128,256]{1,0:T(8,128)S(1)}, f32[128,256]{1,0:T(8,128)S(1)}, u32[]{:S(2)}, u32[]{:S(2)}) collective-permute-start(f32[128,256]{1,0:T(8,128)S(1)} %query_sums.1.refs_3_), channel_id=1, source_target_pairs={{0,16},{16,0},{1,17},{17,1},{2,18},{18,2},{3,19},{19,3},{4,20},{20... | collective-permute-start | bytes 393224 | tf_op jit(solution)/shard_map/ppermute | solution.py:579
  31.9 1.5 collective-permute-start
  33.5 2.2 collective-permute-done.refs_1_.ids_other_ref
  35.7 2.4 %collective-permute-done.2.refs_4_ = f32[128,256]{1,0:T(8,128)S(1)} collective-permute-done((f32[128,256]{1,0:T(8,128)S(1)}, f32[128,256]{1,0:T(8,128)S(1)}, u32[]{:S(2)}, u32[]{:S(2)}) %collective-permute-start.2) | collective-permute-done | bytes 131104 | tf_op jit(solution)/shard_map/ppermute | solution.py:579
  38.1 1.3 attend.1
  39.6 5.7 %collective-permute-done.3.refs_1_ = bf16[128,256]{1,0:T(8,128)(2,1)S(1)} collective-permute-done((bf16[128,256]{1,0:T(8,128)(2,1)S(1)}, bf16[128,256]{1,0:T(8,128)(2,1)S(1)}, u32[]{:S(2)}, u32[]{:S(2)}) %collective-permute-start.3) | collective-permute-done | bytes 65568 | tf_op jit(solution)/shard_map/ppermute | solution.py:579
  46.6 3.7 %all-to-all-start.1 = ((bf16[16,192,128]{2,1,0:T(8,128)(2,1)}), bf16[16,192,128]{2,1,0:T(8,128)(2,1)S(1)}, u32[]{:S(2)}, u32[]{:S(2)}) async-start(bf16[16,192,128]{2,1,0:T(8,128)(2,1)} %copy-done.38), calls=%async_computation.1 | async-start | bytes 1572864 | tf_op jit(solution)/shard_map/all_to_all | solution.py:642
  50.5 2.2 broadcast_multiply_fusion.bg_ref
  52.6 11.0 %all-to-all-done.1.recv_ref = bf16[16,192,128]{2,1,0:T(8,128)(2,1)S(1)} async-done(((bf16[16,192,128]{2,1,0:T(8,128)(2,1)}), bf16[16,192,128]{2,1,0:T(8,128)(2,1)S(1)}, u32[]{:S(2)}, u32[]{:S(2)}) %all-to-all-start.1) | async-done | bytes 786464 | tf_op jit(solution)/shard_map/all_to_all | solution.py:642
  63.6 1.1 copy-done.6
  64.7 6.7 %middle.3 = (bf16[256,384]{1,0:T(8,128)(2,1)S(1)}, f32[256,768]{1,0:T(8,128)S(1)}, bf16[256,768]{1,0:T(8,128)(2,1)S(1)}, bf16[256,1536]{1,0:T(8,128)(2,1)S(1)}, ...) custom-call(bf16[16,192,128]{2,1,0:T(8,128)(2,1)S(1)} %all-to-all-done.1.recv_ref, ...), custom_call_target="tpu_custom_call" | custom-call | flops 2113929216 | bytes 11642880 | tf_op jit(solution)/shard_map/middle/pallas_call | solution.py:45
  75.2 1.1 copy-done.4
  76.3 6.4 %middle.2 = (bf16[256,384]{1,0:T(8,128)(2,1)S(1)}, f32[256,768]{1,0:T(8,128)S(1)}, bf16[256,768]{1,0:T(8,128)(2,1)S(1)}, bf16[256,1536]{1,0:T(8,128)(2,1)S(1)}, ...) custom-call(bf16[16,192,128]{2,1,0:T(8,128)(2,1)S(1)} %copy-done.4, ...), custom_call_target="tpu_custom_call" | custom-call | flops 2113929216 | bytes 11642880 | tf_op jit(solution)/shard_map/middle/pallas_call | solution.py:45
  86.0 1.5 collective-permute-start.6
  87.4 9.9 %collective-permute-done.6.other_one_ref = bf16[256,768]{1,0:T(8,128)(2,1)S(1)} collective-permute-done((bf16[256,768]{1,0:T(8,128)(2,1)S(1)}, bf16[256,768]{1,0:T(8,128)(2,1)S(1)}, u32[]{:S(2)}, u32[]{:S(2)}) %collective-permute-start.6) | collective-permute-done | bytes 393248 | tf_op jit(solution)/shard_map/ppermute | solution.py:666
  97.3 3.0 %turn.1 = (f32[256,768]{1,0:T(8,128)S(1)}, bf16[512,768]{1,0:T(8,128)(2,1)S(1)}, bf16[8,208,128]{2,1,0:T(8,128)(2,1)S(1)}) custom-call(bf16[256,768]{1,0:T(8,128)(2,1)S(1)} %get-tuple-element.86.back_one_ref, bf16[256,768]{1,0:T(8,128)(2,1)S(1)} %get-tuple-element.83.back_two_ref, bf16[256,768]{1,0:T(8,128)(2,1)S(1)} %collective-permute-done.6.other_one_ref, ...), custom_call_target="tpu_custom_call" | custom-call | flops 301989888 | bytes 6548480 | tf_op jit(solution)/shard_map/turn/pallas_call | solution.py:45
  100.4 11.2 %all_to_all.34.recv_ref = bf16[8,208,128]{2,1,0:T(8,128)(2,1)S(1)} all-to-all(bf16[8,208,128]{2,1,0:T(8,128)(2,1)S(1)} %get-tuple-element.89), channel_id=1, replica_groups=mesh['g'=2,'b2'=2,'b1'=2,'b0'=2,'mp'=2] {'b2','b1','b0'}, dimensions={0} | all-to-all | bytes 851968 | tf_op jit(solution)/shard_map/all_to_all | solution.py:679
  111.6 2.3 collective-permute-start.7
  113.9 3.4 %collective-permute-done.7.refs_4_ = bf16[208,128]{1,0:T(8,128)(2,1)S(1)} collective-permute-done((bf16[208,128]{1,0:T(8,128)(2,1)S(1)}, bf16[208,128]{1,0:T(8,128)(2,1)S(1)}, u32[]{:S(2)}, u32[]{:S(2)}) %collective-permute-start.7) | collective-permute-done | bytes 53280 | tf_op jit(solution)/shard_map/ppermute | solution.py:579
  117.3 1.6 attend_back.1
  120.4 3.5 %all-to-all-start.4 = ((bf16[8,128,384]{2,1,0:T(8,128)(2,1)}), bf16[8,128,384]{2,1,0:T(8,128)(2,1)S(1)}, u32[]{:S(2)}, u32[]{:S(2)}) async-start(bf16[8,128,384]{2,1,0:T(8,128)(2,1)} %copy-done.37), calls=%async_computation.4 | async-start | bytes 1572864 | tf_op jit(solution)/shard_map/all_to_all | solution.py:696
  124.1 1.0 copy-done.25
  125.4 2.8 %down_terms.1 = (bf16[384,1536]{1,0:T(8,128)(2,1)S(1)}, bf16[384,1536]{1,0:T(8,128)(2,1)}) custom-call(bf16[256,768]{1,0:T(8,128)(2,1)S(1)} %get-tuple-element.140.refs_0_, bf16[256,1536]{1,0:T(8,128)(2,1)S(1)} %copy-done.28, bf16[256,768]{1,0:T(8,128)(2,1)S(1)} %get-tuple-element.139.refs_2_, bf16[256,1536]{1,0:T(8,128)(2,1)S(1)} %copy-done.25), custom_call_target="tpu_custom_call" | custom-call | flops 1207959552 | bytes 4718592 | tf_op jit(solution)/shard_map/down_terms/pallas_call | solution.py:45
  128.2 1.0 copy-done.18
  129.7 2.8 %up_terms.1 = (bf16[384,1536]{1,0:T(8,128)(2,1)S(1)}, bf16[384,1536]{1,0:T(8,128)(2,1)}) custom-call(bf16[256,768]{1,0:T(8,128)(2,1)S(1)} %copy-done.73, bf16[256,1536]{1,0:T(8,128)(2,1)S(1)} %copy-done.67, bf16[256,768]{1,0:T(8,128)(2,1)S(1)} %copy-done.71, bf16[256,1536]{1,0:T(8,128)(2,1)S(1)} %copy-done.65), custom_call_target="tpu_custom_call" | custom-call | flops 1207959552 | bytes 4718592 | tf_op jit(solution)/shard_map/up_terms/pallas_call | solution.py:45
  139.1 2.7 %kv_terms.1 = (bf16[384,1152]{1,0:T(8,128)(2,1)S(1)}, bf16[384,1152]{1,0:T(8,128)(2,1)}) custom-call(bf16[512,768]{1,0:T(8,128)(2,1)S(1)} %copy-done.31, bf16[512,768]{1,0:T(8,128)(2,1)S(1)} %gather.1.kv_ref.refs_1_, bf16[256,768]{1,0:T(8,128)(2,1)S(1)} %copy-done.48, bf16[256,384]{1,0:T(8,128)(2,1)S(1)} %copy-done.77, bf16[256,768]{1,0:T(8,128)(2,1)S(1)} %copy-done.47, ...), custom_call_target="tpu_custom_call" | custom-call | flops 905969664 | bytes 4521984 | tf_op jit(solution)/shard_map/kv_terms/pallas_call | solution.py:45
  142.7 1.7 collective-permute-start.8
  144.4 4.4 %collective-permute-done.8.refs_3_ = bf16[192,128]{1,0:T(8,128)(2,1)S(1)} collective-permute-done((bf16[192,128]{1,0:T(8,128)(2,1)S(1)}, bf16[192,128]{1,0:T(8,128)(2,1)S(1)}, u32[]{:S(2)}, u32[]{:S(2)}) %collective-permute-start.8) | collective-permute-done | bytes 49184 | tf_op jit(solution)/shard_map/ppermute | solution.py:579
  149.7 4.3 %all-to-all-start.3 = ((bf16[8,208,128]{2,1,0:T(8,128)(2,1)}), bf16[8,208,128]{2,1,0:T(8,128)(2,1)}, u32[]{:S(2)}, u32[]{:S(2)}) async-start(bf16[8,208,128]{2,1,0:T(8,128)(2,1)} %copy-done.12), calls=%async_computation.3 | async-start | bytes 851968 | tf_op jit(solution)/shard_map/all_to_all | solution.py:700
  154.1 1.1 copy-done.26
  155.2 1.1 copy-done.29
  156.3 2.3 branch.1.branch_ref
  158.6 1.3 collective-permute-start.5
  159.9 2.4 %down_b0.1 = (bf16[192,1536]{1,0:T(8,128)(2,1)S(1)}, bf16[192,1536]{1,0:T(8,128)(2,1)}) custom-call(bf16[384,1536]{1,0:T(8,128)(2,1)S(1)} %copy-done.19, bf16[384,1536]{1,0:T(8,128)(2,1)} %collective-permute-done.23.got_ref), custom_call_target="tpu_custom_call" | custom-call | bytes 3538944 | tf_op jit(solution)/shard_map/down_b0/pallas_call | solution.py:45
  163.1 1.7 collective-permute-start.24
  164.8 2.4 %up_b0.1 = (bf16[192,1536]{1,0:T(8,128)(2,1)S(1)}, bf16[192,1536]{1,0:T(8,128)(2,1)}) custom-call(bf16[384,1536]{1,0:T(8,128)(2,1)S(1)} %copy-done.17, bf16[384,1536]{1,0:T(8,128)(2,1)} %collective-permute-done.19.got_ref), custom_call_target="tpu_custom_call" | custom-call | bytes 3538944 | tf_op jit(solution)/shard_map/up_b0/pallas_call | solution.py:45
  167.2 1.5 collective-permute-start.20
  168.7 2.1 kv_b0.1
  172.2 1.1 copy-done.69
  173.2 3.9 %first_back.1 = (bf16[512,384]{1,0:T(8,128)(2,1)S(1)}, bf16[256,768]{1,0:T(8,128)(2,1)S(1)}, bf16[256,768]{1,0:T(8,128)(2,1)}) custom-call(bf16[8,208,128]{2,1,0:T(8,128)(2,1)} %all-to-all-done.3.recv_ref, s32[6,512]{1,0:T(8,128)S(1)} %copy-done.55, bf16[768,384]{1,0:T(8,128)(2,1)S(1)} %copy-done.69, bf16[768,768]{1,0:T(8,128)(2,1)S(1)} %bitcast.13, ...), custom_call_target="tpu_custom_call" | custom-call | flops 905969664 | bytes 4173824 | tf_op jit(solution)/shard_map/first_back/pallas_call | solution.py:45
  178.5 1.9 down_b2.1
  181.2 1.7 collective-permute-start.25
  183.8 2.0 up_b1.1
  186.3 1.4 q_terms.1
  188.6 2.4 %output.1 = bf16[512,768]{1,0:T(8,128)(2,1)} custom-call(f32[256,768]{1,0:T(8,128)S(1)} %copy-done.11, f32[256,768]{1,0:T(8,128)S(1)} %copy-done.9, bf16[512,768]{1,0:T(8,128)(2,1)} %branch.1.branch_ref, bf16[512,768]{1,0:T(8,128)(2,1)S(1)} %collective-permute-done.5.other_ref, f32[1,768]{1,0:T(1,128)S(1)} %reshape.80.bias_ref), custom_call_target="tpu_custom_call" | custom-call | bytes 3935232 | tf_op jit(solution)/shard_map/output/pallas_call | solution.py:45
  191.8 6.4 %collective-permute-done.25.got_ref = bf16[96,1536]{1,0:T(8,128)(2,1)} collective-permute-done((bf16[96,1536]{1,0:T(8,128)(2,1)}, bf16[96,1536]{1,0:T(8,128)(2,1)}, u32[]{:S(2)}, u32[]{:S(2)}) %collective-permute-start.25) | collective-permute-done | bytes 294944 | tf_op jit(solution)/shard_map/ppermute | solution.py:605
  198.2 1.0 down_b1.1
  199.2 1.4 collective-permute-start.26
  200.7 1.0 up_b2.1
  201.7 1.6 collective-permute-start.22
  203.3 1.0 q_b0.1
  204.4 1.5 collective-permute-start.12
  207.5 1.1 kv_b1.1
  210.0 3.3 %all-to-all-start.5 = ((f32[32,1,96]{2,1,0:T(1,128)}), f32[32,1,96]{2,1,0:T(1,128)S(1)}, u32[]{:S(2)}, u32[]{:S(2)}) async-start(f32[32,1,96]{2,1,0:T(1,128)} %bitcast.1), calls=%async_computation.5 | async-start | bytes 32768 | tf_op jit(solution)/shard_map/all_to_all | solution.py:725
  213.4 1.8 collective-permute-start.13
  217.9 2.6 %all-to-all-done.5 = f32[32,1,96]{2,1,0:T(1,128)S(1)} async-done(((f32[32,1,96]{2,1,0:T(1,128)}), f32[32,1,96]{2,1,0:T(1,128)S(1)}, u32[]{:S(2)}, u32[]{:S(2)}) %all-to-all-start.5) | async-done | bytes 12320 | tf_op jit(solution)/shard_map/all_to_all | solution.py:725
  221.2 2.6 %collective-permute-start.18 = (bf16[48,1152]{1,0:T(8,128)(2,1)S(1)}, bf16[48,1152]{1,0:T(8,128)(2,1)S(1)}, u32[]{:S(2)}, u32[]{:S(2)}) collective-permute-start(bf16[48,1152]{1,0:T(8,128)(2,1)S(1)} %get-tuple-element.118), channel_id=1, source_target_pairs={{0,16},{16,0},{1,17},{17,1},{2,18},{18,2},{3,19},{19,3},{4,20},{20... | collective-permute-start | bytes 331784 | tf_op jit(solution)/shard_map/ppermute | solution.py:605
  224.4 3.7 %collective-permute-done.14.got_ref = bf16[48,384]{1,0:T(8,128)(2,1)S(1)} collective-permute-done((bf16[48,384]{1,0:T(8,128)(2,1)S(1)}, bf16[48,384]{1,0:T(8,128)(2,1)S(1)}, u32[]{:S(2)}, u32[]{:S(2)}) %collective-permute-start.14) | collective-permute-done | bytes 36896 | tf_op jit(solution)/shard_map/ppermute | solution.py:605
  (236 shorter events, 38.0 us)
Async XLA Ops:
  6.6 5.4 %copy-start.5 = (bf16[384,768]{1,0:T(8,128)(2,1)S(1)}, bf16[384,768]{1,0:T(8,128)(2,1)}, u32[]{:S(2)}) copy-start(bf16[384,768]{1,0:T(8,128)(2,1)} %wo_ref.5) | copy-start | bytes 1769476
  6.6 22.6 %all-to-all-start = ((bf16[8,128,640]{2,1,0:T(8,128)(2,1)}), bf16[8,128,640]{2,1,0:T(8,128)(2,1)S(1)}, u32[]{:S(2)}, u32[]{:S(2)}) async-start(bf16[8,128,640]{2,1,0:T(8,128)(2,1)} %copy-done.13), calls=%async_computation | async-start | bytes 2621440 | tf_op jit(solution)/shard_map/all_to_all | solution.py:628
  11.9 23.7 %collective-permute-start.1 = (bf16[384,768]{1,0:T(8,128)(2,1)S(1)}, bf16[384,768]{1,0:T(8,128)(2,1)}, u32[]{:S(2)}, u32[]{:S(2)}) collective-permute-start(bf16[384,768]{1,0:T(8,128)(2,1)S(1)} %copy-done.5), channel_id=1, source_target_pairs={{0,1},{1,0},{2,3},{3,2},{4,5},{5,4},{6,7},{7,6},{8,9},{9,8},{10,11... | collective-permute-start | bytes 1769480 | tf_op jit(solution)/shard_map/ppermute | solution.py:616
  29.3 8.8 %collective-permute-start.2 = (f32[128,256]{1,0:T(8,128)S(1)}, f32[128,256]{1,0:T(8,128)S(1)}, u32[]{:S(2)}, u32[]{:S(2)}) collective-permute-start(f32[128,256]{1,0:T(8,128)S(1)} %query_sums.1.refs_3_), channel_id=1, source_target_pairs={{0,16},{16,0},{1,17},{17,1},{2,18},{18,2},{3,19},{19,3},{4,20},{20... | collective-permute-start | bytes 393224 | tf_op jit(solution)/shard_map/ppermute | solution.py:579
  31.9 3.7 %collective-permute-start = (s32[6,512]{1,0:T(8,128)S(1)}, s32[6,512]{1,0:T(8,128)S(1)}, u32[]{:S(2)}, u32[]{:S(2)}) collective-permute-start(s32[6,512]{1,0:T(8,128)S(1)} %copy-done.55), channel_id=1, source_target_pairs={{0,1},{1,0},{2,3},{3,2},{4,5},{5,4},{6,7},{7,6},{8,9},{9,8},{10,11... | collective-permute-start | bytes 36872 | tf_op jit(solution)/shard_map/ppermute | solution.py:615
  39.4 77.9 %copy-start.56 = (f32[128,256]{1,0:T(8,128)}, f32[128,256]{1,0:T(8,128)S(1)}, u32[]{:S(2)}) copy-start(f32[128,256]{1,0:T(8,128)S(1)} %get-tuple-element.84.refs_1_.refs_0_) | copy-start | bytes 393220
  39.4 10.9 %copy-start.86 = (s32[512]{0:T(512)S(1)}, s32[512]{0:T(512)}, u32[]{:S(2)}) copy-start(s32[512]{0:T(512)} %param.29) | copy-start | bytes 6148
  39.4 10.9 %copy-start.83 = (f32[768]{0:T(1024)S(1)}, f32[768]{0:T(1024)}, u32[]{:S(2)}) copy-start(f32[768]{0:T(1024)} %param.22) | copy-start | bytes 9220
  39.5 11.0 %copy-start.80 = (f32[1536]{0:T(1024)S(1)}, f32[1536]{0:T(1024)}, u32[]{:S(2)}) copy-start(f32[1536]{0:T(1024)} %param.25) | copy-start | bytes 18436
  39.5 11.0 %copy-start.84 = (f32[768]{0:T(1024)S(1)}, f32[768]{0:T(1024)}, u32[]{:S(2)}) copy-start(f32[768]{0:T(1024)} %param.23) | copy-start | bytes 9220
  39.5 5.8 %collective-permute-start.3 = (bf16[128,256]{1,0:T(8,128)(2,1)S(1)}, bf16[128,256]{1,0:T(8,128)(2,1)S(1)}, u32[]{:S(2)}, u32[]{:S(2)}) collective-permute-start(bf16[128,256]{1,0:T(8,128)(2,1)S(1)} %get-tuple-element.77.refs_0_), channel_id=1, source_target_pairs={{0,16},{16,0},{1,17},{17,1},{2,18},{18,2},{3,19},{19,3},{4,20},{20... | collective-permute-start | bytes 196616 | tf_op jit(solution)/shard_map/ppermute | solution.py:579
  46.6 6.0 %copy-start.78 = (f32[128,256]{1,0:T(8,128)}, f32[128,256]{1,0:T(8,128)S(1)}, u32[]{:S(2)}) copy-start(f32[128,256]{1,0:T(8,128)S(1)} %get-tuple-element.85.refs_2_) | copy-start | bytes 393220
  46.6 17.0 %all-to-all-start.1 = ((bf16[16,192,128]{2,1,0:T(8,128)(2,1)}), bf16[16,192,128]{2,1,0:T(8,128)(2,1)S(1)}, u32[]{:S(2)}, u32[]{:S(2)}) async-start(bf16[16,192,128]{2,1,0:T(8,128)(2,1)} %copy-done.38), calls=%async_computation.1 | async-start | bytes 1572864 | tf_op jit(solution)/shard_map/all_to_all | solution.py:642
  64.6 6.7 %copy-start.3 = (bf16[16,192,128]{2,1,0:T(8,128)(2,1)}, bf16[16,192,128]{2,1,0:T(8,128)(2,1)S(1)}, u32[]{:S(2)}) copy-start(bf16[16,192,128]{2,1,0:T(8,128)(2,1)S(1)} %all-to-all-done.1.recv_ref) | copy-start | bytes 2359300
  64.7 10.5 %copy-start.7 = (bf16[384,768]{1,0:T(8,128)(2,1)S(1)}, bf16[384,768]{1,0:T(8,128)(2,1)}, u32[]{:S(2)}) copy-start(bf16[384,768]{1,0:T(8,128)(2,1)} %wo_ref.5) | copy-start | bytes 1769476
  74.6 22.7 %copy-start.8 = (f32[256,768]{1,0:T(8,128)}, f32[256,768]{1,0:T(8,128)S(1)}, u32[]{:S(2)}) copy-start(f32[256,768]{1,0:T(8,128)S(1)} %get-tuple-element.80.two_ref.residual_two_ref) | copy-start | bytes 2359300
  74.6 22.7 %copy-start.1 = (bf16[512,768]{1,0:T(8,128)(2,1)S(1)}, bf16[512,768]{1,0:T(8,128)(2,1)}, u32[]{:S(2)}) copy-start(bf16[512,768]{1,0:T(8,128)(2,1)} %broadcast_multiply_fusion.bg_ref) | copy-start | bytes 2359300
  74.6 12.8 %collective-permute-start.4 = (bf16[256,768]{1,0:T(8,128)(2,1)S(1)}, bf16[256,768]{1,0:T(8,128)(2,1)S(1)}, u32[]{:S(2)}, u32[]{:S(2)}) collective-permute-start(bf16[256,768]{1,0:T(8,128)(2,1)S(1)} %get-tuple-element.83.back_two_ref), channel_id=1, source_target_pairs={{0,1},{1,0},{2,3},{3,2},{4,5},{5,4},{6,7},{7,6},{8,9},{9,8},{10,11... | collective-permute-start | bytes 1179656 | tf_op jit(solution)/shard_map/ppermute | solution.py:666
  86.0 14.4 %copy-start.10 = (f32[256,768]{1,0:T(8,128)}, f32[256,768]{1,0:T(8,128)S(1)}, u32[]{:S(2)}) copy-start(f32[256,768]{1,0:T(8,128)S(1)} %get-tuple-element.79.one_ref.residual_one_ref) | copy-start | bytes 2359300
  86.0 11.4 %collective-permute-start.6 = (bf16[256,768]{1,0:T(8,128)(2,1)S(1)}, bf16[256,768]{1,0:T(8,128)(2,1)S(1)}, u32[]{:S(2)}, u32[]{:S(2)}) collective-permute-start(bf16[256,768]{1,0:T(8,128)(2,1)S(1)} %get-tuple-element.86.back_one_ref), channel_id=1, source_target_pairs={{0,1},{1,0},{2,3},{3,2},{4,5},{5,4},{6,7},{7,6},{8,9},{9,8},{10,11... | collective-permute-start | bytes 1179656 | tf_op jit(solution)/shard_map/ppermute | solution.py:666
  100.3 18.6 %copy-start.22 = (f32[256,768]{1,0:T(8,128)}, f32[256,768]{1,0:T(8,128)S(1)}, u32[]{:S(2)}) copy-start(f32[256,768]{1,0:T(8,128)S(1)} %get-tuple-element.95.residual_grad_ref) | copy-start | bytes 2359300
  100.4 18.6 %copy-start.35 = (bf16[512,768]{1,0:T(8,128)(2,1)}, bf16[512,768]{1,0:T(8,128)(2,1)S(1)}, u32[]{:S(2)}) copy-start(bf16[512,768]{1,0:T(8,128)(2,1)S(1)} %get-tuple-element.108) | copy-start | bytes 2359300
  100.4 16.9 %copy-start.79 = (f32[128,256]{1,0:T(8,128)S(1)}, f32[128,256]{1,0:T(8,128)}, u32[]{:S(2)}) copy-start(f32[128,256]{1,0:T(8,128)} %copy-done.78) | copy-start | bytes 393220
  111.6 5.7 %collective-permute-start.7 = (bf16[208,128]{1,0:T(8,128)(2,1)S(1)}, bf16[208,128]{1,0:T(8,128)(2,1)S(1)}, u32[]{:S(2)}, u32[]{:S(2)}) collective-permute-start(bf16[208,128]{1,0:T(8,128)(2,1)S(1)} %grad_sums.1.refs_3_), channel_id=1, source_target_pairs={{0,16},{16,0},{1,17},{17,1},{2,18},{18,2},{3,19},{19,3},{4,20},{20... | collective-permute-start | bytes 159752 | tf_op jit(solution)/shard_map/ppermute | solution.py:579
  120.4 15.1 %all-to-all-start.4 = ((bf16[8,128,384]{2,1,0:T(8,128)(2,1)}), bf16[8,128,384]{2,1,0:T(8,128)(2,1)S(1)}, u32[]{:S(2)}, u32[]{:S(2)}) async-start(bf16[8,128,384]{2,1,0:T(8,128)(2,1)} %copy-done.37), calls=%async_computation.4 | async-start | bytes 1572864 | tf_op jit(solution)/shard_map/all_to_all | solution.py:696
  129.2 30.6 %collective-permute-start.23 = (bf16[384,1536]{1,0:T(8,128)(2,1)}, bf16[384,1536]{1,0:T(8,128)(2,1)}, u32[]{:S(2)}, u32[]{:S(2)}) collective-permute-start(bf16[384,1536]{1,0:T(8,128)(2,1)} %get-tuple-element.132), channel_id=1, source_target_pairs={{0,2},{2,0},{1,3},{3,1},{4,6},{6,4},{5,7},{7,5},{8,10},{10,8},{9,1... | collective-permute-start | bytes 3538952 | tf_op jit(solution)/shard_map/ppermute | solution.py:605
  133.6 31.2 %collective-permute-start.19 = (bf16[384,1536]{1,0:T(8,128)(2,1)}, bf16[384,1536]{1,0:T(8,128)(2,1)}, u32[]{:S(2)}, u32[]{:S(2)}) collective-permute-start(bf16[384,1536]{1,0:T(8,128)(2,1)} %get-tuple-element.124), channel_id=1, source_target_pairs={{0,2},{2,0},{1,3},{3,1},{4,6},{6,4},{5,7},{7,5},{8,10},{10,8},{9,1... | collective-permute-start | bytes 3538952 | tf_op jit(solution)/shard_map/ppermute | solution.py:605
  135.8 6.0 %copy-start.33 = (bf16[512,768]{1,0:T(8,128)(2,1)}, bf16[512,768]{1,0:T(8,128)(2,1)S(1)}, u32[]{:S(2)}) copy-start(bf16[512,768]{1,0:T(8,128)(2,1)S(1)} %gather.1.kv_ref.refs_1_) | copy-start | bytes 2359300
  139.1 9.7 %copy-start.57 = (f32[128,256]{1,0:T(8,128)S(1)}, f32[128,256]{1,0:T(8,128)}, u32[]{:S(2)}) copy-start(f32[128,256]{1,0:T(8,128)} %copy-done.56) | copy-start | bytes 393220
  139.1 9.7 %copy-start.63 = (f32[4,128]{1,0:T(4,128)S(1)}, f32[4,128]{1,0:T(4,128)}, u32[]{:S(2)}) copy-start(f32[4,128]{1,0:T(4,128)} %copy-done.62) | copy-start | bytes 6148
  139.1 15.0 %copy-start = (bf16[1536,768]{1,0:T(8,128)(2,1)S(1)}, bf16[1536,768]{1,0:T(8,128)(2,1)}, u32[]{:S(2)}) copy-start(bf16[1536,768]{1,0:T(8,128)(2,1)} %down_ref.5) | copy-start | bytes 7077892
  142.7 26.1 %collective-permute-start.15 = (bf16[384,1152]{1,0:T(8,128)(2,1)}, bf16[384,1152]{1,0:T(8,128)(2,1)}, u32[]{:S(2)}, u32[]{:S(2)}) collective-permute-start(bf16[384,1152]{1,0:T(8,128)(2,1)} %get-tuple-element.112), channel_id=1, source_target_pairs={{0,2},{2,0},{1,3},{3,1},{4,6},{6,4},{5,7},{7,5},{8,10},{10,8},{9,1... | collective-permute-start | bytes 2654216 | tf_op jit(solution)/shard_map/ppermute | solution.py:605
  142.7 6.1 %collective-permute-start.8 = (bf16[192,128]{1,0:T(8,128)(2,1)S(1)}, bf16[192,128]{1,0:T(8,128)(2,1)S(1)}, u32[]{:S(2)}, u32[]{:S(2)}) collective-permute-start(bf16[192,128]{1,0:T(8,128)(2,1)S(1)} %copy-done.59), channel_id=1, source_target_pairs={{0,16},{16,0},{1,17},{17,1},{2,18},{18,2},{3,19},{19,3},{4,20},{20... | collective-permute-start | bytes 147464 | tf_op jit(solution)/shard_map/ppermute | solution.py:579
  149.7 22.5 %all-to-all-start.3 = ((bf16[8,208,128]{2,1,0:T(8,128)(2,1)}), bf16[8,208,128]{2,1,0:T(8,128)(2,1)}, u32[]{:S(2)}, u32[]{:S(2)}) async-start(bf16[8,208,128]{2,1,0:T(8,128)(2,1)} %copy-done.12), calls=%async_computation.3 | async-start | bytes 851968 | tf_op jit(solution)/shard_map/all_to_all | solution.py:700
  158.6 29.9 %collective-permute-start.5 = (bf16[512,768]{1,0:T(8,128)(2,1)}, bf16[512,768]{1,0:T(8,128)(2,1)S(1)}, u32[]{:S(2)}, u32[]{:S(2)}) collective-permute-start(bf16[512,768]{1,0:T(8,128)(2,1)} %branch.1.branch_ref), channel_id=1, source_target_pairs={{0,1},{1,0},{2,3},{3,2},{4,5},{5,4},{6,7},{7,6},{8,9},{9,8},{10,11... | collective-permute-start | bytes 2359304 | tf_op jit(solution)/shard_map/ppermute | solution.py:686
  159.9 4.9 %copy-start.17 = (bf16[384,1536]{1,0:T(8,128)(2,1)S(1)}, bf16[384,1536]{1,0:T(8,128)(2,1)}, u32[]{:S(2)}) copy-start(bf16[384,1536]{1,0:T(8,128)(2,1)} %copy-done.16) | copy-start | bytes 3538948
  163.1 15.4 %collective-permute-start.24 = (bf16[192,1536]{1,0:T(8,128)(2,1)}, bf16[192,1536]{1,0:T(8,128)(2,1)}, u32[]{:S(2)}, u32[]{:S(2)}) collective-permute-start(bf16[192,1536]{1,0:T(8,128)(2,1)} %get-tuple-element.134), channel_id=1, source_target_pairs={{0,8},{8,0},{1,9},{9,1},{2,10},{10,2},{3,11},{11,3},{4,12},{12,4},... | collective-permute-start | bytes 1769480 | tf_op jit(solution)/shard_map/ppermute | solution.py:605
  164.8 7.4 %copy-start.34 = (bf16[512,768]{1,0:T(8,128)(2,1)S(1)}, bf16[512,768]{1,0:T(8,128)(2,1)}, u32[]{:S(2)}) copy-start(bf16[512,768]{1,0:T(8,128)(2,1)} %copy-done.33) | copy-start | bytes 2359300
  167.2 4.9 %copy-start.15 = (bf16[96,8,2,384]{3,1,2,0:T(8,128)(2,1)S(1)}, bf16[96,8,2,384]{3,1,2,0:T(8,128)(2,1)}, u32[]{:S(2)}) copy-start(bf16[96,8,2,384]{3,1,2,0:T(8,128)(2,1)} %copy-done.14) | copy-start | bytes 3538948
  167.2 16.6 %collective-permute-start.20 = (bf16[192,1536]{1,0:T(8,128)(2,1)}, bf16[192,1536]{1,0:T(8,128)(2,1)}, u32[]{:S(2)}, u32[]{:S(2)}) collective-permute-start(bf16[192,1536]{1,0:T(8,128)(2,1)} %get-tuple-element.126), channel_id=1, source_target_pairs={{0,4},{4,0},{1,5},{5,1},{2,6},{6,2},{3,7},{7,3},{8,12},{12,8},{9,1... | collective-permute-start | bytes 1769480 | tf_op jit(solution)/shard_map/ppermute | solution.py:605
  171.6 35.9 %collective-permute-start.16 = (bf16[192,1152]{1,0:T(8,128)(2,1)}, bf16[192,1152]{1,0:T(8,128)(2,1)}, u32[]{:S(2)}, u32[]{:S(2)}) collective-permute-start(bf16[192,1152]{1,0:T(8,128)(2,1)} %get-tuple-element.114), channel_id=1, source_target_pairs={{0,4},{4,0},{1,5},{5,1},{2,6},{6,2},{3,7},{7,3},{8,12},{12,8},{9,1... | collective-permute-start | bytes 1327112 | tf_op jit(solution)/shard_map/ppermute | solution.py:605
  173.2 5.3 %copy-start.40 = (bf16[192,1536]{1,0:T(8,128)(2,1)S(1)}, bf16[192,1536]{1,0:T(8,128)(2,1)}, u32[]{:S(2)}) copy-start(bf16[192,1536]{1,0:T(8,128)(2,1)} %copy-done.39) | copy-start | bytes 1769476
  177.2 8.6 %copy-start.45 = (bf16[256,768]{1,0:T(8,128)(2,1)}, bf16[256,768]{1,0:T(8,128)(2,1)S(1)}, u32[]{:S(2)}) copy-start(bf16[256,768]{1,0:T(8,128)(2,1)S(1)} %get-tuple-element.93.keep_ref) | copy-start | bytes 1179652
  177.2 6.6 %copy-start.42 = (bf16[192,1536]{1,0:T(8,128)(2,1)S(1)}, bf16[192,1536]{1,0:T(8,128)(2,1)}, u32[]{:S(2)}) copy-start(bf16[192,1536]{1,0:T(8,128)(2,1)} %copy-done.41) | copy-start | bytes 1769476
  177.2 28.7 %collective-permute-start.9 = (bf16[256,768]{1,0:T(8,128)(2,1)}, bf16[256,768]{1,0:T(8,128)(2,1)S(1)}, u32[]{:S(2)}, u32[]{:S(2)}) collective-permute-start(bf16[256,768]{1,0:T(8,128)(2,1)} %get-tuple-element.94), channel_id=1, source_target_pairs={{0,1},{1,0},{2,3},{3,2},{4,5},{5,4},{6,7},{7,6},{8,9},{9,8},{10,11... | collective-permute-start | bytes 1179656 | tf_op jit(solution)/shard_map/ppermute | solution.py:713
  178.5 7.8 %copy-start.32 = (bf16[512,768]{1,0:T(8,128)(2,1)S(1)}, bf16[512,768]{1,0:T(8,128)(2,1)}, u32[]{:S(2)}) copy-start(bf16[512,768]{1,0:T(8,128)(2,1)} %copy-done.30) | copy-start | bytes 2359300
  181.2 17.0 %collective-permute-start.25 = (bf16[96,1536]{1,0:T(8,128)(2,1)}, bf16[96,1536]{1,0:T(8,128)(2,1)}, u32[]{:S(2)}, u32[]{:S(2)}) collective-permute-start(bf16[96,1536]{1,0:T(8,128)(2,1)} %get-tuple-element.136), channel_id=1, source_target_pairs={{0,4},{4,0},{1,5},{5,1},{2,6},{6,2},{3,7},{7,3},{8,12},{12,8},{9,1... | collective-permute-start | bytes 884744 | tf_op jit(solution)/shard_map/ppermute | solution.py:605
  185.8 14.8 %collective-permute-start.21 = (bf16[96,1536]{1,0:T(8,128)(2,1)}, bf16[96,1536]{1,0:T(8,128)(2,1)}, u32[]{:S(2)}, u32[]{:S(2)}) collective-permute-start(bf16[96,1536]{1,0:T(8,128)(2,1)} %get-tuple-element.128), channel_id=1, source_target_pairs={{0,8},{8,0},{1,9},{9,1},{2,10},{10,2},{3,11},{11,3},{4,12},{12,4},... | collective-permute-start | bytes 884744 | tf_op jit(solution)/shard_map/ppermute | solution.py:605
  188.5 14.9 %collective-permute-start.11 = (bf16[384,384]{1,0:T(8,128)(2,1)}, bf16[384,384]{1,0:T(8,128)(2,1)}, u32[]{:S(2)}, u32[]{:S(2)}) collective-permute-start(bf16[384,384]{1,0:T(8,128)(2,1)} %get-tuple-element.101), channel_id=1, source_target_pairs={{0,2},{2,0},{1,3},{3,1},{4,6},{6,4},{5,7},{7,5},{8,10},{10,8},{9,1... | collective-permute-start | bytes 884744 | tf_op jit(solution)/shard_map/ppermute | solution.py:605
  188.5 9.7 %copy-start.52 = (bf16[96,1536]{1,0:T(8,128)(2,1)S(1)}, bf16[96,1536]{1,0:T(8,128)(2,1)}, u32[]{:S(2)}) copy-start(bf16[96,1536]{1,0:T(8,128)(2,1)} %copy-done.51) | copy-start | bytes 884740
  188.5 12.1 %copy-start.54 = (bf16[96,1536]{1,0:T(8,128)(2,1)S(1)}, bf16[96,1536]{1,0:T(8,128)(2,1)}, u32[]{:S(2)}) copy-start(bf16[96,1536]{1,0:T(8,128)(2,1)} %copy-done.53) | copy-start | bytes 884740
  188.6 14.8 %copy-start.50 = (bf16[384,384]{1,0:T(8,128)(2,1)S(1)}, bf16[384,384]{1,0:T(8,128)(2,1)}, u32[]{:S(2)}) copy-start(bf16[384,384]{1,0:T(8,128)(2,1)} %copy-done.49) | copy-start | bytes 884740
  190.9 15.0 %copy-start.23 = (f32[256,768]{1,0:T(8,128)S(1)}, f32[256,768]{1,0:T(8,128)}, u32[]{:S(2)}) copy-start(f32[256,768]{1,0:T(8,128)} %copy-done.22) | copy-start | bytes 2359300
  190.9 15.0 %copy-start.46 = (bf16[256,768]{1,0:T(8,128)(2,1)S(1)}, bf16[256,768]{1,0:T(8,128)(2,1)}, u32[]{:S(2)}) copy-start(bf16[256,768]{1,0:T(8,128)(2,1)} %copy-done.45) | copy-start | bytes 1179652
  190.9 15.0 %copy-start.61 = (f32[1,768]{1,0:T(1,128)S(1)}, f32[1,768]{1,0:T(1,128)}, u32[]{:S(2)}) copy-start(f32[1,768]{1,0:T(1,128)} %copy-done.60) | copy-start | bytes 9220
  199.2 17.2 %collective-permute-start.26 = (bf16[48,1536]{1,0:T(8,128)(2,1)S(1)}, bf16[48,1536]{1,0:T(8,128)(2,1)S(1)}, u32[]{:S(2)}, u32[]{:S(2)}) collective-permute-start(bf16[48,1536]{1,0:T(8,128)(2,1)S(1)} %get-tuple-element.138), channel_id=1, source_target_pairs={{0,16},{16,0},{1,17},{17,1},{2,18},{18,2},{3,19},{19,3},{4,20},{20... | collective-permute-start | bytes 442376 | tf_op jit(solution)/shard_map/ppermute | solution.py:605
  201.7 15.5 %collective-permute-start.22 = (bf16[48,1536]{1,0:T(8,128)(2,1)S(1)}, bf16[48,1536]{1,0:T(8,128)(2,1)S(1)}, u32[]{:S(2)}, u32[]{:S(2)}) collective-permute-start(bf16[48,1536]{1,0:T(8,128)(2,1)S(1)} %get-tuple-element.130), channel_id=1, source_target_pairs={{0,16},{16,0},{1,17},{17,1},{2,18},{18,2},{3,19},{19,3},{4,20},{20... | collective-permute-start | bytes 442376 | tf_op jit(solution)/shard_map/ppermute | solution.py:605
  204.4 9.0 %collective-permute-start.12 = (bf16[192,384]{1,0:T(8,128)(2,1)S(1)}, bf16[192,384]{1,0:T(8,128)(2,1)S(1)}, u32[]{:S(2)}, u32[]{:S(2)}) collective-permute-start(bf16[192,384]{1,0:T(8,128)(2,1)S(1)} %get-tuple-element.103), channel_id=1, source_target_pairs={{0,4},{4,0},{1,5},{5,1},{2,6},{6,2},{3,7},{7,3},{8,12},{12,8},{9,1... | collective-permute-start | bytes 442376 | tf_op jit(solution)/shard_map/ppermute | solution.py:605
  206.6 22.1 %collective-permute-start.10 = (bf16[256,768]{1,0:T(8,128)(2,1)S(1)}, bf16[256,768]{1,0:T(8,128)(2,1)S(1)}, u32[]{:S(2)}, u32[]{:S(2)}) collective-permute-start(bf16[256,768]{1,0:T(8,128)(2,1)S(1)} %get-tuple-element.96.own_ref), channel_id=1, source_target_pairs={{0,1},{1,0},{2,3},{3,2},{4,5},{5,4},{6,7},{7,6},{8,9},{9,8},{10,11... | collective-permute-start | bytes 1179656 | tf_op jit(solution)/shard_map/ppermute | solution.py:719
  208.6 12.5 %collective-permute-start.17 = (bf16[96,1152]{1,0:T(8,128)(2,1)S(1)}, bf16[96,1152]{1,0:T(8,128)(2,1)S(1)}, u32[]{:S(2)}, u32[]{:S(2)}) collective-permute-start(bf16[96,1152]{1,0:T(8,128)(2,1)S(1)} %get-tuple-element.116), channel_id=1, source_target_pairs={{0,8},{8,0},{1,9},{9,1},{2,10},{10,2},{3,11},{11,3},{4,12},{12,4},... | collective-permute-start | bytes 663560 | tf_op jit(solution)/shard_map/ppermute | solution.py:605
  210.0 10.6 %all-to-all-start.5 = ((f32[32,1,96]{2,1,0:T(1,128)}), f32[32,1,96]{2,1,0:T(1,128)S(1)}, u32[]{:S(2)}, u32[]{:S(2)}) async-start(f32[32,1,96]{2,1,0:T(1,128)} %bitcast.1), calls=%async_computation.5 | async-start | bytes 32768 | tf_op jit(solution)/shard_map/all_to_all | solution.py:725
  213.4 7.2 %collective-permute-start.13 = (bf16[96,384]{1,0:T(8,128)(2,1)S(1)}, bf16[96,384]{1,0:T(8,128)(2,1)S(1)}, u32[]{:S(2)}, u32[]{:S(2)}) collective-permute-start(bf16[96,384]{1,0:T(8,128)(2,1)S(1)} %get-tuple-element.105), channel_id=1, source_target_pairs={{0,8},{8,0},{1,9},{9,1},{2,10},{10,2},{3,11},{11,3},{4,12},{12,4},... | collective-permute-start | bytes 221192 | tf_op jit(solution)/shard_map/ppermute | solution.py:605
  220.7 7.4 %collective-permute-start.14 = (bf16[48,384]{1,0:T(8,128)(2,1)S(1)}, bf16[48,384]{1,0:T(8,128)(2,1)S(1)}, u32[]{:S(2)}, u32[]{:S(2)}) collective-permute-start(bf16[48,384]{1,0:T(8,128)(2,1)S(1)} %get-tuple-element.107), channel_id=1, source_target_pairs={{0,16},{16,0},{1,17},{17,1},{2,18},{18,2},{3,19},{19,3},{4,20},{20... | collective-permute-start | bytes 110600 | tf_op jit(solution)/shard_map/ppermute | solution.py:605
  221.2 9.2 %collective-permute-start.18 = (bf16[48,1152]{1,0:T(8,128)(2,1)S(1)}, bf16[48,1152]{1,0:T(8,128)(2,1)S(1)}, u32[]{:S(2)}, u32[]{:S(2)}) collective-permute-start(bf16[48,1152]{1,0:T(8,128)(2,1)S(1)} %get-tuple-element.118), channel_id=1, source_target_pairs={{0,16},{16,0},{1,17},{17,1},{2,18},{18,2},{3,19},{19,3},{4,20},{20... | collective-permute-start | bytes 331784 | tf_op jit(solution)/shard_map/ppermute | solution.py:605
  (55 other events, 102.7 us)

commit v3 on v2

--- a/solution.py
+++ b/solution.py
@@ -34,24 +34,67 @@
     return lax.dot_general(a, b, (((0,), (0,)), ((), ())), preferred_element_type=F32)
 
 
-def call(kernel, outs, *args, scratch=(), flops=0, vmem=None, name=None, aliases=None, specs=None):
-    moved = sum(a.size * a.dtype.itemsize for a in args) + sum(
-        functools.reduce(lambda p, q: p * q, s, 1) * jnp.dtype(d).itemsize for s, d in outs
-    )
-    extra = {}
-    if specs is not None:
-        extra["in_specs"], extra["out_specs"] = specs
-        extra["grid"] = (1,)
+WHOLE = pl.BlockSpec(memory_space=pltpu.VMEM)
+UNREAD = pl.BlockSpec(memory_space=pltpu.HBM)
+TOKEN = ((8, C), F32)
+MAIN = ("turn", "attend_back", "first_back", "last", "join")
+LONG, SHORT = 40 * 10**9, 10**6
+
+
+def size_of(shape, kind):
+    return functools.reduce(lambda p, q: p * q, shape, 1) * jnp.dtype(kind).itemsize
+
+
+def call(
+    kernel, outs, *args, scratch=(), flops=0, extra=6, name=None, specs=None, after=(), token=False, grid=(1,),
+):
+    inside, outside = specs or ([WHOLE] * len(args), [WHOLE] * len(outs))
+    inside = list(inside) + [UNREAD] * len(after)
+    outs, outside = list(outs), list(outside)
+    if token:
+        outs.append(TOKEN)
+        outside.append(UNREAD)
+    moved = sum(a.size * a.dtype.itemsize for a in args) + sum(size_of(*o) for o in outs)
+    room = sum(size_of(v.shape, v.dtype) for v in scratch if getattr(v, "dtype", None) in (F32, BF16))
+    held = [(a.shape, a.dtype) for a in args] + outs
+    for spec, (shape, kind) in zip(inside[: len(args)] + outside, held):
+        if spec.block_shape is not None:
+            room += 2 * size_of(spec.block_shape, kind)
+        elif spec is not UNREAD:
+            room += size_of(shape, kind)
+    first, kept = len(args), len(args) + len(after)
+
+    def body(*refs):
+        results = refs[kept:]
+        if token:
+            spot = len(outs) - 1
+            results = results[:spot] + results[spot + 1 :]
+        kernel(*refs[:first], *results)
+
     return pl.pallas_call(
-        kernel,
-        out_shape=[jax.ShapeDtypeStruct(s, d) for s, d in outs],
+        body,
+        out_shape=[
+            pltpu.HBM(s, d) if spec is UNREAD else jax.ShapeDtypeStruct(s, d)
+            for (s, d), spec in zip(outs, outside)
+        ],
+        in_specs=inside,
+        out_specs=outside,
         scratch_shapes=list(scratch),
-        compiler_params=pltpu.CompilerParams(vmem_limit_bytes=vmem or 32 * 2**20),
-        cost_estimate=pl.CostEstimate(flops=flops, bytes_accessed=moved, transcendentals=0),
-        input_output_aliases=aliases or {},
+        compiler_params=pltpu.CompilerParams(vmem_limit_bytes=room + extra * 2**20),
+        cost_estimate=pl.CostEstimate(flops=LONG if name in MAIN else SHORT, bytes_accessed=1, transcendentals=0),
         name=name,
-        **extra,
-    )(*args)
+        **({"grid": grid} if specs else {}),
+    )(*(pin(v) if spec is UNREAD else v for v, spec in zip((*args, *after), inside)))
+
+
+def pin(v):
+    return pltpu.with_memory_space_constraint(v, pltpu.HBM)
+
+
+def send(source, target, sem):
+    copy = pltpu.make_async_copy(source, target, sem)
+    copy.start()
+    return copy
 
 
 def left_half(shape):
@@ -119,11 +162,15 @@
     return dot_nn(picks, stacked)
 
 
-def project_kernel(x_ref, gain_ref, shift_ref, wq_ref, wkv_ref, ids_ref, normed_ref, send_ref, q_scr, kv_scr):
+def project_kernel(
+    x_ref, gain_ref, shift_ref, wq_ref, wkv_ref, ids_ref, normed_out, send_out, q_scr, kv_scr, normed_ref, send_ref, sems
+):
+    copies = []
     for s in range(SEQS):
         rows = slice(s * C, (s + 1) * C)
         unit, unused = normalise(x_ref[rows, :].astype(F32))
         normed_ref[rows, :] = (unit * gain_ref[...] + shift_ref[...]).astype(BF16)
+    copies.append(send(normed_ref, normed_out, sems.at[0]))
     width = wq_ref.shape[1]
     q_scr[...] = dot_nn(normed_ref[...], wq_ref[...])
     kv_scr[...] = dot_nn(normed_ref[...], wkv_ref[...]).astype(BF16)
@@ -155,19 +202,28 @@
             send_ref[o, :, 2 * C : 3 * C] = keys[full]
             send_ref[o, :, 3 * C : 4 * C] = values[full]
             send_ref[o, :, 4 * C : 5 * C] = mixed.astype(BF16)
+        copies.append(send(send_ref.at[2 * s : 2 * s + 2], send_out.at[2 * s : 2 * s + 2], sems.at[1 + s]))
+    for copy in copies:
+        copy.wait()
 
 
 def sum_kernel(recv_ref, out_ref):
     total = recv_ref[0].astype(F32)
     for i in range(1, SUB):
         total = total + recv_ref[i].astype(F32)
-    out_ref[...] = total
+    lane = lax.broadcasted_iota(jnp.int32, (C, C), 1)
+    tail = total[:, C : 2 * C]
+    high = tail.astype(BF16).astype(F32)
+    low = pltpu.roll(tail - high, 3, 1)
+    spare = (lane >= HD + 3) & (lane < HD + 6)
+    out_ref[:, 0:C] = total[:, 0:C].astype(BF16)
+    out_ref[:, C : 2 * C] = jnp.where(spare, low, high).astype(BF16)
 
 
 def add_all(refs):
-    total = refs[0][...]
+    total = refs[0][...].astype(F32)
     for r in refs[1:]:
-        total = total + r[...]
+        total = total + r[...].astype(F32)
     return total
 
 
@@ -190,11 +246,16 @@
 
 
 def attend_kernel(*refs):
-    recv_ref, sums, (part_ref, total_ref) = refs[0], refs[3:-2], refs[-2:]
+    recv_ref, sums, (part_ref, total_out, total_ref, sem) = refs[0], refs[1:-4], refs[-4:]
     total = add_all(sums)
-    total_ref[...] = total
     left = left_half((C, C))
     lane = lax.broadcasted_iota(jnp.int32, (C, C), 1)
+    tail = total[:, C : 2 * C]
+    counted = (lane >= HD) & (lane < HD + 3)
+    tail = jnp.where(counted, tail + pltpu.roll(tail, C - 3, 1), tail)
+    total = jnp.concatenate([total[:, 0:C], tail], axis=1)
+    total_ref[...] = total
+    copy = send(total_ref, total_out, sem)
     length = SUB * C
     outs = []
     stats = jnp.zeros((C, C), F32)
@@ -211,10 +272,11 @@
             stats = jnp.where(lane == spot, column, stats)
     part_ref[:, 0:C] = jnp.where(left, outs[0], outs[1]).astype(BF16)
     part_ref[:, C : 2 * C] = jnp.where(left, stats, outs[2]).astype(BF16)
+    copy.wait()
 
 
 def merge_kernel(*refs):
-    parts, (fin_ref, send_ref) = refs[:-2], refs[-2:]
+    parts, (fin_out, send_out, fin_ref, send_ref, sems) = refs[:-5], refs[-5:]
     left = left_half((C, C))
     lane = lax.broadcasted_iota(jnp.int32, (C, C), 1)
     tails = [r[:, C : 2 * C].astype(F32) for r in parts]
@@ -237,22 +299,31 @@
     fin_ref[:, 0:C] = pair
     fin_ref[:, C : 2 * C] = jnp.where(left, stats, single)
     short = jnp.where(left_half((HD, C)), roll_half(single[0:HD]), single[HD:C])
-    for o in range(send_ref.shape[0]):
-        send_ref[o, 0:C, :] = pair.astype(BF16)
-        send_ref[o, C : C + HD, :] = short.astype(BF16)
+    send_ref[0:C, :] = pair.astype(BF16)
+    send_ref[C : C + HD, :] = short.astype(BF16)
+    count = send_out.shape[0]
+    copies = [send(send_ref, send_out.at[o], sems.at[o]) for o in range(count)]
+    copies.append(send(fin_ref, fin_out, sems.at[count]))
+    for copy in copies:
+        copy.wait()
 
 
 def middle_kernel(
-    recv_ref, ids_ref, ids_other_ref, x_ref, wo_ref, wo_other_ref, gain_ref, shift_ref, up_ref,
-    up_bias_ref, down_ref, bg_ref, attended_ref, residual_ref, normed_ref, active_ref, hidden_ref,
-    back_ref, up_bias_out_ref, a_scr, w_scr,
+    recv_ref, ids_ref, ids_other_ref, x_ref, gain_ref, shift_ref, up_bias_ref, bg_ref,
+    wo_src, wo_other_src, up_src, down_src,
+    up_bias_out_ref, residual_ref, back_ref, attended_out, normed_out, active_out, hidden_out,
+    a_scr, w_ref, up_ref, down_ref, own_ref, normed_ref, active_ref, hidden_ref, in_sems, out_sems,
 ):
-    half = wo_ref.shape[0]
+    half = wo_src.shape[0]
     me = lax.axis_index("mp")
     mine = pl.multiple_of(me * half, C)
     theirs = pl.multiple_of((1 - me) * half, C)
-    w_scr[pl.ds(mine, half), :] = wo_ref[...]
-    w_scr[pl.ds(theirs, half), :] = wo_other_ref[...]
+    wo_copies = [
+        send(wo_src, w_ref.at[pl.ds(mine, half), :], in_sems.at[0]),
+        send(wo_other_src, w_ref.at[pl.ds(theirs, half), :], in_sems.at[1]),
+    ]
+    up_copy = send(up_src, up_ref, in_sems.at[2])
+    down_copy = send(down_src, down_ref, in_sems.at[3])
     short = left_half((HD, C))
     for s in range(x_ref.shape[0] // C):
         rows = slice(s * C, (s + 1) * C)
@@ -273,40 +344,51 @@
                 a_scr[rows, m * half + p * C : m * half + (p + 1) * C] = spread_pair(
                     columns, spots, pair
                 ).astype(BF16)
-    attended_ref[...] = a_scr[:, pl.ds(mine, half)]
-    residual = x_ref[...].astype(F32) + dot_nn(a_scr[...], w_scr[...])
+    own_ref[...] = a_scr[:, pl.ds(mine, half)]
+    copies = [send(own_ref, attended_out, out_sems.at[0])]
+    for copy in wo_copies:
+        copy.wait()
+    residual = x_ref[...].astype(F32) + dot_nn(a_scr[...], w_ref[...])
     residual_ref[...] = residual
     unit, unused = normalise(residual)
     normed = (unit * gain_ref[...] + shift_ref[...]).astype(BF16)
     normed_ref[...] = normed
+    copies.append(send(normed_ref, normed_out, out_sems.at[1]))
+    up_copy.wait()
     hidden = dot_nn(normed, up_ref[...]) + up_bias_ref[...]
     below = 0.5 * (1.0 + lax.erf(hidden * (0.5**0.5)))
     active_ref[...] = (hidden * below).astype(BF16)
+    copies.append(send(active_ref, active_out, out_sems.at[2]))
     slope = below + hidden * jnp.exp(-0.5 * hidden * hidden) * 0.3989422804014327
+    down_copy.wait()
     hidden_grad = (slope * dot_nt(bg_ref[...], down_ref[...])).astype(BF16)
     hidden_ref[...] = hidden_grad
+    copies.append(send(hidden_ref, hidden_out, out_sems.at[3]))
     up_bias_out_ref[...] = jnp.sum(hidden_grad.astype(F32), axis=0, keepdims=True)
     back_ref[...] = dot_nt(hidden_grad, up_ref[...]).astype(BF16)
-
-
-def branch_kernel(one_ref, two_ref, down_ref, after_ref, branch_ref):
+    for copy in copies:
+        copy.wait()
+
+
+def branch_kernel(active_ref, down_ref, branch_ref):
+    branch_ref[...] = dot_nn(active_ref[...], down_ref[...]).astype(BF16)
+
+
+def output_kernel(
+    one_ref, two_ref, branch_one_ref, branch_two_ref, other_one_ref, other_two_ref, bias_ref, out_ref
+):
     half = one_ref.shape[0]
-    branch_ref[0:half, :] = dot_nn(one_ref[...], down_ref[...]).astype(BF16)
-    branch_ref[half:, :] = dot_nn(two_ref[...], down_ref[...]).astype(BF16)
-
-
-def output_kernel(one_ref, two_ref, branch_ref, other_ref, bias_ref, out_ref):
-    half = one_ref.shape[0]
-    for i, r in enumerate((one_ref, two_ref)):
-        rows = slice(i * half, (i + 1) * half)
-        total = branch_ref[rows, :].astype(F32) + other_ref[rows, :].astype(F32)
-        out_ref[rows, :] = (r[...] + (total + bias_ref[...])).astype(BF16)
+    for i, (r, mine, theirs) in enumerate(
+        ((one_ref, branch_one_ref, other_one_ref), (two_ref, branch_two_ref, other_two_ref))
+    ):
+        total = mine[...].astype(F32) + theirs[...].astype(F32)
+        out_ref[i * half : (i + 1) * half, :] = (r[...] + (total + bias_ref[...])).astype(BF16)
 
 
 def turn_kernel(
     back_one_ref, back_two_ref, other_one_ref, other_two_ref, residual_one_ref, residual_two_ref,
     gain_ref, bg_ref, wo_ref, ids_ref, bias_one_ref, bias_two_ref,
-    residual_grad_ref, mixed_ref, send_ref, ag_scr, vec_scr,
+    residual_grad_out, mixed_out, send_out, ag_scr, vec_scr, residual_grad_ref, mixed_ref, send_ref, sems,
 ):
     me = lax.axis_index("mp")
     gain_sum = jnp.zeros(gain_ref.shape, F32)
@@ -332,6 +414,9 @@
             residual_grad_ref[inner, :] = residual_grad
 
         mixed_ref[rows, :] = residual_grad.astype(BF16)
+    copies = [
+        send(residual_grad_ref, residual_grad_out, sems.at[0]), send(mixed_ref, mixed_out, sems.at[1])
+    ]
     ag_scr[...] = dot_nt(mixed_ref[...], wo_ref[...])
     vec_scr[...] = jnp.zeros(vec_scr.shape, F32)
     spot = 0
@@ -360,6 +445,9 @@
             send_ref[o, C + HD : PACK, :] = jnp.concatenate(
                 [high, vec - high, jnp.zeros((8, C), F32)], axis=0
             ).astype(BF16)
+        copies.append(send(send_ref.at[2 * s : 2 * s + 2], send_out.at[2 * s : 2 * s + 2], sems.at[2 + s]))
+    for copy in copies:
+        copy.wait()
 
 
 def grad_sum_kernel(recv_ref, out_ref):
@@ -379,8 +467,8 @@
 
 
 def attend_back_kernel(*refs):
-    recv_ref, total_ref, fin_ref = refs[:3]
-    sums, (cgrad_ref, vec_ref, send_ref) = refs[3:-3], refs[-3:]
+    sums, (cgrad_ref, vec_ref, send_ref, recv_ref, total_ref, fin_ref, sems) = refs[3:-7], refs[-7:]
+    copies = [send(v, t, sems.at[i]) for i, (v, t) in enumerate(zip(refs[:3], (recv_ref, total_ref, fin_ref)))]
     total = sums[0][...].astype(F32)
     for r in sums[1:]:
         total = total + r[...].astype(F32)
@@ -393,6 +481,8 @@
         jnp.where(left, zero, single).astype(BF16),
     )
     vec_ref[...] = total[C + HD : C + HD + 4] + total[C + HD + 4 : C + HD + 8]
+    for copy in copies:
+        copy.wait()
     centroids = centroid_blocks(total_ref[...])
     tail = fin_ref[:, C : 2 * C]
     outs = (fin_ref[:, 0:C], fin_ref[:, 0:C], tail)
@@ -423,7 +513,7 @@
 
 
 def finish_back_kernel(*refs):
-    total_ref, vec_ref, cgrads, send_ref = refs[0], refs[1], refs[2:-1], refs[-1]
+    total_ref, vec_ref, cgrads, (send_out, send_ref, sems) = refs[0], refs[1], refs[2:-3], refs[-3:]
     grad = cgrads[0][...].astype(F32)
     for r in cgrads[1:]:
         grad = grad + r[...].astype(F32)
@@ -436,10 +526,12 @@
     vec = vec_ref[...]
     high = vec.astype(BF16).astype(F32)
     extra = jnp.concatenate([high, vec - high, jnp.zeros((8, C), F32)], axis=0)
-    for o in range(SUB):
-        send_ref[o, 0:C, :] = pair.astype(BF16)
-        send_ref[o, C : C + HD, :] = single.astype(BF16)
-        send_ref[o, C + HD : PACK, :] = extra.astype(BF16)
+    send_ref[0:C, :] = pair.astype(BF16)
+    send_ref[C : C + HD, :] = single.astype(BF16)
+    send_ref[C + HD : PACK, :] = extra.astype(BF16)
+    copies = [send(send_ref, send_out.at[o], sems.at[o]) for o in range(SUB)]
+    for copy in copies:
+        copy.wait()
 
 
 def gather_kernel(recv_ref, grads_ref):
@@ -459,7 +551,12 @@
             grads_ref[rows, base + 2 * C : base + 3 * C] = blocks[1][:, first : first + C]
 
 
-def first_back_kernel(recv_ref, ids_ref, wq_ref, wkv_ref, kv_ref, grads_ref, keep_ref, give_ref, scr):
+def first_back_kernel(
+    recv_ref, ids_ref, wq_src, wkv_src, kv_src, grads_out, keep_out, give_out,
+    scr, wq_ref, wkv_ref, kv_ref, grads_ref, in_sems, out_sems,
+):
+    kv_copies = [send(kv_src, kv_ref, in_sems.at[0]), send(wkv_src, wkv_ref, in_sems.at[1])]
+    wq_copy = send(wq_src, wq_ref, in_sems.at[2])
     short = left_half((HD, C))
     for s in range(SEQS):
         rows = slice(s * C, (s + 1) * C)
@@ -470,13 +567,20 @@
         middle = jnp.concatenate(first, axis=0).astype(BF16)
         for p, pair in enumerate((packs[0][0:C], middle, packs[1][0:C])):
             grads_ref[rows, p * C : (p + 1) * C] = spread_pair(columns, PAIRS[p], pair).astype(BF16)
-    scr[...] = (
-        dot_nt(grads_ref[...], wq_ref[...]) + dot_nt(kv_ref[...], wkv_ref[...])
-    ).astype(BF16)
-    half = keep_ref.shape[0]
+    copies = [send(grads_ref, grads_out, out_sems.at[0])]
+    for copy in kv_copies:
+        copy.wait()
+    wq_copy.wait()
+    half = keep_out.shape[0]
     me = lax.axis_index("mp")
-    keep_ref[...] = scr[pl.ds(pl.multiple_of(me * half, C), half), :]
-    give_ref[...] = scr[pl.ds(pl.multiple_of((1 - me) * half, C), half), :]
+    for i, (bit, out) in enumerate(((1 - me, give_out), (me, keep_out))):
+        rows = pl.ds(pl.multiple_of(bit * half, C), half)
+        scr[i] = (
+            dot_nt(grads_ref[rows, :], wq_ref[...]) + dot_nt(kv_ref[rows, :], wkv_ref[...])
+        ).astype(BF16)
+        copies.append(send(scr.at[i], out, out_sems.at[1 + i]))
+    for copy in copies:
+        copy.wait()
 
 
 def last_kernel(keep_ref, got_ref, x_ref, gain_ref, residual_grad_ref, input_grad_ref, vec_ref):
@@ -493,8 +597,10 @@
         shift_sum = shift_sum + jnp.sum(grad, axis=0, keepdims=True)
         made = norm_pull(unit, inverse, grad * gain_ref[...])
         input_grad_ref[rows, :] = (residual_grad_ref[rows, :] + made).astype(BF16)
-    vec_ref[0:1, :] = gain_sum
-    vec_ref[1:2, :] = shift_sum
+    both = jnp.concatenate([gain_sum, shift_sum], axis=0)
+    own = vec_ref.shape[2]
+    for r in range(vec_ref.shape[0]):
+        vec_ref[r] = both[:, (r // 2) * own : (r // 2 + 1) * own]
 
 
 def join_kernel(own_ref, got_ref, out_ref):
@@ -504,30 +610,87 @@
     out_ref[pl.ds(pl.multiple_of((1 - me) * half, C), half), :] = got_ref[...]
 
 
-def weight_kernel(order, counts, *refs):
-    pairs, (keep_ref, give_ref, scr) = refs[:-3], refs[-3:]
+def weight_kernel(orders, counts, *refs):
+    n = sum(counts) * 2
+    pairs, (keep_out, give_out, scr), held, (in_sems, out_sems) = refs[:n], refs[n : n + 3], refs[n + 3 : -2], refs[-2:]
+    copies = []
+    for i, (source, target) in enumerate(zip(pairs, held)):
+        if source.shape[0] != target.shape[0]:
+            spot = row_half(counts, i)
+            source = source.at[spot * target.shape[0] : (spot + 1) * target.shape[0], :]
+        copies.append(send(source, target, in_sems.at[i]))
+    own = scr.shape[0] // 16
+    me = lax.axis_index("b0")
+    base = spot = 0
+    sent = []
+    for side, (count, order) in enumerate(zip(counts, orders)):
+        width = held[spot + 1].shape[1]
+        lanes = slice(base, base + width)
+        total = None
+        for i in range(count):
+            copies[spot + 2 * i].wait()
+            copies[spot + 2 * i + 1].wait()
+            made = dot_tn(held[spot + 2 * i][...], held[spot + 2 * i + 1][...])
+            total = made if total is None else total + made
+        scr[:, lanes] = total.astype(BF16)
+        for bit, out in ((1 - me, give_out), (me, keep_out)):
+            for j, place in enumerate(row_order(order)):
+                start = pl.multiple_of((place + bit) * own, 16)
+                sent.append(send(
+                    scr.at[pl.ds(start, own), lanes], out.at[j * own : (j + 1) * own, lanes], out_sems.at[len(sent)]
+                ))
+        base += width
+        spot += 2 * count
+    for copy in sent:
+        copy.wait()
+
+
+def row_half(counts, i):
+    for count in counts:
+        if i < 2 * count:
+            return i // 2
+        i -= 2 * count
+
+
+def fold_kernel(axes, came, *refs):
+    keep_ref, gots, keep_out, gives = refs[0], refs[1 : 1 + came], refs[1 + came], refs[2 + came : -3]
+    keep_scr, give_scr, sems = refs[-3:]
+    half, columns = keep_scr.shape
+    sides = max(came, len(axes))
+    width = columns // sides
+    for i in range(sides):
+        lanes = slice(i * width, (i + 1) * width)
+        got, inner = (gots[i], slice(0, width)) if came == sides else (gots[0], lanes)
+        me = lax.axis_index(axes[i] if len(axes) == sides else axes[0])
+        for bit, out in ((1 - me, give_scr), (me, keep_scr)):
+            rows = pl.ds(pl.multiple_of(bit * half, 16), half)
+            out[:, lanes] = (keep_ref[rows, lanes].astype(F32) + got[rows, inner].astype(F32)).astype(BF16)
+    copies = [send(keep_scr, keep_out, sems.at[0])]
+    wide = columns // len(gives)
+    for i, give in enumerate(gives):
+        copies.append(send(give_scr.at[:, i * wide : (i + 1) * wide], give, sems.at[1 + i]))
+    for copy in copies:
+        copy.wait()
+
+
+def fold_many_kernel(axis, count, *refs):
+    keeps, gots, (keep_out, give_out, keep_scr, give_scr, sems) = refs[:count], refs[count : 2 * count], refs[2 * count :]
+    half = keep_scr.shape[0]
+    me = lax.axis_index(axis)
     base = 0
-    spot = 0
-    for n in counts:
-        width = pairs[spot + 1].shape[1]
-        made = sum(dot_tn(pairs[spot + 2 * i][...], pairs[spot + 2 * i + 1][...]) for i in range(n))
-        scr[:, base : base + width] = made.astype(BF16)
-        base += width
-        spot += 2 * n
-    own = scr.shape[0] // 16
-    me = lax.axis_index(order[0])
-    for j, place in enumerate(row_order(order[1:])):
-        for bit, out_ref in ((me, keep_ref), (1 - me, give_ref)):
-            start = (place + bit * WEIGHT[order[0]]) * own
-            out_ref[j * own : (j + 1) * own, :] = scr[pl.ds(pl.multiple_of(start, 16), own), :]
-
-
-def fold_kernel(axis, keep_ref, got_ref, next_keep_ref, next_give_ref):
-    half = next_keep_ref.shape[0]
-    me = lax.axis_index(axis)
-    for bit, out_ref in ((me, next_keep_ref), (1 - me, next_give_ref)):
-        rows = pl.ds(pl.multiple_of(bit * half, 16), half)
-        out_ref[...] = (keep_ref[rows, :].astype(F32) + got_ref[rows, :].astype(F32)).astype(BF16)
+    for keep, got in zip(keeps, gots):
+        lanes = slice(base, base + keep.shape[1])
+        for bit, out in ((1 - me, give_scr), (me, keep_scr)):
+            rows = pl.ds(pl.multiple_of(bit * half, 16), half)
+            out[:, lanes] = (keep[rows, :].astype(F32) + got[rows, :].astype(F32)).astype(BF16)
+        base += keep.shape[1]
+    copies = [send(give_scr, give_out, sems.at[0]), send(keep_scr, keep_out, sems.at[1])]
+    for copy in copies:
+        copy.wait()
+
+
+def vector_kernel(recv_ref, out_ref):
+    out_ref[...] = jnp.sum(recv_ref[...], axis=0)
 
 
 def close_kernel(keep_ref, got_ref, out_ref):
@@ -569,8 +732,6 @@
     own = model // devices
     other = functools.partial(lax.ppermute, axis_name="mp", perm=SWAP)
     row = lambda v: v.reshape(1, -1)
-    whole = pl.BlockSpec(memory_space=pltpu.VMEM)
-    unread = pl.BlockSpec(memory_space=pl.ANY)
 
     def across(v):
         if groups == 1:
@@ -580,37 +741,67 @@
         gathered = lax.all_gather(v, "g", axis=0)
         return [gathered[i] for i in range(groups)]
 
-    def weight_terms(order, name, *sides):
+    simple = groups != 2 or own % 16
+
+    def weight_terms(orders, name, *sides, after=()):
         counts = tuple(len(side) for side in sides)
         flat = [v for side in sides for pair in side for v in pair]
         columns = sum(side[0][1].shape[1] for side in sides)
-        flops = 2 * tokens * model * columns
-        if groups != 2 or own % 16:
-            (part,) = call(
-                functools.partial(plain_weight_kernel, counts), [((model, columns), F32)], *flat,
-                flops=flops, name=name, vmem=48 * 2**20,
+        rows = [tokens // count for count in counts for i in range(2 * count)]
+        if simple:
+            halves_of = [
+                v if v.shape[0] == r else v[row_half(counts, i) * r :][:r] for i, (v, r) in enumerate(zip(flat, rows))
+            ]
+            part, token = call(
+                functools.partial(plain_weight_kernel, counts), [((model, columns), F32)], *halves_of,
+                name=name, after=after, token=True,
             )
-            return lax.psum_scatter(part, SEQ, scatter_dimension=0, tiled=True)
-        return tuple(call(
-            functools.partial(weight_kernel, order, counts),
-            [((model // 2, columns), BF16), ((model // 2, columns), BF16)], *flat,
-            scratch=[pltpu.VMEM((model, columns), BF16)], flops=flops, name=name, vmem=48 * 2**20,
-        ))
-
-    def reduce_terms(order, terms, name):
-        if groups != 2 or own % 16:
-            return terms
-        keep, give = terms
-        for step, axis in enumerate(order):
-            got = lax.ppermute(give, axis, SWAP)
-            rows, columns = keep.shape
-            if step == len(order) - 1:
-                return call(close_kernel, [(keep.shape, F32)], keep, got, name=name + "_end")[0]
-            shape = (rows // 2, columns)
-            keep, give = call(
-                functools.partial(fold_kernel, order[step + 1]), [(shape, BF16), (shape, BF16)], keep, got,
-                name=name + "_" + axis,
-            )
+            return (part,), token
+        keep, give, token = call(
+            functools.partial(weight_kernel, orders, counts), [((model // 2, columns), BF16)] * 2, *flat,
+            name=name, after=after, token=True,
+            scratch=[pltpu.VMEM((model, columns), BF16)]
+            + [pltpu.VMEM((r, v.shape[1]), BF16) for r, v in zip(rows, flat)]
+            + [pltpu.SemaphoreType.DMA((len(flat),)), pltpu.SemaphoreType.DMA((16 * len(counts),))],
+            specs=([UNREAD] * len(flat), [UNREAD] * 2),
+        )
+        return (keep, [give]), token
+
+    def fold(axes, parts, terms, name, after=()):
+        if simple:
+            if not parts:
+                summed = [lax.psum_scatter(v, SEQ, scatter_dimension=0, tiled=True) for v in terms]
+                return jnp.concatenate(summed, axis=1), None
+            return terms, None
+        keep, gives = terms
+        gots = [lax.ppermute(give, axis, SWAP) for give, axis in zip(gives, axes)]
+        rows, columns = keep.shape
+        if not parts:
+            return call(close_kernel, [(keep.shape, F32)], keep, *gots, name=name, after=after, token=True)
+        outs = [((rows // 2, columns), BF16)] + [((rows // 2, columns // len(parts)), BF16)] * len(parts)
+        keep, *gives, token = call(
+            functools.partial(fold_kernel, parts, len(gots)), outs, keep, *gots, name=name, after=after, token=True,
+            scratch=[pltpu.VMEM((rows // 2, columns), BF16)] * 2 + [pltpu.SemaphoreType.DMA((len(outs),))],
+            specs=([WHOLE] * (1 + len(gots)), [UNREAD] * len(outs)),
+        )
+        return (keep, gives), token
+
+    def fold_many(axes, part, several, name, after=()):
+        if simple:
+            return tuple(v[0] for v in several), None
+        keeps = [v[0] for v in several]
+        gots = [lax.ppermute(v[1][0], axes[0], SWAP) for v in several]
+        rows, columns = keeps[0].shape[0], sum(v.shape[1] for v in keeps)
+        keep, give, token = call(
+            functools.partial(fold_many_kernel, part, len(several)), [((rows // 2, columns), BF16)] * 2,
+            *keeps, *gots, name=name, after=after, token=True,
+            scratch=[pltpu.VMEM((rows // 2, columns), BF16)] * 2 + [pltpu.SemaphoreType.DMA((2,))],
+            specs=([WHOLE] * (2 * len(several)), [UNREAD] * 2),
+        )
+        return (keep, [give]), token
+
+    def tokens_of(*found):
+        return [v for v in found if v is not None]
 
     ids_other = other(cluster_ids)
     wo_other = other(out_weight)
@@ -621,23 +812,32 @@
         project_kernel,
         [((tokens, model), BF16), ((SUB, C, 5 * C), BF16)],
         inputs, row(norm_one_gain), row(norm_one_shift), query_weight, wkv, cluster_ids,
-        scratch=[pltpu.VMEM((tokens, width), F32), pltpu.VMEM((tokens, 2 * width), BF16)],
+        scratch=[
+            pltpu.VMEM((tokens, width), F32), pltpu.VMEM((tokens, 2 * width), BF16),
+            pltpu.VMEM((tokens, model), BF16), pltpu.VMEM((SUB, C, 5 * C), BF16), pltpu.SemaphoreType.DMA((5,)),
+        ],
         flops=2 * tokens * model * 3 * width,
-        name="project",
+        name="project", specs=([WHOLE] * 6, [UNREAD] * 2),
     )
     recv_one = lax.all_to_all(send_one, NEAR, 0, 0)
     (sums,) = call(
-        sum_kernel, [((C, 2 * C), F32)], recv_one, name="query_sums",
+        sum_kernel, [((C, 2 * C), BF16)], recv_one, name="query_sums", after=[ids_other, wo_other],
         specs=([pl.BlockSpec((SUB, C, 2 * C), lambda i: (0, 0, 0))], [pl.BlockSpec((C, 2 * C), lambda i: (0, 0))]),
     )
     sums = across(sums)
     part, total = call(
-        attend_kernel, [((C, 2 * C), BF16), ((C, 2 * C), F32)], recv_one, ids_other, wo_other, *sums,
+        attend_kernel, [((C, 2 * C), BF16), ((C, 2 * C), F32)], recv_one, *sums,
         name="attend", flops=2 * 2 * 3 * C * SUB * C * C,
-        specs=([whole, unread, unread] + [whole] * len(sums), [whole] * 2),
-    )
+        scratch=[pltpu.VMEM((C, 2 * C), F32), pltpu.SemaphoreType.DMA],
+        specs=([WHOLE] * (1 + len(sums)), [WHOLE, UNREAD]),
+    )
+    parts = across(part)
     fin, send_two = call(
-        merge_kernel, [((C, 2 * C), F32), ((2 * SUB, C + HD, C), BF16)], *across(part), name="merge"
+        merge_kernel, [((C, 2 * C), F32), ((2 * SUB, C + HD, C), BF16)], *parts, name="merge",
+        scratch=[
+            pltpu.VMEM((C, 2 * C), F32), pltpu.VMEM((C + HD, C), BF16), pltpu.SemaphoreType.DMA((2 * SUB + 1,))
+        ],
+        specs=([WHOLE] * len(parts), [UNREAD] * 2),
     )
     recv_two = lax.all_to_all(send_two, NEAR + ("mp",), 0, 0)
     halves = []
@@ -647,83 +847,126 @@
         halves.append(call(
             middle_kernel,
             [
-                ((half, width), BF16), ((half, model), F32), ((half, model), BF16),
-                ((half, hidden), BF16), ((half, hidden), BF16), ((half, model), BF16),
-                ((1, hidden), F32),
+                ((1, hidden), F32), ((half, model), F32), ((half, model), BF16), ((half, width), BF16),
+                ((half, model), BF16), ((half, hidden), BF16), ((half, hidden), BF16),
             ],
-            recv_two, cluster_ids, ids_other, inputs, out_weight, wo_other, row(norm_two_gain),
-            row(norm_two_shift), up_weight, row(up_bias), down_weight, bg,
-            scratch=[pltpu.VMEM((half, 2 * width), BF16), pltpu.VMEM((2 * width, model), BF16)],
+            recv_two, cluster_ids, ids_other, inputs, row(norm_two_gain), row(norm_two_shift), row(up_bias), bg,
+            out_weight, wo_other, up_weight, down_weight,
+            scratch=[
+                pltpu.VMEM((half, 2 * width), BF16), pltpu.VMEM((2 * width, model), BF16),
+                pltpu.VMEM((model, hidden), BF16), pltpu.VMEM((hidden, model), BF16),
+                pltpu.VMEM((half, width), BF16), pltpu.VMEM((half, model), BF16),
+                pltpu.VMEM((half, hidden), BF16), pltpu.VMEM((half, hidden), BF16),
+                pltpu.SemaphoreType.DMA((4,)), pltpu.SemaphoreType.DMA((4,)),
+            ],
             flops=2 * half * model * (2 * width + 3 * hidden),
-            vmem=48 * 2**20, name="middle",
+            extra=12, name="middle",
             specs=(
                 [pl.BlockSpec((SUB, C + HD, C), lambda i, n=n: (n, 0, 0)), lanes, lanes, rows(model)]
-                + [whole] * 7 + [rows(model)],
-                [whole] * 7,
+                + [WHOLE] * 3 + [rows(model)] + [UNREAD] * 4,
+                [WHOLE] * 3 + [UNREAD] * 4,
             ),
         ))
-    attended, residual, normed_two, active, hidden_grad, back, bias_part = zip(*halves)
+    bias_part, residual, back, attended, normed_two, active, hidden_grad = zip(*halves)
     back_other = [other(v) for v in back]
-    up_order = ("b0", "b1", "b2", "g")
-    down_order = ("b0", "b2", "b1", "g")
-    up_terms = weight_terms(up_order, "up_terms", list(zip(normed_two, hidden_grad)))
-    bg_halves = (bg[:half], bg[half:])
-    down_terms = weight_terms(down_order, "down_terms", list(zip(bg_halves, active)))
-    residual_grad, mixed_grad, send_three = call(
+    order = ("b1", "b2", "g")
+    ff_terms, ff_token = weight_terms(
+        (order, ("b2", "b1", "g")), "ff_terms", list(zip(normed_two, hidden_grad)), [(bg, v) for v in active]
+    )
+    residual_grad, mixed_grad, send_three, turned = call(
         turn_kernel,
         [((half, model), F32), ((tokens, model), BF16), ((SUB, PACK, C), BF16)],
         *back, *back_other, *residual, row(norm_two_gain), bg, out_weight, cluster_ids, *bias_part,
-        scratch=[pltpu.VMEM((tokens, width), F32), pltpu.VMEM((32, C), F32)],
+        scratch=[
+            pltpu.VMEM((tokens, width), F32), pltpu.VMEM((32, C), F32), pltpu.VMEM((half, model), F32),
+            pltpu.VMEM((tokens, model), BF16), pltpu.VMEM((SUB, PACK, C), BF16), pltpu.SemaphoreType.DMA((6,)),
+        ],
+        specs=([WHOLE] * 12, [UNREAD] * 3),
         flops=2 * tokens * model * width, name="turn",
+        after=[ff_token], token=True,
     )
     recv_three = lax.all_to_all(send_three, NEAR, 0, 0)
-    up_sum = reduce_terms(up_order, up_terms, "up")
-    down_sum = reduce_terms(down_order, down_terms, "down")
-    (branch,) = call(
-        branch_kernel, [((tokens, model), BF16)], *active, down_weight, back_other[1],
-        flops=2 * tokens * model * hidden, name="branch", specs=([whole] * 3 + [unread], [whole]),
-    )
-    branch_other = other(branch)
-    (block_output,) = call(
-        output_kernel, [((tokens, model), BF16)], *residual, branch, branch_other, row(down_bias), name="output"
-    )
-    (grad_sums,) = call(grad_sum_kernel, [((PACK, C), BF16)], recv_three, name="grad_sums")
-    cgrad, vec, send_four = call(
+    branches = [
+        call(
+            branch_kernel, [((half, model), BF16)], v, down_weight, name="branch", token=True,
+            flops=2 * half * model * hidden, after=[turned],
+        )
+        for v in active
+    ]
+    ff_terms, ff_token = fold(("b0",), ("b1", "b2"), ff_terms, "ff_fold", after=[b[1] for b in branches])
+    branch = [b[0] for b in branches]
+    branch_other = [other(b) for b in branch]
+    grad_sums, summed = call(
+        grad_sum_kernel, [((PACK, C), BF16)], recv_three, name="grad_sums",
+        after=tokens_of(ff_token, branches[0][1], branches[1][1]), token=True,
+    )
+    grad_sums = across(grad_sums)
+    cgrad, vec, send_four, attended_back = call(
         attend_back_kernel,
         [((C + HD, C), BF16), ((4, C), F32), ((SUB, C, 3 * C), BF16)],
-        recv_one, total, fin, *across(grad_sums), flops=2 * 5 * 3 * C * SUB * C * C, name="attend_back",
+        recv_one, total, fin, *grad_sums, flops=2 * 5 * 3 * C * SUB * C * C, name="attend_back",
+        scratch=[
+            pltpu.VMEM((SUB, C, 5 * C), BF16), pltpu.VMEM((C, 2 * C), F32), pltpu.VMEM((C, 2 * C), F32),
+            pltpu.SemaphoreType.DMA((3,)),
+        ],
+        specs=([UNREAD] * 3 + [WHOLE] * len(grad_sums), [WHOLE] * 3), after=[branch_other[0]],
+        token=True,
     )
     recv_four = lax.all_to_all(send_four, NEAR, 0, 0)
-    (send_five,) = call(
-        finish_back_kernel, [((SUB, PACK, C), BF16)], total, vec, *across(cgrad), name="finish_back"
+    cgrads = across(cgrad)
+    send_five, finished = call(
+        finish_back_kernel, [((SUB, PACK, C), BF16)], total, vec, *cgrads, name="finish_back",
+        after=[branch_other[1]], token=True,
+        scratch=[pltpu.VMEM((PACK, C), BF16), pltpu.SemaphoreType.DMA((SUB,))],
+        specs=([WHOLE] * (2 + len(cgrads)), [UNREAD]),
     )
     recv_five = lax.all_to_all(send_five, NEAR, 0, 0)
-    (kv_grads,) = call(gather_kernel, [((tokens, 2 * width), BF16)], recv_four, name="gather")
-    kv_order = ("b0", "b1", "b2", "g")
-    mixed_halves = (mixed_grad[:half], mixed_grad[half:])
-    kv_terms = weight_terms(
-        kv_order, "kv_terms", [(normed_one, kv_grads)], list(zip(mixed_halves, attended))
-    )
-    q_grads, keep, give = call(
+    (kv_grads,) = call(
+        gather_kernel, [((tokens, 2 * width), BF16)], recv_four, name="gather", after=[finished],
+    )
+    kv_terms, kv_token = weight_terms(
+        (order, order), "kv_terms", [(normed_one, kv_grads)], [(mixed_grad, v) for v in attended]
+    )
+    q_grads, keep, give, first_token = call(
         first_back_kernel,
         [((tokens, width), BF16), ((half, model), BF16), ((half, model), BF16)],
         recv_five, cluster_ids, query_weight, wkv, kv_grads,
-        scratch=[pltpu.VMEM((tokens, model), BF16)], flops=2 * tokens * model * 3 * width, name="first_back",
+        scratch=[
+            pltpu.VMEM((2, half, model), BF16), pltpu.VMEM((model, width), BF16), pltpu.VMEM((model, 2 * width), BF16),
+            pltpu.VMEM((tokens, 2 * width), BF16), pltpu.VMEM((tokens, width), BF16),
+            pltpu.SemaphoreType.DMA((3,)), pltpu.SemaphoreType.DMA((3,)),
+        ],
+        specs=([WHOLE] * 2 + [UNREAD] * 3, [UNREAD] * 3),
+        flops=2 * tokens * model * 3 * width, name="first_back",
+        after=tokens_of(kv_token), token=True,
     )
     got = other(give)
-    q_terms = weight_terms(kv_order, "q_terms", [(normed_one, q_grads)])
-    grad_half, vec_one = call(
-        last_kernel, [((half, model), BF16), ((2, model), F32)],
+    q_terms, q_token = weight_terms((order,), "q_terms", [(normed_one, q_grads)], after=[first_token])
+    kv_terms, kv_token = fold_many(("b0",), "b1", (kv_terms, q_terms), "kv_fold", after=[q_token])
+    ff_terms, ff_token = fold(("b1", "b2"), ("b2", "b1"), ff_terms, "ff_fold", after=tokens_of(q_token, kv_token))
+    grad_half, vec_one, last_token = call(
+        last_kernel, [((half, model), BF16), ((2 * devices, 2, own), F32)],
         keep, got, inputs, row(norm_one_gain), residual_grad, name="last",
-    )
-    (input_grad,) = call(join_kernel, [((tokens, model), BF16)], grad_half, other(grad_half), name="join")
-    kv_sum = reduce_terms(kv_order, kv_terms, "kv")
-    q_sum = reduce_terms(kv_order, q_terms, "q")
-    vec_send = jnp.broadcast_to(
-        vec_one.reshape(2, devices, own).swapaxes(0, 1).reshape(devices, 1, 2 * own), (devices, 2, 2 * own)
-    ).reshape(2 * devices, 2 * own)
-    vec_recv = lax.all_to_all(vec_send, SEQ + ("mp",), 0, 0, tiled=True)
-    vec_sum = jnp.sum(vec_recv, axis=0).reshape(2, own)
+        after=tokens_of(ff_token), token=True,
+    )
+    grad_other = other(grad_half)
+    kv_terms, kv_token = fold(("b1",), ("b2",), kv_terms, "kv_fold", after=[last_token])
+    ff_terms, ff_token = fold(("b2", "b1"), ("g",), ff_terms, "ff_fold", after=tokens_of(kv_token))
+    vec_recv = lax.all_to_all(vec_one, SEQ + ("mp",), 0, 0, tiled=True)
+    vec_sum, vec_token = call(
+        vector_kernel, [((2, own), F32)], vec_recv, name="vectors", after=tokens_of(ff_token), token=True
+    )
+    kv_terms, kv_token = fold(("b2",), ("g",), kv_terms, "kv_fold", after=[vec_token])
+    block_output, output_token = call(
+        output_kernel, [((tokens, model), BF16)], *residual, *branch, *branch_other, row(down_bias),
+        name="output", after=tokens_of(kv_token, vec_token), token=True,
+    )
+    input_grad, join_token = call(
+        join_kernel, [((tokens, model), BF16)], grad_half, grad_other, name="join",
+        after=[output_token], token=True,
+    )
+    ff_sum, ff_token = fold(("g",), (), ff_terms, "ff_close", after=[join_token])
+    kv_sum, kv_token = fold(("g",), (), kv_terms, "kv_close", after=tokens_of(ff_token))
 
     small = recv_five[:, C + HD : C + HD + 8, :].astype(F32)
     small = (small[:, 0:4] + small[:, 4:8]).reshape(-1)
@@ -734,14 +977,14 @@
         input_grad,
         vec_sum[0],
         vec_sum[1],
-        q_sum,
+        kv_sum[:, 3 * width :],
         kv_sum[:, 0 : 2 * width].reshape(own, 2, width),
-        kv_sum[:, 2 * width :].T,
+        kv_sum[:, 2 * width : 3 * width].T,
         take(hidden),
         take(hidden + model),
-        up_sum,
+        ff_sum[:, 0:hidden],
         small[0:hidden],
-        down_sum.T,
+        ff_sum[:, hidden:].T,
         take(hidden + 2 * model),
     )
 

time: 233 us -> 211 us (0.906)
  local copies, waits for them, and re-layouts: 34.5 us -> 17.8 us
  blocking collectives: 11.2 us -> 0 us
  Pallas kernels: 59.4 us -> 67.8 us
  waiting for transfers between devices: 70.6 us -> 62.9 us
  starting transfers between devices: 51.6 us -> 58.1 us
    unnamed x175 -> x111, local copies, waits for them, and re-layouts: 29.5 us -> 11.7 us
    all_to_all x1, waiting for transfers between devices: 15.7 us -> 1.06 us  [on_device(): recv_one = lax.all_to_all(send_one, NEAR, 0, 0)]
    ppermute x1, waiting for transfers between devices: 2.22 us -> 14 us  [on_device(): ids_other = other(cluster_ids)]
    all_to_all x1 -> x0, blocking collectives: 11.2 us -> none  [on_device(): recv_three = lax.all_to_all(send_three, NEAR, 0, 0)]
    ppermute x18 -> x14, waiting for transfers between devices: 12.4 us -> 22.6 us  [the longest x9 14 us: fold(): gots = [lax.ppermute(give, axis, SWAP) for give, axis in zip(gives, axes)]]
    ppermute x4, waiting for transfers between devices: 15.9 us -> 6.4 us  [across(): return [v, lax.ppermute(v, 'g', SWAP)]]
    pallas_call x36 -> x29, Pallas kernels: 59.4 us -> 67.8 us  [call(): pl.pallas_call(body, out_shape=[pltpu.HBM(s, d) if spec is UNREAD else ja...]
    ppermute x18 -> x14, starting transfers between devices: 18.7 us -> 13.1 us  [the longest x9 9.95 us: fold(): gots = [lax.ppermute(give, axis, SWAP) for give, axis in zip(gives, axes)]]
  transfers between devices with their start and end apart: 32 -> 29, of which waited for: 15 -> 15; matrix products, arithmetic and copies ran while one was open for 3% -> 3% of each run, Pallas kernels for 19% -> 25%
where the time goes in v3:
time: 211 us; the launch traced here: 209 us
  Pallas kernels  67.8 us (32%)
  waiting for transfers between devices  62.9 us (30%)
  starting transfers between devices  58.1 us (28%)
  local copies, waits for them, and re-layouts  17.8 us (8%)
    pallas_call x29, Pallas kernels, call(): pl.pallas_call(body, out_shape=[pltpu.HBM(s, d) if spec is UNREAD else ja...  67.8 us
    ppermute x1, waiting for transfers between devices, on_device(): ids_other = other(cluster_ids)  14 us
    ppermute x9, waiting for transfers between devices, fold(): gots = [lax.ppermute(give, axis, SWAP) for give, axis in zip(gives, axes)]  14 us
    all_to_all x1, waiting for transfers between devices, on_device(): recv_two = lax.all_to_all(send_two, NEAR + ('mp',), 0, 0)  13 us
    unnamed x111, local copies, waits for them, and re-layouts  11.7 us
    ppermute x4, starting transfers between devices, across(): return [v, lax.ppermute(v, 'g', SWAP)]  11.7 us
    ppermute x9, starting transfers between devices, fold(): gots = [lax.ppermute(give, axis, SWAP) for give, axis in zip(gives, axes)]  9.95 us
    ppermute x2, waiting for transfers between devices, on_device(): branch_other = [other(b) for b in branch]  8.21 us
  transfers between devices with their start and end apart: 29, of which 15 were waited for; matrix products, arithmetic and copies ran while one was open for 3% of the time, Pallas kernels for 25%

profile of v3, /device:TPU:0, one launch (start us, length us, event | category | flops | bytes accessed | tf_op | source)
XLA Modules:
  0.0 209.5 jit_solution(14082876635223766795)
XLA Ops:
  0.7 1.6 copy.28
  2.4 3.1 %project.1 = (bf16[512,768]{1,0:T(8,128)(2,1)}, bf16[8,128,640]{2,1,0:T(8,128)(2,1)}) custom-call(bf16[512,768]{1,0:T(8,128)(2,1)S(1)} %copy-done.4, f32[1,768]{1,0:T(1,128)S(1)} %reshape.60.refs_1_.refs_3_, f32[1,768]{1,0:T(1,128)S(1)} %reshape.61.refs_2_, bf16[768,384]{1,0:T(8,128)(2,1)S(1)} %copy-done.24, bf16[768,768]{1,0:T(8,128)(2,1)S(1)} %bitcast.13, ...), custom_call_target="tpu_custom_call" | custom-call | flops 1000000 | bytes 1 | tf_op jit(solution)/shard_map/project/pallas_call | solution.py:74
  5.5 5.2 %all-to-all-start = ((bf16[8,128,640]{2,1,0:T(8,128)(2,1)}), bf16[8,128,640]{2,1,0:T(8,128)(2,1)S(1)}, u32[]{:S(2)}, u32[]{:S(2)}) async-start(bf16[8,128,640]{2,1,0:T(8,128)(2,1)} %get-tuple-element.92), calls=%async_computation | async-start | bytes 2621440 | tf_op jit(solution)/shard_map/all_to_all | solution.py:822
  10.8 1.6 collective-permute-start.1
  12.9 14.0 %collective-permute-done.refs_1_.refs_2_ = s32[6,512]{1,0:T(8,128)S(1)} collective-permute-done((s32[6,512]{1,0:T(8,128)S(1)}, s32[6,512]{1,0:T(8,128)S(1)}, u32[]{:S(2)}, u32[]{:S(2)}) %collective-permute-start) | collective-permute-done | bytes 12320 | tf_op jit(solution)/shard_map/ppermute | solution.py:806
  26.9 1.1 all-to-all-done.refs_0_
  28.2 2.7 %collective-permute-start.2 = (bf16[128,256]{1,0:T(8,128)(2,1)S(1)}, bf16[128,256]{1,0:T(8,128)(2,1)S(1)}, u32[]{:S(2)}, u32[]{:S(2)}) collective-permute-start(bf16[128,256]{1,0:T(8,128)(2,1)S(1)} %query_sums.1.refs_1_), channel_id=1, source_target_pairs={{0,16},{16,0},{1,17},{17,1},{2,18},{18,2},{3,19},{19,3},{4,20},{20... | collective-permute-start | bytes 196616 | tf_op jit(solution)/shard_map/ppermute | solution.py:740
  30.8 2.6 %collective-permute-done.2.refs_2_ = bf16[128,256]{1,0:T(8,128)(2,1)S(1)} collective-permute-done((bf16[128,256]{1,0:T(8,128)(2,1)S(1)}, bf16[128,256]{1,0:T(8,128)(2,1)S(1)}, u32[]{:S(2)}, u32[]{:S(2)}) %collective-permute-start.2) | collective-permute-done | bytes 65568 | tf_op jit(solution)/shard_map/ppermute | solution.py:740
  33.5 1.9 attend.1
  35.3 2.7 %collective-permute-start.3 = (bf16[128,256]{1,0:T(8,128)(2,1)S(1)}, bf16[128,256]{1,0:T(8,128)(2,1)S(1)}, u32[]{:S(2)}, u32[]{:S(2)}) collective-permute-start(bf16[128,256]{1,0:T(8,128)(2,1)S(1)} %get-tuple-element.93.refs_0_), channel_id=1, source_target_pairs={{0,16},{16,0},{1,17},{17,1},{2,18},{18,2},{3,19},{19,3},{4,20},{20... | collective-permute-start | bytes 196616 | tf_op jit(solution)/shard_map/ppermute | solution.py:740
  38.0 2.6 %collective-permute-done.3.refs_1_ = bf16[128,256]{1,0:T(8,128)(2,1)S(1)} collective-permute-done((bf16[128,256]{1,0:T(8,128)(2,1)S(1)}, bf16[128,256]{1,0:T(8,128)(2,1)S(1)}, u32[]{:S(2)}, u32[]{:S(2)}) %collective-permute-start.3) | collective-permute-done | bytes 65568 | tf_op jit(solution)/shard_map/ppermute | solution.py:740
  40.6 1.5 merge.1
  42.1 5.0 %all-to-all-start.1 = ((bf16[16,192,128]{2,1,0:T(8,128)(2,1)}), bf16[16,192,128]{2,1,0:T(8,128)(2,1)S(1)}, u32[]{:S(2)}, u32[]{:S(2)}) async-start(bf16[16,192,128]{2,1,0:T(8,128)(2,1)} %get-tuple-element.94), calls=%async_computation.1 | async-start | bytes 1572864 | tf_op jit(solution)/shard_map/all_to_all | solution.py:842
  47.3 13.0 %all-to-all-done.1.refs_0_ = bf16[16,192,128]{2,1,0:T(8,128)(2,1)S(1)} async-done(((bf16[16,192,128]{2,1,0:T(8,128)(2,1)}), bf16[16,192,128]{2,1,0:T(8,128)(2,1)S(1)}, u32[]{:S(2)}, u32[]{:S(2)}) %all-to-all-start.1) | async-done | bytes 786464 | tf_op jit(solution)/shard_map/all_to_all | solution.py:842
  60.3 1.1 copy-done.5
  61.4 5.5 %middle.3 = (f32[1,1536]{1,0:T(1,128)S(1)}, f32[256,768]{1,0:T(8,128)S(1)}, bf16[256,768]{1,0:T(8,128)(2,1)S(1)}, bf16[256,384]{1,0:T(8,128)(2,1)}, bf16[256,768...) custom-call(bf16[16,192,128]{2,1,0:T(8,128)(2,1)S(1)} %all-to-all-done.1.refs_0_, ...), custom_call_target="tpu_custom_call" | custom-call | flops 1000000 | bytes 1 | tf_op jit(solution)/shard_map/middle/pallas_call | solution.py:74
  67.5 5.5 %middle.2 = (f32[1,1536]{1,0:T(1,128)S(1)}, f32[256,768]{1,0:T(8,128)S(1)}, bf16[256,768]{1,0:T(8,128)(2,1)S(1)}, bf16[256,384]{1,0:T(8,128)(2,1)}, bf16[256,768...) custom-call(bf16[16,192,128]{2,1,0:T(8,128)(2,1)S(1)} %all-to-all-done.1.refs_0_, ...), custom_call_target="tpu_custom_call" | custom-call | flops 1000000 | bytes 1 | tf_op jit(solution)/shard_map/middle/pallas_call | solution.py:74
  73.0 1.5 collective-permute-start.4
  74.6 6.6 %ff_terms.1 = (bf16[384,3072]{1,0:T(8,128)(2,1)}, bf16[384,3072]{1,0:T(8,128)(2,1)}, f32[8,128]{1,0:T(8,128)}) custom-call(bf16[256,768]{1,0:T(8,128)(2,1)} %get-tuple-element.102.refs_0_, bf16[256,1536]{1,0:T(8,128)(2,1)} %get-tuple-element.103.refs_1_, bf16[256,768]{1,0:T(8,128)(2,1)} %get-tuple-element.104.refs_2_, ...), custom_call_target="tpu_custom_call" | custom-call | flops 1000000 | bytes 1 | tf_op jit(solution)/shard_map/ff_terms/pallas_call | solution.py:74
  81.2 5.6 %collective-permute-done.4.refs_2_ = bf16[256,768]{1,0:T(8,128)(2,1)S(1)} collective-permute-done((bf16[256,768]{1,0:T(8,128)(2,1)S(1)}, bf16[256,768]{1,0:T(8,128)(2,1)S(1)}, u32[]{:S(2)}, u32[]{:S(2)}) %collective-permute-start.4) | collective-permute-done | bytes 393248 | tf_op jit(solution)/shard_map/ppermute | solution.py:871
  86.9 3.7 %turn.1 = (f32[256,768]{1,0:T(8,128)}, bf16[512,768]{1,0:T(8,128)(2,1)}, bf16[8,208,128]{2,1,0:T(8,128)(2,1)}, f32[8,128]{1,0:T(8,128)}) custom-call(bf16[256,768]{1,0:T(8,128)(2,1)S(1)} %get-tuple-element.98.refs_0_, bf16[256,768]{1,0:T(8,128)(2,1)S(1)} %get-tuple-element.99.refs_1_, bf16[256,768]{1,0:T(8,128)(2,1)S(1)} %collective-permute-done.4.refs_2_, ...), custom_call_target="tpu_custom_call" | custom-call | flops 40000000000 | bytes 1 | tf_op jit(solution)/shard_map/turn/pallas_call | solution.py:74
  90.6 4.2 %all-to-all-start.2 = ((bf16[8,208,128]{2,1,0:T(8,128)(2,1)}), bf16[8,208,128]{2,1,0:T(8,128)(2,1)}, u32[]{:S(2)}, u32[]{:S(2)}) async-start(bf16[8,208,128]{2,1,0:T(8,128)(2,1)} %get-tuple-element.114), calls=%async_computation.2 | async-start | bytes 851968 | tf_op jit(solution)/shard_map/all_to_all | solution.py:888
  94.9 1.1 copy-done.10
  97.5 0.8 branch.3
  99.0 3.5 %ff_fold.3 = (bf16[192,3072]{1,0:T(8,128)(2,1)}, bf16[192,1536]{1,0:T(8,128)(2,1)}, bf16[192,1536]{1,0:T(8,128)(2,1)}, f32[8,128]{1,0:T(8,128)}) custom-call(bf16[384,3072]{1,0:T(8,128)(2,1)S(1)} %copy-done.13, bf16[384,3072]{1,0:T(8,128)(2,1)} %collective-permute-done.8.refs_1_, f32[8,128]{1,0:T(8,128)} %get-tuple-element.117.refs_2_, ...), custom_call_target="tpu_custom_call" | custom-call | flops 1000000 | bytes 1 | tf_op jit(solution)/shard_map/ff_fold/pallas_call | solution.py:74
  102.7 1.1 grad_sums.1
  103.7 3.1 %collective-permute-start.9 = (bf16[208,128]{1,0:T(8,128)(2,1)S(1)}, bf16[208,128]{1,0:T(8,128)(2,1)S(1)}, u32[]{:S(2)}, u32[]{:S(2)}) collective-permute-start(bf16[208,128]{1,0:T(8,128)(2,1)S(1)} %get-tuple-element.120.refs_3_), channel_id=1, source_target_pairs={{0,16},{16,0},{1,17},{17,1},{2,18},{18,2},{3,19},{19,3},{4,20},{20... | collective-permute-start | bytes 159752 | tf_op jit(solution)/shard_map/ppermute | solution.py:740
  106.9 1.5 collective-permute-done.6.refs_5_.refs_4_
  108.4 1.2 collective-permute-done.9.refs_4_
  109.6 3.9 %attend_back.1 = (bf16[192,128]{1,0:T(8,128)(2,1)S(1)}, f32[4,128]{1,0:T(4,128)S(1)}, bf16[8,128,384]{2,1,0:T(8,128)(2,1)}, f32[8,128]{1,0:T(8,128)}) custom-call(bf16[8,128,640]{2,1,0:T(8,128)(2,1)} %copy-done.3, f32[128,256]{1,0:T(8,128)} %get-tuple-element.112.refs_1_.refs_0_, f32[128,256]{1,0:T(8,128)} %get-tuple-element.113.refs_2_, ...), custom_call_target="tpu_custom_call" | custom-call | flops 40000000000 | bytes 1 | tf_op jit(solution)/shard_map/attend_back/pallas_call | solution.py:74
  113.5 3.6 %all-to-all-start.3 = ((bf16[8,128,384]{2,1,0:T(8,128)(2,1)}), bf16[8,128,384]{2,1,0:T(8,128)(2,1)S(1)}, u32[]{:S(2)}, u32[]{:S(2)}) async-start(bf16[8,128,384]{2,1,0:T(8,128)(2,1)} %get-tuple-element.121), calls=%async_computation.3 | async-start | bytes 1572864 | tf_op jit(solution)/shard_map/all_to_all | solution.py:915
  117.0 1.5 collective-permute-start.7
  118.6 3.3 %collective-permute-start.10 = (bf16[192,128]{1,0:T(8,128)(2,1)S(1)}, bf16[192,128]{1,0:T(8,128)(2,1)S(1)}, u32[]{:S(2)}, u32[]{:S(2)}) collective-permute-start(bf16[192,128]{1,0:T(8,128)(2,1)S(1)} %get-tuple-element.123.refs_2_), channel_id=1, source_target_pairs={{0,16},{16,0},{1,17},{17,1},{2,18},{18,2},{3,19},{19,3},{4,20},{20... | collective-permute-start | bytes 147464 | tf_op jit(solution)/shard_map/ppermute | solution.py:740
  121.9 6.7 %collective-permute-done.7.refs_4_.refs_5_ = bf16[256,768]{1,0:T(8,128)(2,1)S(1)} collective-permute-done((bf16[256,768]{1,0:T(8,128)(2,1)S(1)}, bf16[256,768]{1,0:T(8,128)(2,1)S(1)}, u32[]{:S(2)}, u32[]{:S(2)}) %collective-permute-start.7) | collective-permute-done | bytes 393248 | tf_op jit(solution)/shard_map/ppermute | solution.py:898
  129.3 1.0 finish_back.1
  130.3 5.9 %all-to-all-start.4 = ((bf16[8,208,128]{2,1,0:T(8,128)(2,1)}), bf16[8,208,128]{2,1,0:T(8,128)(2,1)S(1)}, u32[]{:S(2)}, u32[]{:S(2)}) async-start(bf16[8,208,128]{2,1,0:T(8,128)(2,1)} %get-tuple-element.129), calls=%async_computation.4 | async-start | bytes 851968 | tf_op jit(solution)/shard_map/all_to_all | solution.py:923
  136.2 2.0 collective-permute-start.15
  138.3 1.5 collective-permute-start.16
  139.9 0.9 copy-done.8
  140.8 4.8 %kv_terms.1 = (bf16[384,1152]{1,0:T(8,128)(2,1)}, bf16[384,1152]{1,0:T(8,128)(2,1)}, f32[8,128]{1,0:T(8,128)}) custom-call(bf16[512,768]{1,0:T(8,128)(2,1)} %get-tuple-element.111.refs_0_, bf16[512,768]{1,0:T(8,128)(2,1)} %copy-done.8, bf16[512,768]{1,0:T(8,128)(2,1)} %get-tuple-element.125.refs_2_.refs_4_, bf16[256,384]{1,0:T(8,128)(2,1)} %get-tuple-element.126.refs_3_, ...), custom_call_target="tpu_custom_call" | custom-call | flops 1000000 | bytes 1 | tf_op jit(solution)/shard_map/kv_terms/pallas_call | solution.py:74
  146.5 1.0 copy-done.26
  147.5 4.5 %first_back.1 = (bf16[512,384]{1,0:T(8,128)(2,1)}, bf16[256,768]{1,0:T(8,128)(2,1)}, bf16[256,768]{1,0:T(8,128)(2,1)}, f32[8,128]{1,0:T(8,128)}) custom-call(bf16[8,208,128]{2,1,0:T(8,128)(2,1)S(1)} %copy-done.26, s32[6,512]{1,0:T(8,128)S(1)} %copy-done.35, bf16[768,384]{1,0:T(8,128)(2,1)} %refs_2_.2, bf16[768,768]{1,0:T(8,128)(2,1)} %bitcast.14, ...), custom_call_target="tpu_custom_call" | custom-call | flops 40000000000 | bytes 1 | tf_op jit(solution)/shard_map/first_back/pallas_call | solution.py:74
  152.0 1.5 collective-permute-start.14
  153.5 2.8 %q_terms.1 = (bf16[384,384]{1,0:T(8,128)(2,1)}, bf16[384,384]{1,0:T(8,128)(2,1)}, f32[8,128]{1,0:T(8,128)}) custom-call(bf16[512,768]{1,0:T(8,128)(2,1)} %get-tuple-element.111.refs_0_, bf16[512,384]{1,0:T(8,128)(2,1)} %get-tuple-element.131.refs_1_, f32[8,128]{1,0:T(8,128)} %get-tuple-element.132.refs_2_), custom_call_target="tpu_custom_call" | custom-call | flops 1000000 | bytes 1 | tf_op jit(solution)/shard_map/q_terms/pallas_call | solution.py:74
  158.3 1.0 copy-done.32
  159.3 2.3 %kv_fold.3 = (bf16[192,1536]{1,0:T(8,128)(2,1)}, bf16[192,1536]{1,0:T(8,128)(2,1)}, f32[8,128]{1,0:T(8,128)}) custom-call(bf16[384,1152]{1,0:T(8,128)(2,1)S(1)} %copy-done.17, bf16[384,384]{1,0:T(8,128)(2,1)S(1)} %copy-done.32, bf16[384,1152]{1,0:T(8,128)(2,1)S(1)} %collective-permute-done.11.refs_2_, bf16[384,384]{1,0:T(8,128)(2,1)} %collective-permute-done.12.refs_3_, ...), custom_call_target="tpu_custom_call" | custom-call | flops 1000000 | bytes 1 | tf_op jit(solution)/shard_map/kv_fold/pallas_call | solution.py:74
  162.2 2.2 %ff_fold.4 = (bf16[96,3072]{1,0:T(8,128)(2,1)}, bf16[96,1536]{1,0:T(8,128)(2,1)}, bf16[96,1536]{1,0:T(8,128)(2,1)}, f32[8,128]{1,0:T(8,128)}) custom-call(bf16[192,3072]{1,0:T(8,128)(2,1)S(1)} %copy-done.16, bf16[192,1536]{1,0:T(8,128)(2,1)S(1)} %collective-permute-done.15.refs_1_, bf16[192,1536]{1,0:T(8,128)(2,1)} %collective-permute-done.16.refs_2_, ...), custom_call_target="tpu_custom_call" | custom-call | flops 1000000 | bytes 1 | tf_op jit(solution)/shard_map/ff_fold/pallas_call | solution.py:74
  164.8 1.7 collective-permute-start.19
  166.6 2.5 %last.1 = (bf16[256,768]{1,0:T(8,128)(2,1)}, f32[32,2,48]{2,1,0:T(2,128)S(1)}, f32[8,128]{1,0:T(8,128)}) custom-call(bf16[256,768]{1,0:T(8,128)(2,1)S(1)} %copy-done.45, bf16[256,768]{1,0:T(8,128)(2,1)} %collective-permute-done.14.refs_1_, bf16[512,768]{1,0:T(8,128)(2,1)S(1)} %copy-done.6, f32[1,768]{1,0:T(1,128)S(1)} %copy-done.42, ...), custom_call_target="tpu_custom_call" | custom-call | flops 40000000000 | bytes 1 | tf_op jit(solution)/shard_map/last/pallas_call | solution.py:74
  170.9 3.5 %all-to-all-start.5 = ((f32[32,2,48]{2,1,0:T(2,128)}), f32[32,2,48]{2,1,0:T(2,128)}, u32[]{:S(2)}, u32[]{:S(2)}) async-start(f32[32,2,48]{2,1,0:T(2,128)} %copy-done.40), calls=%async_computation.5 | async-start | bytes 65536 | tf_op jit(solution)/shard_map/all_to_all | solution.py:955
  174.5 3.6 %collective-permute-done.13.refs_1_ = bf16[192,1536]{1,0:T(8,128)(2,1)} collective-permute-done((bf16[192,1536]{1,0:T(8,128)(2,1)}, bf16[192,1536]{1,0:T(8,128)(2,1)}, u32[]{:S(2)}, u32[]{:S(2)}) %collective-permute-start.13) | collective-permute-done | bytes 589856 | tf_op jit(solution)/shard_map/ppermute | solution.py:777
  178.1 2.0 kv_fold.4
  180.7 1.4 fusion
  184.0 2.0 ff_fold.5
  186.0 1.3 collective-permute-start.22
  187.3 0.8 vectors.1
  188.6 1.0 copy-done.34
  190.3 1.7 collective-permute-start.21
  192.1 1.0 copy-done.31
  193.1 2.2 %output.1 = (bf16[512,768]{1,0:T(8,128)(2,1)}, f32[8,128]{1,0:T(8,128)}) custom-call(f32[256,768]{1,0:T(8,128)S(1)} %copy-done.21, f32[256,768]{1,0:T(8,128)S(1)} %copy-done.19, bf16[256,768]{1,0:T(8,128)(2,1)S(1)} %copy-done.28, bf16[256,768]{1,0:T(8,128)(2,1)S(1)} %copy-done.31, bf16[256,768]{1,0:T(8,128)(2,1)} %collective-permute-done.6.refs_5_.refs_4_, ...), custom_call_target="tpu_custom_call" | custom-call | flops 1000000 | bytes 1 | tf_op jit(solution)/shard_map/output/pallas_call | solution.py:74
  195.3 2.1 %join.1 = (bf16[512,768]{1,0:T(8,128)(2,1)}, f32[8,128]{1,0:T(8,128)}) custom-call(bf16[256,768]{1,0:T(8,128)(2,1)} %get-tuple-element.159.refs_0_, bf16[256,768]{1,0:T(8,128)(2,1)} %collective-permute-done.20.refs_1_, f32[8,128]{1,0:T(8,128)} %get-tuple-element.160.refs_2_), custom_call_target="tpu_custom_call" | custom-call | flops 40000000000 | bytes 1 | tf_op jit(solution)/shard_map/join/pallas_call | solution.py:74
  197.4 7.6 %collective-permute-done.22.refs_1_ = bf16[48,3072]{1,0:T(8,128)(2,1)S(1)} collective-permute-done((bf16[48,3072]{1,0:T(8,128)(2,1)}, bf16[48,3072]{1,0:T(8,128)(2,1)S(1)}, u32[]{:S(2)}, u32[]{:S(2)}) %collective-permute-start.22) | collective-permute-done | bytes 294944 | tf_op jit(solution)/shard_map/ppermute | solution.py:777
  205.0 0.8 slice_bitcast_fusion
  205.9 2.1 %collective-permute-done.21.refs_1_ = bf16[48,1536]{1,0:T(8,128)(2,1)S(1)} collective-permute-done((bf16[48,1536]{1,0:T(8,128)(2,1)}, bf16[48,1536]{1,0:T(8,128)(2,1)S(1)}, u32[]{:S(2)}, u32[]{:S(2)}) %collective-permute-start.21) | collective-permute-done | bytes 147488 | tf_op jit(solution)/shard_map/ppermute | solution.py:777
  (152 shorter events, 16.1 us)
Async XLA Ops:
  2.3 3.2 %copy-start.7 = (bf16[96,8,2,384]{3,1,2,0:T(8,128)(2,1)}, bf16[96,8,2,384]{3,1,2,0:T(8,128)(2,1)S(1)}, u32[]{:S(2)}) copy-start(bf16[96,8,2,384]{3,1,2,0:T(8,128)(2,1)S(1)} %copy.28) | copy-start | bytes 3538948
  2.4 8.3 %copy-start.11 = (bf16[384,768]{1,0:T(8,128)(2,1)S(1)}, bf16[384,768]{1,0:T(8,128)(2,1)}, u32[]{:S(2)}) copy-start(bf16[384,768]{1,0:T(8,128)(2,1)} %refs_8_.5) | copy-start | bytes 1769476
  5.5 22.5 %all-to-all-start = ((bf16[8,128,640]{2,1,0:T(8,128)(2,1)}), bf16[8,128,640]{2,1,0:T(8,128)(2,1)S(1)}, u32[]{:S(2)}, u32[]{:S(2)}) async-start(bf16[8,128,640]{2,1,0:T(8,128)(2,1)} %get-tuple-element.92), calls=%async_computation | async-start | bytes 2621440 | tf_op jit(solution)/shard_map/all_to_all | solution.py:822
  10.7 36.3 %copy-start.54 = (s32[512]{0:T(512)S(1)}, s32[512]{0:T(512)}, u32[]{:S(2)}) copy-start(s32[512]{0:T(512)} %param.29) | copy-start | bytes 6148
  10.8 36.3 %copy-start.51 = (f32[768]{0:T(1024)S(1)}, f32[768]{0:T(1024)}, u32[]{:S(2)}) copy-start(f32[768]{0:T(1024)} %param.22) | copy-start | bytes 9220
  10.8 36.3 %copy-start.48 = (f32[1536]{0:T(1024)S(1)}, f32[1536]{0:T(1024)}, u32[]{:S(2)}) copy-start(f32[1536]{0:T(1024)} %param.25) | copy-start | bytes 18436
  10.8 36.4 %copy-start.52 = (f32[768]{0:T(1024)S(1)}, f32[768]{0:T(1024)}, u32[]{:S(2)}) copy-start(f32[768]{0:T(1024)} %param.23) | copy-start | bytes 9220
  10.8 36.4 %copy-start.47 = (bf16[512,768]{1,0:T(8,128)(2,1)S(1)}, bf16[512,768]{1,0:T(8,128)(2,1)}, u32[]{:S(2)}) copy-start(bf16[512,768]{1,0:T(8,128)(2,1)} %param.28) | copy-start | bytes 2359300
  10.8 16.1 %collective-permute-start.1 = (bf16[384,768]{1,0:T(8,128)(2,1)S(1)}, bf16[384,768]{1,0:T(8,128)(2,1)S(1)}, u32[]{:S(2)}, u32[]{:S(2)}) collective-permute-start(bf16[384,768]{1,0:T(8,128)(2,1)S(1)} %copy-done.11), channel_id=1, source_target_pairs={{0,1},{1,0},{2,3},{3,2},{4,5},{5,4},{6,7},{7,6},{8,9},{9,8},{10,11... | collective-permute-start | bytes 1769480 | tf_op jit(solution)/shard_map/ppermute | solution.py:807
  12.4 14.6 %collective-permute-start = (s32[6,512]{1,0:T(8,128)S(1)}, s32[6,512]{1,0:T(8,128)S(1)}, u32[]{:S(2)}, u32[]{:S(2)}) collective-permute-start(s32[6,512]{1,0:T(8,128)S(1)} %copy-done.35), channel_id=1, source_target_pairs={{0,1},{1,0},{2,3},{3,2},{4,5},{5,4},{6,7},{7,6},{8,9},{9,8},{10,11... | collective-permute-start | bytes 36872 | tf_op jit(solution)/shard_map/ppermute | solution.py:806
  28.0 14.0 %copy-start.3 = (bf16[8,128,640]{2,1,0:T(8,128)(2,1)}, bf16[8,128,640]{2,1,0:T(8,128)(2,1)S(1)}, u32[]{:S(2)}) copy-start(bf16[8,128,640]{2,1,0:T(8,128)(2,1)S(1)} %all-to-all-done.refs_0_) | copy-start | bytes 3932164
  28.2 32.1 %copy-start.37 = (s32[6,512]{1,0:T(8,128)S(1)}, s32[6,512]{1,0:T(8,128)}, u32[]{:S(2)}) copy-start(s32[6,512]{1,0:T(8,128)} %copy-done.36) | copy-start | bytes 36868
  28.2 5.3 %collective-permute-start.2 = (bf16[128,256]{1,0:T(8,128)(2,1)S(1)}, bf16[128,256]{1,0:T(8,128)(2,1)S(1)}, u32[]{:S(2)}, u32[]{:S(2)}) collective-permute-start(bf16[128,256]{1,0:T(8,128)(2,1)S(1)} %query_sums.1.refs_1_), channel_id=1, source_target_pairs={{0,16},{16,0},{1,17},{17,1},{2,18},{18,2},{3,19},{19,3},{4,20},{20... | collective-permute-start | bytes 196616 | tf_op jit(solution)/shard_map/ppermute | solution.py:740
  35.3 5.2 %collective-permute-start.3 = (bf16[128,256]{1,0:T(8,128)(2,1)S(1)}, bf16[128,256]{1,0:T(8,128)(2,1)S(1)}, u32[]{:S(2)}, u32[]{:S(2)}) collective-permute-start(bf16[128,256]{1,0:T(8,128)(2,1)S(1)} %get-tuple-element.93.refs_0_), channel_id=1, source_target_pairs={{0,16},{16,0},{1,17},{17,1},{2,18},{18,2},{3,19},{19,3},{4,20},{20... | collective-permute-start | bytes 196616 | tf_op jit(solution)/shard_map/ppermute | solution.py:740
  42.1 18.2 %all-to-all-start.1 = ((bf16[16,192,128]{2,1,0:T(8,128)(2,1)}), bf16[16,192,128]{2,1,0:T(8,128)(2,1)S(1)}, u32[]{:S(2)}, u32[]{:S(2)}) async-start(bf16[16,192,128]{2,1,0:T(8,128)(2,1)} %get-tuple-element.94), calls=%async_computation.1 | async-start | bytes 1572864 | tf_op jit(solution)/shard_map/all_to_all | solution.py:842
  47.3 20.2 %copy-start.1 = (bf16[512,768]{1,0:T(8,128)(2,1)}, bf16[512,768]{1,0:T(8,128)(2,1)S(1)}, u32[]{:S(2)}) copy-start(bf16[512,768]{1,0:T(8,128)(2,1)S(1)} %broadcast_multiply_fusion.refs_7_.refs_4_.refs_6_) | copy-start | bytes 2359300
  66.9 20.0 %copy-start.18 = (f32[256,768]{1,0:T(8,128)}, f32[256,768]{1,0:T(8,128)S(1)}, u32[]{:S(2)}) copy-start(f32[256,768]{1,0:T(8,128)S(1)} %get-tuple-element.96.refs_5_.refs_1_) | copy-start | bytes 2359300
  66.9 14.3 %collective-permute-start.5 = (bf16[256,768]{1,0:T(8,128)(2,1)S(1)}, bf16[256,768]{1,0:T(8,128)(2,1)S(1)}, u32[]{:S(2)}, u32[]{:S(2)}) collective-permute-start(bf16[256,768]{1,0:T(8,128)(2,1)S(1)} %get-tuple-element.99.refs_1_), channel_id=1, source_target_pairs={{0,1},{1,0},{2,3},{3,2},{4,5},{5,4},{6,7},{7,6},{8,9},{9,8},{10,11... | collective-permute-start | bytes 1179656 | tf_op jit(solution)/shard_map/ppermute | solution.py:871
  73.0 13.8 %copy-start.20 = (f32[256,768]{1,0:T(8,128)}, f32[256,768]{1,0:T(8,128)S(1)}, u32[]{:S(2)}) copy-start(f32[256,768]{1,0:T(8,128)S(1)} %get-tuple-element.95.refs_4_.refs_0_) | copy-start | bytes 2359300
  73.0 13.8 %collective-permute-start.4 = (bf16[256,768]{1,0:T(8,128)(2,1)S(1)}, bf16[256,768]{1,0:T(8,128)(2,1)S(1)}, u32[]{:S(2)}, u32[]{:S(2)}) collective-permute-start(bf16[256,768]{1,0:T(8,128)(2,1)S(1)} %get-tuple-element.98.refs_0_), channel_id=1, source_target_pairs={{0,1},{1,0},{2,3},{3,2},{4,5},{5,4},{6,7},{7,6},{8,9},{9,8},{10,11... | collective-permute-start | bytes 1179656 | tf_op jit(solution)/shard_map/ppermute | solution.py:871
  74.5 12.3 %copy-start.2 = (bf16[512,768]{1,0:T(8,128)(2,1)S(1)}, bf16[512,768]{1,0:T(8,128)(2,1)}, u32[]{:S(2)}) copy-start(bf16[512,768]{1,0:T(8,128)(2,1)} %copy-done.1) | copy-start | bytes 2359300
  74.6 12.3 %copy-start.12 = (bf16[384,768]{1,0:T(8,128)(2,1)S(1)}, bf16[384,768]{1,0:T(8,128)(2,1)}, u32[]{:S(2)}) copy-start(bf16[384,768]{1,0:T(8,128)(2,1)} %refs_8_.5) | copy-start | bytes 1769476
  81.1 17.9 %collective-permute-start.8 = (bf16[384,3072]{1,0:T(8,128)(2,1)}, bf16[384,3072]{1,0:T(8,128)(2,1)}, u32[]{:S(2)}, u32[]{:S(2)}) collective-permute-start(bf16[384,3072]{1,0:T(8,128)(2,1)} %get-tuple-element.116), channel_id=1, source_target_pairs={{0,2},{2,0},{1,3},{3,1},{4,6},{6,4},{5,7},{7,5},{8,10},{10,8},{9,1... | collective-permute-start | bytes 7077896 | tf_op jit(solution)/shard_map/ppermute | solution.py:777
  86.8 8.0 %copy-start = (bf16[1536,768]{1,0:T(8,128)(2,1)S(1)}, bf16[1536,768]{1,0:T(8,128)(2,1)}, u32[]{:S(2)}) copy-start(bf16[1536,768]{1,0:T(8,128)(2,1)} %refs_1_.8) | copy-start | bytes 7077892
  90.6 6.9 %copy-start.9 = (bf16[256,1536]{1,0:T(8,128)(2,1)S(1)}, bf16[256,1536]{1,0:T(8,128)(2,1)}, u32[]{:S(2)}) copy-start(bf16[256,1536]{1,0:T(8,128)(2,1)} %get-tuple-element.106.refs_7_.refs_0_) | copy-start | bytes 2359300
  90.6 12.1 %all-to-all-start.2 = ((bf16[8,208,128]{2,1,0:T(8,128)(2,1)}), bf16[8,208,128]{2,1,0:T(8,128)(2,1)}, u32[]{:S(2)}, u32[]{:S(2)}) async-start(bf16[8,208,128]{2,1,0:T(8,128)(2,1)} %get-tuple-element.114), calls=%async_computation.2 | async-start | bytes 851968 | tf_op jit(solution)/shard_map/all_to_all | solution.py:888
  96.8 5.7 %copy-start.27 = (bf16[256,768]{1,0:T(8,128)(2,1)}, bf16[256,768]{1,0:T(8,128)(2,1)S(1)}, u32[]{:S(2)}) copy-start(bf16[256,768]{1,0:T(8,128)(2,1)S(1)} %get-tuple-element.109.refs_2_) | copy-start | bytes 1179652
  96.8 11.6 %collective-permute-start.6 = (bf16[256,768]{1,0:T(8,128)(2,1)S(1)}, bf16[256,768]{1,0:T(8,128)(2,1)}, u32[]{:S(2)}, u32[]{:S(2)}) collective-permute-start(bf16[256,768]{1,0:T(8,128)(2,1)S(1)} %get-tuple-element.109.refs_2_), channel_id=1, source_target_pairs={{0,1},{1,0},{2,3},{3,2},{4,5},{5,4},{6,7},{7,6},{8,9},{9,8},{10,11... | collective-permute-start | bytes 1179656 | tf_op jit(solution)/shard_map/ppermute | solution.py:898
  103.7 5.8 %collective-permute-start.9 = (bf16[208,128]{1,0:T(8,128)(2,1)S(1)}, bf16[208,128]{1,0:T(8,128)(2,1)S(1)}, u32[]{:S(2)}, u32[]{:S(2)}) collective-permute-start(bf16[208,128]{1,0:T(8,128)(2,1)S(1)} %get-tuple-element.120.refs_3_), channel_id=1, source_target_pairs={{0,16},{16,0},{1,17},{17,1},{2,18},{18,2},{3,19},{19,3},{4,20},{20... | collective-permute-start | bytes 159752 | tf_op jit(solution)/shard_map/ppermute | solution.py:740
  109.5 7.5 %copy-start.30 = (bf16[256,768]{1,0:T(8,128)(2,1)S(1)}, bf16[256,768]{1,0:T(8,128)(2,1)}, u32[]{:S(2)}) copy-start(bf16[256,768]{1,0:T(8,128)(2,1)} %copy-done.29) | copy-start | bytes 1179652
  109.5 19.8 %copy-start.39 = (f32[128,256]{1,0:T(8,128)S(1)}, f32[128,256]{1,0:T(8,128)}, u32[]{:S(2)}) copy-start(f32[128,256]{1,0:T(8,128)} %get-tuple-element.112.refs_1_.refs_0_) | copy-start | bytes 393220
  113.5 16.8 %all-to-all-start.3 = ((bf16[8,128,384]{2,1,0:T(8,128)(2,1)}), bf16[8,128,384]{2,1,0:T(8,128)(2,1)S(1)}, u32[]{:S(2)}, u32[]{:S(2)}) async-start(bf16[8,128,384]{2,1,0:T(8,128)(2,1)} %get-tuple-element.121), calls=%async_computation.3 | async-start | bytes 1572864 | tf_op jit(solution)/shard_map/all_to_all | solution.py:915
  117.0 11.5 %collective-permute-start.7 = (bf16[256,768]{1,0:T(8,128)(2,1)S(1)}, bf16[256,768]{1,0:T(8,128)(2,1)S(1)}, u32[]{:S(2)}, u32[]{:S(2)}) collective-permute-start(bf16[256,768]{1,0:T(8,128)(2,1)S(1)} %copy-done.30), channel_id=1, source_target_pairs={{0,1},{1,0},{2,3},{3,2},{4,5},{5,4},{6,7},{7,6},{8,9},{9,8},{10,11... | collective-permute-start | bytes 1179656 | tf_op jit(solution)/shard_map/ppermute | solution.py:898
  118.6 10.0 %collective-permute-start.10 = (bf16[192,128]{1,0:T(8,128)(2,1)S(1)}, bf16[192,128]{1,0:T(8,128)(2,1)S(1)}, u32[]{:S(2)}, u32[]{:S(2)}) collective-permute-start(bf16[192,128]{1,0:T(8,128)(2,1)S(1)} %get-tuple-element.123.refs_2_), channel_id=1, source_target_pairs={{0,16},{16,0},{1,17},{17,1},{2,18},{18,2},{3,19},{19,3},{4,20},{20... | collective-permute-start | bytes 147464 | tf_op jit(solution)/shard_map/ppermute | solution.py:740
  130.3 15.4 %all-to-all-start.4 = ((bf16[8,208,128]{2,1,0:T(8,128)(2,1)}), bf16[8,208,128]{2,1,0:T(8,128)(2,1)S(1)}, u32[]{:S(2)}, u32[]{:S(2)}) async-start(bf16[8,208,128]{2,1,0:T(8,128)(2,1)} %get-tuple-element.129), calls=%async_computation.4 | async-start | bytes 851968 | tf_op jit(solution)/shard_map/all_to_all | solution.py:923
  136.2 25.9 %collective-permute-start.15 = (bf16[192,1536]{1,0:T(8,128)(2,1)}, bf16[192,1536]{1,0:T(8,128)(2,1)S(1)}, u32[]{:S(2)}, u32[]{:S(2)}) collective-permute-start(bf16[192,1536]{1,0:T(8,128)(2,1)} %get-tuple-element.143), channel_id=1, source_target_pairs={{0,4},{4,0},{1,5},{5,1},{2,6},{6,2},{3,7},{7,3},{8,12},{12,8},{9,1... | collective-permute-start | bytes 1769480 | tf_op jit(solution)/shard_map/ppermute | solution.py:777
  138.3 23.9 %collective-permute-start.16 = (bf16[192,1536]{1,0:T(8,128)(2,1)}, bf16[192,1536]{1,0:T(8,128)(2,1)}, u32[]{:S(2)}, u32[]{:S(2)}) collective-permute-start(bf16[192,1536]{1,0:T(8,128)(2,1)} %get-tuple-element.144), channel_id=1, source_target_pairs={{0,8},{8,0},{1,9},{9,1},{2,10},{10,2},{3,11},{11,3},{4,12},{12,4},... | collective-permute-start | bytes 1769480 | tf_op jit(solution)/shard_map/ppermute | solution.py:777
  145.6 12.7 %collective-permute-start.11 = (bf16[384,1152]{1,0:T(8,128)(2,1)}, bf16[384,1152]{1,0:T(8,128)(2,1)S(1)}, u32[]{:S(2)}, u32[]{:S(2)}) collective-permute-start(bf16[384,1152]{1,0:T(8,128)(2,1)} %get-tuple-element.134), channel_id=1, source_target_pairs={{0,2},{2,0},{1,3},{3,1},{4,6},{6,4},{5,7},{7,5},{8,10},{10,8},{9,1... | collective-permute-start | bytes 2654216 | tf_op jit(solution)/shard_map/ppermute | solution.py:793
  147.5 9.1 %copy-start.53 = (f32[768]{0:T(1024)S(1)}, f32[768]{0:T(1024)}, u32[]{:S(2)}) copy-start(f32[768]{0:T(1024)} %param.27) | copy-start | bytes 9220
  147.5 10.8 %copy-start.17 = (bf16[384,1152]{1,0:T(8,128)(2,1)S(1)}, bf16[384,1152]{1,0:T(8,128)(2,1)}, u32[]{:S(2)}) copy-start(bf16[384,1152]{1,0:T(8,128)(2,1)} %get-tuple-element.128.refs_0_) | copy-start | bytes 2654212
  152.0 10.2 %copy-start.16 = (bf16[192,3072]{1,0:T(8,128)(2,1)S(1)}, bf16[192,3072]{1,0:T(8,128)(2,1)}, u32[]{:S(2)}) copy-start(bf16[192,3072]{1,0:T(8,128)(2,1)} %get-tuple-element.142.refs_0_) | copy-start | bytes 3538948
  152.0 14.5 %collective-permute-start.14 = (bf16[256,768]{1,0:T(8,128)(2,1)}, bf16[256,768]{1,0:T(8,128)(2,1)}, u32[]{:S(2)}, u32[]{:S(2)}) collective-permute-start(bf16[256,768]{1,0:T(8,128)(2,1)} %get-tuple-element.140), channel_id=1, source_target_pairs={{0,1},{1,0},{2,3},{3,2},{4,5},{5,4},{6,7},{7,6},{8,9},{9,8},{10,11... | collective-permute-start | bytes 1179656 | tf_op jit(solution)/shard_map/ppermute | solution.py:943
  156.3 2.0 collective-permute-start.12
  159.3 7.3 %copy-start.6 = (bf16[512,768]{1,0:T(8,128)(2,1)S(1)}, bf16[512,768]{1,0:T(8,128)(2,1)}, u32[]{:S(2)}) copy-start(bf16[512,768]{1,0:T(8,128)(2,1)} %refs_2_.3) | copy-start | bytes 2359300
  159.3 7.3 %copy-start.42 = (f32[1,768]{1,0:T(1,128)S(1)}, f32[1,768]{1,0:T(1,128)}, u32[]{:S(2)}) copy-start(f32[1,768]{1,0:T(1,128)} %copy-done.41) | copy-start | bytes 9220
  159.3 7.3 %copy-start.44 = (f32[256,768]{1,0:T(8,128)S(1)}, f32[256,768]{1,0:T(8,128)}, u32[]{:S(2)}) copy-start(f32[256,768]{1,0:T(8,128)} %get-tuple-element.141.refs_4_) | copy-start | bytes 2359300
  159.3 7.3 %copy-start.45 = (bf16[256,768]{1,0:T(8,128)(2,1)S(1)}, bf16[256,768]{1,0:T(8,128)(2,1)}, u32[]{:S(2)}) copy-start(bf16[256,768]{1,0:T(8,128)(2,1)} %get-tuple-element.139.refs_0_) | copy-start | bytes 1179652
  161.5 16.5 %collective-permute-start.13 = (bf16[192,1536]{1,0:T(8,128)(2,1)}, bf16[192,1536]{1,0:T(8,128)(2,1)}, u32[]{:S(2)}, u32[]{:S(2)}) collective-permute-start(bf16[192,1536]{1,0:T(8,128)(2,1)} %get-tuple-element.138), channel_id=1, source_target_pairs={{0,4},{4,0},{1,5},{5,1},{2,6},{6,2},{3,7},{7,3},{8,12},{12,8},{9,1... | collective-permute-start | bytes 1769480 | tf_op jit(solution)/shard_map/ppermute | solution.py:777
  164.4 18.9 %collective-permute-start.18 = (bf16[96,1536]{1,0:T(8,128)(2,1)}, bf16[96,1536]{1,0:T(8,128)(2,1)}, u32[]{:S(2)}, u32[]{:S(2)}) collective-permute-start(bf16[96,1536]{1,0:T(8,128)(2,1)} %get-tuple-element.152), channel_id=1, source_target_pairs={{0,8},{8,0},{1,9},{9,1},{2,10},{10,2},{3,11},{11,3},{4,12},{12,4},... | collective-permute-start | bytes 884744 | tf_op jit(solution)/shard_map/ppermute | solution.py:777
  164.8 19.2 %collective-permute-start.19 = (bf16[96,1536]{1,0:T(8,128)(2,1)}, bf16[96,1536]{1,0:T(8,128)(2,1)}, u32[]{:S(2)}, u32[]{:S(2)}) collective-permute-start(bf16[96,1536]{1,0:T(8,128)(2,1)} %get-tuple-element.153), channel_id=1, source_target_pairs={{0,4},{4,0},{1,5},{5,1},{2,6},{6,2},{3,7},{7,3},{8,12},{12,8},{9,1... | collective-permute-start | bytes 884744 | tf_op jit(solution)/shard_map/ppermute | solution.py:777
  166.5 11.5 %copy-start.23 = (bf16[192,1536]{1,0:T(8,128)(2,1)S(1)}, bf16[192,1536]{1,0:T(8,128)(2,1)}, u32[]{:S(2)}) copy-start(bf16[192,1536]{1,0:T(8,128)(2,1)} %get-tuple-element.137.refs_0_) | copy-start | bytes 1769476
  166.6 17.4 %copy-start.22 = (bf16[96,3072]{1,0:T(8,128)(2,1)S(1)}, bf16[96,3072]{1,0:T(8,128)(2,1)}, u32[]{:S(2)}) copy-start(bf16[96,3072]{1,0:T(8,128)(2,1)} %get-tuple-element.151.refs_0_) | copy-start | bytes 1769476
  169.7 22.4 %copy-start.15 = (bf16[256,768]{1,0:T(8,128)(2,1)S(1)}, bf16[256,768]{1,0:T(8,128)(2,1)}, u32[]{:S(2)}) copy-start(bf16[256,768]{1,0:T(8,128)(2,1)} %copy-done.14) | copy-start | bytes 1179652
  169.7 22.4 %copy-start.19 = (f32[256,768]{1,0:T(8,128)S(1)}, f32[256,768]{1,0:T(8,128)}, u32[]{:S(2)}) copy-start(f32[256,768]{1,0:T(8,128)} %copy-done.18) | copy-start | bytes 2359300
  169.7 22.4 %copy-start.21 = (f32[256,768]{1,0:T(8,128)S(1)}, f32[256,768]{1,0:T(8,128)}, u32[]{:S(2)}) copy-start(f32[256,768]{1,0:T(8,128)} %copy-done.20) | copy-start | bytes 2359300
  169.7 22.4 %copy-start.28 = (bf16[256,768]{1,0:T(8,128)(2,1)S(1)}, bf16[256,768]{1,0:T(8,128)(2,1)}, u32[]{:S(2)}) copy-start(bf16[256,768]{1,0:T(8,128)(2,1)} %copy-done.27) | copy-start | bytes 1179652
  169.7 22.4 %copy-start.43 = (f32[1,768]{1,0:T(1,128)S(1)}, f32[1,768]{1,0:T(1,128)}, u32[]{:S(2)}) copy-start(f32[1,768]{1,0:T(1,128)} %reshape.66.refs_6_) | copy-start | bytes 9220
  169.7 25.6 %collective-permute-start.20 = (bf16[256,768]{1,0:T(8,128)(2,1)}, bf16[256,768]{1,0:T(8,128)(2,1)}, u32[]{:S(2)}, u32[]{:S(2)}) collective-permute-start(bf16[256,768]{1,0:T(8,128)(2,1)} %get-tuple-element.159.refs_0_), channel_id=1, source_target_pairs={{0,1},{1,0},{2,3},{3,2},{4,5},{5,4},{6,7},{7,6},{8,9},{9,8},{10,11... | collective-permute-start | bytes 1179656 | tf_op jit(solution)/shard_map/ppermute | solution.py:952
  170.9 16.3 %all-to-all-start.5 = ((f32[32,2,48]{2,1,0:T(2,128)}), f32[32,2,48]{2,1,0:T(2,128)}, u32[]{:S(2)}, u32[]{:S(2)}) async-start(f32[32,2,48]{2,1,0:T(2,128)} %copy-done.40), calls=%async_computation.5 | async-start | bytes 65536 | tf_op jit(solution)/shard_map/all_to_all | solution.py:955
  180.1 8.5 %collective-permute-start.17 = (bf16[96,1536]{1,0:T(8,128)(2,1)}, bf16[96,1536]{1,0:T(8,128)(2,1)S(1)}, u32[]{:S(2)}, u32[]{:S(2)}) collective-permute-start(bf16[96,1536]{1,0:T(8,128)(2,1)} %get-tuple-element.149), channel_id=1, source_target_pairs={{0,8},{8,0},{1,9},{9,1},{2,10},{10,2},{3,11},{11,3},{4,12},{12,4},... | collective-permute-start | bytes 884744 | tf_op jit(solution)/shard_map/ppermute | solution.py:777
  186.0 19.0 %collective-permute-start.22 = (bf16[48,3072]{1,0:T(8,128)(2,1)}, bf16[48,3072]{1,0:T(8,128)(2,1)S(1)}, u32[]{:S(2)}, u32[]{:S(2)}) collective-permute-start(bf16[48,3072]{1,0:T(8,128)(2,1)} %get-tuple-element.166), channel_id=1, source_target_pairs={{0,16},{16,0},{1,17},{17,1},{2,18},{18,2},{3,19},{19,3},{4,20},{20... | collective-permute-start | bytes 884744 | tf_op jit(solution)/shard_map/ppermute | solution.py:777
  190.3 17.7 %collective-permute-start.21 = (bf16[48,1536]{1,0:T(8,128)(2,1)}, bf16[48,1536]{1,0:T(8,128)(2,1)S(1)}, u32[]{:S(2)}, u32[]{:S(2)}) collective-permute-start(bf16[48,1536]{1,0:T(8,128)(2,1)} %get-tuple-element.164), channel_id=1, source_target_pairs={{0,16},{16,0},{1,17},{17,1},{2,18},{18,2},{3,19},{19,3},{4,20},{20... | collective-permute-start | bytes 442376 | tf_op jit(solution)/shard_map/ppermute | solution.py:777
  195.3 9.7 %copy-start.33 = (bf16[48,3072]{1,0:T(8,128)(2,1)S(1)}, bf16[48,3072]{1,0:T(8,128)(2,1)}, u32[]{:S(2)}) copy-start(bf16[48,3072]{1,0:T(8,128)(2,1)} %get-tuple-element.165.refs_0_) | copy-start | bytes 884740
  195.3 12.8 %copy-start.38 = (bf16[48,1536]{1,0:T(8,128)(2,1)S(1)}, bf16[48,1536]{1,0:T(8,128)(2,1)}, u32[]{:S(2)}) copy-start(bf16[48,1536]{1,0:T(8,128)(2,1)} %get-tuple-element.163.refs_0_) | copy-start | bytes 442372
  (20 other events, 26.0 us)

commit v4 on v3

--- a/solution.py
+++ b/solution.py
@@ -97,6 +97,10 @@
     return copy
 
 
+def row(ref):
+    return ref[...][None, :]
+
+
 def left_half(shape):
     return lax.broadcasted_iota(jnp.int32, shape, 1) < HD
 
@@ -169,7 +173,7 @@
     for s in range(SEQS):
         rows = slice(s * C, (s + 1) * C)
         unit, unused = normalise(x_ref[rows, :].astype(F32))
-        normed_ref[rows, :] = (unit * gain_ref[...] + shift_ref[...]).astype(BF16)
+        normed_ref[rows, :] = (unit * row(gain_ref) + row(shift_ref)).astype(BF16)
     copies.append(send(normed_ref, normed_out, sems.at[0]))
     width = wq_ref.shape[1]
     q_scr[...] = dot_nn(normed_ref[...], wq_ref[...])
@@ -351,11 +355,11 @@
     residual = x_ref[...].astype(F32) + dot_nn(a_scr[...], w_ref[...])
     residual_ref[...] = residual
     unit, unused = normalise(residual)
-    normed = (unit * gain_ref[...] + shift_ref[...]).astype(BF16)
+    normed = (unit * row(gain_ref) + row(shift_ref)).astype(BF16)
     normed_ref[...] = normed
     copies.append(send(normed_ref, normed_out, out_sems.at[1]))
     up_copy.wait()
-    hidden = dot_nn(normed, up_ref[...]) + up_bias_ref[...]
+    hidden = dot_nn(normed, up_ref[...]) + row(up_bias_ref)
     below = 0.5 * (1.0 + lax.erf(hidden * (0.5**0.5)))
     active_ref[...] = (hidden * below).astype(BF16)
     copies.append(send(active_ref, active_out, out_sems.at[2]))
@@ -374,15 +378,20 @@
     branch_ref[...] = dot_nn(active_ref[...], down_ref[...]).astype(BF16)
 
 
-def output_kernel(
-    one_ref, two_ref, branch_one_ref, branch_two_ref, other_one_ref, other_two_ref, bias_ref, out_ref
-):
-    half = one_ref.shape[0]
-    for i, (r, mine, theirs) in enumerate(
-        ((one_ref, branch_one_ref, other_one_ref), (two_ref, branch_two_ref, other_two_ref))
-    ):
+def output_kernel(*refs):
+    sources, bias_ref, out, held, total_ref, sems, out_sems = refs[:6], refs[6], refs[7], refs[8:14], refs[14], refs[15], refs[16]
+    half = total_ref.shape[1]
+    copies = [send(v, t, sems.at[i]) for i, (v, t) in enumerate(zip(sources, held))]
+    sent = []
+    for i in range(2):
+        for copy in copies[3 * i : 3 * i + 3]:
+            copy.wait()
+        first, mine, theirs = held[3 * i : 3 * i + 3]
         total = mine[...].astype(F32) + theirs[...].astype(F32)
-        out_ref[i * half : (i + 1) * half, :] = (r[...] + (total + bias_ref[...])).astype(BF16)
+        total_ref[i] = (first[...] + (total + row(bias_ref))).astype(BF16)
+        sent.append(send(total_ref.at[i], out.at[i * half : (i + 1) * half, :], out_sems.at[i]))
+    for copy in sent:
+        copy.wait()
 
 
 def turn_kernel(
@@ -391,9 +400,9 @@
     residual_grad_out, mixed_out, send_out, ag_scr, vec_scr, residual_grad_ref, mixed_ref, send_ref, sems,
 ):
     me = lax.axis_index("mp")
-    gain_sum = jnp.zeros(gain_ref.shape, F32)
-    shift_sum = jnp.zeros(gain_ref.shape, F32)
-    down_sum = jnp.zeros(gain_ref.shape, F32)
+    gain_sum = jnp.zeros((1, gain_ref.shape[0]), F32)
+    shift_sum = jnp.zeros((1, gain_ref.shape[0]), F32)
+    down_sum = jnp.zeros((1, gain_ref.shape[0]), F32)
     halves = (
         (back_one_ref, other_one_ref, residual_one_ref), (back_two_ref, other_two_ref, residual_two_ref)
     )
@@ -407,7 +416,7 @@
         gain_sum = gain_sum + jnp.sum(grad * unit, axis=0, keepdims=True)
         shift_sum = shift_sum + jnp.sum(grad, axis=0, keepdims=True)
         down_sum = down_sum + jnp.sum(out_grad, axis=0, keepdims=True)
-        residual_grad = out_grad + norm_pull(unit, inverse, grad * gain_ref[...])
+        residual_grad = out_grad + norm_pull(unit, inverse, grad * row(gain_ref))
 
         @pl.when(me == s // 2)
         def keep_own():
@@ -551,6 +560,23 @@
             grads_ref[rows, base + 2 * C : base + 3 * C] = blocks[1][:, first : first + C]
 
 
+def kv_kernel(order, recv_ref, normed_src, kv_out, keep_out, give_out, kv_ref, normed_ref, scr, sems, out_sems):
+    copy = send(normed_src, normed_ref, sems.at[0])
+    gather_kernel(recv_ref, kv_ref)
+    kv_copy = send(kv_ref, kv_out, sems.at[1])
+    copy.wait()
+    scr[...] = dot_tn(normed_ref[...], kv_ref[...]).astype(BF16)
+    own = scr.shape[0] // 16
+    me = lax.axis_index("b0")
+    sent = [kv_copy]
+    for bit, out in ((1 - me, give_out), (me, keep_out)):
+        for j, place in enumerate(row_order(order)):
+            start = pl.multiple_of((place + bit) * own, 16)
+            sent.append(send(scr.at[pl.ds(start, own), :], out.at[j * own : (j + 1) * own, :], out_sems.at[len(sent) - 1]))
+    for copy in sent:
+        copy.wait()
+
+
 def first_back_kernel(
     recv_ref, ids_ref, wq_src, wkv_src, kv_src, grads_out, keep_out, give_out,
     scr, wq_ref, wkv_ref, kv_ref, grads_ref, in_sems, out_sems,
@@ -595,7 +621,7 @@
         unit, inverse = normalise(x)
         gain_sum = gain_sum + jnp.sum(grad * unit, axis=0, keepdims=True)
         shift_sum = shift_sum + jnp.sum(grad, axis=0, keepdims=True)
-        made = norm_pull(unit, inverse, grad * gain_ref[...])
+        made = norm_pull(unit, inverse, grad * row(gain_ref))
         input_grad_ref[rows, :] = (residual_grad_ref[rows, :] + made).astype(BF16)
     both = jnp.concatenate([gain_sum, shift_sum], axis=0)
     own = vec_ref.shape[2]
@@ -603,11 +629,15 @@
         vec_ref[r] = both[:, (r // 2) * own : (r // 2 + 1) * own]
 
 
-def join_kernel(own_ref, got_ref, out_ref):
+def join_kernel(own_ref, got_ref, out_ref, sems):
     half = own_ref.shape[0]
     me = lax.axis_index("mp")
-    out_ref[pl.ds(pl.multiple_of(me * half, C), half), :] = own_ref[...]
-    out_ref[pl.ds(pl.multiple_of((1 - me) * half, C), half), :] = got_ref[...]
+    copies = [
+        send(v, out_ref.at[pl.ds(pl.multiple_of(bit * half, C), half), :], sems.at[i])
+        for i, (v, bit) in enumerate(((own_ref, me), (got_ref, 1 - me)))
+    ]
+    for copy in copies:
+        copy.wait()
 
 
 def weight_kernel(orders, counts, *refs):
@@ -633,12 +663,16 @@
             made = dot_tn(held[spot + 2 * i][...], held[spot + 2 * i + 1][...])
             total = made if total is None else total + made
         scr[:, lanes] = total.astype(BF16)
-        for bit, out in ((1 - me, give_out), (me, keep_out)):
-            for j, place in enumerate(row_order(order)):
-                start = pl.multiple_of((place + bit) * own, 16)
-                sent.append(send(
-                    scr.at[pl.ds(start, own), lanes], out.at[j * own : (j + 1) * own, lanes], out_sems.at[len(sent)]
-                ))
+        spread = base
+        for wide, places in order:
+            part = slice(spread, spread + wide)
+            for bit, out in ((1 - me, give_out), (me, keep_out)):
+                for j, place in enumerate(row_order(places)):
+                    start = pl.multiple_of((place + bit) * own, 16)
+                    sent.append(send(
+                        scr.at[pl.ds(start, own), part], out.at[j * own : (j + 1) * own, part], out_sems.at[len(sent)]
+                    ))
+            spread += wide
         base += width
         spot += 2 * count
     for copy in sent:
@@ -652,23 +686,24 @@
         i -= 2 * count
 
 
-def fold_kernel(axes, came, *refs):
+def fold_kernel(axes, came, widths, *refs):
     keep_ref, gots, keep_out, gives = refs[0], refs[1 : 1 + came], refs[1 + came], refs[2 + came : -3]
     keep_scr, give_scr, sems = refs[-3:]
-    half, columns = keep_scr.shape
-    sides = max(came, len(axes))
-    width = columns // sides
-    for i in range(sides):
-        lanes = slice(i * width, (i + 1) * width)
-        got, inner = (gots[i], slice(0, width)) if came == sides else (gots[0], lanes)
-        me = lax.axis_index(axes[i] if len(axes) == sides else axes[0])
+    half = keep_scr.shape[0]
+    ranges = []
+    base = 0
+    for i, width in enumerate(widths):
+        lanes = slice(base, base + width)
+        ranges.append(lanes)
+        base += width
+        got, inner = (gots[i], slice(0, width)) if came == len(widths) else (gots[0], lanes)
+        me = lax.axis_index(axes[i])
         for bit, out in ((1 - me, give_scr), (me, keep_scr)):
             rows = pl.ds(pl.multiple_of(bit * half, 16), half)
             out[:, lanes] = (keep_ref[rows, lanes].astype(F32) + got[rows, inner].astype(F32)).astype(BF16)
     copies = [send(keep_scr, keep_out, sems.at[0])]
-    wide = columns // len(gives)
-    for i, give in enumerate(gives):
-        copies.append(send(give_scr.at[:, i * wide : (i + 1) * wide], give, sems.at[1 + i]))
+    for i, (lanes, give) in enumerate(zip(ranges, gives)):
+        copies.append(send(give_scr.at[:, lanes], give, sems.at[1 + i]))
     for copy in copies:
         copy.wait()
 
@@ -689,12 +724,31 @@
         copy.wait()
 
 
-def vector_kernel(recv_ref, out_ref):
+def vector_kernel(recv_ref, five_ref, out_ref, small_ref):
     out_ref[...] = jnp.sum(recv_ref[...], axis=0)
-
-
-def close_kernel(keep_ref, got_ref, out_ref):
-    out_ref[...] = keep_ref[...].astype(F32) + got_ref[...].astype(F32)
+    for o in range(SUB):
+        block = five_ref[o, C + HD : PACK, :].astype(F32)
+        small_ref[4 * o : 4 * o + 4, :] = block[0:4] + block[4:8]
+
+
+def close_kernel(keep_ref, *refs):
+    outs = [r for r in refs if r.dtype == F32]
+    pieces = []
+    base = 0
+    for got in refs[: len(refs) - len(outs)]:
+        lanes = slice(base, base + got.shape[1])
+        pieces.append(keep_ref[:, lanes].astype(F32) + got[...].astype(F32))
+        base += got.shape[1]
+    total = jnp.concatenate(pieces, axis=1) if len(pieces) > 1 else pieces[0]
+    base = 0
+    for out in outs:
+        if len(out.shape) == 2:
+            out[...] = total[:, base : base + out.shape[1]]
+            base += out.shape[1]
+            continue
+        for i in range(out.shape[1]):
+            out[:, i, :] = total[:, base : base + out.shape[2]]
+            base += out.shape[2]
 
 
 def plain_weight_kernel(counts, *refs):
@@ -731,7 +785,6 @@
     half = tokens // 2
     own = model // devices
     other = functools.partial(lax.ppermute, axis_name="mp", perm=SWAP)
-    row = lambda v: v.reshape(1, -1)
 
     def across(v):
         if groups == 1:
@@ -762,25 +815,35 @@
             name=name, after=after, token=True,
             scratch=[pltpu.VMEM((model, columns), BF16)]
             + [pltpu.VMEM((r, v.shape[1]), BF16) for r, v in zip(rows, flat)]
-            + [pltpu.SemaphoreType.DMA((len(flat),)), pltpu.SemaphoreType.DMA((16 * len(counts),))],
+            + [pltpu.SemaphoreType.DMA((len(flat),)), pltpu.SemaphoreType.DMA((16 * sum(map(len, orders)),))],
             specs=([UNREAD] * len(flat), [UNREAD] * 2),
         )
         return (keep, [give]), token
 
-    def fold(axes, parts, terms, name, after=()):
+    def fold(axes, parts, terms, name, after=(), widths=None):
         if simple:
             if not parts:
                 summed = [lax.psum_scatter(v, SEQ, scatter_dimension=0, tiled=True) for v in terms]
-                return jnp.concatenate(summed, axis=1), None
+                summed = jnp.concatenate(summed, axis=1)
+                pieces = []
+                for w in widths:
+                    size = functools.reduce(lambda p, q: p * q, w)
+                    pieces.append(summed[:, :size].reshape((own,) + w))
+                    summed = summed[:, size:]
+                return pieces, None
             return terms, None
         keep, gives = terms
         gots = [lax.ppermute(give, axis, SWAP) for give, axis in zip(gives, axes)]
         rows, columns = keep.shape
         if not parts:
-            return call(close_kernel, [(keep.shape, F32)], keep, *gots, name=name, after=after, token=True)
-        outs = [((rows // 2, columns), BF16)] + [((rows // 2, columns // len(parts)), BF16)] * len(parts)
+            *pieces, token = call(
+                close_kernel, [((rows,) + w, F32) for w in widths], keep, *gots, name=name, after=after, token=True
+            )
+            return pieces, token
+        widths = widths or [columns]
+        outs = [((rows // 2, w), BF16) for w in [columns] + widths]
         keep, *gives, token = call(
-            functools.partial(fold_kernel, parts, len(gots)), outs, keep, *gots, name=name, after=after, token=True,
+            functools.partial(fold_kernel, parts, len(gots), widths), outs, keep, *gots, name=name, after=after, token=True,
             scratch=[pltpu.VMEM((rows // 2, columns), BF16)] * 2 + [pltpu.SemaphoreType.DMA((len(outs),))],
             specs=([WHOLE] * (1 + len(gots)), [UNREAD] * len(outs)),
         )
@@ -811,7 +874,7 @@
     normed_one, send_one = call(
         project_kernel,
         [((tokens, model), BF16), ((SUB, C, 5 * C), BF16)],
-        inputs, row(norm_one_gain), row(norm_one_shift), query_weight, wkv, cluster_ids,
+        inputs, norm_one_gain, norm_one_shift, query_weight, wkv, cluster_ids,
         scratch=[
             pltpu.VMEM((tokens, width), F32), pltpu.VMEM((tokens, 2 * width), BF16),
             pltpu.VMEM((tokens, model), BF16), pltpu.VMEM((SUB, C, 5 * C), BF16), pltpu.SemaphoreType.DMA((5,)),
@@ -850,7 +913,7 @@
                 ((1, hidden), F32), ((half, model), F32), ((half, model), BF16), ((half, width), BF16),
                 ((half, model), BF16), ((half, hidden), BF16), ((half, hidden), BF16),
             ],
-            recv_two, cluster_ids, ids_other, inputs, row(norm_two_gain), row(norm_two_shift), row(up_bias), bg,
+            recv_two, cluster_ids, ids_other, inputs, norm_two_gain, norm_two_shift, up_bias, bg,
             out_weight, wo_other, up_weight, down_weight,
             scratch=[
                 pltpu.VMEM((half, 2 * width), BF16), pltpu.VMEM((2 * width, model), BF16),
@@ -870,13 +933,15 @@
     bias_part, residual, back, attended, normed_two, active, hidden_grad = zip(*halves)
     back_other = [other(v) for v in back]
     order = ("b1", "b2", "g")
+    ff_widths = [hidden + hidden // 3, hidden - hidden // 3]
     ff_terms, ff_token = weight_terms(
-        (order, ("b2", "b1", "g")), "ff_terms", list(zip(normed_two, hidden_grad)), [(bg, v) for v in active]
+        ([(hidden, order)], [(hidden // 3, order), (hidden - hidden // 3, ("g", "b1", "b2"))]), "ff_terms",
+        list(zip(normed_two, hidden_grad)), [(bg, v) for v in active],
     )
     residual_grad, mixed_grad, send_three, turned = call(
         turn_kernel,
         [((half, model), F32), ((tokens, model), BF16), ((SUB, PACK, C), BF16)],
-        *back, *back_other, *residual, row(norm_two_gain), bg, out_weight, cluster_ids, *bias_part,
+        *back, *back_other, *residual, norm_two_gain, bg, out_weight, cluster_ids, *bias_part,
         scratch=[
             pltpu.VMEM((tokens, width), F32), pltpu.VMEM((32, C), F32), pltpu.VMEM((half, model), F32),
             pltpu.VMEM((tokens, model), BF16), pltpu.VMEM((SUB, PACK, C), BF16), pltpu.SemaphoreType.DMA((6,)),
@@ -893,7 +958,9 @@
         )
         for v in active
     ]
-    ff_terms, ff_token = fold(("b0",), ("b1", "b2"), ff_terms, "ff_fold", after=[b[1] for b in branches])
+    ff_terms, ff_token = fold(
+        ("b0",), ("b1", "g"), ff_terms, "ff_fold", after=[b[1] for b in branches], widths=ff_widths
+    )
     branch = [b[0] for b in branches]
     branch_other = [other(b) for b in branch]
     grad_sums, summed = call(
@@ -914,18 +981,37 @@
     )
     recv_four = lax.all_to_all(send_four, NEAR, 0, 0)
     cgrads = across(cgrad)
+    out_terms, out_token = weight_terms(
+        ([(width, order)],), "out_terms", [(mixed_grad, v) for v in attended], after=[attended_back]
+    )
     send_five, finished = call(
         finish_back_kernel, [((SUB, PACK, C), BF16)], total, vec, *cgrads, name="finish_back",
-        after=[branch_other[1]], token=True,
+        after=[out_token, branch_other[1]], token=True,
         scratch=[pltpu.VMEM((PACK, C), BF16), pltpu.SemaphoreType.DMA((SUB,))],
         specs=([WHOLE] * (2 + len(cgrads)), [UNREAD]),
     )
     recv_five = lax.all_to_all(send_five, NEAR, 0, 0)
-    (kv_grads,) = call(
-        gather_kernel, [((tokens, 2 * width), BF16)], recv_four, name="gather", after=[finished],
-    )
-    kv_terms, kv_token = weight_terms(
-        (order, order), "kv_terms", [(normed_one, kv_grads)], [(mixed_grad, v) for v in attended]
+    if simple:
+        (kv_grads,) = call(gather_kernel, [((tokens, 2 * width), BF16)], recv_four, name="gather")
+        kv_terms, kv_token = weight_terms(None, "kv_terms", [(normed_one, kv_grads)])
+    else:
+        kv_grads, kv_keep, kv_give, kv_token = call(
+            functools.partial(kv_kernel, order),
+            [((tokens, 2 * width), BF16)] + [((model // 2, 2 * width), BF16)] * 2, recv_four, normed_one,
+            name="kv_terms", after=[finished], token=True,
+            scratch=[
+                pltpu.VMEM((tokens, 2 * width), BF16), pltpu.VMEM((tokens, model), BF16),
+                pltpu.VMEM((model, 2 * width), BF16), pltpu.SemaphoreType.DMA((2,)), pltpu.SemaphoreType.DMA((16,)),
+            ],
+            specs=([WHOLE, UNREAD], [UNREAD] * 3),
+        )
+        kv_terms = (kv_keep, [kv_give])
+    pieces = [v for three in zip(residual, branch, branch_other) for v in three]
+    block_output, output_token = call(
+        output_kernel, [((tokens, model), BF16)], *pieces, down_bias, name="output", after=tokens_of(kv_token), token=True,
+        scratch=[pltpu.VMEM(v.shape, v.dtype) for v in pieces]
+        + [pltpu.VMEM((2, half, model), BF16), pltpu.SemaphoreType.DMA((6,)), pltpu.SemaphoreType.DMA((2,))],
+        specs=([UNREAD] * 6 + [WHOLE], [UNREAD]),
     )
     q_grads, keep, give, first_token = call(
         first_back_kernel,
@@ -938,38 +1024,41 @@
         ],
         specs=([WHOLE] * 2 + [UNREAD] * 3, [UNREAD] * 3),
         flops=2 * tokens * model * 3 * width, name="first_back",
-        after=tokens_of(kv_token), token=True,
+        after=tokens_of(kv_token, output_token), token=True,
     )
     got = other(give)
-    q_terms, q_token = weight_terms((order,), "q_terms", [(normed_one, q_grads)], after=[first_token])
-    kv_terms, kv_token = fold_many(("b0",), "b1", (kv_terms, q_terms), "kv_fold", after=[q_token])
-    ff_terms, ff_token = fold(("b1", "b2"), ("b2", "b1"), ff_terms, "ff_fold", after=tokens_of(q_token, kv_token))
+    q_terms, q_token = weight_terms(([(width, order)],), "q_terms", [(normed_one, q_grads)], after=[first_token])
+    kv_terms, kv_token = fold_many(("b0",), "b1", (kv_terms, out_terms, q_terms), "kv_fold", after=[q_token])
+    ff_terms, ff_token = fold(("b1", "g"), ("b2", "b1"), ff_terms, "ff_fold", after=tokens_of(kv_token, q_token), widths=ff_widths)
     grad_half, vec_one, last_token = call(
         last_kernel, [((half, model), BF16), ((2 * devices, 2, own), F32)],
-        keep, got, inputs, row(norm_one_gain), residual_grad, name="last",
-        after=tokens_of(ff_token), token=True,
+        keep, got, inputs, norm_one_gain, residual_grad, name="last",
+        after=tokens_of(kv_token, ff_token), token=True,
     )
     grad_other = other(grad_half)
     kv_terms, kv_token = fold(("b1",), ("b2",), kv_terms, "kv_fold", after=[last_token])
-    ff_terms, ff_token = fold(("b2", "b1"), ("g",), ff_terms, "ff_fold", after=tokens_of(kv_token))
+    ff_terms, ff_token = fold(
+        ("b2", "b1"), ("g", "b2"), ff_terms, "ff_fold", after=tokens_of(kv_token), widths=ff_widths
+    )
     vec_recv = lax.all_to_all(vec_one, SEQ + ("mp",), 0, 0, tiled=True)
-    vec_sum, vec_token = call(
-        vector_kernel, [((2, own), F32)], vec_recv, name="vectors", after=tokens_of(ff_token), token=True
+    vec_sum, small, vec_token = call(
+        vector_kernel, [((2, own), F32), ((4 * SUB, C), F32)], vec_recv, recv_five, name="vectors",
+        after=tokens_of(ff_token), token=True,
     )
     kv_terms, kv_token = fold(("b2",), ("g",), kv_terms, "kv_fold", after=[vec_token])
-    block_output, output_token = call(
-        output_kernel, [((tokens, model), BF16)], *residual, *branch, *branch_other, row(down_bias),
-        name="output", after=tokens_of(kv_token, vec_token), token=True,
-    )
     input_grad, join_token = call(
         join_kernel, [((tokens, model), BF16)], grad_half, grad_other, name="join",
-        after=[output_token], token=True,
-    )
-    ff_sum, ff_token = fold(("g",), (), ff_terms, "ff_close", after=[join_token])
-    kv_sum, kv_token = fold(("g",), (), kv_terms, "kv_close", after=tokens_of(ff_token))
-
-    small = recv_five[:, C + HD : C + HD + 8, :].astype(F32)
-    small = (small[:, 0:4] + small[:, 4:8]).reshape(-1)
+        after=tokens_of(kv_token, vec_token), token=True, scratch=[pltpu.SemaphoreType.DMA((2,))],
+        specs=([WHOLE] * 2, [UNREAD]),
+    )
+    (up_sum, down_sum), ff_token = fold(
+        ("g", "b2"), (), ff_terms, "ff_close", after=[join_token], widths=[(hidden,), (hidden,)]
+    )
+    (kv_sum, out_sum, q_sum), kv_token = fold(
+        ("g",), (), kv_terms, "kv_close", after=tokens_of(ff_token), widths=[(2, width), (width,), (width,)]
+    )
+
+    small = small.reshape(-1)
     start = lax.axis_index(SEQ) * own
     take = lambda base: lax.dynamic_slice(small, (base + start,), (own,))
     return (
@@ -977,14 +1066,14 @@
         input_grad,
         vec_sum[0],
         vec_sum[1],
-        kv_sum[:, 3 * width :],
-        kv_sum[:, 0 : 2 * width].reshape(own, 2, width),
-        kv_sum[:, 2 * width : 3 * width].T,
+        q_sum,
+        kv_sum,
+        out_sum.T,
         take(hidden),
         take(hidden + model),
-        ff_sum[:, 0:hidden],
+        up_sum,
         small[0:hidden],
-        ff_sum[:, hidden:].T,
+        down_sum.T,
         take(hidden + 2 * model),
     )
 

time: 211 us -> 201 us (0.953)
  local copies, waits for them, and re-layouts: 17.8 us -> 9.14 us
  waiting for transfers between devices: 62.9 us -> 67.3 us
  Pallas kernels: 67.8 us -> 64.6 us
    ppermute x9 -> x10, waiting for transfers between devices: 14 us -> 18.3 us  [fold(): gots = [lax.ppermute(give, axis, SWAP) for give, axis in zip(gives, axes)]]
    unnamed x111 -> x89, local copies, waits for them, and re-layouts: 11.7 us -> 7.43 us
    pallas_call x29, Pallas kernels: 67.8 us -> 64.6 us  [call(): pl.pallas_call(body, out_shape=[pltpu.HBM(s, d) if spec is UNREAD else ja...]
    ppermute x2, waiting for transfers between devices: 8.21 us -> 5.95 us  [on_device(): branch_other = [other(b) for b in branch]]
    ppermute x9 -> x10, starting transfers between devices: 9.95 us -> 8.21 us  [fold(): gots = [lax.ppermute(give, axis, SWAP) for give, axis in zip(gives, axes)]]
  transfers between devices with their start and end apart: 29 -> 31, of which waited for: 15 -> 17; matrix products, arithmetic and copies ran while one was open for 3% -> 1% of each run, Pallas kernels for 25% -> 24%
where the time goes in v4:
time: 201 us; the launch traced here: 200 us
  waiting for transfers between devices  67.3 us (33%)
  Pallas kernels  64.6 us (32%)
  starting transfers between devices  56.6 us (28%)
  local copies, waits for them, and re-layouts  9.14 us (5%)
    pallas_call x29, Pallas kernels, call(): pl.pallas_call(body, out_shape=[pltpu.HBM(s, d) if spec is UNREAD else ja...  64.6 us
    ppermute x10, waiting for transfers between devices, fold(): gots = [lax.ppermute(give, axis, SWAP) for give, axis in zip(gives, axes)]  18.3 us
    ppermute x1, waiting for transfers between devices, on_device(): ids_other = other(cluster_ids)  14 us
    all_to_all x1, waiting for transfers between devices, on_device(): recv_two = lax.all_to_all(send_two, NEAR + ('mp',), 0, 0)  11.9 us
    ppermute x4, starting transfers between devices, across(): return [v, lax.ppermute(v, 'g', SWAP)]  11.7 us
    ppermute x10, starting transfers between devices, fold(): gots = [lax.ppermute(give, axis, SWAP) for give, axis in zip(gives, axes)]  8.21 us
    unnamed x89, local copies, waits for them, and re-layouts  7.43 us
    ppermute x4, waiting for transfers between devices, across(): return [v, lax.ppermute(v, 'g', SWAP)]  6.99 us
  transfers between devices with their start and end apart: 31, of which 17 were waited for; matrix products, arithmetic and copies ran while one was open for 1% of the time, Pallas kernels for 24%

profile of v4, /device:TPU:0, one launch (start us, length us, event | category | flops | bytes accessed | tf_op | source)
XLA Modules:
  0.0 200.2 jit_solution(16520977742948471153)
XLA Ops:
  0.7 1.6 copy.28
  2.4 3.1 %project.1 = (bf16[512,768]{1,0:T(8,128)(2,1)}, bf16[8,128,640]{2,1,0:T(8,128)(2,1)}) custom-call(bf16[512,768]{1,0:T(8,128)(2,1)S(1)} %copy-done.4, f32[768]{0:T(1024)S(1)} %copy-done.37, f32[768]{0:T(1024)S(1)} %copy-done.35, bf16[768,384]{1,0:T(8,128)(2,1)S(1)} %copy-done.16, bf16[768,768]{1,0:T(8,128)(2,1)S(1)} %bitcast.11, s32[6,512]{1,0:T(8,128)S(1)} %copy-done.27), custom_call_target="tpu_custom_call" | custom-call | flops 1000000 | bytes 1 | tf_op jit(solution)/shard_map/project/pallas_call | solution.py:74
  5.4 5.2 %all-to-all-start = ((bf16[8,128,640]{2,1,0:T(8,128)(2,1)}), bf16[8,128,640]{2,1,0:T(8,128)(2,1)S(1)}, u32[]{:S(2)}, u32[]{:S(2)}) async-start(bf16[8,128,640]{2,1,0:T(8,128)(2,1)} %get-tuple-element.102), calls=%async_computation | async-start | bytes 2621440 | tf_op jit(solution)/shard_map/all_to_all | solution.py:885
  10.7 1.6 collective-permute-start.1
  12.8 14.0 %collective-permute-done.refs_1_.refs_2_ = s32[6,512]{1,0:T(8,128)S(1)} collective-permute-done((s32[6,512]{1,0:T(8,128)S(1)}, s32[6,512]{1,0:T(8,128)S(1)}, u32[]{:S(2)}, u32[]{:S(2)}) %collective-permute-start) | collective-permute-done | bytes 12320 | tf_op jit(solution)/shard_map/ppermute | solution.py:869
  26.8 1.1 all-to-all-done.refs_0_
  28.1 2.7 %collective-permute-start.2 = (bf16[128,256]{1,0:T(8,128)(2,1)S(1)}, bf16[128,256]{1,0:T(8,128)(2,1)S(1)}, u32[]{:S(2)}, u32[]{:S(2)}) collective-permute-start(bf16[128,256]{1,0:T(8,128)(2,1)S(1)} %query_sums.1.refs_1_), channel_id=1, source_target_pairs={{0,16},{16,0},{1,17},{17,1},{2,18},{18,2},{3,19},{19,3},{4,20},{20... | collective-permute-start | bytes 196616 | tf_op jit(solution)/shard_map/ppermute | solution.py:793
  30.8 2.6 %collective-permute-done.2.refs_2_ = bf16[128,256]{1,0:T(8,128)(2,1)S(1)} collective-permute-done((bf16[128,256]{1,0:T(8,128)(2,1)S(1)}, bf16[128,256]{1,0:T(8,128)(2,1)S(1)}, u32[]{:S(2)}, u32[]{:S(2)}) %collective-permute-start.2) | collective-permute-done | bytes 65568 | tf_op jit(solution)/shard_map/ppermute | solution.py:793
  33.4 1.8 attend.1
  35.3 2.7 %collective-permute-start.3 = (bf16[128,256]{1,0:T(8,128)(2,1)S(1)}, bf16[128,256]{1,0:T(8,128)(2,1)S(1)}, u32[]{:S(2)}, u32[]{:S(2)}) collective-permute-start(bf16[128,256]{1,0:T(8,128)(2,1)S(1)} %get-tuple-element.103.refs_0_), channel_id=1, source_target_pairs={{0,16},{16,0},{1,17},{17,1},{2,18},{18,2},{3,19},{19,3},{4,20},{20... | collective-permute-start | bytes 196616 | tf_op jit(solution)/shard_map/ppermute | solution.py:793
  37.9 2.6 %collective-permute-done.3.refs_1_ = bf16[128,256]{1,0:T(8,128)(2,1)S(1)} collective-permute-done((bf16[128,256]{1,0:T(8,128)(2,1)S(1)}, bf16[128,256]{1,0:T(8,128)(2,1)S(1)}, u32[]{:S(2)}, u32[]{:S(2)}) %collective-permute-start.3) | collective-permute-done | bytes 65568 | tf_op jit(solution)/shard_map/ppermute | solution.py:793
  40.5 1.5 merge.1
  42.0 5.0 %all-to-all-start.1 = ((bf16[16,192,128]{2,1,0:T(8,128)(2,1)}), bf16[16,192,128]{2,1,0:T(8,128)(2,1)S(1)}, u32[]{:S(2)}, u32[]{:S(2)}) async-start(bf16[16,192,128]{2,1,0:T(8,128)(2,1)} %get-tuple-element.104), calls=%async_computation.1 | async-start | bytes 1572864 | tf_op jit(solution)/shard_map/all_to_all | solution.py:905
  47.0 1.3 broadcast_multiply_fusion.refs_7_.refs_4_.refs_6_
  48.3 11.9 %all-to-all-done.1.refs_0_ = bf16[16,192,128]{2,1,0:T(8,128)(2,1)S(1)} async-done(((bf16[16,192,128]{2,1,0:T(8,128)(2,1)}), bf16[16,192,128]{2,1,0:T(8,128)(2,1)S(1)}, u32[]{:S(2)}, u32[]{:S(2)}) %all-to-all-start.1) | async-done | bytes 786464 | tf_op jit(solution)/shard_map/all_to_all | solution.py:905
  60.2 1.1 copy-done.5
  61.4 5.5 %middle.3 = (f32[1,1536]{1,0:T(1,128)S(1)}, f32[256,768]{1,0:T(8,128)S(1)}, bf16[256,768]{1,0:T(8,128)(2,1)S(1)}, bf16[256,384]{1,0:T(8,128)(2,1)}, bf16[256,768...) custom-call(bf16[16,192,128]{2,1,0:T(8,128)(2,1)S(1)} %all-to-all-done.1.refs_0_, ...), custom_call_target="tpu_custom_call" | custom-call | flops 1000000 | bytes 1 | tf_op jit(solution)/shard_map/middle/pallas_call | solution.py:74
  67.5 5.5 %middle.2 = (f32[1,1536]{1,0:T(1,128)S(1)}, f32[256,768]{1,0:T(8,128)S(1)}, bf16[256,768]{1,0:T(8,128)(2,1)S(1)}, bf16[256,384]{1,0:T(8,128)(2,1)}, bf16[256,768...) custom-call(bf16[16,192,128]{2,1,0:T(8,128)(2,1)S(1)} %all-to-all-done.1.refs_0_, ...), custom_call_target="tpu_custom_call" | custom-call | flops 1000000 | bytes 1 | tf_op jit(solution)/shard_map/middle/pallas_call | solution.py:74
  73.0 1.5 collective-permute-start.4
  74.5 6.6 %ff_terms.1 = (bf16[384,3072]{1,0:T(8,128)(2,1)}, bf16[384,3072]{1,0:T(8,128)(2,1)}, f32[8,128]{1,0:T(8,128)}) custom-call(bf16[256,768]{1,0:T(8,128)(2,1)} %get-tuple-element.112.refs_0_, bf16[256,1536]{1,0:T(8,128)(2,1)} %get-tuple-element.113.refs_1_, bf16[256,768]{1,0:T(8,128)(2,1)} %get-tuple-element.114.refs_2_, ...), custom_call_target="tpu_custom_call" | custom-call | flops 1000000 | bytes 1 | tf_op jit(solution)/shard_map/ff_terms/pallas_call | solution.py:74
  81.2 5.6 %collective-permute-done.4.refs_2_ = bf16[256,768]{1,0:T(8,128)(2,1)S(1)} collective-permute-done((bf16[256,768]{1,0:T(8,128)(2,1)S(1)}, bf16[256,768]{1,0:T(8,128)(2,1)S(1)}, u32[]{:S(2)}, u32[]{:S(2)}) %collective-permute-start.4) | collective-permute-done | bytes 393248 | tf_op jit(solution)/shard_map/ppermute | solution.py:934
  86.8 3.7 %turn.1 = (f32[256,768]{1,0:T(8,128)}, bf16[512,768]{1,0:T(8,128)(2,1)}, bf16[8,208,128]{2,1,0:T(8,128)(2,1)}, f32[8,128]{1,0:T(8,128)}) custom-call(bf16[256,768]{1,0:T(8,128)(2,1)S(1)} %get-tuple-element.107.refs_0_, bf16[256,768]{1,0:T(8,128)(2,1)S(1)} %get-tuple-element.108.refs_1_, bf16[256,768]{1,0:T(8,128)(2,1)S(1)} %collective-permute-done.4.refs_2_, ...), custom_call_target="tpu_custom_call" | custom-call | flops 40000000000 | bytes 1 | tf_op jit(solution)/shard_map/turn/pallas_call | solution.py:74
  90.6 4.3 %all-to-all-start.2 = ((bf16[8,208,128]{2,1,0:T(8,128)(2,1)}), bf16[8,208,128]{2,1,0:T(8,128)(2,1)}, u32[]{:S(2)}, u32[]{:S(2)}) async-start(bf16[8,208,128]{2,1,0:T(8,128)(2,1)} %get-tuple-element.123), calls=%async_computation.2 | async-start | bytes 851968 | tf_op jit(solution)/shard_map/all_to_all | solution.py:953
  94.9 1.1 copy-done.9
  99.0 3.3 %ff_fold.3 = (bf16[192,3072]{1,0:T(8,128)(2,1)}, bf16[192,2048]{1,0:T(8,128)(2,1)}, bf16[192,1024]{1,0:T(8,128)(2,1)}, f32[8,128]{1,0:T(8,128)}) custom-call(bf16[384,3072]{1,0:T(8,128)(2,1)S(1)} %copy-done.12, bf16[384,3072]{1,0:T(8,128)(2,1)} %collective-permute-done.8.refs_1_, f32[8,128]{1,0:T(8,128)} %get-tuple-element.126.refs_2_, ...), custom_call_target="tpu_custom_call" | custom-call | flops 1000000 | bytes 1 | tf_op jit(solution)/shard_map/ff_fold/pallas_call | solution.py:74
  102.7 1.1 grad_sums.1
  103.8 3.1 %collective-permute-start.9 = (bf16[208,128]{1,0:T(8,128)(2,1)S(1)}, bf16[208,128]{1,0:T(8,128)(2,1)S(1)}, u32[]{:S(2)}, u32[]{:S(2)}) collective-permute-start(bf16[208,128]{1,0:T(8,128)(2,1)S(1)} %get-tuple-element.129.refs_3_), channel_id=1, source_target_pairs={{0,16},{16,0},{1,17},{17,1},{2,18},{18,2},{3,19},{19,3},{4,20},{20... | collective-permute-start | bytes 159752 | tf_op jit(solution)/shard_map/ppermute | solution.py:793
  106.9 1.5 collective-permute-done.6.refs_5_.refs_2_
  108.4 1.8 collective-permute-done.9.refs_4_
  110.2 3.9 %attend_back.1 = (bf16[192,128]{1,0:T(8,128)(2,1)S(1)}, f32[4,128]{1,0:T(4,128)S(1)}, bf16[8,128,384]{2,1,0:T(8,128)(2,1)}, f32[8,128]{1,0:T(8,128)}) custom-call(bf16[8,128,640]{2,1,0:T(8,128)(2,1)} %copy-done.3, f32[128,256]{1,0:T(8,128)} %get-tuple-element.121.refs_1_.refs_0_, f32[128,256]{1,0:T(8,128)} %get-tuple-element.122.refs_2_, ...), custom_call_target="tpu_custom_call" | custom-call | flops 40000000000 | bytes 1 | tf_op jit(solution)/shard_map/attend_back/pallas_call | solution.py:74
  114.1 3.7 %all-to-all-start.3 = ((bf16[8,128,384]{2,1,0:T(8,128)(2,1)}), bf16[8,128,384]{2,1,0:T(8,128)(2,1)S(1)}, u32[]{:S(2)}, u32[]{:S(2)}) async-start(bf16[8,128,384]{2,1,0:T(8,128)(2,1)} %get-tuple-element.130), calls=%async_computation.3 | async-start | bytes 1572864 | tf_op jit(solution)/shard_map/all_to_all | solution.py:982
  117.8 0.8 collective-permute-start.7
  118.6 3.3 %collective-permute-start.10 = (bf16[192,128]{1,0:T(8,128)(2,1)S(1)}, bf16[192,128]{1,0:T(8,128)(2,1)S(1)}, u32[]{:S(2)}, u32[]{:S(2)}) collective-permute-start(bf16[192,128]{1,0:T(8,128)(2,1)S(1)} %get-tuple-element.133.refs_2_), channel_id=1, source_target_pairs={{0,16},{16,0},{1,17},{17,1},{2,18},{18,2},{3,19},{19,3},{4,20},{20... | collective-permute-start | bytes 147464 | tf_op jit(solution)/shard_map/ppermute | solution.py:793
  121.9 2.8 %out_terms.1 = (bf16[384,384]{1,0:T(8,128)(2,1)}, bf16[384,384]{1,0:T(8,128)(2,1)}, f32[8,128]{1,0:T(8,128)}) custom-call(bf16[512,768]{1,0:T(8,128)(2,1)} %get-tuple-element.134.refs_0_.refs_2_, bf16[256,384]{1,0:T(8,128)(2,1)} %get-tuple-element.135.refs_1_, bf16[512,768]{1,0:T(8,128)(2,1)} %get-tuple-element.134.refs_0_.refs_2_, ...), custom_call_target="tpu_custom_call" | custom-call | flops 1000000 | bytes 1 | tf_op jit(solution)/shard_map/out_terms/pallas_call | solution.py:74
  124.7 4.5 %collective-permute-done.7.refs_5_ = bf16[256,768]{1,0:T(8,128)(2,1)S(1)} collective-permute-done((bf16[256,768]{1,0:T(8,128)(2,1)S(1)}, bf16[256,768]{1,0:T(8,128)(2,1)S(1)}, u32[]{:S(2)}, u32[]{:S(2)}) %collective-permute-start.7) | collective-permute-done | bytes 393248 | tf_op jit(solution)/shard_map/ppermute | solution.py:965
  129.9 1.0 finish_back.1
  130.9 5.3 %all-to-all-start.4 = ((bf16[8,208,128]{2,1,0:T(8,128)(2,1)}), bf16[8,208,128]{2,1,0:T(8,128)(2,1)S(1)}, u32[]{:S(2)}, u32[]{:S(2)}) async-start(bf16[8,208,128]{2,1,0:T(8,128)(2,1)} %get-tuple-element.142), calls=%async_computation.4 | async-start | bytes 851968 | tf_op jit(solution)/shard_map/all_to_all | solution.py:993
  136.2 2.0 %collective-permute-start.15 = (bf16[192,2048]{1,0:T(8,128)(2,1)}, bf16[192,2048]{1,0:T(8,128)(2,1)S(1)}, u32[]{:S(2)}, u32[]{:S(2)}) collective-permute-start(bf16[192,2048]{1,0:T(8,128)(2,1)} %get-tuple-element.159), channel_id=1, source_target_pairs={{0,4},{4,0},{1,5},{5,1},{2,6},{6,2},{3,7},{7,3},{8,12},{12,8},{9,1... | collective-permute-start | bytes 2359304 | tf_op jit(solution)/shard_map/ppermute | solution.py:836
  138.2 1.2 collective-permute-start.16
  139.5 3.2 %kv_terms.1 = (bf16[512,768]{1,0:T(8,128)(2,1)}, bf16[384,768]{1,0:T(8,128)(2,1)}, bf16[384,768]{1,0:T(8,128)(2,1)}, f32[8,128]{1,0:T(8,128)}) custom-call(bf16[8,128,384]{2,1,0:T(8,128)(2,1)S(1)} %all-to-all-done.3.refs_0_, bf16[512,768]{1,0:T(8,128)(2,1)} %get-tuple-element.131.refs_1_.refs_0_, f32[8,128]{1,0:T(8,128)} %get-tuple-element.139.refs_2_), custom_call_target="tpu_custom_call" | custom-call | flops 1000000 | bytes 1 | tf_op jit(solution)/shard_map/kv_terms/pallas_call | solution.py:74
  143.3 2.8 %output.1 = (bf16[512,768]{1,0:T(8,128)(2,1)}, f32[8,128]{1,0:T(8,128)}) custom-call(f32[256,768]{1,0:T(8,128)} %copy-done.15, bf16[256,768]{1,0:T(8,128)(2,1)} %copy-done.20, bf16[256,768]{1,0:T(8,128)(2,1)} %collective-permute-done.6.refs_5_.refs_2_, f32[256,768]{1,0:T(8,128)} %copy-done.14, bf16[256,768]{1,0:T(8,128)(2,1)} %copy-done.21, ...), custom_call_target="tpu_custom_call" | custom-call | flops 1000000 | bytes 1 | tf_op jit(solution)/shard_map/output/pallas_call | solution.py:74
  146.1 1.2 all-to-all-done.4.refs_0_.refs_1_
  147.4 4.5 %first_back.1 = (bf16[512,384]{1,0:T(8,128)(2,1)}, bf16[256,768]{1,0:T(8,128)(2,1)}, bf16[256,768]{1,0:T(8,128)(2,1)}, f32[8,128]{1,0:T(8,128)}) custom-call(bf16[8,208,128]{2,1,0:T(8,128)(2,1)S(1)} %all-to-all-done.4.refs_0_.refs_1_, s32[6,512]{1,0:T(8,128)S(1)} %copy-done.27, bf16[768,384]{1,0:T(8,128)(2,1)} %refs_2_.4, bf16[768,768]{1,0:T(8,128)(2,1)} %bitcast.12, ...), custom_call_target="tpu_custom_call" | custom-call | flops 40000000000 | bytes 1 | tf_op jit(solution)/shard_map/first_back/pallas_call | solution.py:74
  151.9 1.5 collective-permute-start.11
  153.4 2.8 %q_terms.1 = (bf16[384,384]{1,0:T(8,128)(2,1)}, bf16[384,384]{1,0:T(8,128)(2,1)}, f32[8,128]{1,0:T(8,128)}) custom-call(bf16[512,768]{1,0:T(8,128)(2,1)} %get-tuple-element.131.refs_1_.refs_0_, bf16[512,384]{1,0:T(8,128)(2,1)} %get-tuple-element.150.refs_1_, f32[8,128]{1,0:T(8,128)} %get-tuple-element.151.refs_2_), custom_call_target="tpu_custom_call" | custom-call | flops 1000000 | bytes 1 | tf_op jit(solution)/shard_map/q_terms/pallas_call | solution.py:74
  156.3 1.8 collective-permute-done.14.refs_5_
  158.1 1.0 copy-done.24
  159.1 1.2 kv_fold.3
  160.2 2.2 %collective-permute-start.18 = (bf16[192,1536]{1,0:T(8,128)(2,1)}, bf16[192,1536]{1,0:T(8,128)(2,1)S(1)}, u32[]{:S(2)}, u32[]{:S(2)}) collective-permute-start(bf16[192,1536]{1,0:T(8,128)(2,1)} %get-tuple-element.164), channel_id=1, source_target_pairs={{0,4},{4,0},{1,5},{5,1},{2,6},{6,2},{3,7},{7,3},{8,12},{12,8},{9,1... | collective-permute-start | bytes 1769480 | tf_op jit(solution)/shard_map/ppermute | solution.py:836
  162.5 1.2 ff_fold.4
  164.2 1.3 last.1
  165.5 3.5 %all-to-all-start.5 = ((f32[32,2,48]{2,1,0:T(2,128)}), f32[32,2,48]{2,1,0:T(2,128)S(1)}, u32[]{:S(2)}, u32[]{:S(2)}) async-start(f32[32,2,48]{2,1,0:T(2,128)} %get-tuple-element.168), calls=%async_computation.5 | async-start | bytes 65536 | tf_op jit(solution)/shard_map/all_to_all | solution.py:1043
  169.0 1.8 collective-permute-start.17
  170.8 6.2 %collective-permute-done.18.refs_1_ = bf16[192,1536]{1,0:T(8,128)(2,1)S(1)} collective-permute-done((bf16[192,1536]{1,0:T(8,128)(2,1)}, bf16[192,1536]{1,0:T(8,128)(2,1)S(1)}, u32[]{:S(2)}, u32[]{:S(2)}) %collective-permute-start.18) | collective-permute-done | bytes 589856 | tf_op jit(solution)/shard_map/ppermute | solution.py:836
  177.1 0.9 kv_fold.4
  178.2 2.7 %collective-permute-done.21.refs_2_ = bf16[96,1024]{1,0:T(8,128)(2,1)S(1)} collective-permute-done((bf16[96,1024]{1,0:T(8,128)(2,1)}, bf16[96,1024]{1,0:T(8,128)(2,1)S(1)}, u32[]{:S(2)}, u32[]{:S(2)}) %collective-permute-start.21) | collective-permute-done | bytes 196640 | tf_op jit(solution)/shard_map/ppermute | solution.py:836
  180.9 0.9 ff_fold.5
  181.9 1.5 collective-permute-start.24
  185.1 3.2 %collective-permute-done.19.refs_1_ = bf16[96,1536]{1,0:T(8,128)(2,1)S(1)} collective-permute-done((bf16[96,1536]{1,0:T(8,128)(2,1)}, bf16[96,1536]{1,0:T(8,128)(2,1)S(1)}, u32[]{:S(2)}, u32[]{:S(2)}) %collective-permute-start.19) | collective-permute-done | bytes 294944 | tf_op jit(solution)/shard_map/ppermute | solution.py:836
  188.3 1.0 copy-done.26
  190.5 1.9 join.1
  192.4 4.6 %collective-permute-done.23.refs_1_ = bf16[48,2048]{1,0:T(8,128)(2,1)S(1)} collective-permute-done((bf16[48,2048]{1,0:T(8,128)(2,1)}, bf16[48,2048]{1,0:T(8,128)(2,1)S(1)}, u32[]{:S(2)}, u32[]{:S(2)}) %collective-permute-start.23) | collective-permute-done | bytes 196640 | tf_op jit(solution)/shard_map/ppermute | solution.py:836
  197.0 0.8 ff_close.1
  197.9 1.6 collective-permute-done.22.refs_1_
  (121 shorter events, 10.6 us)
Async XLA Ops:
  0.6 1.7 copy-start.4
  0.7 1.7 copy-start.16
  2.3 3.1 %copy-start.7 = (bf16[96,8,2,384]{3,1,2,0:T(8,128)(2,1)}, bf16[96,8,2,384]{3,1,2,0:T(8,128)(2,1)S(1)}, u32[]{:S(2)}) copy-start(bf16[96,8,2,384]{3,1,2,0:T(8,128)(2,1)S(1)} %copy.28) | copy-start | bytes 3538948
  2.4 8.3 %copy-start.10 = (bf16[384,768]{1,0:T(8,128)(2,1)S(1)}, bf16[384,768]{1,0:T(8,128)(2,1)}, u32[]{:S(2)}) copy-start(bf16[384,768]{1,0:T(8,128)(2,1)} %refs_8_.5) | copy-start | bytes 1769476
  5.4 22.5 %all-to-all-start = ((bf16[8,128,640]{2,1,0:T(8,128)(2,1)}), bf16[8,128,640]{2,1,0:T(8,128)(2,1)S(1)}, u32[]{:S(2)}, u32[]{:S(2)}) async-start(bf16[8,128,640]{2,1,0:T(8,128)(2,1)} %get-tuple-element.102), calls=%async_computation | async-start | bytes 2621440 | tf_op jit(solution)/shard_map/all_to_all | solution.py:885
  10.7 36.3 %copy-start.43 = (s32[512]{0:T(512)S(1)}, s32[512]{0:T(512)}, u32[]{:S(2)}) copy-start(s32[512]{0:T(512)} %param.29) | copy-start | bytes 6148
  10.7 16.1 %collective-permute-start.1 = (bf16[384,768]{1,0:T(8,128)(2,1)S(1)}, bf16[384,768]{1,0:T(8,128)(2,1)S(1)}, u32[]{:S(2)}, u32[]{:S(2)}) collective-permute-start(bf16[384,768]{1,0:T(8,128)(2,1)S(1)} %copy-done.10), channel_id=1, source_target_pairs={{0,1},{1,0},{2,3},{3,2},{4,5},{5,4},{6,7},{7,6},{8,9},{9,8},{10,11... | collective-permute-start | bytes 1769480 | tf_op jit(solution)/shard_map/ppermute | solution.py:870
  12.3 14.5 %collective-permute-start = (s32[6,512]{1,0:T(8,128)S(1)}, s32[6,512]{1,0:T(8,128)S(1)}, u32[]{:S(2)}, u32[]{:S(2)}) collective-permute-start(s32[6,512]{1,0:T(8,128)S(1)} %copy-done.27), channel_id=1, source_target_pairs={{0,1},{1,0},{2,3},{3,2},{4,5},{5,4},{6,7},{7,6},{8,9},{9,8},{10,11... | collective-permute-start | bytes 36872 | tf_op jit(solution)/shard_map/ppermute | solution.py:869
  28.0 14.1 %copy-start.3 = (bf16[8,128,640]{2,1,0:T(8,128)(2,1)}, bf16[8,128,640]{2,1,0:T(8,128)(2,1)S(1)}, u32[]{:S(2)}) copy-start(bf16[8,128,640]{2,1,0:T(8,128)(2,1)S(1)} %all-to-all-done.refs_0_) | copy-start | bytes 3932164
  28.1 32.1 %copy-start.29 = (s32[6,512]{1,0:T(8,128)S(1)}, s32[6,512]{1,0:T(8,128)}, u32[]{:S(2)}) copy-start(s32[6,512]{1,0:T(8,128)} %copy-done.28) | copy-start | bytes 36868
  28.1 32.1 %copy-start.32 = (f32[1536]{0:T(1024)S(1)}, f32[1536]{0:T(1024)}, u32[]{:S(2)}) copy-start(f32[1536]{0:T(1024)} %refs_6_.5) | copy-start | bytes 18436
  28.1 32.1 %copy-start.33 = (f32[768]{0:T(1024)S(1)}, f32[768]{0:T(1024)}, u32[]{:S(2)}) copy-start(f32[768]{0:T(1024)} %refs_5_.5) | copy-start | bytes 9220
  28.1 32.1 %copy-start.34 = (f32[768]{0:T(1024)S(1)}, f32[768]{0:T(1024)}, u32[]{:S(2)}) copy-start(f32[768]{0:T(1024)} %refs_6_.6) | copy-start | bytes 9220
  28.1 5.3 %collective-permute-start.2 = (bf16[128,256]{1,0:T(8,128)(2,1)S(1)}, bf16[128,256]{1,0:T(8,128)(2,1)S(1)}, u32[]{:S(2)}, u32[]{:S(2)}) collective-permute-start(bf16[128,256]{1,0:T(8,128)(2,1)S(1)} %query_sums.1.refs_1_), channel_id=1, source_target_pairs={{0,16},{16,0},{1,17},{17,1},{2,18},{18,2},{3,19},{19,3},{4,20},{20... | collective-permute-start | bytes 196616 | tf_op jit(solution)/shard_map/ppermute | solution.py:793
  35.3 5.2 %collective-permute-start.3 = (bf16[128,256]{1,0:T(8,128)(2,1)S(1)}, bf16[128,256]{1,0:T(8,128)(2,1)S(1)}, u32[]{:S(2)}, u32[]{:S(2)}) collective-permute-start(bf16[128,256]{1,0:T(8,128)(2,1)S(1)} %get-tuple-element.103.refs_0_), channel_id=1, source_target_pairs={{0,16},{16,0},{1,17},{17,1},{2,18},{18,2},{3,19},{19,3},{4,20},{20... | collective-permute-start | bytes 196616 | tf_op jit(solution)/shard_map/ppermute | solution.py:793
  42.0 18.2 %all-to-all-start.1 = ((bf16[16,192,128]{2,1,0:T(8,128)(2,1)}), bf16[16,192,128]{2,1,0:T(8,128)(2,1)S(1)}, u32[]{:S(2)}, u32[]{:S(2)}) async-start(bf16[16,192,128]{2,1,0:T(8,128)(2,1)} %get-tuple-element.104), calls=%async_computation.1 | async-start | bytes 1572864 | tf_op jit(solution)/shard_map/all_to_all | solution.py:905
  48.3 19.2 %copy-start.1 = (bf16[512,768]{1,0:T(8,128)(2,1)}, bf16[512,768]{1,0:T(8,128)(2,1)S(1)}, u32[]{:S(2)}) copy-start(bf16[512,768]{1,0:T(8,128)(2,1)S(1)} %broadcast_multiply_fusion.refs_7_.refs_4_.refs_6_) | copy-start | bytes 2359300
  66.9 20.0 %copy-start.14 = (f32[256,768]{1,0:T(8,128)}, f32[256,768]{1,0:T(8,128)S(1)}, u32[]{:S(2)}) copy-start(f32[256,768]{1,0:T(8,128)S(1)} %get-tuple-element.109.refs_5_.refs_3_) | copy-start | bytes 2359300
  66.9 14.3 %collective-permute-start.5 = (bf16[256,768]{1,0:T(8,128)(2,1)S(1)}, bf16[256,768]{1,0:T(8,128)(2,1)S(1)}, u32[]{:S(2)}, u32[]{:S(2)}) collective-permute-start(bf16[256,768]{1,0:T(8,128)(2,1)S(1)} %get-tuple-element.108.refs_1_), channel_id=1, source_target_pairs={{0,1},{1,0},{2,3},{3,2},{4,5},{5,4},{6,7},{7,6},{8,9},{9,8},{10,11... | collective-permute-start | bytes 1179656 | tf_op jit(solution)/shard_map/ppermute | solution.py:934
  73.0 13.8 %copy-start.15 = (f32[256,768]{1,0:T(8,128)}, f32[256,768]{1,0:T(8,128)S(1)}, u32[]{:S(2)}) copy-start(f32[256,768]{1,0:T(8,128)S(1)} %get-tuple-element.105.refs_4_.refs_0_) | copy-start | bytes 2359300
  73.0 13.8 %collective-permute-start.4 = (bf16[256,768]{1,0:T(8,128)(2,1)S(1)}, bf16[256,768]{1,0:T(8,128)(2,1)S(1)}, u32[]{:S(2)}, u32[]{:S(2)}) collective-permute-start(bf16[256,768]{1,0:T(8,128)(2,1)S(1)} %get-tuple-element.107.refs_0_), channel_id=1, source_target_pairs={{0,1},{1,0},{2,3},{3,2},{4,5},{5,4},{6,7},{7,6},{8,9},{9,8},{10,11... | collective-permute-start | bytes 1179656 | tf_op jit(solution)/shard_map/ppermute | solution.py:934
  74.5 12.3 %copy-start.2 = (bf16[512,768]{1,0:T(8,128)(2,1)S(1)}, bf16[512,768]{1,0:T(8,128)(2,1)}, u32[]{:S(2)}) copy-start(bf16[512,768]{1,0:T(8,128)(2,1)} %copy-done.1) | copy-start | bytes 2359300
  74.5 12.3 %copy-start.11 = (bf16[384,768]{1,0:T(8,128)(2,1)S(1)}, bf16[384,768]{1,0:T(8,128)(2,1)}, u32[]{:S(2)}) copy-start(bf16[384,768]{1,0:T(8,128)(2,1)} %refs_8_.5) | copy-start | bytes 1769476
  81.1 17.9 %collective-permute-start.8 = (bf16[384,3072]{1,0:T(8,128)(2,1)}, bf16[384,3072]{1,0:T(8,128)(2,1)}, u32[]{:S(2)}, u32[]{:S(2)}) collective-permute-start(bf16[384,3072]{1,0:T(8,128)(2,1)} %get-tuple-element.125), channel_id=1, source_target_pairs={{0,2},{2,0},{1,3},{3,1},{4,6},{6,4},{5,7},{7,5},{8,10},{10,8},{9,1... | collective-permute-start | bytes 7077896 | tf_op jit(solution)/shard_map/ppermute | solution.py:836
  86.8 8.0 %copy-start = (bf16[1536,768]{1,0:T(8,128)(2,1)S(1)}, bf16[1536,768]{1,0:T(8,128)(2,1)}, u32[]{:S(2)}) copy-start(bf16[1536,768]{1,0:T(8,128)(2,1)} %refs_1_.10) | copy-start | bytes 7077892
  90.6 6.9 %copy-start.8 = (bf16[256,1536]{1,0:T(8,128)(2,1)S(1)}, bf16[256,1536]{1,0:T(8,128)(2,1)}, u32[]{:S(2)}) copy-start(bf16[256,1536]{1,0:T(8,128)(2,1)} %get-tuple-element.116.refs_7_.refs_0_) | copy-start | bytes 2359300
  90.6 12.1 %all-to-all-start.2 = ((bf16[8,208,128]{2,1,0:T(8,128)(2,1)}), bf16[8,208,128]{2,1,0:T(8,128)(2,1)}, u32[]{:S(2)}, u32[]{:S(2)}) async-start(bf16[8,208,128]{2,1,0:T(8,128)(2,1)} %get-tuple-element.123), calls=%async_computation.2 | async-start | bytes 851968 | tf_op jit(solution)/shard_map/all_to_all | solution.py:953
  96.8 5.6 %copy-start.20 = (bf16[256,768]{1,0:T(8,128)(2,1)}, bf16[256,768]{1,0:T(8,128)(2,1)S(1)}, u32[]{:S(2)}) copy-start(bf16[256,768]{1,0:T(8,128)(2,1)S(1)} %get-tuple-element.119.refs_1_) | copy-start | bytes 1179652
  96.8 2.2 %copy-start.12 = (bf16[384,3072]{1,0:T(8,128)(2,1)S(1)}, bf16[384,3072]{1,0:T(8,128)(2,1)}, u32[]{:S(2)}) copy-start(bf16[384,3072]{1,0:T(8,128)(2,1)} %get-tuple-element.124.refs_0_) | copy-start | bytes 7077892
  96.8 11.6 %collective-permute-start.6 = (bf16[256,768]{1,0:T(8,128)(2,1)S(1)}, bf16[256,768]{1,0:T(8,128)(2,1)}, u32[]{:S(2)}, u32[]{:S(2)}) collective-permute-start(bf16[256,768]{1,0:T(8,128)(2,1)S(1)} %get-tuple-element.119.refs_1_), channel_id=1, source_target_pairs={{0,1},{1,0},{2,3},{3,2},{4,5},{5,4},{6,7},{7,6},{8,9},{9,8},{10,11... | collective-permute-start | bytes 1179656 | tf_op jit(solution)/shard_map/ppermute | solution.py:965
  103.8 6.4 %collective-permute-start.9 = (bf16[208,128]{1,0:T(8,128)(2,1)S(1)}, bf16[208,128]{1,0:T(8,128)(2,1)S(1)}, u32[]{:S(2)}, u32[]{:S(2)}) collective-permute-start(bf16[208,128]{1,0:T(8,128)(2,1)S(1)} %get-tuple-element.129.refs_3_), channel_id=1, source_target_pairs={{0,16},{16,0},{1,17},{17,1},{2,18},{18,2},{3,19},{19,3},{4,20},{20... | collective-permute-start | bytes 159752 | tf_op jit(solution)/shard_map/ppermute | solution.py:793
  110.1 7.6 %copy-start.22 = (bf16[256,768]{1,0:T(8,128)(2,1)S(1)}, bf16[256,768]{1,0:T(8,128)(2,1)}, u32[]{:S(2)}) copy-start(bf16[256,768]{1,0:T(8,128)(2,1)} %copy-done.21) | copy-start | bytes 1179652
  114.1 15.9 %copy-start.31 = (f32[128,256]{1,0:T(8,128)S(1)}, f32[128,256]{1,0:T(8,128)}, u32[]{:S(2)}) copy-start(f32[128,256]{1,0:T(8,128)} %get-tuple-element.121.refs_1_.refs_0_) | copy-start | bytes 393220
  114.1 16.9 %all-to-all-start.3 = ((bf16[8,128,384]{2,1,0:T(8,128)(2,1)}), bf16[8,128,384]{2,1,0:T(8,128)(2,1)S(1)}, u32[]{:S(2)}, u32[]{:S(2)}) async-start(bf16[8,128,384]{2,1,0:T(8,128)(2,1)} %get-tuple-element.130), calls=%async_computation.3 | async-start | bytes 1572864 | tf_op jit(solution)/shard_map/all_to_all | solution.py:982
  117.8 11.4 %collective-permute-start.7 = (bf16[256,768]{1,0:T(8,128)(2,1)S(1)}, bf16[256,768]{1,0:T(8,128)(2,1)S(1)}, u32[]{:S(2)}, u32[]{:S(2)}) collective-permute-start(bf16[256,768]{1,0:T(8,128)(2,1)S(1)} %copy-done.22), channel_id=1, source_target_pairs={{0,1},{1,0},{2,3},{3,2},{4,5},{5,4},{6,7},{7,6},{8,9},{9,8},{10,11... | collective-permute-start | bytes 1179656 | tf_op jit(solution)/shard_map/ppermute | solution.py:965
  118.6 10.6 %collective-permute-start.10 = (bf16[192,128]{1,0:T(8,128)(2,1)S(1)}, bf16[192,128]{1,0:T(8,128)(2,1)S(1)}, u32[]{:S(2)}, u32[]{:S(2)}) collective-permute-start(bf16[192,128]{1,0:T(8,128)(2,1)S(1)} %get-tuple-element.133.refs_2_), channel_id=1, source_target_pairs={{0,16},{16,0},{1,17},{17,1},{2,18},{18,2},{3,19},{19,3},{4,20},{20... | collective-permute-start | bytes 147464 | tf_op jit(solution)/shard_map/ppermute | solution.py:793
  121.9 21.4 %copy-start.36 = (f32[768]{0:T(1024)S(1)}, f32[768]{0:T(1024)}, u32[]{:S(2)}) copy-start(f32[768]{0:T(1024)} %refs_6_.7) | copy-start | bytes 9220
  130.9 16.4 %all-to-all-start.4 = ((bf16[8,208,128]{2,1,0:T(8,128)(2,1)}), bf16[8,208,128]{2,1,0:T(8,128)(2,1)S(1)}, u32[]{:S(2)}, u32[]{:S(2)}) async-start(bf16[8,208,128]{2,1,0:T(8,128)(2,1)} %get-tuple-element.142), calls=%async_computation.4 | async-start | bytes 851968 | tf_op jit(solution)/shard_map/all_to_all | solution.py:993
  136.2 26.3 %collective-permute-start.15 = (bf16[192,2048]{1,0:T(8,128)(2,1)}, bf16[192,2048]{1,0:T(8,128)(2,1)S(1)}, u32[]{:S(2)}, u32[]{:S(2)}) collective-permute-start(bf16[192,2048]{1,0:T(8,128)(2,1)} %get-tuple-element.159), channel_id=1, source_target_pairs={{0,4},{4,0},{1,5},{5,1},{2,6},{6,2},{3,7},{7,3},{8,12},{12,8},{9,1... | collective-permute-start | bytes 2359304 | tf_op jit(solution)/shard_map/ppermute | solution.py:836
  138.2 24.2 %collective-permute-start.16 = (bf16[192,1024]{1,0:T(8,128)(2,1)}, bf16[192,1024]{1,0:T(8,128)(2,1)S(1)}, u32[]{:S(2)}, u32[]{:S(2)}) collective-permute-start(bf16[192,1024]{1,0:T(8,128)(2,1)} %get-tuple-element.160), channel_id=1, source_target_pairs={{0,16},{16,0},{1,17},{17,1},{2,18},{18,2},{3,19},{19,3},{4,20},{20... | collective-permute-start | bytes 1179656 | tf_op jit(solution)/shard_map/ppermute | solution.py:836
  139.5 16.7 %collective-permute-start.13 = (bf16[384,384]{1,0:T(8,128)(2,1)}, bf16[384,384]{1,0:T(8,128)(2,1)S(1)}, u32[]{:S(2)}, u32[]{:S(2)}) collective-permute-start(bf16[384,384]{1,0:T(8,128)(2,1)} %get-tuple-element.154), channel_id=1, source_target_pairs={{0,2},{2,0},{1,3},{3,1},{4,6},{6,4},{5,7},{7,5},{8,10},{10,8},{9,1... | collective-permute-start | bytes 884744 | tf_op jit(solution)/shard_map/ppermute | solution.py:856
  142.7 15.3 %collective-permute-start.12 = (bf16[384,768]{1,0:T(8,128)(2,1)}, bf16[384,768]{1,0:T(8,128)(2,1)S(1)}, u32[]{:S(2)}, u32[]{:S(2)}) collective-permute-start(bf16[384,768]{1,0:T(8,128)(2,1)} %get-tuple-element.153), channel_id=1, source_target_pairs={{0,2},{2,0},{1,3},{3,1},{4,6},{6,4},{5,7},{7,5},{8,10},{10,8},{9,1... | collective-permute-start | bytes 1769480 | tf_op jit(solution)/shard_map/ppermute | solution.py:856
  147.4 10.7 %copy-start.19 = (bf16[384,768]{1,0:T(8,128)(2,1)S(1)}, bf16[384,768]{1,0:T(8,128)(2,1)}, u32[]{:S(2)}) copy-start(bf16[384,768]{1,0:T(8,128)(2,1)} %get-tuple-element.148.refs_0_) | copy-start | bytes 1769476
  147.4 10.7 %copy-start.23 = (bf16[384,384]{1,0:T(8,128)(2,1)S(1)}, bf16[384,384]{1,0:T(8,128)(2,1)}, u32[]{:S(2)}) copy-start(bf16[384,384]{1,0:T(8,128)(2,1)} %get-tuple-element.149.refs_1_) | copy-start | bytes 884740
  151.8 10.7 %copy-start.13 = (bf16[192,3072]{1,0:T(8,128)(2,1)S(1)}, bf16[192,3072]{1,0:T(8,128)(2,1)}, u32[]{:S(2)}) copy-start(bf16[192,3072]{1,0:T(8,128)(2,1)} %get-tuple-element.158.refs_0_) | copy-start | bytes 3538948
  151.9 12.3 %collective-permute-start.11 = (bf16[256,768]{1,0:T(8,128)(2,1)}, bf16[256,768]{1,0:T(8,128)(2,1)S(1)}, u32[]{:S(2)}, u32[]{:S(2)}) collective-permute-start(bf16[256,768]{1,0:T(8,128)(2,1)} %get-tuple-element.146), channel_id=1, source_target_pairs={{0,1},{1,0},{2,3},{3,2},{4,5},{5,4},{6,7},{7,6},{8,9},{9,8},{10,11... | collective-permute-start | bytes 1179656 | tf_op jit(solution)/shard_map/ppermute | solution.py:1029
  156.2 1.9 collective-permute-start.14
  159.0 5.1 %copy-start.6 = (bf16[512,768]{1,0:T(8,128)(2,1)S(1)}, bf16[512,768]{1,0:T(8,128)(2,1)}, u32[]{:S(2)}) copy-start(bf16[512,768]{1,0:T(8,128)(2,1)} %refs_2_.5) | copy-start | bytes 2359300
  159.0 5.1 %copy-start.38 = (f32[768]{0:T(1024)S(1)}, f32[768]{0:T(1024)}, u32[]{:S(2)}) copy-start(f32[768]{0:T(1024)} %refs_3_.7) | copy-start | bytes 9220
  159.1 5.1 %copy-start.39 = (f32[256,768]{1,0:T(8,128)S(1)}, f32[256,768]{1,0:T(8,128)}, u32[]{:S(2)}) copy-start(f32[256,768]{1,0:T(8,128)} %get-tuple-element.147.refs_4_) | copy-start | bytes 2359300
  159.1 5.1 %copy-start.40 = (bf16[256,768]{1,0:T(8,128)(2,1)S(1)}, bf16[256,768]{1,0:T(8,128)(2,1)}, u32[]{:S(2)}) copy-start(bf16[256,768]{1,0:T(8,128)(2,1)} %get-tuple-element.145.refs_0_) | copy-start | bytes 1179652
  160.2 16.8 %collective-permute-start.18 = (bf16[192,1536]{1,0:T(8,128)(2,1)}, bf16[192,1536]{1,0:T(8,128)(2,1)S(1)}, u32[]{:S(2)}, u32[]{:S(2)}) collective-permute-start(bf16[192,1536]{1,0:T(8,128)(2,1)} %get-tuple-element.164), channel_id=1, source_target_pairs={{0,4},{4,0},{1,5},{5,1},{2,6},{6,2},{3,7},{7,3},{8,12},{12,8},{9,1... | collective-permute-start | bytes 1769480 | tf_op jit(solution)/shard_map/ppermute | solution.py:836
  163.7 17.2 %collective-permute-start.20 = (bf16[96,2048]{1,0:T(8,128)(2,1)}, bf16[96,2048]{1,0:T(8,128)(2,1)S(1)}, u32[]{:S(2)}, u32[]{:S(2)}) collective-permute-start(bf16[96,2048]{1,0:T(8,128)(2,1)} %get-tuple-element.170), channel_id=1, source_target_pairs={{0,8},{8,0},{1,9},{9,1},{2,10},{10,2},{3,11},{11,3},{4,12},{12,4},... | collective-permute-start | bytes 1179656 | tf_op jit(solution)/shard_map/ppermute | solution.py:836
  163.8 17.1 %collective-permute-start.21 = (bf16[96,1024]{1,0:T(8,128)(2,1)}, bf16[96,1024]{1,0:T(8,128)(2,1)S(1)}, u32[]{:S(2)}, u32[]{:S(2)}) collective-permute-start(bf16[96,1024]{1,0:T(8,128)(2,1)} %get-tuple-element.171), channel_id=1, source_target_pairs={{0,4},{4,0},{1,5},{5,1},{2,6},{6,2},{3,7},{7,3},{8,12},{12,8},{9,1... | collective-permute-start | bytes 589832 | tf_op jit(solution)/shard_map/ppermute | solution.py:836
  164.2 12.9 %copy-start.17 = (bf16[192,1536]{1,0:T(8,128)(2,1)S(1)}, bf16[192,1536]{1,0:T(8,128)(2,1)}, u32[]{:S(2)}) copy-start(bf16[192,1536]{1,0:T(8,128)(2,1)} %get-tuple-element.163.refs_0_) | copy-start | bytes 1769476
  164.2 16.7 %copy-start.18 = (bf16[96,3072]{1,0:T(8,128)(2,1)S(1)}, bf16[96,3072]{1,0:T(8,128)(2,1)}, u32[]{:S(2)}) copy-start(bf16[96,3072]{1,0:T(8,128)(2,1)} %get-tuple-element.169.refs_0_) | copy-start | bytes 1769476
  165.5 17.9 %all-to-all-start.5 = ((f32[32,2,48]{2,1,0:T(2,128)}), f32[32,2,48]{2,1,0:T(2,128)S(1)}, u32[]{:S(2)}, u32[]{:S(2)}) async-start(f32[32,2,48]{2,1,0:T(2,128)} %get-tuple-element.168), calls=%async_computation.5 | async-start | bytes 65536 | tf_op jit(solution)/shard_map/all_to_all | solution.py:1043
  169.0 21.5 %collective-permute-start.17 = (bf16[256,768]{1,0:T(8,128)(2,1)S(1)}, bf16[256,768]{1,0:T(8,128)(2,1)}, u32[]{:S(2)}, u32[]{:S(2)}) collective-permute-start(bf16[256,768]{1,0:T(8,128)(2,1)S(1)} %get-tuple-element.162.refs_0_), channel_id=1, source_target_pairs={{0,1},{1,0},{2,3},{3,2},{4,5},{5,4},{6,7},{7,6},{8,9},{9,8},{10,11... | collective-permute-start | bytes 1179656 | tf_op jit(solution)/shard_map/ppermute | solution.py:1038
  178.0 10.3 %collective-permute-start.19 = (bf16[96,1536]{1,0:T(8,128)(2,1)}, bf16[96,1536]{1,0:T(8,128)(2,1)S(1)}, u32[]{:S(2)}, u32[]{:S(2)}) collective-permute-start(bf16[96,1536]{1,0:T(8,128)(2,1)} %get-tuple-element.167), channel_id=1, source_target_pairs={{0,8},{8,0},{1,9},{9,1},{2,10},{10,2},{3,11},{11,3},{4,12},{12,4},... | collective-permute-start | bytes 884744 | tf_op jit(solution)/shard_map/ppermute | solution.py:836
  181.8 15.2 %collective-permute-start.23 = (bf16[48,2048]{1,0:T(8,128)(2,1)}, bf16[48,2048]{1,0:T(8,128)(2,1)S(1)}, u32[]{:S(2)}, u32[]{:S(2)}) collective-permute-start(bf16[48,2048]{1,0:T(8,128)(2,1)} %get-tuple-element.181), channel_id=1, source_target_pairs={{0,16},{16,0},{1,17},{17,1},{2,18},{18,2},{3,19},{19,3},{4,20},{20... | collective-permute-start | bytes 589832 | tf_op jit(solution)/shard_map/ppermute | solution.py:836
  181.9 10.6 %collective-permute-start.24 = (bf16[48,1024]{1,0:T(8,128)(2,1)}, bf16[48,1024]{1,0:T(8,128)(2,1)S(1)}, u32[]{:S(2)}, u32[]{:S(2)}) collective-permute-start(bf16[48,1024]{1,0:T(8,128)(2,1)} %get-tuple-element.182), channel_id=1, source_target_pairs={{0,8},{8,0},{1,9},{9,1},{2,10},{10,2},{3,11},{11,3},{4,12},{12,4},... | collective-permute-start | bytes 294920 | tf_op jit(solution)/shard_map/ppermute | solution.py:836
  190.0 9.5 %collective-permute-start.22 = (bf16[48,1536]{1,0:T(8,128)(2,1)}, bf16[48,1536]{1,0:T(8,128)(2,1)S(1)}, u32[]{:S(2)}, u32[]{:S(2)}) collective-permute-start(bf16[48,1536]{1,0:T(8,128)(2,1)} %get-tuple-element.179), channel_id=1, source_target_pairs={{0,16},{16,0},{1,17},{17,1},{2,18},{18,2},{3,19},{19,3},{4,20},{20... | collective-permute-start | bytes 442376 | tf_op jit(solution)/shard_map/ppermute | solution.py:836
  190.5 6.5 %copy-start.25 = (bf16[48,3072]{1,0:T(8,128)(2,1)S(1)}, bf16[48,3072]{1,0:T(8,128)(2,1)}, u32[]{:S(2)}) copy-start(bf16[48,3072]{1,0:T(8,128)(2,1)} %get-tuple-element.180.refs_0_) | copy-start | bytes 884740
  190.5 9.0 %copy-start.30 = (bf16[48,1536]{1,0:T(8,128)(2,1)S(1)}, bf16[48,1536]{1,0:T(8,128)(2,1)}, u32[]{:S(2)}) copy-start(bf16[48,1536]{1,0:T(8,128)(2,1)} %get-tuple-element.178.refs_0_) | copy-start | bytes 442372
  (11 other events, 12.9 us)

commit v5 on v4

--- a/solution.py
+++ b/solution.py
@@ -37,7 +37,7 @@
 WHOLE = pl.BlockSpec(memory_space=pltpu.VMEM)
 UNREAD = pl.BlockSpec(memory_space=pltpu.HBM)
 TOKEN = ((8, C), F32)
-MAIN = ("turn", "attend_back", "first_back", "last", "join")
+MAIN = ("turn", "grad_sums", "first_back", "last", "join")
 LONG, SHORT = 40 * 10**9, 10**6
 
 
@@ -46,7 +46,7 @@
 
 
 def call(
-    kernel, outs, *args, scratch=(), flops=0, extra=6, name=None, specs=None, after=(), token=False, grid=(1,),
+    kernel, outs, *args, scratch=(), flops=0, extra=6, name=None, specs=None, after=(), token=False, grid=(1,), aliases=None,
 ):
     inside, outside = specs or ([WHOLE] * len(args), [WHOLE] * len(outs))
     inside = list(inside) + [UNREAD] * len(after)
@@ -83,6 +83,7 @@
         compiler_params=pltpu.CompilerParams(vmem_limit_bytes=room + extra * 2**20),
         cost_estimate=pl.CostEstimate(flops=LONG if name in MAIN else SHORT, bytes_accessed=1, transcendentals=0),
         name=name,
+        input_output_aliases=aliases or {},
         **({"grid": grid} if specs else {}),
     )(*(pin(v) if spec is UNREAD else v for v, spec in zip((*args, *after), inside)))
 
@@ -476,7 +477,7 @@
 
 
 def attend_back_kernel(*refs):
-    sums, (cgrad_ref, vec_ref, send_ref, recv_ref, total_ref, fin_ref, sems) = refs[3:-7], refs[-7:]
+    sums, (cgrad_ref, vec_ref, send_out, send_ref, recv_ref, total_ref, fin_ref, sems, out_sems) = refs[3:-9], refs[-9:]
     copies = [send(v, t, sems.at[i]) for i, (v, t) in enumerate(zip(refs[:3], (recv_ref, total_ref, fin_ref)))]
     total = sums[0][...].astype(F32)
     for r in sums[1:]:
@@ -512,97 +513,76 @@
     cgrad_ref[C : C + HD, :] = jnp.where(
         left_half((HD, C)), single[0:HD], roll_half(single[HD:C])
     ).astype(BF16)
+    sent = []
     for n, (lhs, rhs) in enumerate((
         (score_grads[0:2], centroids[0:2]),
         (probs[0:2], grads[0:2]),
         ((score_grads[2], probs[2]), (centroids[2], grads[2])),
     )):
         made = dot_tn(jnp.concatenate(lhs, axis=0), jnp.concatenate(rhs, axis=0))
-        send_ref[:, :, n * C : (n + 1) * C] = made.astype(BF16).reshape(SUB, C, C)
+        send_ref[n] = made.astype(BF16).reshape(SUB, C, C)
+        sent.append(send(send_ref.at[n], send_out.at[:, :, (2 + n) * C : (3 + n) * C], out_sems.at[n]))
+    for copy in sent:
+        copy.wait()
 
 
 def finish_back_kernel(*refs):
-    total_ref, vec_ref, cgrads, (send_out, send_ref, sems) = refs[0], refs[1], refs[2:-3], refs[-3:]
+    total_ref, vec_ref, cgrads, (send_out, block_ref, sems) = refs[1], refs[2], refs[3:-3], refs[-3:]
     grad = cgrads[0][...].astype(F32)
     for r in cgrads[1:]:
         grad = grad + r[...].astype(F32)
     left = left_half((C, C))
-    short = left_half((HD, C))
     tail = total_ref[:, C : 2 * C]
     count = [jnp.maximum(tail[:, HD + i : HD + i + 1], 1.0) for i in range(3)]
     pair = grad[0:C] / jnp.where(left, count[0], count[1])
-    single = grad[C : C + HD] / jnp.where(short, count[2][0:HD], count[2][HD:C])
+    short = grad[C : C + HD]
+    single = jnp.concatenate([short, roll_half(short)], axis=0) / count[2]
     vec = vec_ref[...]
     high = vec.astype(BF16).astype(F32)
-    extra = jnp.concatenate([high, vec - high, jnp.zeros((8, C), F32)], axis=0)
-    send_ref[0:C, :] = pair.astype(BF16)
-    send_ref[C : C + HD, :] = single.astype(BF16)
-    send_ref[C + HD : PACK, :] = extra.astype(BF16)
-    copies = [send(send_ref, send_out.at[o], sems.at[o]) for o in range(SUB)]
+    rows = []
+    for v in (high, vec - high):
+        rows += [roll_half(v), v]
+    extra = jnp.concatenate(rows + [jnp.zeros((C - 16, C), F32)], axis=0)
+    block_ref[:, 0:C] = pair.astype(BF16)
+    block_ref[:, C : 2 * C] = jnp.where(left, single, extra).astype(BF16)
+    copies = [send(block_ref, send_out.at[o, :, 0 : 2 * C], sems.at[o]) for o in range(SUB)]
     for copy in copies:
         copy.wait()
 
 
-def gather_kernel(recv_ref, grads_ref):
+def first_back_kernel(
+    recv_ref, ids_ref, wq_src, wkv_src, grads_out, keep_out, give_out,
+    scr, wq_ref, wkv_ref, grads_ref, in_sems, out_sems,
+):
+    wkv_copy = send(wkv_src, wkv_ref, in_sems.at[0])
+    wq_copy = send(wq_src, wq_ref, in_sems.at[1])
     left = left_half((C, C))
-    width = grads_ref.shape[1] // 2
+    width = wq_ref.shape[1]
     for s in range(SEQS):
         rows = slice(s * C, (s + 1) * C)
+        columns = label_columns((ids_ref[:, rows],))
         blocks = [recv_ref[s * 2 + t] for t in range(2)]
-        tail = [b[:, 2 * C : 3 * C].astype(F32) for b in blocks]
-        k_mid = jnp.where(left, tail[0], roll_half(tail[1])).astype(BF16)
-        v_mid = jnp.where(left, roll_half(tail[0]), tail[1]).astype(BF16)
-        for n, mid in enumerate((k_mid, v_mid)):
-            base = n * width
-            first = n * C
+        q_tail = [b[:, C : 2 * C].astype(F32) for b in blocks]
+        kv_tail = [b[:, 4 * C : 5 * C].astype(F32) for b in blocks]
+        q_mid = jnp.where(left, q_tail[0], roll_half(q_tail[1])).astype(BF16)
+        k_mid = jnp.where(left, kv_tail[0], roll_half(kv_tail[1])).astype(BF16)
+        v_mid = jnp.where(left, roll_half(kv_tail[0]), kv_tail[1]).astype(BF16)
+        for p, pair in enumerate((blocks[0][:, 0:C], q_mid, blocks[1][:, 0:C])):
+            grads_ref[rows, p * C : (p + 1) * C] = spread_pair(columns, PAIRS[p], pair).astype(BF16)
+        for n, (first, mid) in enumerate(((2 * C, k_mid), (3 * C, v_mid))):
+            base = (n + 1) * width
             grads_ref[rows, base : base + C] = blocks[0][:, first : first + C]
             grads_ref[rows, base + C : base + 2 * C] = mid
             grads_ref[rows, base + 2 * C : base + 3 * C] = blocks[1][:, first : first + C]
-
-
-def kv_kernel(order, recv_ref, normed_src, kv_out, keep_out, give_out, kv_ref, normed_ref, scr, sems, out_sems):
-    copy = send(normed_src, normed_ref, sems.at[0])
-    gather_kernel(recv_ref, kv_ref)
-    kv_copy = send(kv_ref, kv_out, sems.at[1])
-    copy.wait()
-    scr[...] = dot_tn(normed_ref[...], kv_ref[...]).astype(BF16)
-    own = scr.shape[0] // 16
-    me = lax.axis_index("b0")
-    sent = [kv_copy]
-    for bit, out in ((1 - me, give_out), (me, keep_out)):
-        for j, place in enumerate(row_order(order)):
-            start = pl.multiple_of((place + bit) * own, 16)
-            sent.append(send(scr.at[pl.ds(start, own), :], out.at[j * own : (j + 1) * own, :], out_sems.at[len(sent) - 1]))
-    for copy in sent:
-        copy.wait()
-
-
-def first_back_kernel(
-    recv_ref, ids_ref, wq_src, wkv_src, kv_src, grads_out, keep_out, give_out,
-    scr, wq_ref, wkv_ref, kv_ref, grads_ref, in_sems, out_sems,
-):
-    kv_copies = [send(kv_src, kv_ref, in_sems.at[0]), send(wkv_src, wkv_ref, in_sems.at[1])]
-    wq_copy = send(wq_src, wq_ref, in_sems.at[2])
-    short = left_half((HD, C))
-    for s in range(SEQS):
-        rows = slice(s * C, (s + 1) * C)
-        columns = label_columns((ids_ref[:, rows],))
-        packs = [recv_ref[s * 2 + t] for t in range(2)]
-        tails = [v[C : C + HD].astype(F32) for v in packs]
-        first = [jnp.where(short, tails[0], roll_half(tails[1])), jnp.where(short, roll_half(tails[0]), tails[1])]
-        middle = jnp.concatenate(first, axis=0).astype(BF16)
-        for p, pair in enumerate((packs[0][0:C], middle, packs[1][0:C])):
-            grads_ref[rows, p * C : (p + 1) * C] = spread_pair(columns, PAIRS[p], pair).astype(BF16)
     copies = [send(grads_ref, grads_out, out_sems.at[0])]
-    for copy in kv_copies:
-        copy.wait()
+    wkv_copy.wait()
     wq_copy.wait()
     half = keep_out.shape[0]
     me = lax.axis_index("mp")
     for i, (bit, out) in enumerate(((1 - me, give_out), (me, keep_out))):
         rows = pl.ds(pl.multiple_of(bit * half, C), half)
         scr[i] = (
-            dot_nt(grads_ref[rows, :], wq_ref[...]) + dot_nt(kv_ref[rows, :], wkv_ref[...])
+            dot_nt(grads_ref[rows, 0:width], wq_ref[...]) + dot_nt(grads_ref[rows, width : 3 * width], wkv_ref[...])
         ).astype(BF16)
         copies.append(send(scr.at[i], out, out_sems.at[1 + i]))
     for copy in copies:
@@ -640,9 +620,11 @@
         copy.wait()
 
 
-def weight_kernel(orders, counts, *refs):
+def weight_kernel(orders, counts, parts, *refs):
     n = sum(counts) * 2
-    pairs, (keep_out, give_out, scr), held, (in_sems, out_sems) = refs[:n], refs[n : n + 3], refs[n + 3 : -2], refs[-2:]
+    pairs, keep_out, gives, scr = refs[:n], refs[n], refs[n + 1 : n + 1 + parts], refs[n + 1 + parts]
+    held, (in_sems, out_sems) = refs[n + 2 + parts : -2], refs[-2:]
+    region = 0
     copies = []
     for i, (source, target) in enumerate(zip(pairs, held)):
         if source.shape[0] != target.shape[0]:
@@ -666,13 +648,15 @@
         spread = base
         for wide, places in order:
             part = slice(spread, spread + wide)
-            for bit, out in ((1 - me, give_out), (me, keep_out)):
+            give = (gives[0], part) if parts == 1 else (gives[region], slice(0, wide))
+            for bit, (out, inner) in ((1 - me, give), (me, (keep_out, part))):
                 for j, place in enumerate(row_order(places)):
                     start = pl.multiple_of((place + bit) * own, 16)
                     sent.append(send(
-                        scr.at[pl.ds(start, own), part], out.at[j * own : (j + 1) * own, part], out_sems.at[len(sent)]
+                        scr.at[pl.ds(start, own), part], out.at[j * own : (j + 1) * own, inner], out_sems.at[len(sent)]
                     ))
             spread += wide
+            region += 1
         base += width
         spot += 2 * count
     for copy in sent:
@@ -697,11 +681,13 @@
         ranges.append(lanes)
         base += width
         got, inner = (gots[i], slice(0, width)) if came == len(widths) else (gots[0], lanes)
-        me = lax.axis_index(axes[i])
+        me = lax.axis_index(axes[min(i, len(axes) - 1)])
         for bit, out in ((1 - me, give_scr), (me, keep_scr)):
             rows = pl.ds(pl.multiple_of(bit * half, 16), half)
             out[:, lanes] = (keep_ref[rows, lanes].astype(F32) + got[rows, inner].astype(F32)).astype(BF16)
     copies = [send(keep_scr, keep_out, sems.at[0])]
+    if len(gives) == 1:
+        ranges = [slice(0, base)]
     for i, (lanes, give) in enumerate(zip(ranges, gives)):
         copies.append(send(give_scr.at[:, lanes], give, sems.at[1 + i]))
     for copy in copies:
@@ -724,11 +710,12 @@
         copy.wait()
 
 
-def vector_kernel(recv_ref, five_ref, out_ref, small_ref):
+def vector_kernel(recv_ref, four_ref, out_ref, small_ref):
     out_ref[...] = jnp.sum(recv_ref[...], axis=0)
     for o in range(SUB):
-        block = five_ref[o, C + HD : PACK, :].astype(F32)
-        small_ref[4 * o : 4 * o + 4, :] = block[0:4] + block[4:8]
+        block = four_ref[o, 0:16, C : 2 * C].astype(F32)
+        block = block[0:8] + block[8:16]
+        small_ref[4 * o : 4 * o + 4, :] = jnp.where(left_half((4, C)), roll_half(block[0:4]), block[4:8])
 
 
 def close_kernel(keep_ref, *refs):
@@ -796,7 +783,7 @@
 
     simple = groups != 2 or own % 16
 
-    def weight_terms(orders, name, *sides, after=()):
+    def weight_terms(orders, name, *sides, after=(), parts=1):
         counts = tuple(len(side) for side in sides)
         flat = [v for side in sides for pair in side for v in pair]
         columns = sum(side[0][1].shape[1] for side in sides)
@@ -810,15 +797,16 @@
                 name=name, after=after, token=True,
             )
             return (part,), token
-        keep, give, token = call(
-            functools.partial(weight_kernel, orders, counts), [((model // 2, columns), BF16)] * 2, *flat,
+        keep, *gives, token = call(
+            functools.partial(weight_kernel, orders, counts, parts),
+            [((model // 2, columns), BF16)] + [((model // 2, columns // parts), BF16)] * parts, *flat,
             name=name, after=after, token=True,
             scratch=[pltpu.VMEM((model, columns), BF16)]
             + [pltpu.VMEM((r, v.shape[1]), BF16) for r, v in zip(rows, flat)]
             + [pltpu.SemaphoreType.DMA((len(flat),)), pltpu.SemaphoreType.DMA((16 * sum(map(len, orders)),))],
-            specs=([UNREAD] * len(flat), [UNREAD] * 2),
+            specs=([UNREAD] * len(flat), [UNREAD] * (1 + parts)),
         )
-        return (keep, [give]), token
+        return (keep, gives), token
 
     def fold(axes, parts, terms, name, after=(), widths=None):
         if simple:
@@ -833,15 +821,15 @@
                 return pieces, None
             return terms, None
         keep, gives = terms
-        gots = [lax.ppermute(give, axis, SWAP) for give, axis in zip(gives, axes)]
+        gots = [lax.ppermute(give, axes[min(i, len(axes) - 1)], SWAP) for i, give in enumerate(gives)]
         rows, columns = keep.shape
         if not parts:
             *pieces, token = call(
                 close_kernel, [((rows,) + w, F32) for w in widths], keep, *gots, name=name, after=after, token=True
             )
             return pieces, token
-        widths = widths or [columns]
-        outs = [((rows // 2, w), BF16) for w in [columns] + widths]
+        widths = widths or [v.shape[1] for v in gots]
+        outs = [((rows // 2, w), BF16) for w in [columns] + (widths if len(parts) > 1 else [columns])]
         keep, *gives, token = call(
             functools.partial(fold_kernel, parts, len(gots), widths), outs, keep, *gots, name=name, after=after, token=True,
             scratch=[pltpu.VMEM((rows // 2, columns), BF16)] * 2 + [pltpu.SemaphoreType.DMA((len(outs),))],
@@ -933,11 +921,9 @@
     bias_part, residual, back, attended, normed_two, active, hidden_grad = zip(*halves)
     back_other = [other(v) for v in back]
     order = ("b1", "b2", "g")
-    ff_widths = [hidden + hidden // 3, hidden - hidden // 3]
-    ff_terms, ff_token = weight_terms(
-        ([(hidden, order)], [(hidden // 3, order), (hidden - hidden // 3, ("g", "b1", "b2"))]), "ff_terms",
-        list(zip(normed_two, hidden_grad)), [(bg, v) for v in active],
-    )
+    down_order = ("b2", "b1", "g")
+    up_terms, up_token = weight_terms(([(hidden, order)],), "up_terms", list(zip(normed_two, hidden_grad)))
+    down_terms, down_token = weight_terms(([(hidden, down_order)],), "down_terms", [(bg, v) for v in active])
     residual_grad, mixed_grad, send_three, turned = call(
         turn_kernel,
         [((half, model), F32), ((tokens, model), BF16), ((SUB, PACK, C), BF16)],
@@ -948,7 +934,7 @@
         ],
         specs=([WHOLE] * 12, [UNREAD] * 3),
         flops=2 * tokens * model * width, name="turn",
-        after=[ff_token], token=True,
+        after=[up_token, down_token], token=True,
     )
     recv_three = lax.all_to_all(send_three, NEAR, 0, 0)
     branches = [
@@ -958,104 +944,90 @@
         )
         for v in active
     ]
-    ff_terms, ff_token = fold(
-        ("b0",), ("b1", "g"), ff_terms, "ff_fold", after=[b[1] for b in branches], widths=ff_widths
-    )
+    up_terms, up_token = fold(("b0",), ("b1",), up_terms, "up_fold", after=[b[1] for b in branches])
     branch = [b[0] for b in branches]
     branch_other = [other(b) for b in branch]
     grad_sums, summed = call(
         grad_sum_kernel, [((PACK, C), BF16)], recv_three, name="grad_sums",
-        after=tokens_of(ff_token, branches[0][1], branches[1][1]), token=True,
+        after=tokens_of(up_token, branches[0][1], branches[1][1]), token=True,
     )
     grad_sums = across(grad_sums)
+    out_terms, out_token = weight_terms(
+        ([(width, down_order)],), "out_terms", [(mixed_grad, v) for v in attended], after=[summed]
+    )
     cgrad, vec, send_four, attended_back = call(
         attend_back_kernel,
-        [((C + HD, C), BF16), ((4, C), F32), ((SUB, C, 3 * C), BF16)],
+        [((C + HD, C), BF16), ((4, C), F32), ((SUB, C, 5 * C), BF16)],
         recv_one, total, fin, *grad_sums, flops=2 * 5 * 3 * C * SUB * C * C, name="attend_back",
         scratch=[
+            pltpu.VMEM((3, SUB, C, C), BF16),
             pltpu.VMEM((SUB, C, 5 * C), BF16), pltpu.VMEM((C, 2 * C), F32), pltpu.VMEM((C, 2 * C), F32),
-            pltpu.SemaphoreType.DMA((3,)),
+            pltpu.SemaphoreType.DMA((3,)), pltpu.SemaphoreType.DMA((3,)),
         ],
-        specs=([UNREAD] * 3 + [WHOLE] * len(grad_sums), [WHOLE] * 3), after=[branch_other[0]],
+        specs=([UNREAD] * 3 + [WHOLE] * len(grad_sums), [WHOLE] * 2 + [UNREAD]), after=[out_token],
         token=True,
     )
+    cgrads = across(cgrad)
+    up_terms, up_token = fold(("b1",), ("b2",), up_terms, "up_fold", after=[attended_back])
+    send_four, finished = call(
+        finish_back_kernel, [((SUB, C, 5 * C), BF16)], send_four, total, vec, *cgrads, name="finish_back",
+        aliases={0: 0}, token=True, after=tokens_of(up_token, branch_other[0]),
+        scratch=[pltpu.VMEM((C, 2 * C), BF16), pltpu.SemaphoreType.DMA((SUB,))],
+        specs=([UNREAD] + [WHOLE] * (2 + len(cgrads)), [UNREAD]),
+    )
     recv_four = lax.all_to_all(send_four, NEAR, 0, 0)
-    cgrads = across(cgrad)
-    out_terms, out_token = weight_terms(
-        ([(width, order)],), "out_terms", [(mixed_grad, v) for v in attended], after=[attended_back]
-    )
-    send_five, finished = call(
-        finish_back_kernel, [((SUB, PACK, C), BF16)], total, vec, *cgrads, name="finish_back",
-        after=[out_token, branch_other[1]], token=True,
-        scratch=[pltpu.VMEM((PACK, C), BF16), pltpu.SemaphoreType.DMA((SUB,))],
-        specs=([WHOLE] * (2 + len(cgrads)), [UNREAD]),
-    )
-    recv_five = lax.all_to_all(send_five, NEAR, 0, 0)
-    if simple:
-        (kv_grads,) = call(gather_kernel, [((tokens, 2 * width), BF16)], recv_four, name="gather")
-        kv_terms, kv_token = weight_terms(None, "kv_terms", [(normed_one, kv_grads)])
-    else:
-        kv_grads, kv_keep, kv_give, kv_token = call(
-            functools.partial(kv_kernel, order),
-            [((tokens, 2 * width), BF16)] + [((model // 2, 2 * width), BF16)] * 2, recv_four, normed_one,
-            name="kv_terms", after=[finished], token=True,
-            scratch=[
-                pltpu.VMEM((tokens, 2 * width), BF16), pltpu.VMEM((tokens, model), BF16),
-                pltpu.VMEM((model, 2 * width), BF16), pltpu.SemaphoreType.DMA((2,)), pltpu.SemaphoreType.DMA((16,)),
-            ],
-            specs=([WHOLE, UNREAD], [UNREAD] * 3),
-        )
-        kv_terms = (kv_keep, [kv_give])
     pieces = [v for three in zip(residual, branch, branch_other) for v in three]
     block_output, output_token = call(
-        output_kernel, [((tokens, model), BF16)], *pieces, down_bias, name="output", after=tokens_of(kv_token), token=True,
+        output_kernel, [((tokens, model), BF16)], *pieces, down_bias, name="output", after=tokens_of(finished), token=True,
         scratch=[pltpu.VMEM(v.shape, v.dtype) for v in pieces]
         + [pltpu.VMEM((2, half, model), BF16), pltpu.SemaphoreType.DMA((6,)), pltpu.SemaphoreType.DMA((2,))],
         specs=([UNREAD] * 6 + [WHOLE], [UNREAD]),
     )
-    q_grads, keep, give, first_token = call(
+    down_terms, down_token = fold_many(("b0",), "b2", (down_terms, out_terms), "down_fold", after=[output_token])
+    qkv_grads, keep, give, first_token = call(
         first_back_kernel,
-        [((tokens, width), BF16), ((half, model), BF16), ((half, model), BF16)],
-        recv_five, cluster_ids, query_weight, wkv, kv_grads,
+        [((tokens, 3 * width), BF16), ((half, model), BF16), ((half, model), BF16)],
+        recv_four, cluster_ids, query_weight, wkv,
         scratch=[
             pltpu.VMEM((2, half, model), BF16), pltpu.VMEM((model, width), BF16), pltpu.VMEM((model, 2 * width), BF16),
-            pltpu.VMEM((tokens, 2 * width), BF16), pltpu.VMEM((tokens, width), BF16),
-            pltpu.SemaphoreType.DMA((3,)), pltpu.SemaphoreType.DMA((3,)),
+            pltpu.VMEM((tokens, 3 * width), BF16), pltpu.SemaphoreType.DMA((2,)), pltpu.SemaphoreType.DMA((3,)),
         ],
-        specs=([WHOLE] * 2 + [UNREAD] * 3, [UNREAD] * 3),
+        specs=([WHOLE] * 2 + [UNREAD] * 2, [UNREAD] * 3),
         flops=2 * tokens * model * 3 * width, name="first_back",
-        after=tokens_of(kv_token, output_token), token=True,
+        after=tokens_of(output_token, down_token), token=True,
     )
     got = other(give)
-    q_terms, q_token = weight_terms(([(width, order)],), "q_terms", [(normed_one, q_grads)], after=[first_token])
-    kv_terms, kv_token = fold_many(("b0",), "b1", (kv_terms, out_terms, q_terms), "kv_fold", after=[q_token])
-    ff_terms, ff_token = fold(("b1", "g"), ("b2", "b1"), ff_terms, "ff_fold", after=tokens_of(kv_token, q_token), widths=ff_widths)
+    kv_terms, kv_token = weight_terms(
+        ([(width, order)] * 3,), "qkv_terms", [(normed_one, qkv_grads)], after=[first_token], parts=3
+    )
+    kv_terms, kv_token = fold(("b0",), ("b1",), kv_terms, "qkv_fold", after=[kv_token])
+    down_terms, down_token = fold(("b2",), ("b1",), down_terms, "down_fold", after=tokens_of(kv_token))
     grad_half, vec_one, last_token = call(
         last_kernel, [((half, model), BF16), ((2 * devices, 2, own), F32)],
         keep, got, inputs, norm_one_gain, residual_grad, name="last",
-        after=tokens_of(kv_token, ff_token), token=True,
+        after=tokens_of(kv_token), token=True,
     )
     grad_other = other(grad_half)
-    kv_terms, kv_token = fold(("b1",), ("b2",), kv_terms, "kv_fold", after=[last_token])
-    ff_terms, ff_token = fold(
-        ("b2", "b1"), ("g", "b2"), ff_terms, "ff_fold", after=tokens_of(kv_token), widths=ff_widths
-    )
+    up_terms, up_token = fold(("b2",), ("g",), up_terms, "up_fold", after=[last_token])
+    kv_terms, kv_token = fold(("b1",), ("b2",), kv_terms, "qkv_fold", after=tokens_of(up_token))
     vec_recv = lax.all_to_all(vec_one, SEQ + ("mp",), 0, 0, tiled=True)
     vec_sum, small, vec_token = call(
-        vector_kernel, [((2, own), F32), ((4 * SUB, C), F32)], vec_recv, recv_five, name="vectors",
-        after=tokens_of(ff_token), token=True,
-    )
-    kv_terms, kv_token = fold(("b2",), ("g",), kv_terms, "kv_fold", after=[vec_token])
+        vector_kernel, [((2, own), F32), ((4 * SUB, C), F32)], vec_recv, recv_four, name="vectors",
+        after=tokens_of(kv_token), token=True,
+    )
+    down_terms, down_token = fold(("b1",), ("g",), down_terms, "down_fold", after=[vec_token])
+    kv_terms, kv_token = fold(("b2",), ("g",), kv_terms, "qkv_fold", after=tokens_of(down_token))
     input_grad, join_token = call(
         join_kernel, [((tokens, model), BF16)], grad_half, grad_other, name="join",
         after=tokens_of(kv_token, vec_token), token=True, scratch=[pltpu.SemaphoreType.DMA((2,))],
         specs=([WHOLE] * 2, [UNREAD]),
     )
-    (up_sum, down_sum), ff_token = fold(
-        ("g", "b2"), (), ff_terms, "ff_close", after=[join_token], widths=[(hidden,), (hidden,)]
-    )
-    (kv_sum, out_sum, q_sum), kv_token = fold(
-        ("g",), (), kv_terms, "kv_close", after=tokens_of(ff_token), widths=[(2, width), (width,), (width,)]
+    (up_sum,), up_token = fold(("g",), (), up_terms, "up_close", after=[join_token], widths=[(hidden,)])
+    (down_sum, out_sum), down_token = fold(
+        ("g",), (), down_terms, "down_close", after=tokens_of(up_token), widths=[(hidden,), (width,)]
+    )
+    (q_sum, kv_sum), kv_token = fold(
+        ("g",), (), kv_terms, "qkv_close", after=tokens_of(down_token), widths=[(width,), (2, width)]
     )
 
     small = small.reshape(-1)

time: 201 us -> 195 us (0.970)
  waiting for transfers between devices: 67.3 us -> 61.7 us
  local copies, waits for them, and re-layouts: 9.14 us -> 6.23 us
  Pallas kernels: 64.6 us -> 67.2 us
    ppermute x10 -> x13, starting transfers between devices: 8.21 us -> 14.8 us  [fold(): lax.ppermute(give, axes[min(i, len(axes) - 1)], SWAP)]
    ppermute x10 -> x13, waiting for transfers between devices: 18.3 us -> 12.3 us  [fold(): lax.ppermute(give, axes[min(i, len(axes) - 1)], SWAP)]
    all_to_all x1 -> x0, starting transfers between devices: 5.29 us -> none  [on_device(): recv_five = lax.all_to_all(send_five, NEAR, 0, 0)]
    ppermute x2, waiting for transfers between devices: 5.95 us -> 10.6 us  [on_device(): branch_other = [other(b) for b in branch]]
    unnamed x89 -> x99, local copies, waits for them, and re-layouts: 7.43 us -> 4.52 us
    ppermute x2, waiting for transfers between devices: 5.63 us -> 2.78 us  [on_device(): back_other = [other(v) for v in back]]
    pallas_call x29 -> x33, Pallas kernels: 64.6 us -> 67.2 us  [call(): pl.pallas_call(body, out_shape=[pltpu.HBM(s, d) if spec is UNREAD else ja...]
  transfers between devices with their start and end apart: 31 -> 32, of which waited for: 17 -> 17; matrix products, arithmetic and copies ran while one was open for 1% -> 2% of each run, Pallas kernels for 24% -> 28%
where the time goes in v5:
time: 195 us; the launch traced here: 194 us
  Pallas kernels  67.2 us (34%)
  waiting for transfers between devices  61.7 us (32%)
  starting transfers between devices  56 us (29%)
  local copies, waits for them, and re-layouts  6.23 us (3%)
    pallas_call x33, Pallas kernels, call(): pl.pallas_call(body, out_shape=[pltpu.HBM(s, d) if spec is UNREAD else ja...  67.2 us
    ppermute x13, starting transfers between devices, fold(): lax.ppermute(give, axes[min(i, len(axes) - 1)], SWAP)  14.8 us
    ppermute x1, waiting for transfers between devices, on_device(): ids_other = other(cluster_ids)  14 us
    ppermute x13, waiting for transfers between devices, fold(): lax.ppermute(give, axes[min(i, len(axes) - 1)], SWAP)  12.3 us
    all_to_all x1, waiting for transfers between devices, on_device(): recv_two = lax.all_to_all(send_two, NEAR + ('mp',), 0, 0)  11.8 us
    ppermute x2, waiting for transfers between devices, on_device(): branch_other = [other(b) for b in branch]  10.6 us
    ppermute x4, starting transfers between devices, across(): return [v, lax.ppermute(v, 'g', SWAP)]  10.5 us
    ppermute x4, waiting for transfers between devices, across(): return [v, lax.ppermute(v, 'g', SWAP)]  7.02 us
  transfers between devices with their start and end apart: 32, of which 17 were waited for; matrix products, arithmetic and copies ran while one was open for 2% of the time, Pallas kernels for 28%

profile of v5, /device:TPU:0, one launch (start us, length us, event | category | flops | bytes accessed | tf_op | source)
XLA Modules:
  0.0 194.0 jit_solution(14933666514722710775)
XLA Ops:
  0.7 1.6 copy.29
  2.4 3.0 %project.1 = (bf16[512,768]{1,0:T(8,128)(2,1)}, bf16[8,128,640]{2,1,0:T(8,128)(2,1)}) custom-call(bf16[512,768]{1,0:T(8,128)(2,1)S(1)} %copy-done.4, f32[768]{0:T(1024)S(1)} %copy-done.38, f32[768]{0:T(1024)S(1)} %copy-done.36, bf16[768,384]{1,0:T(8,128)(2,1)S(1)} %copy-done.17, bf16[768,768]{1,0:T(8,128)(2,1)S(1)} %bitcast.11, s32[6,512]{1,0:T(8,128)S(1)} %copy-done.28), custom_call_target="tpu_custom_call" | custom-call | flops 1000000 | bytes 1 | tf_op jit(solution)/shard_map/project/pallas_call | solution.py:74
  5.4 5.4 %all-to-all-start = ((bf16[8,128,640]{2,1,0:T(8,128)(2,1)}), bf16[8,128,640]{2,1,0:T(8,128)(2,1)S(1)}, u32[]{:S(2)}, u32[]{:S(2)}) async-start(bf16[8,128,640]{2,1,0:T(8,128)(2,1)} %get-tuple-element.110), calls=%async_computation | async-start | bytes 2621440 | tf_op jit(solution)/shard_map/all_to_all | solution.py:873
  10.8 1.6 collective-permute-start.1
  12.9 14.0 %collective-permute-done.refs_1_.refs_2_ = s32[6,512]{1,0:T(8,128)S(1)} collective-permute-done((s32[6,512]{1,0:T(8,128)S(1)}, s32[6,512]{1,0:T(8,128)S(1)}, u32[]{:S(2)}, u32[]{:S(2)}) %collective-permute-start) | collective-permute-done | bytes 12320 | tf_op jit(solution)/shard_map/ppermute | solution.py:857
  26.9 1.2 all-to-all-done.refs_0_
  28.2 2.6 %collective-permute-start.2 = (bf16[128,256]{1,0:T(8,128)(2,1)S(1)}, bf16[128,256]{1,0:T(8,128)(2,1)S(1)}, u32[]{:S(2)}, u32[]{:S(2)}) collective-permute-start(bf16[128,256]{1,0:T(8,128)(2,1)S(1)} %query_sums.1.refs_1_), channel_id=1, source_target_pairs={{0,16},{16,0},{1,17},{17,1},{2,18},{18,2},{3,19},{19,3},{4,20},{20... | collective-permute-start | bytes 196616 | tf_op jit(solution)/shard_map/ppermute | solution.py:780
  30.9 2.6 %collective-permute-done.2.refs_2_ = bf16[128,256]{1,0:T(8,128)(2,1)S(1)} collective-permute-done((bf16[128,256]{1,0:T(8,128)(2,1)S(1)}, bf16[128,256]{1,0:T(8,128)(2,1)S(1)}, u32[]{:S(2)}, u32[]{:S(2)}) %collective-permute-start.2) | collective-permute-done | bytes 65568 | tf_op jit(solution)/shard_map/ppermute | solution.py:780
  33.5 1.8 attend.1
  35.4 2.7 %collective-permute-start.3 = (bf16[128,256]{1,0:T(8,128)(2,1)S(1)}, bf16[128,256]{1,0:T(8,128)(2,1)S(1)}, u32[]{:S(2)}, u32[]{:S(2)}) collective-permute-start(bf16[128,256]{1,0:T(8,128)(2,1)S(1)} %get-tuple-element.111.refs_0_), channel_id=1, source_target_pairs={{0,16},{16,0},{1,17},{17,1},{2,18},{18,2},{3,19},{19,3},{4,20},{20... | collective-permute-start | bytes 196616 | tf_op jit(solution)/shard_map/ppermute | solution.py:780
  38.0 2.6 %collective-permute-done.3.refs_1_ = bf16[128,256]{1,0:T(8,128)(2,1)S(1)} collective-permute-done((bf16[128,256]{1,0:T(8,128)(2,1)S(1)}, bf16[128,256]{1,0:T(8,128)(2,1)S(1)}, u32[]{:S(2)}, u32[]{:S(2)}) %collective-permute-start.3) | collective-permute-done | bytes 65568 | tf_op jit(solution)/shard_map/ppermute | solution.py:780
  40.6 1.5 merge.1
  42.1 5.2 %all-to-all-start.1 = ((bf16[16,192,128]{2,1,0:T(8,128)(2,1)}), bf16[16,192,128]{2,1,0:T(8,128)(2,1)S(1)}, u32[]{:S(2)}, u32[]{:S(2)}) async-start(bf16[16,192,128]{2,1,0:T(8,128)(2,1)} %get-tuple-element.112), calls=%async_computation.1 | async-start | bytes 1572864 | tf_op jit(solution)/shard_map/all_to_all | solution.py:893
  47.4 1.3 broadcast_multiply_fusion.refs_7_.refs_0_.refs_2_
  48.7 11.8 %all-to-all-done.1.refs_0_ = bf16[16,192,128]{2,1,0:T(8,128)(2,1)S(1)} async-done(((bf16[16,192,128]{2,1,0:T(8,128)(2,1)}), bf16[16,192,128]{2,1,0:T(8,128)(2,1)S(1)}, u32[]{:S(2)}, u32[]{:S(2)}) %all-to-all-start.1) | async-done | bytes 786464 | tf_op jit(solution)/shard_map/all_to_all | solution.py:893
  60.5 5.5 %middle.3 = (f32[1,1536]{1,0:T(1,128)S(1)}, f32[256,768]{1,0:T(8,128)S(1)}, bf16[256,768]{1,0:T(8,128)(2,1)S(1)}, bf16[256,384]{1,0:T(8,128)(2,1)}, bf16[256,768...) custom-call(bf16[16,192,128]{2,1,0:T(8,128)(2,1)S(1)} %all-to-all-done.1.refs_0_, ...), custom_call_target="tpu_custom_call" | custom-call | flops 1000000 | bytes 1 | tf_op jit(solution)/shard_map/middle/pallas_call | solution.py:74
  66.7 5.5 %middle.2 = (f32[1,1536]{1,0:T(1,128)S(1)}, f32[256,768]{1,0:T(8,128)S(1)}, bf16[256,768]{1,0:T(8,128)(2,1)S(1)}, bf16[256,384]{1,0:T(8,128)(2,1)}, bf16[256,768...) custom-call(bf16[16,192,128]{2,1,0:T(8,128)(2,1)S(1)} %all-to-all-done.1.refs_0_, ...), custom_call_target="tpu_custom_call" | custom-call | flops 1000000 | bytes 1 | tf_op jit(solution)/shard_map/middle/pallas_call | solution.py:74
  72.2 1.5 collective-permute-start.4
  73.7 4.6 %up_terms.1 = (bf16[384,1536]{1,0:T(8,128)(2,1)}, bf16[384,1536]{1,0:T(8,128)(2,1)}, f32[8,128]{1,0:T(8,128)}) custom-call(bf16[256,768]{1,0:T(8,128)(2,1)} %get-tuple-element.120.refs_0_, bf16[256,1536]{1,0:T(8,128)(2,1)} %get-tuple-element.121.refs_1_, bf16[256,768]{1,0:T(8,128)(2,1)} %get-tuple-element.122.refs_2_, ...), custom_call_target="tpu_custom_call" | custom-call | flops 1000000 | bytes 1 | tf_op jit(solution)/shard_map/up_terms/pallas_call | solution.py:74
  78.4 4.7 %down_terms.1 = (bf16[384,1536]{1,0:T(8,128)(2,1)}, bf16[384,1536]{1,0:T(8,128)(2,1)}, f32[8,128]{1,0:T(8,128)}) custom-call(bf16[512,768]{1,0:T(8,128)(2,1)} %copy-done.2, bf16[256,1536]{1,0:T(8,128)(2,1)} %get-tuple-element.114.refs_1_.refs_0_, bf16[512,768]{1,0:T(8,128)(2,1)} %copy-done.2, bf16[256,1536]{1,0:T(8,128)(2,1)} %get-tuple-element.125.refs_3_.refs_0_), custom_call_target="tpu_custom_call" | custom-call | flops 1000000 | bytes 1 | tf_op jit(solution)/shard_map/down_terms/pallas_call | solution.py:74
  83.2 2.8 %collective-permute-done.4.refs_2_ = bf16[256,768]{1,0:T(8,128)(2,1)S(1)} collective-permute-done((bf16[256,768]{1,0:T(8,128)(2,1)S(1)}, bf16[256,768]{1,0:T(8,128)(2,1)S(1)}, u32[]{:S(2)}, u32[]{:S(2)}) %collective-permute-start.4) | collective-permute-done | bytes 393248 | tf_op jit(solution)/shard_map/ppermute | solution.py:922
  86.0 3.7 %turn.1 = (f32[256,768]{1,0:T(8,128)}, bf16[512,768]{1,0:T(8,128)(2,1)}, bf16[8,208,128]{2,1,0:T(8,128)(2,1)}, f32[8,128]{1,0:T(8,128)}) custom-call(bf16[256,768]{1,0:T(8,128)(2,1)S(1)} %get-tuple-element.115.refs_0_, bf16[256,768]{1,0:T(8,128)(2,1)S(1)} %get-tuple-element.116.refs_1_, bf16[256,768]{1,0:T(8,128)(2,1)S(1)} %collective-permute-done.4.refs_2_, ...), custom_call_target="tpu_custom_call" | custom-call | flops 40000000000 | bytes 1 | tf_op jit(solution)/shard_map/turn/pallas_call | solution.py:74
  89.8 4.3 %all-to-all-start.2 = ((bf16[8,208,128]{2,1,0:T(8,128)(2,1)}), bf16[8,208,128]{2,1,0:T(8,128)(2,1)}, u32[]{:S(2)}, u32[]{:S(2)}) async-start(bf16[8,208,128]{2,1,0:T(8,128)(2,1)} %get-tuple-element.132), calls=%async_computation.2 | async-start | bytes 851968 | tf_op jit(solution)/shard_map/all_to_all | solution.py:939
  94.0 0.8 branch.2
  95.5 0.8 branch.3
  96.3 2.6 %up_fold.3 = (bf16[192,1536]{1,0:T(8,128)(2,1)}, bf16[192,1536]{1,0:T(8,128)(2,1)}, f32[8,128]{1,0:T(8,128)}) custom-call(bf16[384,1536]{1,0:T(8,128)(2,1)S(1)} %copy-done.12, bf16[384,1536]{1,0:T(8,128)(2,1)} %collective-permute-done.8.refs_1_, f32[8,128]{1,0:T(8,128)} %get-tuple-element.135.refs_2_, f32[8,128]{1,0:T(8,128)} %get-tuple-element.136.refs_3_), custom_call_target="tpu_custom_call" | custom-call | flops 1000000 | bytes 1 | tf_op jit(solution)/shard_map/up_fold/pallas_call | solution.py:74
  98.9 1.9 %collective-permute-start.11 = (bf16[192,1536]{1,0:T(8,128)(2,1)}, bf16[192,1536]{1,0:T(8,128)(2,1)S(1)}, u32[]{:S(2)}, u32[]{:S(2)}) collective-permute-start(bf16[192,1536]{1,0:T(8,128)(2,1)} %get-tuple-element.148), channel_id=1, source_target_pairs={{0,4},{4,0},{1,5},{5,1},{2,6},{6,2},{3,7},{7,3},{8,12},{12,8},{9,1... | collective-permute-start | bytes 1769480 | tf_op jit(solution)/shard_map/ppermute | solution.py:824
  100.8 1.0 all-to-all-done.2.refs_0_
  101.8 1.1 grad_sums.1
  102.9 2.9 %collective-permute-start.9 = (bf16[208,128]{1,0:T(8,128)(2,1)S(1)}, bf16[208,128]{1,0:T(8,128)(2,1)S(1)}, u32[]{:S(2)}, u32[]{:S(2)}) collective-permute-start(bf16[208,128]{1,0:T(8,128)(2,1)S(1)} %get-tuple-element.138.refs_3_), channel_id=1, source_target_pairs={{0,16},{16,0},{1,17},{17,1},{2,18},{18,2},{3,19},{19,3},{4,20},{20... | collective-permute-start | bytes 159752 | tf_op jit(solution)/shard_map/ppermute | solution.py:780
  105.8 2.8 %out_terms.1 = (bf16[384,384]{1,0:T(8,128)(2,1)}, bf16[384,384]{1,0:T(8,128)(2,1)}, f32[8,128]{1,0:T(8,128)}) custom-call(bf16[512,768]{1,0:T(8,128)(2,1)} %get-tuple-element.139.refs_0_.refs_2_, bf16[256,384]{1,0:T(8,128)(2,1)} %get-tuple-element.140.refs_1_, bf16[512,768]{1,0:T(8,128)(2,1)} %get-tuple-element.139.refs_0_.refs_2_, ...), custom_call_target="tpu_custom_call" | custom-call | flops 1000000 | bytes 1 | tf_op jit(solution)/shard_map/out_terms/pallas_call | solution.py:74
  108.7 3.9 %attend_back.1 = (bf16[192,128]{1,0:T(8,128)(2,1)S(1)}, f32[4,128]{1,0:T(4,128)S(1)}, bf16[8,128,640]{2,1,0:T(8,128)(2,1)}, f32[8,128]{1,0:T(8,128)}) custom-call(bf16[8,128,640]{2,1,0:T(8,128)(2,1)} %copy-done.1, f32[128,256]{1,0:T(8,128)} %get-tuple-element.130.refs_1_, f32[128,256]{1,0:T(8,128)} %get-tuple-element.131.refs_2_, ...), custom_call_target="tpu_custom_call" | custom-call | flops 1000000 | bytes 1 | tf_op jit(solution)/shard_map/attend_back/pallas_call | solution.py:74
  112.6 2.3 %collective-permute-start.10 = (bf16[192,128]{1,0:T(8,128)(2,1)S(1)}, bf16[192,128]{1,0:T(8,128)(2,1)S(1)}, u32[]{:S(2)}, u32[]{:S(2)}) collective-permute-start(bf16[192,128]{1,0:T(8,128)(2,1)S(1)} %get-tuple-element.146.refs_3_), channel_id=1, source_target_pairs={{0,16},{16,0},{1,17},{17,1},{2,18},{18,2},{3,19},{19,3},{4,20},{20... | collective-permute-start | bytes 147464 | tf_op jit(solution)/shard_map/ppermute | solution.py:780
  114.9 0.9 up_fold.4
  115.8 1.8 collective-permute-done.10.refs_4_
  117.6 1.0 finish_back.1
  118.7 3.7 %all-to-all-start.3 = ((bf16[8,128,640]{2,1,0:T(8,128)(2,1)}), bf16[8,128,640]{2,1,0:T(8,128)(2,1)S(1)}, u32[]{:S(2)}, u32[]{:S(2)}) async-start(bf16[8,128,640]{2,1,0:T(8,128)(2,1)} %get-tuple-element.153), calls=%async_computation.3 | async-start | bytes 2621440 | tf_op jit(solution)/shard_map/all_to_all | solution.py:978
  123.4 10.6 %collective-permute-done.7.refs_5_ = bf16[256,768]{1,0:T(8,128)(2,1)S(1)} collective-permute-done((bf16[256,768]{1,0:T(8,128)(2,1)S(1)}, bf16[256,768]{1,0:T(8,128)(2,1)S(1)}, u32[]{:S(2)}, u32[]{:S(2)}) %collective-permute-start.7) | collective-permute-done | bytes 393248 | tf_op jit(solution)/shard_map/ppermute | solution.py:949
  134.0 0.8 copy-done.45
  134.8 2.9 %output.1 = (bf16[512,768]{1,0:T(8,128)(2,1)}, f32[8,128]{1,0:T(8,128)}) custom-call(f32[256,768]{1,0:T(8,128)} %copy-done.15, bf16[256,768]{1,0:T(8,128)(2,1)} %copy-done.21, bf16[256,768]{1,0:T(8,128)(2,1)} %copy-done.44, f32[256,768]{1,0:T(8,128)} %copy-done.14, bf16[256,768]{1,0:T(8,128)(2,1)} %copy-done.22, bf16[256,768]{1,0:T(8,128)(2,1)} %copy-done.45, ...), custom_call_target="tpu_custom_call" | custom-call | flops 1000000 | bytes 1 | tf_op jit(solution)/shard_map/output/pallas_call | solution.py:74
  137.7 1.3 down_fold.3
  139.1 1.9 %collective-permute-start.22 = (bf16[192,1920]{1,0:T(8,128)(2,1)}, bf16[192,1920]{1,0:T(8,128)(2,1)S(1)}, u32[]{:S(2)}, u32[]{:S(2)}) collective-permute-start(bf16[192,1920]{1,0:T(8,128)(2,1)} %get-tuple-element.182), channel_id=1, source_target_pairs={{0,8},{8,0},{1,9},{9,1},{2,10},{10,2},{3,11},{11,3},{4,12},{12,4},... | collective-permute-start | bytes 2211848 | tf_op jit(solution)/shard_map/ppermute | solution.py:824
  141.0 3.4 %first_back.1 = (bf16[512,1152]{1,0:T(8,128)(2,1)}, bf16[256,768]{1,0:T(8,128)(2,1)}, bf16[256,768]{1,0:T(8,128)(2,1)}, f32[8,128]{1,0:T(8,128)}) custom-call(bf16[8,128,640]{2,1,0:T(8,128)(2,1)S(1)} %all-to-all-done.3.refs_0_.refs_1_, s32[6,512]{1,0:T(8,128)S(1)} %copy-done.28, bf16[768,384]{1,0:T(8,128)(2,1)} %refs_2_.4, bf16[768,768]{1,0:T(8,128)(2,1)} %bitcast.12, ...), custom_call_target="tpu_custom_call" | custom-call | flops 40000000000 | bytes 1 | tf_op jit(solution)/shard_map/first_back/pallas_call | solution.py:74
  145.1 4.4 %qkv_terms.1 = (bf16[384,1152]{1,0:T(8,128)(2,1)}, bf16[384,384]{1,0:T(8,128)(2,1)}, bf16[384,384]{1,0:T(8,128)(2,1)}, bf16[384,384]{1,0:T(8,128)(2,1)}, f32[8,128]{1,0:T(8,128)}) custom-call(bf16[512,768]{1,0:T(8,128)(2,1)} %get-tuple-element.163.refs_0_, bf16[512,1152]{1,0:T(8,128)(2,1)} %get-tuple-element.164.refs_1_, f32[8,128]{1,0:T(8,128)} %get-tuple-element.165.refs_2_), custom_call_target="tpu_custom_call" | custom-call | flops 1000000 | bytes 1 | tf_op jit(solution)/shard_map/qkv_terms/pallas_call | solution.py:74
  150.2 1.2 collective-permute-done.15.refs_1_
  152.2 1.2 copy-done.13
  153.4 1.1 qkv_fold.3
  154.5 1.5 collective-permute-start.19
  156.0 2.7 %collective-permute-done.22.refs_1_ = bf16[192,1920]{1,0:T(8,128)(2,1)S(1)} collective-permute-done((bf16[192,1920]{1,0:T(8,128)(2,1)}, bf16[192,1920]{1,0:T(8,128)(2,1)S(1)}, u32[]{:S(2)}, u32[]{:S(2)}) %collective-permute-start.22) | collective-permute-done | bytes 737312 | tf_op jit(solution)/shard_map/ppermute | solution.py:824
  158.7 1.0 down_fold.4
  159.7 2.0 %collective-permute-start.23 = (bf16[96,1920]{1,0:T(8,128)(2,1)}, bf16[96,1920]{1,0:T(8,128)(2,1)S(1)}, u32[]{:S(2)}, u32[]{:S(2)}) collective-permute-start(bf16[96,1920]{1,0:T(8,128)(2,1)} %get-tuple-element.184), channel_id=1, source_target_pairs={{0,4},{4,0},{1,5},{5,1},{2,6},{6,2},{3,7},{7,3},{8,12},{12,8},{9,1... | collective-permute-start | bytes 1105928 | tf_op jit(solution)/shard_map/ppermute | solution.py:824
  161.8 1.3 last.1
  163.8 3.9 %all-to-all-start.4 = ((f32[32,2,48]{2,1,0:T(2,128)}), f32[32,2,48]{2,1,0:T(2,128)S(1)}, u32[]{:S(2)}, u32[]{:S(2)}) async-start(f32[32,2,48]{2,1,0:T(2,128)} %get-tuple-element.185), calls=%async_computation.4 | async-start | bytes 65536 | tf_op jit(solution)/shard_map/all_to_all | solution.py:1013
  167.7 1.8 collective-permute-start.18
  170.4 2.4 %collective-permute-start.26 = (bf16[48,1536]{1,0:T(8,128)(2,1)}, bf16[48,1536]{1,0:T(8,128)(2,1)S(1)}, u32[]{:S(2)}, u32[]{:S(2)}) collective-permute-start(bf16[48,1536]{1,0:T(8,128)(2,1)} %get-tuple-element.197), channel_id=1, source_target_pairs={{0,16},{16,0},{1,17},{17,1},{2,18},{18,2},{3,19},{19,3},{4,20},{20... | collective-permute-start | bytes 442376 | tf_op jit(solution)/shard_map/ppermute | solution.py:824
  172.8 0.8 qkv_fold.4
  173.7 1.6 collective-permute-start.21
  175.3 0.9 all-to-all-done.4.refs_0_
  176.3 0.8 down_fold.5
  177.1 2.4 %collective-permute-start.25 = (bf16[48,1920]{1,0:T(8,128)(2,1)}, bf16[48,1920]{1,0:T(8,128)(2,1)S(1)}, u32[]{:S(2)}, u32[]{:S(2)}) collective-permute-start(bf16[48,1920]{1,0:T(8,128)(2,1)} %get-tuple-element.195), channel_id=1, source_target_pairs={{0,16},{16,0},{1,17},{17,1},{2,18},{18,2},{3,19},{19,3},{4,20},{20... | collective-permute-start | bytes 552968 | tf_op jit(solution)/shard_map/ppermute | solution.py:824
  181.2 4.1 %collective-permute-done.21.refs_1_ = bf16[96,1152]{1,0:T(8,128)(2,1)S(1)} collective-permute-done((bf16[96,1152]{1,0:T(8,128)(2,1)}, bf16[96,1152]{1,0:T(8,128)(2,1)S(1)}, u32[]{:S(2)}, u32[]{:S(2)}) %collective-permute-start.21) | collective-permute-done | bytes 221216 | tf_op jit(solution)/shard_map/ppermute | solution.py:824
  186.2 1.9 join.1
  188.9 2.9 %collective-permute-done.25.refs_1_ = bf16[48,1920]{1,0:T(8,128)(2,1)S(1)} collective-permute-done((bf16[48,1920]{1,0:T(8,128)(2,1)}, bf16[48,1920]{1,0:T(8,128)(2,1)S(1)}, u32[]{:S(2)}, u32[]{:S(2)}) %collective-permute-start.25) | collective-permute-done | bytes 184352 | tf_op jit(solution)/shard_map/ppermute | solution.py:824
  191.8 0.8 down_close.1
  (137 shorter events, 11.6 us)
Async XLA Ops:
  5.4 5.4 %copy-start.9 = (bf16[384,768]{1,0:T(8,128)(2,1)S(1)}, bf16[384,768]{1,0:T(8,128)(2,1)}, u32[]{:S(2)}) copy-start(bf16[384,768]{1,0:T(8,128)(2,1)} %refs_8_.5) | copy-start | bytes 1769476
  5.4 22.6 %all-to-all-start = ((bf16[8,128,640]{2,1,0:T(8,128)(2,1)}), bf16[8,128,640]{2,1,0:T(8,128)(2,1)S(1)}, u32[]{:S(2)}, u32[]{:S(2)}) async-start(bf16[8,128,640]{2,1,0:T(8,128)(2,1)} %get-tuple-element.110), calls=%async_computation | async-start | bytes 2621440 | tf_op jit(solution)/shard_map/all_to_all | solution.py:873
  10.8 16.1 %collective-permute-start.1 = (bf16[384,768]{1,0:T(8,128)(2,1)S(1)}, bf16[384,768]{1,0:T(8,128)(2,1)}, u32[]{:S(2)}, u32[]{:S(2)}) collective-permute-start(bf16[384,768]{1,0:T(8,128)(2,1)S(1)} %copy-done.9), channel_id=1, source_target_pairs={{0,1},{1,0},{2,3},{3,2},{4,5},{5,4},{6,7},{7,6},{8,9},{9,8},{10,11... | collective-permute-start | bytes 1769480 | tf_op jit(solution)/shard_map/ppermute | solution.py:858
  12.4 14.5 %collective-permute-start = (s32[6,512]{1,0:T(8,128)S(1)}, s32[6,512]{1,0:T(8,128)S(1)}, u32[]{:S(2)}, u32[]{:S(2)}) collective-permute-start(s32[6,512]{1,0:T(8,128)S(1)} %copy-done.28), channel_id=1, source_target_pairs={{0,1},{1,0},{2,3},{3,2},{4,5},{5,4},{6,7},{7,6},{8,9},{9,8},{10,11... | collective-permute-start | bytes 36872 | tf_op jit(solution)/shard_map/ppermute | solution.py:857
  28.1 7.3 %copy-start.1 = (bf16[8,128,640]{2,1,0:T(8,128)(2,1)}, bf16[8,128,640]{2,1,0:T(8,128)(2,1)S(1)}, u32[]{:S(2)}) copy-start(bf16[8,128,640]{2,1,0:T(8,128)(2,1)S(1)} %all-to-all-done.refs_0_) | copy-start | bytes 3932164
  28.2 5.3 %collective-permute-start.2 = (bf16[128,256]{1,0:T(8,128)(2,1)S(1)}, bf16[128,256]{1,0:T(8,128)(2,1)S(1)}, u32[]{:S(2)}, u32[]{:S(2)}) collective-permute-start(bf16[128,256]{1,0:T(8,128)(2,1)S(1)} %query_sums.1.refs_1_), channel_id=1, source_target_pairs={{0,16},{16,0},{1,17},{17,1},{2,18},{18,2},{3,19},{19,3},{4,20},{20... | collective-permute-start | bytes 196616 | tf_op jit(solution)/shard_map/ppermute | solution.py:780
  35.4 12.0 %copy-start.46 = (s32[512]{0:T(512)S(1)}, s32[512]{0:T(512)}, u32[]{:S(2)}) copy-start(s32[512]{0:T(512)} %param.29) | copy-start | bytes 6148
  35.4 5.2 %collective-permute-start.3 = (bf16[128,256]{1,0:T(8,128)(2,1)S(1)}, bf16[128,256]{1,0:T(8,128)(2,1)S(1)}, u32[]{:S(2)}, u32[]{:S(2)}) collective-permute-start(bf16[128,256]{1,0:T(8,128)(2,1)S(1)} %get-tuple-element.111.refs_0_), channel_id=1, source_target_pairs={{0,16},{16,0},{1,17},{17,1},{2,18},{18,2},{3,19},{19,3},{4,20},{20... | collective-permute-start | bytes 196616 | tf_op jit(solution)/shard_map/ppermute | solution.py:780
  42.1 18.4 %all-to-all-start.1 = ((bf16[16,192,128]{2,1,0:T(8,128)(2,1)}), bf16[16,192,128]{2,1,0:T(8,128)(2,1)S(1)}, u32[]{:S(2)}, u32[]{:S(2)}) async-start(bf16[16,192,128]{2,1,0:T(8,128)(2,1)} %get-tuple-element.112), calls=%async_computation.1 | async-start | bytes 1572864 | tf_op jit(solution)/shard_map/all_to_all | solution.py:893
  47.3 13.2 %copy-start.30 = (s32[6,512]{1,0:T(8,128)S(1)}, s32[6,512]{1,0:T(8,128)}, u32[]{:S(2)}) copy-start(s32[6,512]{1,0:T(8,128)} %copy-done.29) | copy-start | bytes 36868
  47.3 13.2 %copy-start.33 = (f32[1536]{0:T(1024)S(1)}, f32[1536]{0:T(1024)}, u32[]{:S(2)}) copy-start(f32[1536]{0:T(1024)} %refs_6_.5) | copy-start | bytes 18436
  47.4 13.2 %copy-start.34 = (f32[768]{0:T(1024)S(1)}, f32[768]{0:T(1024)}, u32[]{:S(2)}) copy-start(f32[768]{0:T(1024)} %refs_5_.5) | copy-start | bytes 9220
  47.4 13.2 %copy-start.35 = (f32[768]{0:T(1024)S(1)}, f32[768]{0:T(1024)}, u32[]{:S(2)}) copy-start(f32[768]{0:T(1024)} %refs_6_.6) | copy-start | bytes 9220
  48.7 18.0 %copy-start.2 = (bf16[512,768]{1,0:T(8,128)(2,1)}, bf16[512,768]{1,0:T(8,128)(2,1)S(1)}, u32[]{:S(2)}) copy-start(bf16[512,768]{1,0:T(8,128)(2,1)S(1)} %broadcast_multiply_fusion.refs_7_.refs_0_.refs_2_) | copy-start | bytes 2359300
  66.0 20.0 %copy-start.14 = (f32[256,768]{1,0:T(8,128)}, f32[256,768]{1,0:T(8,128)S(1)}, u32[]{:S(2)}) copy-start(f32[256,768]{1,0:T(8,128)S(1)} %get-tuple-element.117.refs_5_.refs_3_) | copy-start | bytes 2359300
  66.0 17.2 %collective-permute-start.5 = (bf16[256,768]{1,0:T(8,128)(2,1)S(1)}, bf16[256,768]{1,0:T(8,128)(2,1)S(1)}, u32[]{:S(2)}, u32[]{:S(2)}) collective-permute-start(bf16[256,768]{1,0:T(8,128)(2,1)S(1)} %get-tuple-element.116.refs_1_), channel_id=1, source_target_pairs={{0,1},{1,0},{2,3},{3,2},{4,5},{5,4},{6,7},{7,6},{8,9},{9,8},{10,11... | collective-permute-start | bytes 1179656 | tf_op jit(solution)/shard_map/ppermute | solution.py:922
  72.2 13.8 %copy-start.15 = (f32[256,768]{1,0:T(8,128)}, f32[256,768]{1,0:T(8,128)S(1)}, u32[]{:S(2)}) copy-start(f32[256,768]{1,0:T(8,128)S(1)} %get-tuple-element.113.refs_4_.refs_0_) | copy-start | bytes 2359300
  72.2 13.8 %collective-permute-start.4 = (bf16[256,768]{1,0:T(8,128)(2,1)S(1)}, bf16[256,768]{1,0:T(8,128)(2,1)S(1)}, u32[]{:S(2)}, u32[]{:S(2)}) collective-permute-start(bf16[256,768]{1,0:T(8,128)(2,1)S(1)} %get-tuple-element.115.refs_0_), channel_id=1, source_target_pairs={{0,1},{1,0},{2,3},{3,2},{4,5},{5,4},{6,7},{7,6},{8,9},{9,8},{10,11... | collective-permute-start | bytes 1179656 | tf_op jit(solution)/shard_map/ppermute | solution.py:922
  78.3 18.0 %collective-permute-start.8 = (bf16[384,1536]{1,0:T(8,128)(2,1)}, bf16[384,1536]{1,0:T(8,128)(2,1)}, u32[]{:S(2)}, u32[]{:S(2)}) collective-permute-start(bf16[384,1536]{1,0:T(8,128)(2,1)} %get-tuple-element.134), channel_id=1, source_target_pairs={{0,2},{2,0},{1,3},{3,1},{4,6},{6,4},{5,7},{7,5},{8,10},{10,8},{9,1... | collective-permute-start | bytes 3538952 | tf_op jit(solution)/shard_map/ppermute | solution.py:824
  78.4 7.5 %copy-start.3 = (bf16[512,768]{1,0:T(8,128)(2,1)S(1)}, bf16[512,768]{1,0:T(8,128)(2,1)}, u32[]{:S(2)}) copy-start(bf16[512,768]{1,0:T(8,128)(2,1)} %copy-done.2) | copy-start | bytes 2359300
  78.4 7.5 %copy-start.10 = (bf16[384,768]{1,0:T(8,128)(2,1)S(1)}, bf16[384,768]{1,0:T(8,128)(2,1)}, u32[]{:S(2)}) copy-start(bf16[384,768]{1,0:T(8,128)(2,1)} %refs_8_.5) | copy-start | bytes 1769476
  86.0 8.0 %copy-start = (bf16[1536,768]{1,0:T(8,128)(2,1)S(1)}, bf16[1536,768]{1,0:T(8,128)(2,1)}, u32[]{:S(2)}) copy-start(bf16[1536,768]{1,0:T(8,128)(2,1)} %refs_1_.10) | copy-start | bytes 7077892
  89.7 4.3 %copy-start.8 = (bf16[256,1536]{1,0:T(8,128)(2,1)S(1)}, bf16[256,1536]{1,0:T(8,128)(2,1)}, u32[]{:S(2)}) copy-start(bf16[256,1536]{1,0:T(8,128)(2,1)} %get-tuple-element.114.refs_1_.refs_0_) | copy-start | bytes 2359300
  89.8 12.1 %all-to-all-start.2 = ((bf16[8,208,128]{2,1,0:T(8,128)(2,1)}), bf16[8,208,128]{2,1,0:T(8,128)(2,1)}, u32[]{:S(2)}, u32[]{:S(2)}) async-start(bf16[8,208,128]{2,1,0:T(8,128)(2,1)} %get-tuple-element.132), calls=%async_computation.2 | async-start | bytes 851968 | tf_op jit(solution)/shard_map/all_to_all | solution.py:939
  94.9 20.9 %collective-permute-start.6 = (bf16[256,768]{1,0:T(8,128)(2,1)S(1)}, bf16[256,768]{1,0:T(8,128)(2,1)S(1)}, u32[]{:S(2)}, u32[]{:S(2)}) collective-permute-start(bf16[256,768]{1,0:T(8,128)(2,1)S(1)} %get-tuple-element.128.refs_1_), channel_id=1, source_target_pairs={{0,1},{1,0},{2,3},{3,2},{4,5},{5,4},{6,7},{7,6},{8,9},{9,8},{10,11... | collective-permute-start | bytes 1179656 | tf_op jit(solution)/shard_map/ppermute | solution.py:949
  96.3 26.5 %copy-start.22 = (bf16[256,768]{1,0:T(8,128)(2,1)}, bf16[256,768]{1,0:T(8,128)(2,1)S(1)}, u32[]{:S(2)}) copy-start(bf16[256,768]{1,0:T(8,128)(2,1)S(1)} %get-tuple-element.129.refs_4_) | copy-start | bytes 1179652
  98.9 16.0 %collective-permute-start.11 = (bf16[192,1536]{1,0:T(8,128)(2,1)}, bf16[192,1536]{1,0:T(8,128)(2,1)S(1)}, u32[]{:S(2)}, u32[]{:S(2)}) collective-permute-start(bf16[192,1536]{1,0:T(8,128)(2,1)} %get-tuple-element.148), channel_id=1, source_target_pairs={{0,4},{4,0},{1,5},{5,1},{2,6},{6,2},{3,7},{7,3},{8,12},{12,8},{9,1... | collective-permute-start | bytes 1769480 | tf_op jit(solution)/shard_map/ppermute | solution.py:824
  102.9 5.7 %collective-permute-start.9 = (bf16[208,128]{1,0:T(8,128)(2,1)S(1)}, bf16[208,128]{1,0:T(8,128)(2,1)S(1)}, u32[]{:S(2)}, u32[]{:S(2)}) collective-permute-start(bf16[208,128]{1,0:T(8,128)(2,1)S(1)} %get-tuple-element.138.refs_3_), channel_id=1, source_target_pairs={{0,16},{16,0},{1,17},{17,1},{2,18},{18,2},{3,19},{19,3},{4,20},{20... | collective-permute-start | bytes 159752 | tf_op jit(solution)/shard_map/ppermute | solution.py:780
  108.6 6.2 %copy-start.18 = (bf16[192,1536]{1,0:T(8,128)(2,1)S(1)}, bf16[192,1536]{1,0:T(8,128)(2,1)}, u32[]{:S(2)}) copy-start(bf16[192,1536]{1,0:T(8,128)(2,1)} %get-tuple-element.147.refs_0_) | copy-start | bytes 1769476
  108.6 9.0 %copy-start.19 = (f32[128,256]{1,0:T(8,128)S(1)}, f32[128,256]{1,0:T(8,128)}, u32[]{:S(2)}) copy-start(f32[128,256]{1,0:T(8,128)} %get-tuple-element.130.refs_1_) | copy-start | bytes 393220
  112.6 5.1 %collective-permute-start.10 = (bf16[192,128]{1,0:T(8,128)(2,1)S(1)}, bf16[192,128]{1,0:T(8,128)(2,1)S(1)}, u32[]{:S(2)}, u32[]{:S(2)}) collective-permute-start(bf16[192,128]{1,0:T(8,128)(2,1)S(1)} %get-tuple-element.146.refs_3_), channel_id=1, source_target_pairs={{0,16},{16,0},{1,17},{17,1},{2,18},{18,2},{3,19},{19,3},{4,20},{20... | collective-permute-start | bytes 147464 | tf_op jit(solution)/shard_map/ppermute | solution.py:780
  118.7 4.7 %copy-start.48 = (bf16[384,384]{1,0:T(8,128)(2,1)S(1)}, bf16[384,384]{1,0:T(8,128)(2,1)}, u32[]{:S(2)}) copy-start(bf16[384,384]{1,0:T(8,128)(2,1)} %get-tuple-element.158) | copy-start | bytes 884740
  118.7 16.1 %copy-start.37 = (f32[768]{0:T(1024)S(1)}, f32[768]{0:T(1024)}, u32[]{:S(2)}) copy-start(f32[768]{0:T(1024)} %refs_6_.7) | copy-start | bytes 9220
  118.7 22.3 %all-to-all-start.3 = ((bf16[8,128,640]{2,1,0:T(8,128)(2,1)}), bf16[8,128,640]{2,1,0:T(8,128)(2,1)S(1)}, u32[]{:S(2)}, u32[]{:S(2)}) async-start(bf16[8,128,640]{2,1,0:T(8,128)(2,1)} %get-tuple-element.153), calls=%async_computation.3 | async-start | bytes 2621440 | tf_op jit(solution)/shard_map/all_to_all | solution.py:978
  122.4 15.3 %collective-permute-start.12 = (bf16[384,1536]{1,0:T(8,128)(2,1)}, bf16[384,1536]{1,0:T(8,128)(2,1)S(1)}, u32[]{:S(2)}, u32[]{:S(2)}) collective-permute-start(bf16[384,1536]{1,0:T(8,128)(2,1)} %get-tuple-element.157), channel_id=1, source_target_pairs={{0,2},{2,0},{1,3},{3,1},{4,6},{6,4},{5,7},{7,5},{8,10},{10,8},{9,1... | collective-permute-start | bytes 3538952 | tf_op jit(solution)/shard_map/ppermute | solution.py:844
  122.8 11.2 %collective-permute-start.7 = (bf16[256,768]{1,0:T(8,128)(2,1)S(1)}, bf16[256,768]{1,0:T(8,128)(2,1)S(1)}, u32[]{:S(2)}, u32[]{:S(2)}) collective-permute-start(bf16[256,768]{1,0:T(8,128)(2,1)S(1)} %get-tuple-element.129.refs_4_), channel_id=1, source_target_pairs={{0,1},{1,0},{2,3},{3,2},{4,5},{5,4},{6,7},{7,6},{8,9},{9,8},{10,11... | collective-permute-start | bytes 1179656 | tf_op jit(solution)/shard_map/ppermute | solution.py:949
  123.4 14.3 %collective-permute-start.13 = (bf16[384,384]{1,0:T(8,128)(2,1)S(1)}, bf16[384,384]{1,0:T(8,128)(2,1)S(1)}, u32[]{:S(2)}, u32[]{:S(2)}) collective-permute-start(bf16[384,384]{1,0:T(8,128)(2,1)S(1)} %copy-done.48), channel_id=1, source_target_pairs={{0,2},{2,0},{1,3},{3,1},{4,6},{6,4},{5,7},{7,5},{8,10},{10,8},{9,1... | collective-permute-start | bytes 884744 | tf_op jit(solution)/shard_map/ppermute | solution.py:844
  139.1 19.7 %collective-permute-start.22 = (bf16[192,1920]{1,0:T(8,128)(2,1)}, bf16[192,1920]{1,0:T(8,128)(2,1)S(1)}, u32[]{:S(2)}, u32[]{:S(2)}) collective-permute-start(bf16[192,1920]{1,0:T(8,128)(2,1)} %get-tuple-element.182), channel_id=1, source_target_pairs={{0,8},{8,0},{1,9},{9,1},{2,10},{10,2},{3,11},{11,3},{4,12},{12,4},... | collective-permute-start | bytes 2211848 | tf_op jit(solution)/shard_map/ppermute | solution.py:824
  144.4 6.9 %copy-start.47 = (bf16[96,1536]{1,0:T(8,128)(2,1)S(1)}, bf16[96,1536]{1,0:T(8,128)(2,1)}, u32[]{:S(2)}) copy-start(bf16[96,1536]{1,0:T(8,128)(2,1)} %get-tuple-element.176) | copy-start | bytes 884740
  144.4 17.3 %collective-permute-start.14 = (bf16[256,768]{1,0:T(8,128)(2,1)}, bf16[256,768]{1,0:T(8,128)(2,1)S(1)}, u32[]{:S(2)}, u32[]{:S(2)}) collective-permute-start(bf16[256,768]{1,0:T(8,128)(2,1)} %get-tuple-element.161), channel_id=1, source_target_pairs={{0,1},{1,0},{2,3},{3,2},{4,5},{5,4},{6,7},{7,6},{8,9},{9,8},{10,11... | collective-permute-start | bytes 1179656 | tf_op jit(solution)/shard_map/ppermute | solution.py:999
  145.1 13.7 %copy-start.16 = (bf16[192,1920]{1,0:T(8,128)(2,1)S(1)}, bf16[192,1920]{1,0:T(8,128)(2,1)}, u32[]{:S(2)}) copy-start(bf16[192,1920]{1,0:T(8,128)(2,1)} %get-tuple-element.181.refs_0_) | copy-start | bytes 2211844
  149.5 1.9 collective-permute-start.15
  149.6 2.2 %collective-permute-start.16 = (bf16[384,384]{1,0:T(8,128)(2,1)}, bf16[384,384]{1,0:T(8,128)(2,1)S(1)}, u32[]{:S(2)}, u32[]{:S(2)}) collective-permute-start(bf16[384,384]{1,0:T(8,128)(2,1)} %get-tuple-element.168), channel_id=1, source_target_pairs={{0,2},{2,0},{1,3},{3,1},{4,6},{6,4},{5,7},{7,5},{8,10},{10,8},{9,1... | collective-permute-start | bytes 884744 | tf_op jit(solution)/shard_map/ppermute | solution.py:824
  150.1 2.1 %collective-permute-start.17 = (bf16[384,384]{1,0:T(8,128)(2,1)}, bf16[384,384]{1,0:T(8,128)(2,1)S(1)}, u32[]{:S(2)}, u32[]{:S(2)}) collective-permute-start(bf16[384,384]{1,0:T(8,128)(2,1)} %get-tuple-element.169), channel_id=1, source_target_pairs={{0,2},{2,0},{1,3},{3,1},{4,6},{6,4},{5,7},{7,5},{8,10},{10,8},{9,1... | collective-permute-start | bytes 884744 | tf_op jit(solution)/shard_map/ppermute | solution.py:824
  151.4 18.2 %collective-permute-start.20 = (bf16[96,1536]{1,0:T(8,128)(2,1)S(1)}, bf16[96,1536]{1,0:T(8,128)(2,1)S(1)}, u32[]{:S(2)}, u32[]{:S(2)}) collective-permute-start(bf16[96,1536]{1,0:T(8,128)(2,1)S(1)} %copy-done.47), channel_id=1, source_target_pairs={{0,8},{8,0},{1,9},{9,1},{2,10},{10,2},{3,11},{11,3},{4,12},{12,4},... | collective-permute-start | bytes 884744 | tf_op jit(solution)/shard_map/ppermute | solution.py:824
  153.4 8.3 %copy-start.42 = (f32[256,768]{1,0:T(8,128)S(1)}, f32[256,768]{1,0:T(8,128)}, u32[]{:S(2)}) copy-start(f32[256,768]{1,0:T(8,128)} %get-tuple-element.162.refs_4_) | copy-start | bytes 2359300
  154.5 7.3 %copy-start.5 = (bf16[512,768]{1,0:T(8,128)(2,1)S(1)}, bf16[512,768]{1,0:T(8,128)(2,1)}, u32[]{:S(2)}) copy-start(bf16[512,768]{1,0:T(8,128)(2,1)} %refs_2_.5) | copy-start | bytes 2359300
  154.5 7.3 %copy-start.39 = (f32[768]{0:T(1024)S(1)}, f32[768]{0:T(1024)}, u32[]{:S(2)}) copy-start(f32[768]{0:T(1024)} %refs_3_.7) | copy-start | bytes 9220
  154.5 7.3 %copy-start.43 = (bf16[256,768]{1,0:T(8,128)(2,1)S(1)}, bf16[256,768]{1,0:T(8,128)(2,1)}, u32[]{:S(2)}) copy-start(bf16[256,768]{1,0:T(8,128)(2,1)} %get-tuple-element.160.refs_0_) | copy-start | bytes 1179652
  154.5 18.3 %collective-permute-start.19 = (bf16[192,1152]{1,0:T(8,128)(2,1)}, bf16[192,1152]{1,0:T(8,128)(2,1)S(1)}, u32[]{:S(2)}, u32[]{:S(2)}) collective-permute-start(bf16[192,1152]{1,0:T(8,128)(2,1)} %get-tuple-element.174), channel_id=1, source_target_pairs={{0,4},{4,0},{1,5},{5,1},{2,6},{6,2},{3,7},{7,3},{8,12},{12,8},{9,1... | collective-permute-start | bytes 1327112 | tf_op jit(solution)/shard_map/ppermute | solution.py:824
  159.7 16.6 %collective-permute-start.23 = (bf16[96,1920]{1,0:T(8,128)(2,1)}, bf16[96,1920]{1,0:T(8,128)(2,1)S(1)}, u32[]{:S(2)}, u32[]{:S(2)}) collective-permute-start(bf16[96,1920]{1,0:T(8,128)(2,1)} %get-tuple-element.184), channel_id=1, source_target_pairs={{0,4},{4,0},{1,5},{5,1},{2,6},{6,2},{3,7},{7,3},{8,12},{12,8},{9,1... | collective-permute-start | bytes 1105928 | tf_op jit(solution)/shard_map/ppermute | solution.py:824
  161.8 7.8 %copy-start.25 = (bf16[96,1536]{1,0:T(8,128)(2,1)S(1)}, bf16[96,1536]{1,0:T(8,128)(2,1)}, u32[]{:S(2)}) copy-start(bf16[96,1536]{1,0:T(8,128)(2,1)} %get-tuple-element.175.refs_0_) | copy-start | bytes 884740
  161.8 11.0 %copy-start.20 = (bf16[192,1152]{1,0:T(8,128)(2,1)S(1)}, bf16[192,1152]{1,0:T(8,128)(2,1)}, u32[]{:S(2)}) copy-start(bf16[192,1152]{1,0:T(8,128)(2,1)} %get-tuple-element.173.refs_0_) | copy-start | bytes 1327108
  163.8 12.3 %all-to-all-start.4 = ((f32[32,2,48]{2,1,0:T(2,128)}), f32[32,2,48]{2,1,0:T(2,128)S(1)}, u32[]{:S(2)}, u32[]{:S(2)}) async-start(f32[32,2,48]{2,1,0:T(2,128)} %get-tuple-element.185), calls=%async_computation.4 | async-start | bytes 65536 | tf_op jit(solution)/shard_map/all_to_all | solution.py:1013
  167.7 18.4 %collective-permute-start.18 = (bf16[256,768]{1,0:T(8,128)(2,1)}, bf16[256,768]{1,0:T(8,128)(2,1)}, u32[]{:S(2)}, u32[]{:S(2)}) collective-permute-start(bf16[256,768]{1,0:T(8,128)(2,1)} %copy-done.40), channel_id=1, source_target_pairs={{0,1},{1,0},{2,3},{3,2},{4,5},{5,4},{6,7},{7,6},{8,9},{9,8},{10,11... | collective-permute-start | bytes 1179656 | tf_op jit(solution)/shard_map/ppermute | solution.py:1010
  170.3 5.9 %copy-start.23 = (bf16[96,1920]{1,0:T(8,128)(2,1)S(1)}, bf16[96,1920]{1,0:T(8,128)(2,1)}, u32[]{:S(2)}) copy-start(bf16[96,1920]{1,0:T(8,128)(2,1)} %get-tuple-element.183.refs_0_) | copy-start | bytes 1105924
  170.4 17.8 %collective-permute-start.26 = (bf16[48,1536]{1,0:T(8,128)(2,1)}, bf16[48,1536]{1,0:T(8,128)(2,1)S(1)}, u32[]{:S(2)}, u32[]{:S(2)}) collective-permute-start(bf16[48,1536]{1,0:T(8,128)(2,1)} %get-tuple-element.197), channel_id=1, source_target_pairs={{0,16},{16,0},{1,17},{17,1},{2,18},{18,2},{3,19},{19,3},{4,20},{20... | collective-permute-start | bytes 442376 | tf_op jit(solution)/shard_map/ppermute | solution.py:824
  173.6 11.7 %copy-start.26 = (bf16[96,1152]{1,0:T(8,128)(2,1)S(1)}, bf16[96,1152]{1,0:T(8,128)(2,1)}, u32[]{:S(2)}) copy-start(bf16[96,1152]{1,0:T(8,128)(2,1)} %get-tuple-element.179.refs_0_) | copy-start | bytes 663556
  173.7 11.7 %collective-permute-start.21 = (bf16[96,1152]{1,0:T(8,128)(2,1)}, bf16[96,1152]{1,0:T(8,128)(2,1)S(1)}, u32[]{:S(2)}, u32[]{:S(2)}) collective-permute-start(bf16[96,1152]{1,0:T(8,128)(2,1)} %get-tuple-element.180), channel_id=1, source_target_pairs={{0,8},{8,0},{1,9},{9,1},{2,10},{10,2},{3,11},{11,3},{4,12},{12,4},... | collective-permute-start | bytes 663560 | tf_op jit(solution)/shard_map/ppermute | solution.py:824
  176.2 10.0 %copy-start.41 = (bf16[256,768]{1,0:T(8,128)(2,1)S(1)}, bf16[256,768]{1,0:T(8,128)(2,1)}, u32[]{:S(2)}) copy-start(bf16[256,768]{1,0:T(8,128)(2,1)} %copy-done.40) | copy-start | bytes 1179652
  177.1 14.7 %collective-permute-start.25 = (bf16[48,1920]{1,0:T(8,128)(2,1)}, bf16[48,1920]{1,0:T(8,128)(2,1)S(1)}, u32[]{:S(2)}, u32[]{:S(2)}) collective-permute-start(bf16[48,1920]{1,0:T(8,128)(2,1)} %get-tuple-element.195), channel_id=1, source_target_pairs={{0,16},{16,0},{1,17},{17,1},{2,18},{18,2},{3,19},{19,3},{4,20},{20... | collective-permute-start | bytes 552968 | tf_op jit(solution)/shard_map/ppermute | solution.py:824
  186.1 7.2 %collective-permute-start.24 = (bf16[48,1152]{1,0:T(8,128)(2,1)}, bf16[48,1152]{1,0:T(8,128)(2,1)S(1)}, u32[]{:S(2)}, u32[]{:S(2)}) collective-permute-start(bf16[48,1152]{1,0:T(8,128)(2,1)} %get-tuple-element.193), channel_id=1, source_target_pairs={{0,16},{16,0},{1,17},{17,1},{2,18},{18,2},{3,19},{19,3},{4,20},{20... | collective-permute-start | bytes 331784 | tf_op jit(solution)/shard_map/ppermute | solution.py:824
  186.2 5.6 %copy-start.27 = (bf16[48,1920]{1,0:T(8,128)(2,1)S(1)}, bf16[48,1920]{1,0:T(8,128)(2,1)}, u32[]{:S(2)}) copy-start(bf16[48,1920]{1,0:T(8,128)(2,1)} %get-tuple-element.194.refs_0_) | copy-start | bytes 552964
  186.2 7.1 %copy-start.32 = (bf16[48,1152]{1,0:T(8,128)(2,1)S(1)}, bf16[48,1152]{1,0:T(8,128)(2,1)}, u32[]{:S(2)}) copy-start(bf16[48,1152]{1,0:T(8,128)(2,1)} %get-tuple-element.192.refs_0_) | copy-start | bytes 331780
  (17 other events, 29.4 us)

commit v6 on v5

--- a/solution.py
+++ b/solution.py
@@ -37,7 +37,7 @@
 WHOLE = pl.BlockSpec(memory_space=pltpu.VMEM)
 UNREAD = pl.BlockSpec(memory_space=pltpu.HBM)
 TOKEN = ((8, C), F32)
-MAIN = ("turn", "grad_sums", "first_back", "last", "join")
+MAIN = ("turn", "grad_sums", "finish_back", "first_back", "last", "join")
 LONG, SHORT = 40 * 10**9, 10**6
 
 
@@ -313,11 +313,24 @@
         copy.wait()
 
 
+def active_grad_kernel(bg_ref, down_src, out, down_ref, grad_ref, sem, out_sems):
+    copy = send(down_src, down_ref, sem)
+    half = grad_ref.shape[1]
+    copy.wait()
+    copies = []
+    for i in range(2):
+        rows = slice(i * half, (i + 1) * half)
+        grad_ref[i] = dot_nt(bg_ref[rows, :], down_ref[...])
+        copies.append(send(grad_ref.at[i], out.at[rows, :], out_sems.at[i]))
+    for copy in copies:
+        copy.wait()
+
+
 def middle_kernel(
-    recv_ref, ids_ref, ids_other_ref, x_ref, gain_ref, shift_ref, up_bias_ref, bg_ref,
-    wo_src, wo_other_src, up_src, down_src,
+    part, recv_ref, ids_ref, ids_other_ref, x_ref, gain_ref, shift_ref, up_bias_ref,
+    wo_src, wo_other_src, up_src, active_grad_src,
     up_bias_out_ref, residual_ref, back_ref, attended_out, normed_out, active_out, hidden_out,
-    a_scr, w_ref, up_ref, down_ref, own_ref, normed_ref, active_ref, hidden_ref, in_sems, out_sems,
+    a_scr, w_ref, up_ref, active_grad_ref, own_ref, normed_ref, active_ref, hidden_ref, in_sems, out_sems,
 ):
     half = wo_src.shape[0]
     me = lax.axis_index("mp")
@@ -328,7 +341,8 @@
         send(wo_other_src, w_ref.at[pl.ds(theirs, half), :], in_sems.at[1]),
     ]
     up_copy = send(up_src, up_ref, in_sems.at[2])
-    down_copy = send(down_src, down_ref, in_sems.at[3])
+    size = x_ref.shape[0]
+    active_grad_copy = send(active_grad_src.at[part * size : (part + 1) * size, :], active_grad_ref, in_sems.at[3])
     short = left_half((HD, C))
     for s in range(x_ref.shape[0] // C):
         rows = slice(s * C, (s + 1) * C)
@@ -365,8 +379,8 @@
     active_ref[...] = (hidden * below).astype(BF16)
     copies.append(send(active_ref, active_out, out_sems.at[2]))
     slope = below + hidden * jnp.exp(-0.5 * hidden * hidden) * 0.3989422804014327
-    down_copy.wait()
-    hidden_grad = (slope * dot_nt(bg_ref[...], down_ref[...])).astype(BF16)
+    active_grad_copy.wait()
+    hidden_grad = (slope * active_grad_ref[...]).astype(BF16)
     hidden_ref[...] = hidden_grad
     copies.append(send(hidden_ref, hidden_out, out_sems.at[3]))
     up_bias_out_ref[...] = jnp.sum(hidden_grad.astype(F32), axis=0, keepdims=True)
@@ -637,17 +651,19 @@
     sent = []
     for side, (count, order) in enumerate(zip(counts, orders)):
         width = held[spot + 1].shape[1]
-        lanes = slice(base, base + width)
-        total = None
+        turned = []
         for i in range(count):
             copies[spot + 2 * i].wait()
+            turned.append(held[spot + 2 * i][...].T)
+        for i in range(count):
             copies[spot + 2 * i + 1].wait()
-            made = dot_tn(held[spot + 2 * i][...], held[spot + 2 * i + 1][...])
-            total = made if total is None else total + made
-        scr[:, lanes] = total.astype(BF16)
         spread = base
         for wide, places in order:
             part = slice(spread, spread + wide)
+            inside = slice(spread - base, spread - base + wide)
+            scr[:, part] = sum(
+                dot_nn(t, held[spot + 2 * i + 1][:, inside]) for i, t in enumerate(turned)
+            ).astype(BF16)
             give = (gives[0], part) if parts == 1 else (gives[region], slice(0, wide))
             for bit, (out, inner) in ((1 - me, give), (me, (keep_out, part))):
                 for j, place in enumerate(row_order(places)):
@@ -891,21 +907,29 @@
         specs=([WHOLE] * len(parts), [UNREAD] * 2),
     )
     recv_two = lax.all_to_all(send_two, NEAR + ("mp",), 0, 0)
+    (active_grad,) = call(
+        active_grad_kernel, [((tokens, hidden), F32)], bg, down_weight, name="active_grad", after=[part],
+        scratch=[
+            pltpu.VMEM((hidden, model), BF16), pltpu.VMEM((2, half, hidden), F32), pltpu.SemaphoreType.DMA,
+            pltpu.SemaphoreType.DMA((2,)),
+        ],
+        specs=([WHOLE, UNREAD], [UNREAD]),
+    )
     halves = []
     for n in range(2):
         rows = lambda cols, n=n: pl.BlockSpec((half, cols), lambda i: (n, 0))
         lanes = pl.BlockSpec((cluster_ids.shape[0], half), lambda i, n=n: (0, n))
         halves.append(call(
-            middle_kernel,
+            functools.partial(middle_kernel, n),
             [
                 ((1, hidden), F32), ((half, model), F32), ((half, model), BF16), ((half, width), BF16),
                 ((half, model), BF16), ((half, hidden), BF16), ((half, hidden), BF16),
             ],
-            recv_two, cluster_ids, ids_other, inputs, norm_two_gain, norm_two_shift, up_bias, bg,
-            out_weight, wo_other, up_weight, down_weight,
+            recv_two, cluster_ids, ids_other, inputs, norm_two_gain, norm_two_shift, up_bias,
+            out_weight, wo_other, up_weight, active_grad,
             scratch=[
                 pltpu.VMEM((half, 2 * width), BF16), pltpu.VMEM((2 * width, model), BF16),
-                pltpu.VMEM((model, hidden), BF16), pltpu.VMEM((hidden, model), BF16),
+                pltpu.VMEM((model, hidden), BF16), pltpu.VMEM((half, hidden), F32),
                 pltpu.VMEM((half, width), BF16), pltpu.VMEM((half, model), BF16),
                 pltpu.VMEM((half, hidden), BF16), pltpu.VMEM((half, hidden), BF16),
                 pltpu.SemaphoreType.DMA((4,)), pltpu.SemaphoreType.DMA((4,)),
@@ -914,7 +938,7 @@
             extra=12, name="middle",
             specs=(
                 [pl.BlockSpec((SUB, C + HD, C), lambda i, n=n: (n, 0, 0)), lanes, lanes, rows(model)]
-                + [WHOLE] * 3 + [rows(model)] + [UNREAD] * 4,
+                + [WHOLE] * 3 + [UNREAD] * 4,
                 [WHOLE] * 3 + [UNREAD] * 4,
             ),
         ))

time: 195 us -> 195 us (level)
  waiting for transfers between devices: 61.7 us -> 57.7 us
  Pallas kernels: 67.2 us -> 71.1 us
    all_to_all x1, waiting for transfers between devices: 11.8 us -> 7.18 us  [on_device(): recv_two = lax.all_to_all(send_two, NEAR + ('mp',), 0, 0)]
    pallas_call x33 -> x34, Pallas kernels: 67.2 us -> 71.1 us  [call(): pl.pallas_call(body, out_shape=[pltpu.HBM(s, d) if spec is UNREAD else ja...]
    unnamed x99 -> x101, local copies, waits for them, and re-layouts: 4.52 us -> 4.54 us
  transfers between devices with their start and end apart: 32 -> 32, of which waited for: 17 -> 17; matrix products, arithmetic and copies ran while one was open for 2% -> 2% of each run, Pallas kernels for 28% -> 30%
where the time goes in v6:
time: 195 us; the launch traced here: 194 us
  Pallas kernels  71.1 us (36%)
  waiting for transfers between devices  57.7 us (30%)
  starting transfers between devices  55.7 us (29%)
  local copies, waits for them, and re-layouts  6.25 us (3%)
    pallas_call x34, Pallas kernels, call(): pl.pallas_call(body, out_shape=[pltpu.HBM(s, d) if spec is UNREAD else ja...  71.1 us
    ppermute x13, starting transfers between devices, fold(): lax.ppermute(give, axes[min(i, len(axes) - 1)], SWAP)  14.7 us
    ppermute x1, waiting for transfers between devices, on_device(): ids_other = other(cluster_ids)  14 us
    ppermute x13, waiting for transfers between devices, fold(): lax.ppermute(give, axes[min(i, len(axes) - 1)], SWAP)  12.6 us
    ppermute x2, waiting for transfers between devices, on_device(): branch_other = [other(b) for b in branch]  10.6 us
    ppermute x4, starting transfers between devices, across(): return [v, lax.ppermute(v, 'g', SWAP)]  10.4 us
    all_to_all x1, waiting for transfers between devices, on_device(): recv_two = lax.all_to_all(send_two, NEAR + ('mp',), 0, 0)  7.18 us
    ppermute x4, waiting for transfers between devices, across(): return [v, lax.ppermute(v, 'g', SWAP)]  7.12 us
  transfers between devices with their start and end apart: 32, of which 17 were waited for; matrix products, arithmetic and copies ran while one was open for 2% of the time, Pallas kernels for 30%

profile of v6, /device:TPU:0, one launch (start us, length us, event | category | flops | bytes accessed | tf_op | source)
XLA Modules:
  0.0 193.6 jit_solution(8428709774043724990)
XLA Ops:
  0.7 1.6 copy.29
  2.4 3.0 %project.1 = (bf16[512,768]{1,0:T(8,128)(2,1)}, bf16[8,128,640]{2,1,0:T(8,128)(2,1)}) custom-call(bf16[512,768]{1,0:T(8,128)(2,1)S(1)} %copy-done.4, f32[768]{0:T(1024)S(1)} %copy-done.39, f32[768]{0:T(1024)S(1)} %copy-done.37, bf16[768,384]{1,0:T(8,128)(2,1)S(1)} %copy-done.17, bf16[768,768]{1,0:T(8,128)(2,1)S(1)} %bitcast.11, s32[6,512]{1,0:T(8,128)S(1)} %copy-done.28), custom_call_target="tpu_custom_call" | custom-call | flops 1000000 | bytes 1 | tf_op jit(solution)/shard_map/project/pallas_call | solution.py:74
  5.4 5.4 %all-to-all-start = ((bf16[8,128,640]{2,1,0:T(8,128)(2,1)}), bf16[8,128,640]{2,1,0:T(8,128)(2,1)S(1)}, u32[]{:S(2)}, u32[]{:S(2)}) async-start(bf16[8,128,640]{2,1,0:T(8,128)(2,1)} %get-tuple-element.110), calls=%async_computation | async-start | bytes 2621440 | tf_op jit(solution)/shard_map/all_to_all | solution.py:889
  10.8 1.6 collective-permute-start.1
  12.9 14.0 %collective-permute-done.refs_1_.refs_2_ = s32[6,512]{1,0:T(8,128)S(1)} collective-permute-done((s32[6,512]{1,0:T(8,128)S(1)}, s32[6,512]{1,0:T(8,128)S(1)}, u32[]{:S(2)}, u32[]{:S(2)}) %collective-permute-start) | collective-permute-done | bytes 12320 | tf_op jit(solution)/shard_map/ppermute | solution.py:873
  26.9 1.2 all-to-all-done.refs_0_
  28.2 2.6 %collective-permute-start.2 = (bf16[128,256]{1,0:T(8,128)(2,1)S(1)}, bf16[128,256]{1,0:T(8,128)(2,1)S(1)}, u32[]{:S(2)}, u32[]{:S(2)}) collective-permute-start(bf16[128,256]{1,0:T(8,128)(2,1)S(1)} %query_sums.1.refs_1_), channel_id=1, source_target_pairs={{0,16},{16,0},{1,17},{17,1},{2,18},{18,2},{3,19},{19,3},{4,20},{20... | collective-permute-start | bytes 196616 | tf_op jit(solution)/shard_map/ppermute | solution.py:796
  30.9 2.6 %collective-permute-done.2.refs_2_ = bf16[128,256]{1,0:T(8,128)(2,1)S(1)} collective-permute-done((bf16[128,256]{1,0:T(8,128)(2,1)S(1)}, bf16[128,256]{1,0:T(8,128)(2,1)S(1)}, u32[]{:S(2)}, u32[]{:S(2)}) %collective-permute-start.2) | collective-permute-done | bytes 65568 | tf_op jit(solution)/shard_map/ppermute | solution.py:796
  33.5 1.8 attend.1
  35.4 2.7 %collective-permute-start.3 = (bf16[128,256]{1,0:T(8,128)(2,1)S(1)}, bf16[128,256]{1,0:T(8,128)(2,1)S(1)}, u32[]{:S(2)}, u32[]{:S(2)}) collective-permute-start(bf16[128,256]{1,0:T(8,128)(2,1)S(1)} %get-tuple-element.111.refs_0_.refs_2_), channel_id=1, source_target_pairs={{0,16},{16,0},{1,17},{17,1},{2,18},{18,2},{3,19},{19,3},{4,20},{20... | collective-permute-start | bytes 196616 | tf_op jit(solution)/shard_map/ppermute | solution.py:796
  38.0 2.6 %collective-permute-done.3.refs_1_ = bf16[128,256]{1,0:T(8,128)(2,1)S(1)} collective-permute-done((bf16[128,256]{1,0:T(8,128)(2,1)S(1)}, bf16[128,256]{1,0:T(8,128)(2,1)S(1)}, u32[]{:S(2)}, u32[]{:S(2)}) %collective-permute-start.3) | collective-permute-done | bytes 65568 | tf_op jit(solution)/shard_map/ppermute | solution.py:796
  40.6 1.5 merge.1
  42.1 5.2 %all-to-all-start.1 = ((bf16[16,192,128]{2,1,0:T(8,128)(2,1)}), bf16[16,192,128]{2,1,0:T(8,128)(2,1)S(1)}, u32[]{:S(2)}, u32[]{:S(2)}) async-start(bf16[16,192,128]{2,1,0:T(8,128)(2,1)} %get-tuple-element.112), calls=%async_computation.1 | async-start | bytes 1572864 | tf_op jit(solution)/shard_map/all_to_all | solution.py:909
  47.4 1.3 broadcast_multiply_fusion.refs_0_.refs_2_.refs_7_
  48.7 4.6 %active_grad.1.refs_10_ = f32[512,1536]{1,0:T(8,128)} custom-call(bf16[512,768]{1,0:T(8,128)(2,1)S(1)} %broadcast_multiply_fusion.refs_0_.refs_2_.refs_7_, bf16[1536,768]{1,0:T(8,128)(2,1)} %refs_1_.12, bf16[128,256]{1,0:T(8,128)(2,1)} %copy-done.25), custom_call_target="tpu_custom_call" | custom-call | flops 1000000 | bytes 1 | tf_op jit(solution)/shard_map/active_grad/pallas_call | solution.py:74
  53.4 7.2 %all-to-all-done.1.refs_0_ = bf16[16,192,128]{2,1,0:T(8,128)(2,1)S(1)} async-done(((bf16[16,192,128]{2,1,0:T(8,128)(2,1)}), bf16[16,192,128]{2,1,0:T(8,128)(2,1)S(1)}, u32[]{:S(2)}, u32[]{:S(2)}) %all-to-all-start.1) | async-done | bytes 786464 | tf_op jit(solution)/shard_map/all_to_all | solution.py:909
  60.6 5.1 %middle.3 = (f32[1,1536]{1,0:T(1,128)S(1)}, f32[256,768]{1,0:T(8,128)S(1)}, bf16[256,768]{1,0:T(8,128)(2,1)S(1)}, bf16[256,384]{1,0:T(8,128)(2,1)}, bf16[256,768...) custom-call(bf16[16,192,128]{2,1,0:T(8,128)(2,1)S(1)} %all-to-all-done.1.refs_0_, ...), custom_call_target="tpu_custom_call" | custom-call | flops 1000000 | bytes 1 | tf_op jit(solution)/shard_map/middle/pallas_call | solution.py:74
  66.3 5.1 %middle.2 = (f32[1,1536]{1,0:T(1,128)S(1)}, f32[256,768]{1,0:T(8,128)S(1)}, bf16[256,768]{1,0:T(8,128)(2,1)S(1)}, bf16[256,384]{1,0:T(8,128)(2,1)}, bf16[256,768...) custom-call(bf16[16,192,128]{2,1,0:T(8,128)(2,1)S(1)} %all-to-all-done.1.refs_0_, ...), custom_call_target="tpu_custom_call" | custom-call | flops 1000000 | bytes 1 | tf_op jit(solution)/shard_map/middle/pallas_call | solution.py:74
  71.4 1.5 collective-permute-start.4
  73.0 4.6 %up_terms.1 = (bf16[384,1536]{1,0:T(8,128)(2,1)}, bf16[384,1536]{1,0:T(8,128)(2,1)}, f32[8,128]{1,0:T(8,128)}) custom-call(bf16[256,768]{1,0:T(8,128)(2,1)} %get-tuple-element.120.refs_0_, bf16[256,1536]{1,0:T(8,128)(2,1)} %get-tuple-element.121.refs_1_, bf16[256,768]{1,0:T(8,128)(2,1)} %get-tuple-element.122.refs_2_, ...), custom_call_target="tpu_custom_call" | custom-call | flops 1000000 | bytes 1 | tf_op jit(solution)/shard_map/up_terms/pallas_call | solution.py:74
  77.7 4.7 %down_terms.1 = (bf16[384,1536]{1,0:T(8,128)(2,1)}, bf16[384,1536]{1,0:T(8,128)(2,1)}, f32[8,128]{1,0:T(8,128)}) custom-call(bf16[512,768]{1,0:T(8,128)(2,1)} %copy-done.2, bf16[256,1536]{1,0:T(8,128)(2,1)} %get-tuple-element.114.refs_1_.refs_0_, bf16[512,768]{1,0:T(8,128)(2,1)} %copy-done.2, bf16[256,1536]{1,0:T(8,128)(2,1)} %get-tuple-element.125.refs_3_.refs_0_), custom_call_target="tpu_custom_call" | custom-call | flops 1000000 | bytes 1 | tf_op jit(solution)/shard_map/down_terms/pallas_call | solution.py:74
  82.4 3.2 %collective-permute-done.4.refs_2_ = bf16[256,768]{1,0:T(8,128)(2,1)S(1)} collective-permute-done((bf16[256,768]{1,0:T(8,128)(2,1)S(1)}, bf16[256,768]{1,0:T(8,128)(2,1)S(1)}, u32[]{:S(2)}, u32[]{:S(2)}) %collective-permute-start.4) | collective-permute-done | bytes 393248 | tf_op jit(solution)/shard_map/ppermute | solution.py:946
  85.6 3.8 %turn.1 = (f32[256,768]{1,0:T(8,128)}, bf16[512,768]{1,0:T(8,128)(2,1)}, bf16[8,208,128]{2,1,0:T(8,128)(2,1)}, f32[8,128]{1,0:T(8,128)}) custom-call(bf16[256,768]{1,0:T(8,128)(2,1)S(1)} %get-tuple-element.115.refs_0_, bf16[256,768]{1,0:T(8,128)(2,1)S(1)} %get-tuple-element.116.refs_1_, bf16[256,768]{1,0:T(8,128)(2,1)S(1)} %collective-permute-done.4.refs_2_, ...), custom_call_target="tpu_custom_call" | custom-call | flops 40000000000 | bytes 1 | tf_op jit(solution)/shard_map/turn/pallas_call | solution.py:74
  89.4 4.3 %all-to-all-start.2 = ((bf16[8,208,128]{2,1,0:T(8,128)(2,1)}), bf16[8,208,128]{2,1,0:T(8,128)(2,1)}, u32[]{:S(2)}, u32[]{:S(2)}) async-start(bf16[8,208,128]{2,1,0:T(8,128)(2,1)} %get-tuple-element.132), calls=%async_computation.2 | async-start | bytes 851968 | tf_op jit(solution)/shard_map/all_to_all | solution.py:963
  93.7 0.8 branch.2
  96.0 2.6 %up_fold.3 = (bf16[192,1536]{1,0:T(8,128)(2,1)}, bf16[192,1536]{1,0:T(8,128)(2,1)}, f32[8,128]{1,0:T(8,128)}) custom-call(bf16[384,1536]{1,0:T(8,128)(2,1)S(1)} %copy-done.12, bf16[384,1536]{1,0:T(8,128)(2,1)} %collective-permute-done.8.refs_1_, f32[8,128]{1,0:T(8,128)} %get-tuple-element.135.refs_2_, f32[8,128]{1,0:T(8,128)} %get-tuple-element.136.refs_3_), custom_call_target="tpu_custom_call" | custom-call | flops 1000000 | bytes 1 | tf_op jit(solution)/shard_map/up_fold/pallas_call | solution.py:74
  98.6 1.9 %collective-permute-start.11 = (bf16[192,1536]{1,0:T(8,128)(2,1)}, bf16[192,1536]{1,0:T(8,128)(2,1)S(1)}, u32[]{:S(2)}, u32[]{:S(2)}) collective-permute-start(bf16[192,1536]{1,0:T(8,128)(2,1)} %get-tuple-element.148), channel_id=1, source_target_pairs={{0,4},{4,0},{1,5},{5,1},{2,6},{6,2},{3,7},{7,3},{8,12},{12,8},{9,1... | collective-permute-start | bytes 1769480 | tf_op jit(solution)/shard_map/ppermute | solution.py:840
  100.5 1.0 all-to-all-done.2.refs_0_
  101.5 1.1 grad_sums.1
  102.6 2.9 %collective-permute-start.9 = (bf16[208,128]{1,0:T(8,128)(2,1)S(1)}, bf16[208,128]{1,0:T(8,128)(2,1)S(1)}, u32[]{:S(2)}, u32[]{:S(2)}) collective-permute-start(bf16[208,128]{1,0:T(8,128)(2,1)S(1)} %get-tuple-element.138.refs_3_), channel_id=1, source_target_pairs={{0,16},{16,0},{1,17},{17,1},{2,18},{18,2},{3,19},{19,3},{4,20},{20... | collective-permute-start | bytes 159752 | tf_op jit(solution)/shard_map/ppermute | solution.py:796
  105.5 2.9 %out_terms.1 = (bf16[384,384]{1,0:T(8,128)(2,1)}, bf16[384,384]{1,0:T(8,128)(2,1)}, f32[8,128]{1,0:T(8,128)}) custom-call(bf16[512,768]{1,0:T(8,128)(2,1)} %get-tuple-element.139.refs_0_.refs_2_, bf16[256,384]{1,0:T(8,128)(2,1)} %get-tuple-element.140.refs_1_, bf16[512,768]{1,0:T(8,128)(2,1)} %get-tuple-element.139.refs_0_.refs_2_, ...), custom_call_target="tpu_custom_call" | custom-call | flops 1000000 | bytes 1 | tf_op jit(solution)/shard_map/out_terms/pallas_call | solution.py:74
  108.4 3.9 %attend_back.1 = (bf16[192,128]{1,0:T(8,128)(2,1)S(1)}, f32[4,128]{1,0:T(4,128)S(1)}, bf16[8,128,640]{2,1,0:T(8,128)(2,1)}, f32[8,128]{1,0:T(8,128)}) custom-call(bf16[8,128,640]{2,1,0:T(8,128)(2,1)} %copy-done.1, f32[128,256]{1,0:T(8,128)} %get-tuple-element.130.refs_1_, f32[128,256]{1,0:T(8,128)} %get-tuple-element.131.refs_2_, ...), custom_call_target="tpu_custom_call" | custom-call | flops 1000000 | bytes 1 | tf_op jit(solution)/shard_map/attend_back/pallas_call | solution.py:74
  112.3 2.2 %collective-permute-start.10 = (bf16[192,128]{1,0:T(8,128)(2,1)S(1)}, bf16[192,128]{1,0:T(8,128)(2,1)S(1)}, u32[]{:S(2)}, u32[]{:S(2)}) collective-permute-start(bf16[192,128]{1,0:T(8,128)(2,1)S(1)} %get-tuple-element.146.refs_3_), channel_id=1, source_target_pairs={{0,16},{16,0},{1,17},{17,1},{2,18},{18,2},{3,19},{19,3},{4,20},{20... | collective-permute-start | bytes 147464 | tf_op jit(solution)/shard_map/ppermute | solution.py:796
  114.6 0.9 up_fold.4
  115.5 1.9 collective-permute-done.10.refs_4_
  117.4 1.0 finish_back.1
  118.5 3.7 %all-to-all-start.3 = ((bf16[8,128,640]{2,1,0:T(8,128)(2,1)}), bf16[8,128,640]{2,1,0:T(8,128)(2,1)S(1)}, u32[]{:S(2)}, u32[]{:S(2)}) async-start(bf16[8,128,640]{2,1,0:T(8,128)(2,1)} %get-tuple-element.153), calls=%async_computation.3 | async-start | bytes 2621440 | tf_op jit(solution)/shard_map/all_to_all | solution.py:1002
  123.1 10.6 %collective-permute-done.7.refs_5_ = bf16[256,768]{1,0:T(8,128)(2,1)S(1)} collective-permute-done((bf16[256,768]{1,0:T(8,128)(2,1)S(1)}, bf16[256,768]{1,0:T(8,128)(2,1)S(1)}, u32[]{:S(2)}, u32[]{:S(2)}) %collective-permute-start.7) | collective-permute-done | bytes 393248 | tf_op jit(solution)/shard_map/ppermute | solution.py:973
  133.8 0.8 copy-done.46
  134.6 2.9 %output.1 = (bf16[512,768]{1,0:T(8,128)(2,1)}, f32[8,128]{1,0:T(8,128)}) custom-call(f32[256,768]{1,0:T(8,128)} %copy-done.15, bf16[256,768]{1,0:T(8,128)(2,1)} %copy-done.20, bf16[256,768]{1,0:T(8,128)(2,1)} %copy-done.45, f32[256,768]{1,0:T(8,128)} %copy-done.14, bf16[256,768]{1,0:T(8,128)(2,1)} %copy-done.21, bf16[256,768]{1,0:T(8,128)(2,1)} %copy-done.46, ...), custom_call_target="tpu_custom_call" | custom-call | flops 1000000 | bytes 1 | tf_op jit(solution)/shard_map/output/pallas_call | solution.py:74
  137.5 1.3 down_fold.3
  138.9 1.9 %collective-permute-start.22 = (bf16[192,1920]{1,0:T(8,128)(2,1)}, bf16[192,1920]{1,0:T(8,128)(2,1)S(1)}, u32[]{:S(2)}, u32[]{:S(2)}) collective-permute-start(bf16[192,1920]{1,0:T(8,128)(2,1)} %get-tuple-element.182), channel_id=1, source_target_pairs={{0,8},{8,0},{1,9},{9,1},{2,10},{10,2},{3,11},{11,3},{4,12},{12,4},... | collective-permute-start | bytes 2211848 | tf_op jit(solution)/shard_map/ppermute | solution.py:840
  140.8 3.4 %first_back.1 = (bf16[512,1152]{1,0:T(8,128)(2,1)}, bf16[256,768]{1,0:T(8,128)(2,1)}, bf16[256,768]{1,0:T(8,128)(2,1)}, f32[8,128]{1,0:T(8,128)}) custom-call(bf16[8,128,640]{2,1,0:T(8,128)(2,1)S(1)} %all-to-all-done.3.refs_0_.refs_1_, s32[6,512]{1,0:T(8,128)S(1)} %copy-done.28, bf16[768,384]{1,0:T(8,128)(2,1)} %refs_2_.4, bf16[768,768]{1,0:T(8,128)(2,1)} %bitcast.12, ...), custom_call_target="tpu_custom_call" | custom-call | flops 40000000000 | bytes 1 | tf_op jit(solution)/shard_map/first_back/pallas_call | solution.py:74
  144.9 4.2 %qkv_terms.1 = (bf16[384,1152]{1,0:T(8,128)(2,1)}, bf16[384,384]{1,0:T(8,128)(2,1)}, bf16[384,384]{1,0:T(8,128)(2,1)}, bf16[384,384]{1,0:T(8,128)(2,1)}, f32[8,128]{1,0:T(8,128)}) custom-call(bf16[512,768]{1,0:T(8,128)(2,1)} %get-tuple-element.163.refs_0_, bf16[512,1152]{1,0:T(8,128)(2,1)} %get-tuple-element.164.refs_1_, f32[8,128]{1,0:T(8,128)} %get-tuple-element.165.refs_2_), custom_call_target="tpu_custom_call" | custom-call | flops 1000000 | bytes 1 | tf_op jit(solution)/shard_map/qkv_terms/pallas_call | solution.py:74
  149.7 1.2 collective-permute-done.15.refs_1_
  151.8 1.2 copy-done.13
  153.0 1.1 qkv_fold.3
  154.1 1.5 collective-permute-start.19
  155.6 2.9 %collective-permute-done.22.refs_1_ = bf16[192,1920]{1,0:T(8,128)(2,1)S(1)} collective-permute-done((bf16[192,1920]{1,0:T(8,128)(2,1)}, bf16[192,1920]{1,0:T(8,128)(2,1)S(1)}, u32[]{:S(2)}, u32[]{:S(2)}) %collective-permute-start.22) | collective-permute-done | bytes 737312 | tf_op jit(solution)/shard_map/ppermute | solution.py:840
  158.5 1.0 down_fold.4
  159.5 2.0 %collective-permute-start.23 = (bf16[96,1920]{1,0:T(8,128)(2,1)}, bf16[96,1920]{1,0:T(8,128)(2,1)S(1)}, u32[]{:S(2)}, u32[]{:S(2)}) collective-permute-start(bf16[96,1920]{1,0:T(8,128)(2,1)} %get-tuple-element.184), channel_id=1, source_target_pairs={{0,4},{4,0},{1,5},{5,1},{2,6},{6,2},{3,7},{7,3},{8,12},{12,8},{9,1... | collective-permute-start | bytes 1105928 | tf_op jit(solution)/shard_map/ppermute | solution.py:840
  161.6 1.3 last.1
  163.7 3.8 %all-to-all-start.4 = ((f32[32,2,48]{2,1,0:T(2,128)}), f32[32,2,48]{2,1,0:T(2,128)S(1)}, u32[]{:S(2)}, u32[]{:S(2)}) async-start(f32[32,2,48]{2,1,0:T(2,128)} %get-tuple-element.185), calls=%async_computation.4 | async-start | bytes 65536 | tf_op jit(solution)/shard_map/all_to_all | solution.py:1037
  167.4 1.8 collective-permute-start.18
  170.1 2.4 %collective-permute-start.26 = (bf16[48,1536]{1,0:T(8,128)(2,1)}, bf16[48,1536]{1,0:T(8,128)(2,1)S(1)}, u32[]{:S(2)}, u32[]{:S(2)}) collective-permute-start(bf16[48,1536]{1,0:T(8,128)(2,1)} %get-tuple-element.197), channel_id=1, source_target_pairs={{0,16},{16,0},{1,17},{17,1},{2,18},{18,2},{3,19},{19,3},{4,20},{20... | collective-permute-start | bytes 442376 | tf_op jit(solution)/shard_map/ppermute | solution.py:840
  172.5 0.8 qkv_fold.4
  173.4 1.6 collective-permute-start.21
  175.0 0.8 all-to-all-done.4.refs_0_
  175.9 0.8 down_fold.5
  176.7 2.3 %collective-permute-start.25 = (bf16[48,1920]{1,0:T(8,128)(2,1)}, bf16[48,1920]{1,0:T(8,128)(2,1)S(1)}, u32[]{:S(2)}, u32[]{:S(2)}) collective-permute-start(bf16[48,1920]{1,0:T(8,128)(2,1)} %get-tuple-element.195), channel_id=1, source_target_pairs={{0,16},{16,0},{1,17},{17,1},{2,18},{18,2},{3,19},{19,3},{4,20},{20... | collective-permute-start | bytes 552968 | tf_op jit(solution)/shard_map/ppermute | solution.py:840
  180.7 4.4 %collective-permute-done.21.refs_1_ = bf16[96,1152]{1,0:T(8,128)(2,1)S(1)} collective-permute-done((bf16[96,1152]{1,0:T(8,128)(2,1)}, bf16[96,1152]{1,0:T(8,128)(2,1)S(1)}, u32[]{:S(2)}, u32[]{:S(2)}) %collective-permute-start.21) | collective-permute-done | bytes 221216 | tf_op jit(solution)/shard_map/ppermute | solution.py:840
  186.0 1.9 %join.1 = (bf16[512,768]{1,0:T(8,128)(2,1)}, f32[8,128]{1,0:T(8,128)}) custom-call(bf16[256,768]{1,0:T(8,128)(2,1)S(1)} %copy-done.42, bf16[256,768]{1,0:T(8,128)(2,1)} %collective-permute-done.18.refs_1_, f32[8,128]{1,0:T(8,128)} %get-tuple-element.189.refs_2_, f32[8,128]{1,0:T(8,128)} %get-tuple-element.187.refs_2_.refs_3_), custom_call_target="tpu_custom_call" | custom-call | flops 40000000000 | bytes 1 | tf_op jit(solution)/shard_map/join/pallas_call | solution.py:74
  188.7 2.5 %collective-permute-done.25.refs_1_ = bf16[48,1920]{1,0:T(8,128)(2,1)S(1)} collective-permute-done((bf16[48,1920]{1,0:T(8,128)(2,1)}, bf16[48,1920]{1,0:T(8,128)(2,1)S(1)}, u32[]{:S(2)}, u32[]{:S(2)}) %collective-permute-start.25) | collective-permute-done | bytes 184352 | tf_op jit(solution)/shard_map/ppermute | solution.py:840
  192.0 0.9 collective-permute-done.24.refs_1_
  (140 shorter events, 12.5 us)
Async XLA Ops:
  5.4 5.4 %copy-start.9 = (bf16[384,768]{1,0:T(8,128)(2,1)S(1)}, bf16[384,768]{1,0:T(8,128)(2,1)}, u32[]{:S(2)}) copy-start(bf16[384,768]{1,0:T(8,128)(2,1)} %refs_8_.1) | copy-start | bytes 1769476
  5.4 22.6 %all-to-all-start = ((bf16[8,128,640]{2,1,0:T(8,128)(2,1)}), bf16[8,128,640]{2,1,0:T(8,128)(2,1)S(1)}, u32[]{:S(2)}, u32[]{:S(2)}) async-start(bf16[8,128,640]{2,1,0:T(8,128)(2,1)} %get-tuple-element.110), calls=%async_computation | async-start | bytes 2621440 | tf_op jit(solution)/shard_map/all_to_all | solution.py:889
  10.8 16.1 %collective-permute-start.1 = (bf16[384,768]{1,0:T(8,128)(2,1)S(1)}, bf16[384,768]{1,0:T(8,128)(2,1)}, u32[]{:S(2)}, u32[]{:S(2)}) collective-permute-start(bf16[384,768]{1,0:T(8,128)(2,1)S(1)} %copy-done.9), channel_id=1, source_target_pairs={{0,1},{1,0},{2,3},{3,2},{4,5},{5,4},{6,7},{7,6},{8,9},{9,8},{10,11... | collective-permute-start | bytes 1769480 | tf_op jit(solution)/shard_map/ppermute | solution.py:874
  12.4 14.5 %collective-permute-start = (s32[6,512]{1,0:T(8,128)S(1)}, s32[6,512]{1,0:T(8,128)S(1)}, u32[]{:S(2)}, u32[]{:S(2)}) collective-permute-start(s32[6,512]{1,0:T(8,128)S(1)} %copy-done.28), channel_id=1, source_target_pairs={{0,1},{1,0},{2,3},{3,2},{4,5},{5,4},{6,7},{7,6},{8,9},{9,8},{10,11... | collective-permute-start | bytes 36872 | tf_op jit(solution)/shard_map/ppermute | solution.py:873
  28.1 7.3 %copy-start.1 = (bf16[8,128,640]{2,1,0:T(8,128)(2,1)}, bf16[8,128,640]{2,1,0:T(8,128)(2,1)S(1)}, u32[]{:S(2)}) copy-start(bf16[8,128,640]{2,1,0:T(8,128)(2,1)S(1)} %all-to-all-done.refs_0_) | copy-start | bytes 3932164
  28.2 5.3 %collective-permute-start.2 = (bf16[128,256]{1,0:T(8,128)(2,1)S(1)}, bf16[128,256]{1,0:T(8,128)(2,1)S(1)}, u32[]{:S(2)}, u32[]{:S(2)}) collective-permute-start(bf16[128,256]{1,0:T(8,128)(2,1)S(1)} %query_sums.1.refs_1_), channel_id=1, source_target_pairs={{0,16},{16,0},{1,17},{17,1},{2,18},{18,2},{3,19},{19,3},{4,20},{20... | collective-permute-start | bytes 196616 | tf_op jit(solution)/shard_map/ppermute | solution.py:796
  35.4 13.3 %copy-start.25 = (bf16[128,256]{1,0:T(8,128)(2,1)}, bf16[128,256]{1,0:T(8,128)(2,1)S(1)}, u32[]{:S(2)}) copy-start(bf16[128,256]{1,0:T(8,128)(2,1)S(1)} %get-tuple-element.111.refs_0_.refs_2_) | copy-start | bytes 196612
  35.4 12.0 %copy-start.47 = (s32[512]{0:T(512)S(1)}, s32[512]{0:T(512)}, u32[]{:S(2)}) copy-start(s32[512]{0:T(512)} %param.29) | copy-start | bytes 6148
  35.4 5.2 %collective-permute-start.3 = (bf16[128,256]{1,0:T(8,128)(2,1)S(1)}, bf16[128,256]{1,0:T(8,128)(2,1)S(1)}, u32[]{:S(2)}, u32[]{:S(2)}) collective-permute-start(bf16[128,256]{1,0:T(8,128)(2,1)S(1)} %get-tuple-element.111.refs_0_.refs_2_), channel_id=1, source_target_pairs={{0,16},{16,0},{1,17},{17,1},{2,18},{18,2},{3,19},{19,3},{4,20},{20... | collective-permute-start | bytes 196616 | tf_op jit(solution)/shard_map/ppermute | solution.py:796
  42.1 18.4 %all-to-all-start.1 = ((bf16[16,192,128]{2,1,0:T(8,128)(2,1)}), bf16[16,192,128]{2,1,0:T(8,128)(2,1)S(1)}, u32[]{:S(2)}, u32[]{:S(2)}) async-start(bf16[16,192,128]{2,1,0:T(8,128)(2,1)} %get-tuple-element.112), calls=%async_computation.1 | async-start | bytes 1572864 | tf_op jit(solution)/shard_map/all_to_all | solution.py:909
  48.7 4.7 %copy-start.2 = (bf16[512,768]{1,0:T(8,128)(2,1)}, bf16[512,768]{1,0:T(8,128)(2,1)S(1)}, u32[]{:S(2)}) copy-start(bf16[512,768]{1,0:T(8,128)(2,1)S(1)} %broadcast_multiply_fusion.refs_0_.refs_2_.refs_7_) | copy-start | bytes 2359300
  48.7 11.9 %copy-start.30 = (s32[6,512]{1,0:T(8,128)S(1)}, s32[6,512]{1,0:T(8,128)}, u32[]{:S(2)}) copy-start(s32[6,512]{1,0:T(8,128)} %copy-done.29) | copy-start | bytes 36868
  48.7 11.9 %copy-start.34 = (f32[1536]{0:T(1024)S(1)}, f32[1536]{0:T(1024)}, u32[]{:S(2)}) copy-start(f32[1536]{0:T(1024)} %refs_6_.5) | copy-start | bytes 18436
  48.7 11.9 %copy-start.35 = (f32[768]{0:T(1024)S(1)}, f32[768]{0:T(1024)}, u32[]{:S(2)}) copy-start(f32[768]{0:T(1024)} %refs_5_.5) | copy-start | bytes 9220
  48.7 11.9 %copy-start.36 = (f32[768]{0:T(1024)S(1)}, f32[768]{0:T(1024)}, u32[]{:S(2)}) copy-start(f32[768]{0:T(1024)} %refs_6_.6) | copy-start | bytes 9220
  65.6 20.0 %copy-start.14 = (f32[256,768]{1,0:T(8,128)}, f32[256,768]{1,0:T(8,128)S(1)}, u32[]{:S(2)}) copy-start(f32[256,768]{1,0:T(8,128)S(1)} %get-tuple-element.117.refs_5_.refs_3_) | copy-start | bytes 2359300
  65.7 16.8 %collective-permute-start.5 = (bf16[256,768]{1,0:T(8,128)(2,1)S(1)}, bf16[256,768]{1,0:T(8,128)(2,1)S(1)}, u32[]{:S(2)}, u32[]{:S(2)}) collective-permute-start(bf16[256,768]{1,0:T(8,128)(2,1)S(1)} %get-tuple-element.116.refs_1_), channel_id=1, source_target_pairs={{0,1},{1,0},{2,3},{3,2},{4,5},{5,4},{6,7},{7,6},{8,9},{9,8},{10,11... | collective-permute-start | bytes 1179656 | tf_op jit(solution)/shard_map/ppermute | solution.py:946
  71.4 14.2 %copy-start.15 = (f32[256,768]{1,0:T(8,128)}, f32[256,768]{1,0:T(8,128)S(1)}, u32[]{:S(2)}) copy-start(f32[256,768]{1,0:T(8,128)S(1)} %get-tuple-element.113.refs_4_.refs_0_) | copy-start | bytes 2359300
  71.4 14.2 %collective-permute-start.4 = (bf16[256,768]{1,0:T(8,128)(2,1)S(1)}, bf16[256,768]{1,0:T(8,128)(2,1)S(1)}, u32[]{:S(2)}, u32[]{:S(2)}) collective-permute-start(bf16[256,768]{1,0:T(8,128)(2,1)S(1)} %get-tuple-element.115.refs_0_), channel_id=1, source_target_pairs={{0,1},{1,0},{2,3},{3,2},{4,5},{5,4},{6,7},{7,6},{8,9},{9,8},{10,11... | collective-permute-start | bytes 1179656 | tf_op jit(solution)/shard_map/ppermute | solution.py:946
  77.6 18.4 %collective-permute-start.8 = (bf16[384,1536]{1,0:T(8,128)(2,1)}, bf16[384,1536]{1,0:T(8,128)(2,1)}, u32[]{:S(2)}, u32[]{:S(2)}) collective-permute-start(bf16[384,1536]{1,0:T(8,128)(2,1)} %get-tuple-element.134), channel_id=1, source_target_pairs={{0,2},{2,0},{1,3},{3,1},{4,6},{6,4},{5,7},{7,5},{8,10},{10,8},{9,1... | collective-permute-start | bytes 3538952 | tf_op jit(solution)/shard_map/ppermute | solution.py:840
  77.7 7.9 %copy-start.3 = (bf16[512,768]{1,0:T(8,128)(2,1)S(1)}, bf16[512,768]{1,0:T(8,128)(2,1)}, u32[]{:S(2)}) copy-start(bf16[512,768]{1,0:T(8,128)(2,1)} %copy-done.2) | copy-start | bytes 2359300
  77.7 7.9 %copy-start.10 = (bf16[384,768]{1,0:T(8,128)(2,1)S(1)}, bf16[384,768]{1,0:T(8,128)(2,1)}, u32[]{:S(2)}) copy-start(bf16[384,768]{1,0:T(8,128)(2,1)} %refs_8_.1) | copy-start | bytes 1769476
  85.6 8.1 %copy-start = (bf16[1536,768]{1,0:T(8,128)(2,1)S(1)}, bf16[1536,768]{1,0:T(8,128)(2,1)}, u32[]{:S(2)}) copy-start(bf16[1536,768]{1,0:T(8,128)(2,1)} %refs_1_.12) | copy-start | bytes 7077892
  89.4 12.1 %all-to-all-start.2 = ((bf16[8,208,128]{2,1,0:T(8,128)(2,1)}), bf16[8,208,128]{2,1,0:T(8,128)(2,1)}, u32[]{:S(2)}, u32[]{:S(2)}) async-start(bf16[8,208,128]{2,1,0:T(8,128)(2,1)} %get-tuple-element.132), calls=%async_computation.2 | async-start | bytes 851968 | tf_op jit(solution)/shard_map/all_to_all | solution.py:963
  94.5 21.0 %collective-permute-start.6 = (bf16[256,768]{1,0:T(8,128)(2,1)S(1)}, bf16[256,768]{1,0:T(8,128)(2,1)S(1)}, u32[]{:S(2)}, u32[]{:S(2)}) collective-permute-start(bf16[256,768]{1,0:T(8,128)(2,1)S(1)} %get-tuple-element.128.refs_1_), channel_id=1, source_target_pairs={{0,1},{1,0},{2,3},{3,2},{4,5},{5,4},{6,7},{7,6},{8,9},{9,8},{10,11... | collective-permute-start | bytes 1179656 | tf_op jit(solution)/shard_map/ppermute | solution.py:973
  96.0 26.6 %copy-start.21 = (bf16[256,768]{1,0:T(8,128)(2,1)}, bf16[256,768]{1,0:T(8,128)(2,1)S(1)}, u32[]{:S(2)}) copy-start(bf16[256,768]{1,0:T(8,128)(2,1)S(1)} %get-tuple-element.129.refs_4_) | copy-start | bytes 1179652
  98.6 16.0 %collective-permute-start.11 = (bf16[192,1536]{1,0:T(8,128)(2,1)}, bf16[192,1536]{1,0:T(8,128)(2,1)S(1)}, u32[]{:S(2)}, u32[]{:S(2)}) collective-permute-start(bf16[192,1536]{1,0:T(8,128)(2,1)} %get-tuple-element.148), channel_id=1, source_target_pairs={{0,4},{4,0},{1,5},{5,1},{2,6},{6,2},{3,7},{7,3},{8,12},{12,8},{9,1... | collective-permute-start | bytes 1769480 | tf_op jit(solution)/shard_map/ppermute | solution.py:840
  102.6 5.8 %collective-permute-start.9 = (bf16[208,128]{1,0:T(8,128)(2,1)S(1)}, bf16[208,128]{1,0:T(8,128)(2,1)S(1)}, u32[]{:S(2)}, u32[]{:S(2)}) collective-permute-start(bf16[208,128]{1,0:T(8,128)(2,1)S(1)} %get-tuple-element.138.refs_3_), channel_id=1, source_target_pairs={{0,16},{16,0},{1,17},{17,1},{2,18},{18,2},{3,19},{19,3},{4,20},{20... | collective-permute-start | bytes 159752 | tf_op jit(solution)/shard_map/ppermute | solution.py:796
  108.4 6.2 %copy-start.18 = (bf16[192,1536]{1,0:T(8,128)(2,1)S(1)}, bf16[192,1536]{1,0:T(8,128)(2,1)}, u32[]{:S(2)}) copy-start(bf16[192,1536]{1,0:T(8,128)(2,1)} %get-tuple-element.147.refs_0_) | copy-start | bytes 1769476
  108.4 9.0 %copy-start.32 = (f32[128,256]{1,0:T(8,128)S(1)}, f32[128,256]{1,0:T(8,128)}, u32[]{:S(2)}) copy-start(f32[128,256]{1,0:T(8,128)} %get-tuple-element.130.refs_1_) | copy-start | bytes 393220
  112.3 5.1 %collective-permute-start.10 = (bf16[192,128]{1,0:T(8,128)(2,1)S(1)}, bf16[192,128]{1,0:T(8,128)(2,1)S(1)}, u32[]{:S(2)}, u32[]{:S(2)}) collective-permute-start(bf16[192,128]{1,0:T(8,128)(2,1)S(1)} %get-tuple-element.146.refs_3_), channel_id=1, source_target_pairs={{0,16},{16,0},{1,17},{17,1},{2,18},{18,2},{3,19},{19,3},{4,20},{20... | collective-permute-start | bytes 147464 | tf_op jit(solution)/shard_map/ppermute | solution.py:796
  118.4 4.7 %copy-start.49 = (bf16[384,384]{1,0:T(8,128)(2,1)S(1)}, bf16[384,384]{1,0:T(8,128)(2,1)}, u32[]{:S(2)}) copy-start(bf16[384,384]{1,0:T(8,128)(2,1)} %get-tuple-element.158) | copy-start | bytes 884740
  118.5 16.1 %copy-start.38 = (f32[768]{0:T(1024)S(1)}, f32[768]{0:T(1024)}, u32[]{:S(2)}) copy-start(f32[768]{0:T(1024)} %refs_6_.7) | copy-start | bytes 9220
  118.5 22.3 %all-to-all-start.3 = ((bf16[8,128,640]{2,1,0:T(8,128)(2,1)}), bf16[8,128,640]{2,1,0:T(8,128)(2,1)S(1)}, u32[]{:S(2)}, u32[]{:S(2)}) async-start(bf16[8,128,640]{2,1,0:T(8,128)(2,1)} %get-tuple-element.153), calls=%async_computation.3 | async-start | bytes 2621440 | tf_op jit(solution)/shard_map/all_to_all | solution.py:1002
  122.2 15.3 %collective-permute-start.12 = (bf16[384,1536]{1,0:T(8,128)(2,1)}, bf16[384,1536]{1,0:T(8,128)(2,1)S(1)}, u32[]{:S(2)}, u32[]{:S(2)}) collective-permute-start(bf16[384,1536]{1,0:T(8,128)(2,1)} %get-tuple-element.157), channel_id=1, source_target_pairs={{0,2},{2,0},{1,3},{3,1},{4,6},{6,4},{5,7},{7,5},{8,10},{10,8},{9,1... | collective-permute-start | bytes 3538952 | tf_op jit(solution)/shard_map/ppermute | solution.py:860
  122.6 11.2 %collective-permute-start.7 = (bf16[256,768]{1,0:T(8,128)(2,1)S(1)}, bf16[256,768]{1,0:T(8,128)(2,1)S(1)}, u32[]{:S(2)}, u32[]{:S(2)}) collective-permute-start(bf16[256,768]{1,0:T(8,128)(2,1)S(1)} %get-tuple-element.129.refs_4_), channel_id=1, source_target_pairs={{0,1},{1,0},{2,3},{3,2},{4,5},{5,4},{6,7},{7,6},{8,9},{9,8},{10,11... | collective-permute-start | bytes 1179656 | tf_op jit(solution)/shard_map/ppermute | solution.py:973
  123.1 14.4 %collective-permute-start.13 = (bf16[384,384]{1,0:T(8,128)(2,1)S(1)}, bf16[384,384]{1,0:T(8,128)(2,1)S(1)}, u32[]{:S(2)}, u32[]{:S(2)}) collective-permute-start(bf16[384,384]{1,0:T(8,128)(2,1)S(1)} %copy-done.49), channel_id=1, source_target_pairs={{0,2},{2,0},{1,3},{3,1},{4,6},{6,4},{5,7},{7,5},{8,10},{10,8},{9,1... | collective-permute-start | bytes 884744 | tf_op jit(solution)/shard_map/ppermute | solution.py:860
  138.9 19.7 %collective-permute-start.22 = (bf16[192,1920]{1,0:T(8,128)(2,1)}, bf16[192,1920]{1,0:T(8,128)(2,1)S(1)}, u32[]{:S(2)}, u32[]{:S(2)}) collective-permute-start(bf16[192,1920]{1,0:T(8,128)(2,1)} %get-tuple-element.182), channel_id=1, source_target_pairs={{0,8},{8,0},{1,9},{9,1},{2,10},{10,2},{3,11},{11,3},{4,12},{12,4},... | collective-permute-start | bytes 2211848 | tf_op jit(solution)/shard_map/ppermute | solution.py:840
  144.2 6.7 %copy-start.48 = (bf16[96,1536]{1,0:T(8,128)(2,1)S(1)}, bf16[96,1536]{1,0:T(8,128)(2,1)}, u32[]{:S(2)}) copy-start(bf16[96,1536]{1,0:T(8,128)(2,1)} %get-tuple-element.176) | copy-start | bytes 884740
  144.3 17.3 %collective-permute-start.14 = (bf16[256,768]{1,0:T(8,128)(2,1)}, bf16[256,768]{1,0:T(8,128)(2,1)S(1)}, u32[]{:S(2)}, u32[]{:S(2)}) collective-permute-start(bf16[256,768]{1,0:T(8,128)(2,1)} %get-tuple-element.161), channel_id=1, source_target_pairs={{0,1},{1,0},{2,3},{3,2},{4,5},{5,4},{6,7},{7,6},{8,9},{9,8},{10,11... | collective-permute-start | bytes 1179656 | tf_op jit(solution)/shard_map/ppermute | solution.py:1023
  144.9 13.7 %copy-start.16 = (bf16[192,1920]{1,0:T(8,128)(2,1)S(1)}, bf16[192,1920]{1,0:T(8,128)(2,1)}, u32[]{:S(2)}) copy-start(bf16[192,1920]{1,0:T(8,128)(2,1)} %get-tuple-element.181.refs_0_) | copy-start | bytes 2211844
  149.1 1.9 collective-permute-start.15
  149.2 2.2 %collective-permute-start.16 = (bf16[384,384]{1,0:T(8,128)(2,1)}, bf16[384,384]{1,0:T(8,128)(2,1)S(1)}, u32[]{:S(2)}, u32[]{:S(2)}) collective-permute-start(bf16[384,384]{1,0:T(8,128)(2,1)} %get-tuple-element.168), channel_id=1, source_target_pairs={{0,2},{2,0},{1,3},{3,1},{4,6},{6,4},{5,7},{7,5},{8,10},{10,8},{9,1... | collective-permute-start | bytes 884744 | tf_op jit(solution)/shard_map/ppermute | solution.py:840
  149.7 2.1 %collective-permute-start.17 = (bf16[384,384]{1,0:T(8,128)(2,1)}, bf16[384,384]{1,0:T(8,128)(2,1)S(1)}, u32[]{:S(2)}, u32[]{:S(2)}) collective-permute-start(bf16[384,384]{1,0:T(8,128)(2,1)} %get-tuple-element.169), channel_id=1, source_target_pairs={{0,2},{2,0},{1,3},{3,1},{4,6},{6,4},{5,7},{7,5},{8,10},{10,8},{9,1... | collective-permute-start | bytes 884744 | tf_op jit(solution)/shard_map/ppermute | solution.py:840
  150.9 18.3 %collective-permute-start.20 = (bf16[96,1536]{1,0:T(8,128)(2,1)S(1)}, bf16[96,1536]{1,0:T(8,128)(2,1)S(1)}, u32[]{:S(2)}, u32[]{:S(2)}) collective-permute-start(bf16[96,1536]{1,0:T(8,128)(2,1)S(1)} %copy-done.48), channel_id=1, source_target_pairs={{0,8},{8,0},{1,9},{9,1},{2,10},{10,2},{3,11},{11,3},{4,12},{12,4},... | collective-permute-start | bytes 884744 | tf_op jit(solution)/shard_map/ppermute | solution.py:840
  153.0 8.6 %copy-start.43 = (f32[256,768]{1,0:T(8,128)S(1)}, f32[256,768]{1,0:T(8,128)}, u32[]{:S(2)}) copy-start(f32[256,768]{1,0:T(8,128)} %get-tuple-element.162.refs_4_) | copy-start | bytes 2359300
  154.0 7.5 %copy-start.5 = (bf16[512,768]{1,0:T(8,128)(2,1)S(1)}, bf16[512,768]{1,0:T(8,128)(2,1)}, u32[]{:S(2)}) copy-start(bf16[512,768]{1,0:T(8,128)(2,1)} %refs_2_.5) | copy-start | bytes 2359300
  154.1 7.5 %copy-start.40 = (f32[768]{0:T(1024)S(1)}, f32[768]{0:T(1024)}, u32[]{:S(2)}) copy-start(f32[768]{0:T(1024)} %refs_3_.7) | copy-start | bytes 9220
  154.1 7.5 %copy-start.44 = (bf16[256,768]{1,0:T(8,128)(2,1)S(1)}, bf16[256,768]{1,0:T(8,128)(2,1)}, u32[]{:S(2)}) copy-start(bf16[256,768]{1,0:T(8,128)(2,1)} %get-tuple-element.160.refs_0_) | copy-start | bytes 1179652
  154.1 18.4 %collective-permute-start.19 = (bf16[192,1152]{1,0:T(8,128)(2,1)}, bf16[192,1152]{1,0:T(8,128)(2,1)S(1)}, u32[]{:S(2)}, u32[]{:S(2)}) collective-permute-start(bf16[192,1152]{1,0:T(8,128)(2,1)} %get-tuple-element.174), channel_id=1, source_target_pairs={{0,4},{4,0},{1,5},{5,1},{2,6},{6,2},{3,7},{7,3},{8,12},{12,8},{9,1... | collective-permute-start | bytes 1327112 | tf_op jit(solution)/shard_map/ppermute | solution.py:840
  159.5 16.3 %collective-permute-start.23 = (bf16[96,1920]{1,0:T(8,128)(2,1)}, bf16[96,1920]{1,0:T(8,128)(2,1)S(1)}, u32[]{:S(2)}, u32[]{:S(2)}) collective-permute-start(bf16[96,1920]{1,0:T(8,128)(2,1)} %get-tuple-element.184), channel_id=1, source_target_pairs={{0,4},{4,0},{1,5},{5,1},{2,6},{6,2},{3,7},{7,3},{8,12},{12,8},{9,1... | collective-permute-start | bytes 1105928 | tf_op jit(solution)/shard_map/ppermute | solution.py:840
  161.6 7.7 %copy-start.24 = (bf16[96,1536]{1,0:T(8,128)(2,1)S(1)}, bf16[96,1536]{1,0:T(8,128)(2,1)}, u32[]{:S(2)}) copy-start(bf16[96,1536]{1,0:T(8,128)(2,1)} %get-tuple-element.175.refs_0_) | copy-start | bytes 884740
  161.6 10.9 %copy-start.19 = (bf16[192,1152]{1,0:T(8,128)(2,1)S(1)}, bf16[192,1152]{1,0:T(8,128)(2,1)}, u32[]{:S(2)}) copy-start(bf16[192,1152]{1,0:T(8,128)(2,1)} %get-tuple-element.173.refs_0_) | copy-start | bytes 1327108
  163.7 12.1 %all-to-all-start.4 = ((f32[32,2,48]{2,1,0:T(2,128)}), f32[32,2,48]{2,1,0:T(2,128)S(1)}, u32[]{:S(2)}, u32[]{:S(2)}) async-start(f32[32,2,48]{2,1,0:T(2,128)} %get-tuple-element.185), calls=%async_computation.4 | async-start | bytes 65536 | tf_op jit(solution)/shard_map/all_to_all | solution.py:1037
  167.4 18.5 %collective-permute-start.18 = (bf16[256,768]{1,0:T(8,128)(2,1)}, bf16[256,768]{1,0:T(8,128)(2,1)}, u32[]{:S(2)}, u32[]{:S(2)}) collective-permute-start(bf16[256,768]{1,0:T(8,128)(2,1)} %copy-done.41), channel_id=1, source_target_pairs={{0,1},{1,0},{2,3},{3,2},{4,5},{5,4},{6,7},{7,6},{8,9},{9,8},{10,11... | collective-permute-start | bytes 1179656 | tf_op jit(solution)/shard_map/ppermute | solution.py:1034
  170.1 5.8 %copy-start.22 = (bf16[96,1920]{1,0:T(8,128)(2,1)S(1)}, bf16[96,1920]{1,0:T(8,128)(2,1)}, u32[]{:S(2)}) copy-start(bf16[96,1920]{1,0:T(8,128)(2,1)} %get-tuple-element.183.refs_0_) | copy-start | bytes 1105924
  170.1 17.9 %collective-permute-start.26 = (bf16[48,1536]{1,0:T(8,128)(2,1)}, bf16[48,1536]{1,0:T(8,128)(2,1)S(1)}, u32[]{:S(2)}, u32[]{:S(2)}) collective-permute-start(bf16[48,1536]{1,0:T(8,128)(2,1)} %get-tuple-element.197), channel_id=1, source_target_pairs={{0,16},{16,0},{1,17},{17,1},{2,18},{18,2},{3,19},{19,3},{4,20},{20... | collective-permute-start | bytes 442376 | tf_op jit(solution)/shard_map/ppermute | solution.py:840
  173.4 11.8 %copy-start.26 = (bf16[96,1152]{1,0:T(8,128)(2,1)S(1)}, bf16[96,1152]{1,0:T(8,128)(2,1)}, u32[]{:S(2)}) copy-start(bf16[96,1152]{1,0:T(8,128)(2,1)} %get-tuple-element.179.refs_0_) | copy-start | bytes 663556
  173.4 11.8 %collective-permute-start.21 = (bf16[96,1152]{1,0:T(8,128)(2,1)}, bf16[96,1152]{1,0:T(8,128)(2,1)S(1)}, u32[]{:S(2)}, u32[]{:S(2)}) collective-permute-start(bf16[96,1152]{1,0:T(8,128)(2,1)} %get-tuple-element.180), channel_id=1, source_target_pairs={{0,8},{8,0},{1,9},{9,1},{2,10},{10,2},{3,11},{11,3},{4,12},{12,4},... | collective-permute-start | bytes 663560 | tf_op jit(solution)/shard_map/ppermute | solution.py:840
  175.8 10.2 %copy-start.42 = (bf16[256,768]{1,0:T(8,128)(2,1)S(1)}, bf16[256,768]{1,0:T(8,128)(2,1)}, u32[]{:S(2)}) copy-start(bf16[256,768]{1,0:T(8,128)(2,1)} %copy-done.41) | copy-start | bytes 1179652
  176.7 14.5 %collective-permute-start.25 = (bf16[48,1920]{1,0:T(8,128)(2,1)}, bf16[48,1920]{1,0:T(8,128)(2,1)S(1)}, u32[]{:S(2)}, u32[]{:S(2)}) collective-permute-start(bf16[48,1920]{1,0:T(8,128)(2,1)} %get-tuple-element.195), channel_id=1, source_target_pairs={{0,16},{16,0},{1,17},{17,1},{2,18},{18,2},{3,19},{19,3},{4,20},{20... | collective-permute-start | bytes 552968 | tf_op jit(solution)/shard_map/ppermute | solution.py:840
  185.9 7.0 %collective-permute-start.24 = (bf16[48,1152]{1,0:T(8,128)(2,1)}, bf16[48,1152]{1,0:T(8,128)(2,1)S(1)}, u32[]{:S(2)}, u32[]{:S(2)}) collective-permute-start(bf16[48,1152]{1,0:T(8,128)(2,1)} %get-tuple-element.193), channel_id=1, source_target_pairs={{0,16},{16,0},{1,17},{17,1},{2,18},{18,2},{3,19},{19,3},{4,20},{20... | collective-permute-start | bytes 331784 | tf_op jit(solution)/shard_map/ppermute | solution.py:840
  186.0 5.2 %copy-start.27 = (bf16[48,1920]{1,0:T(8,128)(2,1)S(1)}, bf16[48,1920]{1,0:T(8,128)(2,1)}, u32[]{:S(2)}) copy-start(bf16[48,1920]{1,0:T(8,128)(2,1)} %get-tuple-element.194.refs_0_) | copy-start | bytes 552964
  186.0 6.8 %copy-start.33 = (bf16[48,1152]{1,0:T(8,128)(2,1)S(1)}, bf16[48,1152]{1,0:T(8,128)(2,1)}, u32[]{:S(2)}) copy-start(bf16[48,1152]{1,0:T(8,128)(2,1)} %get-tuple-element.192.refs_0_) | copy-start | bytes 331780
  (18 other events, 33.8 us)
